TPU v7x, 32 devices: a whole 2x2x4 slice. The times are simulated.
32 devices in a mesh: fsdp: 4 (over y, x), tp: 8 (over z, core).
Axes of the slice: x: 2, y: 2, z: 4, core: 2. Of those that a mesh axis runs over, the one named last changes fastest.
Arguments:
- layer_input: bfloat16 [16384, 2048], P(('fsdp', 'tp')), may hold values from -10 to 10
- inward_weight: float32 [3, 2048, 2048], P(None, 'fsdp', 'tp'), may hold values from -1 to 1
- outward_weight: float32 [2048, 2048], P('fsdp', 'tp'), may hold values from -1.5 to 1.5
- expand_weight: float32 [2, 2048, 8192], P(None, 'fsdp', 'tp'), may hold values from -0.125 to 0.125
- shrink_weight: float32 [2048, 8192], P('fsdp', 'tp'), may hold values from -0.0625 to 0.0625
- norm_gains: float32 [2, 2048], replicated, may hold values from 0.5 to 1.5
- cotangent: bfloat16 [16384, 2048], P(('fsdp', 'tp')), may hold values from -6 to 6
- inward_momentum: float32 [3, 2048, 2048], P(None, 'fsdp', 'tp'), may hold values from -0.00024414062 to 0.00024414062
- inward_variance: float32 [3, 2048, 2048], P(None, 'fsdp', 'tp'), may hold values from 4.0233136e-11 to 4.0233137e-09
- outward_momentum: float32 [2048, 2048], P('fsdp', 'tp'), may hold values from -6.1035156e-05 to 6.1035156e-05
- outward_variance: float32 [2048, 2048], P('fsdp', 'tp'), may hold values from 2.026558e-12 to 2.026558e-10
- expand_momentum: float32 [2, 2048, 8192], P(None, 'fsdp', 'tp'), may hold values from -7.6293945e-05 to 7.6293945e-05
- expand_variance: float32 [2, 2048, 8192], P(None, 'fsdp', 'tp'), may hold values from 3.6507845e-12 to 3.6507844e-10
- shrink_momentum: float32 [2048, 8192], P('fsdp', 'tp'), may hold values from -0.00015258789 to 0.00015258789
- shrink_variance: float32 [2048, 8192], P('fsdp', 'tp'), may hold values from 1.3411045e-11 to 1.3411046e-09
- gains_momentum: float32 [2, 2048], replicated, may hold values from -0.00036621094 to 0.00036621094
- gains_variance: float32 [2, 2048], replicated, may hold values from 8.046627e-11 to 8.046627e-09
Outputs:
- layer_output: bfloat16 [16384, 2048], P(('fsdp', 'tp'))
- input_grad: bfloat16 [16384, 2048], P(('fsdp', 'tp'))
- inward_grad: float32 [3, 2048, 2048], P(None, 'fsdp', 'tp')
- outward_grad: float32 [2048, 2048], P('fsdp', 'tp')
- expand_grad: float32 [2, 2048, 8192], P(None, 'fsdp', 'tp')
- shrink_grad: float32 [2048, 8192], P('fsdp', 'tp')
- gains_grad: float32 [2, 2048], replicated
- inward_updated: float32 [3, 2048, 2048], P(None, 'fsdp', 'tp')
- outward_updated: float32 [2048, 2048], P('fsdp', 'tp')
- expand_updated: float32 [2, 2048, 8192], P(None, 'fsdp', 'tp')
- shrink_updated: float32 [2048, 8192], P('fsdp', 'tp')
- gains_updated: float32 [2, 2048], replicated
- inward_momentum_next: float32 [3, 2048, 2048], P(None, 'fsdp', 'tp')
- inward_variance_next: float32 [3, 2048, 2048], P(None, 'fsdp', 'tp')
- outward_momentum_next: float32 [2048, 2048], P('fsdp', 'tp')
- outward_variance_next: float32 [2048, 2048], P('fsdp', 'tp')
- expand_momentum_next: float32 [2, 2048, 8192], P(None, 'fsdp', 'tp')
- expand_variance_next: float32 [2, 2048, 8192], P(None, 'fsdp', 'tp')
- shrink_momentum_next: float32 [2048, 8192], P('fsdp', 'tp')
- shrink_variance_next: float32 [2048, 8192], P('fsdp', 'tp')
- gains_momentum_next: float32 [2, 2048], replicated
- gains_variance_next: float32 [2, 2048], replicated
All inputs are finite; a program needn't handle non-finite values.
Results may differ from a plain program's by a relative error of at most 0.022.
Values may be sent and summed in bfloat16 or wider, within the bound.
A program may use at most 320 MiB of HBM per device.

v0:
```python
import jax
import jax.numpy as jnp
from jax import lax
from jax.sharding import PartitionSpec as P

HD = 64
LEN = 1024
STEP = 4


epsilon = 1e-05
rope_base = 130000.0
beta_first = 0.9
beta_second = 0.95
matrix_rate = 0.01
outward_rate = 0.1
gains_rate = 0.4
decay_rate = 0.1
adam_epsilon = 1e-08
clip_bound = 1.0
masked_score = -1e30
contract_last = (((1,), (1,)), ((), ()))


def rope_tables(length, width):
    half = width // 2
    frequency = rope_base ** (-jnp.arange(half, dtype=jnp.float32) * 2.0 / width)
    angle = jnp.arange(length, dtype=jnp.float32)[:, None] * frequency[None, :]
    return (jnp.cos(angle)[:, None, :], jnp.sin(angle)[:, None, :])


def rotate(value, cosine, sine):
    half = value.shape[-1] // 2
    first_half = value[..., :half]
    second_half = value[..., half:]
    return jnp.concatenate(
        [first_half * cosine - second_half * sine, second_half * cosine + first_half * sine],
        axis=-1,
    )


def unrotate(grad, cosine, sine):
    half = grad.shape[-1] // 2
    first_half = grad[..., :half]
    second_half = grad[..., half:]
    return jnp.concatenate(
        [first_half * cosine + second_half * sine, second_half * cosine - first_half * sine],
        axis=-1,
    )


def norm_scale(value):
    return lax.rsqrt(jnp.mean(value * value, axis=-1, keepdims=True) + epsilon)


def norm_back(grad, normed, scale, gain):
    scaled = grad * gain
    inner = jnp.mean(scaled * normed, axis=-1, keepdims=True)
    return (scale * (scaled - normed * inner), jnp.sum(grad * normed, axis=0))


def causal(begin, block, length):
    return jnp.arange(length)[None, :] <= (begin + jnp.arange(block))[:, None]


def block_scores(query_block, keys, begin, block, length, scale):
    scores = (
        jnp.einsum("qhd,khd->hqk", query_block, keys, preferred_element_type=jnp.float32) * scale
    )
    return jnp.where(causal(begin, block, length)[None], scores, masked_score)


def attend_forward(query, keys, values):
    length = query.shape[1]
    block = min(length, 512)
    scale = query.shape[-1] ** (-0.5)

    def per_sequence(triple):
        query_seq, keys_seq, values_seq = triple
        outputs = []
        logsums = []
        for begin in range(0, length, block):
            scores = block_scores(
                query_seq[begin : begin + block], keys_seq, begin, block, length, scale
            )
            largest = jnp.max(scores, axis=-1, keepdims=True)
            expo = jnp.exp(scores - largest)
            totals = jnp.sum(expo, axis=-1, keepdims=True)
            prob = (expo / totals).astype(jnp.bfloat16)
            outputs.append(
                jnp.einsum(
                    "hqk,khd->qhd", prob, values_seq, preferred_element_type=jnp.float32
                ).astype(jnp.bfloat16)
            )
            logsums.append(largest + jnp.log(totals))
        return (jnp.concatenate(outputs, axis=0), jnp.concatenate(logsums, axis=1))

    return lax.map(per_sequence, (query, keys, values))


def attend_backward(query, keys, values, grad_mixed, logsum):
    length = query.shape[1]
    block = min(length, 512)
    scale = query.shape[-1] ** (-0.5)

    def per_sequence(items):
        query_seq, keys_seq, values_seq, grad_seq, logsum_seq = items
        grad_keys = jnp.zeros(keys_seq.shape, jnp.float32)
        grad_values = jnp.zeros(values_seq.shape, jnp.float32)
        grad_queries = []
        for begin in range(0, length, block):
            query_block = query_seq[begin : begin + block]
            grad_block = grad_seq[begin : begin + block]
            scores = block_scores(query_block, keys_seq, begin, block, length, scale)
            prob = jnp.exp(scores - logsum_seq[:, begin : begin + block])
            grad_values = grad_values + jnp.einsum(
                "hqk,qhd->khd",
                prob.astype(jnp.bfloat16),
                grad_block,
                preferred_element_type=jnp.float32,
            )
            grad_prob = jnp.einsum(
                "qhd,khd->hqk", grad_block, values_seq, preferred_element_type=jnp.float32
            )
            delta = jnp.sum(prob * grad_prob, axis=-1, keepdims=True)
            grad_scores = (prob * (grad_prob - delta)).astype(jnp.bfloat16)
            grad_queries.append(
                jnp.einsum(
                    "hqk,khd->qhd", grad_scores, keys_seq, preferred_element_type=jnp.float32
                )
                * scale
            )
            grad_keys = (
                grad_keys
                + jnp.einsum(
                    "hqk,qhd->khd", grad_scores, query_block, preferred_element_type=jnp.float32
                )
                * scale
            )
        return (jnp.concatenate(grad_queries, axis=0), grad_keys, grad_values)

    return lax.map(per_sequence, (query, keys, values, grad_mixed, logsum))


def adamw(weight, grad, first, second, decay, rate):
    first = beta_first * first + (1.0 - beta_first) * grad
    second = beta_second * second + (1.0 - beta_second) * grad * grad
    first_hat = first / (1.0 - beta_first**STEP)
    second_hat = second / (1.0 - beta_second**STEP)
    weight = weight - rate * (first_hat / (jnp.sqrt(second_hat) + adam_epsilon) + decay * weight)
    return (weight, first, second)


def expand_rows(feed_all, expand_full):
    gate_up = jnp.einsum("td,cdf->ctf", feed_all, expand_full, preferred_element_type=jnp.float32)
    hidden = (jax.nn.silu(gate_up[0]) * gate_up[1]).astype(jnp.bfloat16)
    return (gate_up, hidden)


def body(
    layer_input,
    inward_weight,
    outward_weight,
    expand_weight,
    shrink_weight,
    norm_gains,
    cotangent,
    inward_momentum,
    inward_variance,
    outward_momentum,
    outward_variance,
    expand_momentum,
    expand_variance,
    shrink_momentum,
    shrink_variance,
    gains_momentum,
    gains_variance,
):
    local_rows = layer_input.shape[0]
    shards = (
        inward_weight.astype(jnp.bfloat16),
        outward_weight.astype(jnp.bfloat16),
        expand_weight.astype(jnp.bfloat16),
        shrink_weight.astype(jnp.bfloat16),
    )
    gathered = (
        lax.all_gather(shards[0], "fsdp", axis=1, tiled=True),
        lax.all_gather(shards[1], "fsdp", axis=0, tiled=True),
        lax.all_gather(shards[2], "fsdp", axis=1, tiled=True),
        lax.all_gather(shards[3], "fsdp", axis=0, tiled=True),
    )
    inward_full, outward_full, expand_full, shrink_full = gathered
    source = layer_input.astype(jnp.float32)
    scale_one = norm_scale(source)
    normed_one = source * scale_one
    acts = lax.all_gather(
        (normed_one * norm_gains[0]).astype(jnp.bfloat16), "tp", axis=0, tiled=True
    )
    group_rows = acts.shape[0]
    seqs = group_rows // LEN
    local_width = inward_full.shape[2]
    heads = local_width // HD
    cosine, sine = rope_tables(LEN, HD)
    shape = (seqs, LEN, heads, HD)
    proj = jnp.einsum("td,cde->cte", acts, inward_full, preferred_element_type=jnp.float32)
    query = rotate(proj[0].reshape(shape), cosine, sine).astype(jnp.bfloat16)
    keys = rotate(proj[1].reshape(shape), cosine, sine).astype(jnp.bfloat16)
    values = proj[2].reshape(shape).astype(jnp.bfloat16)
    mixed, logsum = attend_forward(query, keys, values)
    mixed = mixed.reshape(group_rows, local_width)
    part_rows = lax.slice_in_dim(mixed, 0, local_rows * lax.axis_size("tp"), axis=0)
    resid = source + lax.psum_scatter(
        lax.dot_general(part_rows, outward_full, contract_last, preferred_element_type=jnp.float32),
        "tp",
        scatter_dimension=0,
        tiled=True,
    )
    scale_two = norm_scale(resid)
    normed_two = resid * scale_two
    feed_local = (normed_two * norm_gains[1]).astype(jnp.bfloat16)
    feed_all = lax.all_gather(feed_local, "tp", axis=0, tiled=True)
    gate_up, hidden = expand_rows(feed_all, expand_full)
    part_rows = lax.slice_in_dim(hidden, 0, lax.axis_size("tp") * local_rows, axis=0)
    fed = lax.psum_scatter(
        lax.dot_general(
            part_rows, shrink_full, contract_last, preferred_element_type=jnp.float32
        ).astype(jnp.bfloat16),
        "tp",
        scatter_dimension=0,
        tiled=True,
    ).astype(jnp.float32)
    layer_output = (resid + fed).astype(jnp.bfloat16)
    inward_back, outward_back, expand_back, shrink_back = (
        lax.all_gather(shards[0], "fsdp", axis=1, tiled=True),
        lax.all_gather(shards[1], "fsdp", axis=0, tiled=True),
        lax.all_gather(shards[2], "fsdp", axis=1, tiled=True),
        lax.all_gather(shards[3], "fsdp", axis=0, tiled=True),
    )
    grad_out = lax.all_gather(cotangent, "tp", axis=0, tiled=True)
    grad_hidden = jnp.dot(grad_out, shrink_back, preferred_element_type=jnp.float32)
    gate = gate_up[0]
    sigma = jax.nn.sigmoid(gate)
    grad_gate = grad_hidden * gate_up[1] * sigma * (1.0 + gate * (1.0 - sigma))
    grad_up = grad_hidden * (gate * sigma)
    grad_gate_up = jnp.stack([grad_gate, grad_up]).astype(jnp.bfloat16)
    shrink_full_grad = jnp.einsum("td,tf->df", grad_out, hidden, preferred_element_type=jnp.float32)
    expand_full_grad = jnp.einsum(
        "td,ctf->cdf", feed_all, grad_gate_up, preferred_element_type=jnp.float32
    )
    part_rows = lax.slice_in_dim(grad_gate_up, 0, lax.axis_size("tp") * local_rows, axis=1)
    grad_feed = lax.psum_scatter(
        jnp.einsum(
            "ctf,cdf->td", part_rows, expand_back, preferred_element_type=jnp.float32
        ).astype(jnp.bfloat16),
        "tp",
        scatter_dimension=0,
        tiled=True,
    ).astype(jnp.float32)
    resid_back, gain_two = norm_back(grad_feed, normed_two, scale_two, norm_gains[1])
    grad_resid = cotangent.astype(jnp.float32) + resid_back
    grad_attn = lax.all_gather(grad_resid.astype(jnp.bfloat16), "tp", axis=0, tiled=True)
    outward_full_grad = jnp.einsum(
        "td,te->de", grad_attn, mixed, preferred_element_type=jnp.float32
    )
    grad_mixed = jnp.dot(grad_attn, outward_back, preferred_element_type=jnp.float32).astype(
        jnp.bfloat16
    )
    grad_query, grad_keys, grad_values = attend_backward(
        query, keys, values, grad_mixed.reshape(shape), logsum
    )
    grad_proj = jnp.stack(
        [
            unrotate(grad_query, cosine, sine).reshape(group_rows, local_width),
            unrotate(grad_keys, cosine, sine).reshape(group_rows, local_width),
            grad_values.reshape(group_rows, local_width),
        ]
    ).astype(jnp.bfloat16)
    inward_full_grad = jnp.einsum(
        "td,cte->cde", acts, grad_proj, preferred_element_type=jnp.float32
    )
    part_rows = lax.slice_in_dim(grad_proj, 0, lax.axis_size("tp") * local_rows, axis=1)
    grad_acts = lax.psum_scatter(
        jnp.einsum(
            "cte,cde->td", part_rows, inward_back, preferred_element_type=jnp.float32
        ).astype(jnp.bfloat16),
        "tp",
        scatter_dimension=0,
        tiled=True,
    ).astype(jnp.float32)
    input_back, gain_one = norm_back(grad_acts, normed_one, scale_one, norm_gains[0])
    input_grad = (grad_resid + input_back).astype(jnp.bfloat16)
    inward_grad, outward_grad, expand_grad, shrink_grad = (
        lax.psum_scatter(
            inward_full_grad.astype(jnp.bfloat16), "fsdp", scatter_dimension=1, tiled=True
        ).astype(jnp.float32),
        lax.psum_scatter(
            outward_full_grad.astype(jnp.bfloat16), "fsdp", scatter_dimension=0, tiled=True
        ).astype(jnp.float32),
        lax.psum_scatter(
            expand_full_grad.astype(jnp.bfloat16), "fsdp", scatter_dimension=1, tiled=True
        ).astype(jnp.float32),
        lax.psum_scatter(
            shrink_full_grad.astype(jnp.bfloat16), "fsdp", scatter_dimension=0, tiled=True
        ).astype(jnp.float32),
    )
    owned_squares = (
        jnp.sum(inward_grad * inward_grad)
        + jnp.sum(outward_grad * outward_grad)
        + jnp.sum(expand_grad * expand_grad)
        + jnp.sum(shrink_grad * shrink_grad)
    )
    gains_grad, squares = lax.psum((jnp.stack([gain_one, gain_two]), owned_squares), ("fsdp", "tp"))
    norm = jnp.sqrt(squares + jnp.sum(gains_grad * gains_grad))
    factor = jnp.minimum(1.0, clip_bound / (norm + 1e-06))
    inward_new = adamw(
        inward_weight,
        factor * inward_grad,
        inward_momentum,
        inward_variance,
        decay_rate,
        matrix_rate,
    )
    outward_new = adamw(
        outward_weight,
        factor * outward_grad,
        outward_momentum,
        outward_variance,
        decay_rate,
        outward_rate,
    )
    expand_new = adamw(
        expand_weight,
        factor * expand_grad,
        expand_momentum,
        expand_variance,
        decay_rate,
        matrix_rate,
    )
    shrink_new = adamw(
        shrink_weight,
        factor * shrink_grad,
        shrink_momentum,
        shrink_variance,
        decay_rate,
        matrix_rate,
    )
    gains_new = adamw(
        norm_gains, factor * gains_grad, gains_momentum, gains_variance, 0.0, gains_rate
    )
    return (
        layer_output,
        input_grad,
        inward_grad,
        outward_grad,
        expand_grad,
        shrink_grad,
        gains_grad,
        inward_new[0],
        outward_new[0],
        expand_new[0],
        shrink_new[0],
        gains_new[0],
        inward_new[1],
        inward_new[2],
        outward_new[1],
        outward_new[2],
        expand_new[1],
        expand_new[2],
        shrink_new[1],
        shrink_new[2],
        gains_new[1],
        gains_new[2],
    )


def solution(mesh):
    placed = (
        P(("fsdp", "tp"), None),
        P(None, "fsdp", "tp"),
        P("fsdp", "tp"),
        P(None, "fsdp", "tp"),
        P("fsdp", "tp"),
        P(),
        P(("fsdp", "tp"), None),
        P(None, "fsdp", "tp"),
        P(None, "fsdp", "tp"),
        P("fsdp", "tp"),
        P("fsdp", "tp"),
        P(None, "fsdp", "tp"),
        P(None, "fsdp", "tp"),
        P("fsdp", "tp"),
        P("fsdp", "tp"),
        P(),
        P(),
    )
    return jax.shard_map(
        body,
        mesh=mesh,
        in_specs=placed,
        out_specs=(
            P(("fsdp", "tp"), None),
            P(("fsdp", "tp"), None),
            P(None, "fsdp", "tp"),
            P("fsdp", "tp"),
            P(None, "fsdp", "tp"),
            P("fsdp", "tp"),
            P(),
            P(None, "fsdp", "tp"),
            P("fsdp", "tp"),
            P(None, "fsdp", "tp"),
            P("fsdp", "tp"),
            P(),
            P(None, "fsdp", "tp"),
            P(None, "fsdp", "tp"),
            P("fsdp", "tp"),
            P("fsdp", "tp"),
            P(None, "fsdp", "tp"),
            P(None, "fsdp", "tp"),
            P("fsdp", "tp"),
            P("fsdp", "tp"),
            P(),
            P(),
        ),
        check_vma=False,
    )
```

profile of v0, /device:TPU:0, one launch (start us, length us, event | category | flops | bytes accessed | tf_op | source)
XLA Modules:
  0.0 2413.2 jit_solution(14397855553712930378)
XLA Ops:
  14.9 42.2 %all-gather.11.cloned.1.call-done = bf16[3,2048,256]{2,1,0:T(8,128)(2,1)} async-done(((bf16[3,512,256]{2,1,0:T(8,128)(2,1)}), bf16[3,2048,256]{2,1,0:T(8,128)(2,1)}) %all-gather.11.cloned.1.call-update) | async-done | bytes 3145744 | tf_op jit(solution)/shard_map/all_gather | solution.py:187
  57.2 153.3 %all-gather.9.cloned.1.call-done = bf16[4096,2048]{1,0:T(8,128)(2,1)} async-done(((bf16[512,2048]{1,0:T(8,128)(2,1)}), bf16[4096,2048]{1,0:T(8,128)(2,1)}) %all-gather.9.cloned.1.call-update) | async-done | bytes 16777232 | tf_op jit(solution)/shard_map/all_gather | solution.py:196
  280.9 75.3 %while.26 = (s32[]{:T(128)}, bf16[4,1024,4,64]{1,3,2,0:T(8,128)(2,1)}, f32[4,4,1024,1]{2,1,3,0:T(4,128)}, bf16[4,1024,4,64]{1,3,2,0:T(8,128)(2,1)}, bf16[4,1024,...) while((s32[]{:T(128)}, ...), condition=%wide.region_6.7_spmd, body=%wide.region_1.6_spmd.sunk | while | flops 1126433280 | bytes 134388944 | solution.py:98
  384.0 319.8 %reduce-scatter.9.cloned.1.call-done = f32[512,2048]{1,0:T(8,128)} async-done(((f32[4096,2048]{1,0:T(8,128)}), f32[512,2048]{1,0:T(8,128)}) %reduce-scatter.9.cloned.1.call-update) | async-done | bytes 4194320 | tf_op jit(solution)/shard_map/reduce_scatter | solution.py:212
  712.6 79.6 %all-gather.17.cloned.1.call-done = bf16[2,2048,1024]{2,1,0:T(8,128)(2,1)} async-done(((bf16[2,512,1024]{2,1,0:T(8,128)(2,1)}), bf16[2,2048,1024]{2,1,0:T(8,128)(2,1)}) %all-gather.17.cloned.1.call-update) | async-done | bytes 8388624 | tf_op jit(solution)/shard_map/all_gather | solution.py:189
  792.2 153.3 %all-gather.15.cloned.1.call-done = bf16[4096,2048]{1,0:T(8,128)(2,1)} async-done(((bf16[512,2048]{1,0:T(8,128)(2,1)}), bf16[4096,2048]{1,0:T(8,128)(2,1)}) %all-gather.15.cloned.1.call-update) | async-done | bytes 16777232 | tf_op jit(solution)/shard_map/all_gather | solution.py:221
  945.5 43.3 %fusion.91 = f32[2,4096,1024]{2,1,0:T(8,128)} fusion(bf16[2,2048,1024]{2,1,0:T(8,128)(2,1)} %all-gather.17.cloned.1.call-done, bf16[4096,2048]{1,0:T(8,128)(2,1)} %all-gather.15.cloned.1.call-done), kind=kOutput, calls=%fused_computation.128 | convolution fusion | flops 34359738368 | bytes 58720256 | tf_op jit(solution)/shard_map/td,cdf->ctf/dot_general | solution.py:155
  999.0 152.8 %all-gather.21.cloned.1.call-done = bf16[4096,2048]{1,0:T(8,128)(2,1)} async-done(((bf16[512,2048]{1,0:T(8,128)(2,1)}), bf16[4096,2048]{1,0:T(8,128)(2,1)}) %all-gather.21.cloned.1.call-update) | async-done | bytes 16777232 | tf_op jit(solution)/shard_map/all_gather | solution.py:239
  1151.8 34.4 %fusion.95 = (bf16[1,4096,1024]{2,1,0:T(8,128)(2,1)}, bf16[1,4096,1024]{2,1,0:T(8,128)(2,1)}, bf16[4096,1024]{1,0:T(8,128)(2,1)}) fusion(f32[2,4096,1024]{2,1,0:T(8,128)} %fusion.91, bf16[4096,2048]{1,0:T(8,128)(2,1)} %all-gather.21.cloned.1.call-done, bf16[2048,1024]{1,0:T(8,128)(2,1)} %all-gather.19.cloned.1.call-done), kind=kOutput, calls=%fused_computation.131 | convolution fusion | flops 17242783744 | bytes 79691776 | tf_op jit(solution)/shard_map/dot_general | solution.py:240
  1186.3 42.2 %bitcast_convert_fusion.1 = bf16[4096,2048]{1,0:T(8,128)(2,1)} fusion(bf16[2,2048,1024]{2,1,0:T(8,128)(2,1)} %all-gather.17.cloned.1.call-done, bf16[1,4096,1024]{2,1,0:T(8,128)(2,1)} %get-tuple-element.253, bf16[1,4096,1024]{2,1,0:T(8,128)(2,1)} %get-tuple-element.252), kind=kOutput, calls=%fused_computation.110 | convolution fusion | flops 34376515584 | bytes 41943040 | tf_op jit(solution)/shard_map/ctf,cdf->td/dot_general | solution.py:252
  1228.6 166.6 %reduce-scatter.13.cloned.1.call-done = bf16[512,2048]{1,0:T(8,128)(2,1)} async-done(((bf16[4096,2048]{1,0:T(8,128)(2,1)}), bf16[512,2048]{1,0:T(8,128)(2,1)}) %reduce-scatter.13.cloned.1.call-update) | async-done | bytes 2097168 | tf_op jit(solution)/shard_map/reduce_scatter | solution.py:251
  1404.8 23.8 convert_bitcast_fusion.1
  1428.7 44.0 %convert_bitcast_fusion = bf16[2,2048,1024]{1,2,0:T(8,128)(2,1)} fusion(bf16[4096,2048]{1,0:T(8,128)(2,1)} %all-gather.15.cloned.1.call-done, bf16[1,4096,1024]{2,1,0:T(8,128)(2,1)} %get-tuple-element.253, bf16[1,4096,1024]{2,1,0:T(8,128)(2,1)} %get-tuple-element.252), kind=kOutput, calls=%fused_computation.130 | convolution fusion | flops 34372321280 | bytes 41943040 | tf_op jit(solution)/shard_map/td,ctf->cdf/dot_general | solution.py:247
  1472.8 81.5 %all-gather.23.cloned.1.call-done = bf16[4096,2048]{1,0:T(8,128)(2,1)} async-done(((bf16[512,2048]{1,0:T(8,128)(2,1)}), bf16[4096,2048]{1,0:T(8,128)(2,1)}) %all-gather.23.cloned.1.call-update) | async-done | bytes 16777232 | tf_op jit(solution)/shard_map/all_gather | solution.py:261
  1573.0 375.8 %while.27 = (s32[]{:T(128)}, f32[4,1024,4,64]{1,0,3,2:T(4,128)}, f32[4,1024,4,64]{1,0,3,2:T(4,128)}, bf16[4,1024,4,64]{1,3,2,0:T(8,128)(2,1)}, bf16[4,1024,4,64]...) while((s32[]{:T(128)}, f32[4,1024,4,64]{1,0,3,2:T(4,128)}, ...), condition=%wide.region_15.16_spmd, body=%wide.region_12.15_spmd.sunk | while | flops 2749624832 | bytes 279079744 | solution.py:142
  1607.6 20.1 dynamic_update_slice.30
  1635.1 20.2 dynamic_update_slice.29
  1702.0 20.0 dynamic_update_slice.30
  1729.3 20.0 dynamic_update_slice.29
  1795.4 20.0 dynamic_update_slice.30
  2035.7 23.8 convolution_convert_fusion
  2111.4 117.6 %reduce-scatter.15.cloned.1.call-done = bf16[512,2048]{1,0:T(8,128)(2,1)} async-done(((bf16[4096,2048]{1,0:T(8,128)(2,1)}), bf16[512,2048]{1,0:T(8,128)(2,1)}) %reduce-scatter.15.cloned.1.call-update) | async-done | bytes 2097168 | tf_op jit(solution)/shard_map/reduce_scatter | solution.py:282
  2231.9 40.2 %all-reduce = (f32[2,2048]{1,0:T(2,128)S(1)}, f32[]{:T(128)}) all-reduce(f32[2,2048]{1,0:T(2,128)S(1)} %pad_maximum_fusion.12, f32[]{:T(128)S(6)} %add.233), channel_id=1, replica_groups=mesh['fsdp'=4,'tp'=8] {'fsdp','tp'}, use_global_device_ids=true, to_apply=%region_24.25 | all-reduce | flops 4097 | bytes 32776 | tf_op jit(solution)/shard_map/psum | solution.py:312
  2334.2 64.7 %reduce-scatter.11.cloned.1.call-done = bf16[512,2048]{1,0:T(8,128)(2,1)} async-done(((bf16[4096,2048]{1,0:T(8,128)(2,1)}), bf16[512,2048]{1,0:T(8,128)(2,1)}) %reduce-scatter.11.cloned.1.call-update) | async-done | bytes 2097168 | tf_op jit(solution)/shard_map/reduce_scatter | solution.py:224
  (410 shorter events, 709.1 us)
Async XLA Ops:
  7.2 50.0 %all-gather.11.cloned.1.call-start = ((), (), s32[]{:S(2)}) async-start(), calls=%async_computation.9 | async-start | bytes 3932160 | tf_op jit(solution)/shard_map/all_gather | solution.py:187
  9.8 200.7 %all-gather.9.cloned.1.call-start = ((), (), s32[]{:S(2)}) async-start(), calls=%async_computation.8 | async-start | bytes 18874368 | tf_op jit(solution)/shard_map/all_gather | solution.py:196
  13.5 348.9 %all-gather.13.cloned.1.call-start = ((), (), s32[]{:S(2)}) async-start(), calls=%async_computation.10 | async-start | bytes 1310720 | tf_op jit(solution)/shard_map/all_gather | solution.py:188
  14.3 689.5 %reduce-scatter.9.cloned.1.call-start = ((), (), s32[]{:S(2)}) async-start(), calls=%async_computation.11 | async-start | bytes 37748736 | tf_op jit(solution)/shard_map/reduce_scatter | solution.py:212
  14.9 241.8 %copy-start.29 = (f32[1024,32]{0,1:T(8,128)}, f32[1024,32]{0,1:T(8,128)S(1)}, u32[]{:S(2)}) copy-start(f32[1024,32]{0,1:T(8,128)S(1)} %get-tuple-element.273) | copy-start | bytes 393220
  14.9 241.8 %copy-start.31 = (f32[1024,32]{0,1:T(8,128)}, f32[1024,32]{0,1:T(8,128)S(1)}, u32[]{:S(2)}) copy-start(f32[1024,32]{0,1:T(8,128)S(1)} %get-tuple-element.274) | copy-start | bytes 393220
  379.9 323.9 %copy-start.12 = (bf16[512,2048]{1,0:T(8,128)(2,1)S(1)}, bf16[512,2048]{1,0:T(8,128)(2,1)}, u32[]{:S(2)}) copy-start(bf16[512,2048]{1,0:T(8,128)(2,1)} %param.21) | copy-start | bytes 6291460
  379.9 412.3 %all-gather.17.cloned.1.call-start = ((), (), s32[]{:S(2)}) async-start(), calls=%async_computation.13 | async-start | bytes 10485760 | tf_op jit(solution)/shard_map/all_gather | solution.py:189
  383.9 324.7 %copy-start.34 = (f32[1,2048]{1,0:T(1,128)S(1)}, f32[1,2048]{1,0:T(1,128)}, u32[]{:S(2)}) copy-start(f32[1,2048]{1,0:T(1,128)} %get-tuple-element.271) | copy-start | bytes 24580
  383.9 561.5 %all-gather.15.cloned.1.call-start = ((), (), s32[]{:S(2)}) async-start(), calls=%async_computation.12 | async-start | bytes 18874368 | tf_op jit(solution)/shard_map/all_gather | solution.py:221
  710.4 288.6 %all-gather.19.cloned.1.call-start = ((), (), s32[]{:S(2)}) async-start(), calls=%async_computation.14 | async-start | bytes 5242880 | tf_op jit(solution)/shard_map/all_gather | solution.py:190
  711.8 440.0 %all-gather.21.cloned.1.call-start = ((), (), s32[]{:S(2)}) async-start(), calls=%async_computation.16 | async-start | bytes 18874368 | tf_op jit(solution)/shard_map/all_gather | solution.py:239
  712.6 682.5 %reduce-scatter.13.cloned.1.call-start = ((), (), s32[]{:S(2)}) async-start(), calls=%async_computation.17 | async-start | bytes 18874368 | tf_op jit(solution)/shard_map/reduce_scatter | solution.py:251
  1228.5 171.9 %copy-start.16 = (bf16[512,2048]{1,0:T(8,128)(2,1)S(1)}, bf16[512,2048]{1,0:T(8,128)(2,1)}, u32[]{:S(2)}) copy-start(bf16[512,2048]{1,0:T(8,128)(2,1)} %param.27) | copy-start | bytes 6291460
  1228.5 325.9 %all-gather.23.cloned.1.call-start = ((), (), s32[]{:S(2)}) async-start(), calls=%async_computation.18 | async-start | bytes 18874368 | tf_op jit(solution)/shard_map/all_gather | solution.py:261
  1404.8 684.3 %reduce-scatter.23.cloned.1.call-start = ((), (), s32[]{:S(2)}) async-start(), calls=%async_computation.23 | async-start | bytes 5242880 | tf_op jit(solution)/shard_map/reduce_scatter | solution.py:302
  1428.7 665.3 %reduce-scatter.21.cloned.1.call-start = ((), (), s32[]{:S(2)}) async-start(), calls=%async_computation.22 | async-start | bytes 10485760 | tf_op jit(solution)/shard_map/reduce_scatter | solution.py:299
  1472.8 628.8 %reduce-scatter.19.cloned.1.call-start = ((), (), s32[]{:S(2)}) async-start(), calls=%async_computation.21 | async-start | bytes 1310720 | tf_op jit(solution)/shard_map/reduce_scatter | solution.py:296
  1573.0 375.8 %copy-start.30 = (f32[1024,32]{0,1:T(8,128)S(1)}, f32[1024,32]{0,1:T(8,128)}, u32[]{:S(2)}) copy-start(f32[1024,32]{0,1:T(8,128)} %copy-done.29) | copy-start | bytes 393220
  1573.0 375.8 %copy-start.32 = (f32[1024,32]{0,1:T(8,128)S(1)}, f32[1024,32]{0,1:T(8,128)}, u32[]{:S(2)}) copy-start(f32[1024,32]{0,1:T(8,128)} %copy-done.31) | copy-start | bytes 393220
  1964.2 139.8 %reduce-scatter.17.cloned.1.call-start = ((), (), s32[]{:S(2)}) async-start(), calls=%async_computation.20 | async-start | bytes 3932160 | tf_op jit(solution)/shard_map/reduce_scatter | solution.py:293
  2015.9 213.1 %reduce-scatter.15.cloned.1.call-start = ((), (), s32[]{:S(2)}) async-start(), calls=%async_computation.19 | async-start | bytes 18874368 | tf_op jit(solution)/shard_map/reduce_scatter | solution.py:282
  2035.7 363.2 %reduce-scatter.11.cloned.1.call-start = ((), (), s32[]{:S(2)}) async-start(), calls=%async_computation.15 | async-start | bytes 18874368 | tf_op jit(solution)/shard_map/reduce_scatter | solution.py:224
  2101.6 172.5 %copy-start.18 = (bf16[512,1024]{0,1:T(8,128)(2,1)S(1)}, bf16[512,1024]{0,1:T(8,128)(2,1)}, u32[]{:S(2)}) copy-start(bf16[512,1024]{0,1:T(8,128)(2,1)} %reduce-scatter.23.cloned.1.call-done) | copy-start | bytes 3145732
  (71 other events, 1525.5 us)
Sparse Core Ops, SparseCore 0:
  10.5 46.6 all-gather.10
  59.4 151.0 all-gather.8
  212.9 24.8 all-gather.12
  380.0 323.7 reduce-scatter.8
  706.2 85.9 all-gather.16
  794.3 151.0 all-gather.14
  948.0 50.9 all-gather.18
  1000.7 151.0 all-gather.20
  1228.6 166.4 reduce-scatter.12
  1404.9 149.4 all-gather.22
  1558.2 50.9 reduce-scatter.22
  1612.1 86.3 reduce-scatter.20
  1964.4 26.2 reduce-scatter.18
  2016.0 42.4 reduce-scatter.16
  2060.7 168.2 reduce-scatter.14
  2231.2 167.6 reduce-scatter.10
where the time goes:
time: 2430 us; the launch traced here: 2410 us
  waiting for transfers between devices  1340 us (55%)
  matrix products  504 us (21%)
  local copies, waits for them, and re-layouts  350 us (14%)
  other arithmetic  155 us (6%)
  blocking collectives  40.2 us (2%)
    reduce_scatter x1, waiting for transfers between devices, body(): lax.psum_scatter(lax.dot_general(part_rows, outward_full, contract_last,...  320 us
    dynamic_update_slice x16, local copies, waits for them, and re-layouts, attend_backward(): return lax.map(per_sequence, (query, keys, values, grad_mixed, logsum))  177 us
    reduce_scatter x1, waiting for transfers between devices, body(): lax.psum_scatter(jnp.einsum('ctf,cdf->td', part_rows, expand_back, prefer...  167 us
    all_gather x1, waiting for transfers between devices, body(): lax.all_gather((normed_one * norm_gains[0]).astype(jnp.bfloat16), 'tp', a...  153 us
    all_gather x1, waiting for transfers between devices, body(): feed_all = lax.all_gather(feed_local, 'tp', axis=0, tiled=True)  153 us
    all_gather x1, waiting for transfers between devices, body(): grad_out = lax.all_gather(cotangent, 'tp', axis=0, tiled=True)  153 us
    reduce_scatter x1, waiting for transfers between devices, body(): lax.psum_scatter(jnp.einsum('cte,cde->td', part_rows, inward_back, prefer...  118 us
    all_gather x1, waiting for transfers between devices, body(): lax.all_gather(grad_resid.astype(jnp.bfloat16), 'tp', axis=0, tiled=True)  81.5 us
  transfers between devices with their start and end apart: 16, of which 11 were waited for; matrix products, arithmetic and copies ran while one was open for 37% of the time, Pallas kernels for 0%

commit v1 on v0

v1 whole, which is shorter than its diff:
```python
import functools

import jax
import jax.numpy as jnp
from jax import lax
from jax.experimental import pallas as pl
from jax.experimental.pallas import tpu as pltpu
from jax.sharding import PartitionSpec as P

HD = 64
LEN = 1024
STEP = 4


epsilon = 1e-05
rope_base = 130000.0
beta_first = 0.9
beta_second = 0.95
matrix_rate = 0.01
outward_rate = 0.1
gains_rate = 0.4
decay_rate = 0.1
adam_epsilon = 1e-08
clip_bound = 1.0
masked_score = -1e30
low = jnp.bfloat16
f32 = jnp.float32


def dot(a, b, dims):
    return lax.dot_general(a, b, (dims, ((), ())), preferred_element_type=f32)


NN = ((1,), (0,))
NT = ((1,), (1,))
TN = ((0,), (0,))


class Moves:
    def __init__(self, seq_parts):
        self.F = lax.axis_size("fsdp")
        self.T = lax.axis_size("tp")
        self.S = seq_parts
        self.Z = self.T // self.S
        self.f = lax.axis_index("fsdp")
        self.t = lax.axis_index("tp")
        self.s = lax.rem(self.t, self.S)

    def plane(self, value, mask):
        return lax.ppermute(value, "fsdp", [(i, i ^ mask) for i in range(self.F)])

    def mate(self, value, mask):
        return lax.ppermute(value, "tp", [(i, i ^ mask) for i in range(self.T)])

    def ring(self, value):
        step = [
            (z * self.S + s, ((z + 1) % self.Z) * self.S + s)
            for z in range(self.Z)
            for s in range(self.S)
        ]
        return lax.ppermute(value, "tp", step)

    def place(self, pieces, axis, index):
        width = pieces[0].shape[axis]
        whole = jnp.concatenate([pieces[0]] * len(pieces), axis=axis)
        for d in range(1, len(pieces)):
            whole = lax.dynamic_update_slice_in_dim(whole, pieces[d], (index ^ d) * width, axis)
        return whole

    def mates(self, value):
        return [value] + [self.mate(value, d) for d in range(1, self.S)]

    def mates_sum(self, blocks):
        total = blocks[0].astype(f32)
        for d in range(1, self.S):
            total = total + self.mate(blocks[d], d).astype(f32)
        return total

    def plane_gather(self, value, first):
        if self.F != 4:
            whole = lax.all_gather(value, "fsdp", axis=0)
            return [lax.dynamic_index_in_dim(whole, self.f ^ d, 0, False) for d in range(self.F)]
        one = self.plane(value, 1)
        two = self.plane(value, 2)
        three = self.plane(one, 2) if first == 1 else self.plane(two, 1)
        return [value, one, two, three]

    def plane_gather_rows(self, value):
        if self.F != 4:
            return self.plane_gather(value, 1)
        half = value.shape[0] // 2
        one = self.plane(value, 1)
        two = self.plane(value, 2)
        three = jnp.concatenate([self.plane(one[:half], 2), self.plane(two[half:], 1)], axis=0)
        return [value, one, two, three]

    def plane_sum(self, blocks, first):
        if self.F != 4:
            whole = self.place([b[None] for b in blocks], 0, self.f)
            return lax.psum_scatter(whole, "fsdp", scatter_dimension=0).astype(f32)
        here, one, two, three = blocks
        if first == 1:
            two = (two.astype(f32) + self.plane(three, 1).astype(f32)).astype(low)
        else:
            one = (one.astype(f32) + self.plane(three, 2).astype(f32)).astype(low)
        return here.astype(f32) + self.plane(one, 1).astype(f32) + self.plane(two, 2).astype(f32)

    def plane_sum_rows(self, blocks):
        if self.F != 4:
            return self.plane_sum(blocks, 1)
        here, one, two, three = blocks
        half = here.shape[0] // 2
        to_two = self.plane(three[:half], 1)
        to_one = self.plane(three[half:], 2)
        two = jnp.concatenate(
            [(two[:half].astype(f32) + to_two.astype(f32)).astype(low), two[half:]], axis=0
        )
        one = jnp.concatenate(
            [one[:half], (one[half:].astype(f32) + to_one.astype(f32)).astype(low)], axis=0
        )
        return here.astype(f32) + self.plane(one, 1).astype(f32) + self.plane(two, 2).astype(f32)

    def ring_gather(self, value):
        pieces = [value]
        for _ in range(self.Z - 1):
            pieces.append(self.ring(pieces[-1]))
        return pieces

    def ring_sum(self, blocks):
        total = blocks[1]
        for k in list(range(2, self.Z)) + [0]:
            total = self.ring(total.astype(low)).astype(f32) + blocks[k].astype(f32)
        return total

    def total(self, value):
        for d in range(self.F.bit_length() - 1):
            value = value + self.plane(value, 1 << d)
        for d in range(self.T.bit_length() - 1):
            value = value + self.mate(value, 1 << d)
        return value


def rope_tables(length, width):
    half = HD // 2
    frequency = rope_base ** (-jnp.arange(half, dtype=f32) * 2.0 / HD)
    angle = jnp.arange(length, dtype=f32)[:, None] * frequency[None, :]
    cosine, sine = jnp.cos(angle), jnp.sin(angle)
    copies = width // HD
    return (
        jnp.tile(cosine, (1, 2 * copies)),
        jnp.tile(jnp.concatenate([-sine, sine], axis=1), (1, copies)),
    )


def turn(value, cosine, sine):
    width = value.shape[1]
    lane = lax.broadcasted_iota(jnp.int32, value.shape, 1)
    ahead = pltpu.roll(value, width - HD // 2, 1)
    behind = pltpu.roll(value, HD // 2, 1)
    return value * cosine + jnp.where(lane % HD < HD // 2, ahead, behind) * sine


def of_head(value, head):
    lane = lax.broadcasted_iota(jnp.int32, value.shape, 1)
    return jnp.where(lane // HD == head, value, jnp.zeros_like(value))


def causal_tail(scores, block):
    rows, columns = scores.shape
    row = lax.broadcasted_iota(jnp.int32, (rows, block), 0)
    column = lax.broadcasted_iota(jnp.int32, (rows, block), 1)
    last = jnp.where(column <= row, scores[:, columns - block :], masked_score)
    if columns == block:
        return last
    return jnp.concatenate([scores[:, : columns - block], last], axis=1)


def forward_kernel(block, proj, cosine, sine, query, keys, values, mixed, logsum):
    length, width = query.shape
    heads = width // HD
    query[...] = turn(proj[0], cosine[...], sine[...]).astype(low)
    keys[...] = turn(proj[1], cosine[...], sine[...]).astype(low)
    values[...] = proj[2].astype(low)
    for begin in range(0, length, block):
        end = begin + block
        total = jnp.zeros((block, width), f32)
        lane = lax.broadcasted_iota(jnp.int32, (block, 128), 1)
        sums = jnp.zeros((block, 128), f32)
        for head in range(heads):
            one = of_head(query[begin:end, :].astype(f32) * HD**-0.5, head).astype(low)
            scores = causal_tail(dot(one, keys[:end, :], NT), block)
            largest = jnp.max(scores, axis=1, keepdims=True)
            expo = jnp.exp(scores - largest)
            totals = jnp.sum(expo, axis=1, keepdims=True)
            part = dot(expo.astype(low), values[:end, :], NN)
            total = total + of_head(part / totals, head)
            sums = jnp.where(lane == head, largest + jnp.log(totals), sums)
        mixed[begin:end, :] = total.astype(low)
        logsum[begin:end, :] = sums


def attend_forward(proj, tables):
    length, width = proj.shape[1:]
    block = min(length, 256)
    flat = jax.ShapeDtypeStruct((length, width), low)
    heads = width // HD
    return pl.pallas_call(
        functools.partial(forward_kernel, block),
        out_shape=[flat, flat, flat, flat, jax.ShapeDtypeStruct((length, 128), f32)],
        compiler_params=pltpu.CompilerParams(vmem_limit_bytes=40 * 1024 * 1024),
        cost_estimate=pl.CostEstimate(
            flops=4 * length * length * 256 * heads,
            bytes_accessed=length * width * 30,
            transcendentals=heads * length * length // 2,
        ),
        name="attend_forward",
    )(proj, *tables)


def backward_kernel(
    block, query, keys, values, mixed, logsum, grad, cosine, sine, out, grad_keys, grad_values
):
    length, width = query.shape
    heads = width // HD
    scale = HD**-0.5
    grad_keys[...] = jnp.zeros_like(grad_keys)
    grad_values[...] = jnp.zeros_like(grad_values)
    for begin in range(0, length, block):
        end = begin + block
        total = jnp.zeros((block, width), f32)
        product = grad[begin:end, :].astype(f32) * mixed[begin:end, :].astype(f32)
        for head in range(heads):
            one = of_head(query[begin:end, :].astype(f32) * scale, head).astype(low)
            grad_one = of_head(grad[begin:end, :].astype(f32), head).astype(low)
            delta = jnp.sum(of_head(product, head), axis=1, keepdims=True)
            scores = causal_tail(dot(one, keys[:end, :], NT), block)
            prob = jnp.exp(scores - logsum[begin:end, head : head + 1])
            grad_prob = dot(grad_one, values[:end, :], NT)
            grad_scores = (prob * (grad_prob - delta)).astype(low)
            total = total + of_head(dot(grad_scores, keys[:end, :], NN), head)
            grad_keys[:end, :] += dot(grad_scores, one, TN)
            grad_values[:end, :] += dot(prob.astype(low), grad_one, TN)
        out[0, begin:end, :] = turn(
            total * scale, cosine[begin:end, :], -sine[begin:end, :]
        ).astype(low)
    out[1] = turn(grad_keys[...], cosine[...], -sine[...]).astype(low)
    out[2] = grad_values[...].astype(low)


def attend_backward(saved, grad, tables):
    length, width = grad.shape
    block = min(length, 256)
    heads = width // HD
    return pl.pallas_call(
        functools.partial(backward_kernel, block),
        out_shape=jax.ShapeDtypeStruct((3, length, width), low),
        scratch_shapes=[pltpu.VMEM((length, width), f32)] * 2,
        compiler_params=pltpu.CompilerParams(vmem_limit_bytes=48 * 1024 * 1024),
        cost_estimate=pl.CostEstimate(
            flops=10 * length * length * 256 * heads,
            bytes_accessed=length * width * 30,
            transcendentals=heads * length * length // 2,
        ),
        name="attend_backward",
    )(*saved, grad, *tables)


def norm_scale(value):
    return lax.rsqrt(jnp.mean(value * value, axis=-1, keepdims=True) + epsilon)


def norm_back(grad, normed, scale, gain):
    scaled = grad * gain
    inner = jnp.mean(scaled * normed, axis=-1, keepdims=True)
    return (scale * (scaled - normed * inner), jnp.sum(grad * normed, axis=0))


def adamw(weight, grad, first, second, decay, rate):
    first = beta_first * first + (1.0 - beta_first) * grad
    second = beta_second * second + (1.0 - beta_second) * grad * grad
    first_hat = first / (1.0 - beta_first**STEP)
    second_hat = second / (1.0 - beta_second**STEP)
    weight = weight - rate * (first_hat / (jnp.sqrt(second_hat) + adam_epsilon) + decay * weight)
    return (weight, first, second)


def body(
    layer_input,
    inward_weight,
    outward_weight,
    expand_weight,
    shrink_weight,
    norm_gains,
    cotangent,
    inward_momentum,
    inward_variance,
    outward_momentum,
    outward_variance,
    expand_momentum,
    expand_variance,
    shrink_momentum,
    shrink_variance,
    gains_momentum,
    gains_variance,
):
    rows = layer_input.shape[0]
    mv = Moves(LEN // rows)
    F, Z, S = mv.F, mv.Z, mv.S
    own_width = inward_weight.shape[2]
    hidden_width = shrink_weight.shape[1] // F
    row_block = shrink_weight.shape[0]
    planes = range(F)
    ks = range(Z)

    attn_own = jnp.concatenate([inward_weight, outward_weight[None]], axis=0).astype(low)
    attn_blocks = mv.ring_gather(attn_own)
    attn_full = []
    for k in ks:
        pieces = mv.plane_gather(attn_blocks[k], 1 + k % 2)
        attn_full.append(mv.place(pieces, 1, mv.f))

    def quarter(d):
        begin = (mv.f ^ d) * hidden_width
        both = lax.dynamic_slice_in_dim(expand_weight, begin, hidden_width, 2)
        last = lax.dynamic_slice_in_dim(shrink_weight, begin, hidden_width, 1)
        return jnp.concatenate([both, last[None]], axis=0).astype(low)

    ff_own = mv.place([quarter(0)] + [mv.plane(quarter(d), d) for d in planes if d], 1, mv.f)
    expand_full = jnp.concatenate(mv.ring_gather(ff_own[:2]), axis=2)
    shrink_full = jnp.concatenate(mv.ring_gather(ff_own[2]), axis=1)

    source = layer_input.astype(f32)
    scale_one = norm_scale(source)
    normed_one = source * scale_one
    acts = mv.place(mv.mates((normed_one * norm_gains[0]).astype(low)), 0, mv.s)
    tables = rope_tables(LEN, own_width)
    saved = []
    for k in ks:
        proj = jnp.einsum("td,cde->cte", acts, attn_full[k][:3], preferred_element_type=f32)
        saved.append(attend_forward(proj, tables))
    mixed = jnp.concatenate([s[3] for s in saved], axis=1)
    outward_full = jnp.concatenate([w[3] for w in attn_full], axis=1)
    attended = dot(mixed, outward_full, NT).astype(low)

    def part(value, d):
        return lax.dynamic_slice_in_dim(value, (mv.s ^ d) * rows, rows, 0)

    resid = source + mv.mates_sum([part(attended, d) for d in range(S)])
    scale_two = norm_scale(resid)
    normed_two = resid * scale_two
    feed_local = (normed_two * norm_gains[1]).astype(low)

    feed_blocks = [
        jnp.concatenate(mv.mates(block), axis=0) for block in mv.plane_gather_rows(feed_local)
    ]
    grad_blocks = [
        jnp.concatenate(mv.mates(block), axis=0) for block in mv.plane_gather_rows(cotangent)
    ]
    hidden, grad_gate_up, grad_feed, fed = [], [], [], []
    for d in planes:
        gate_up = jnp.einsum(
            "td,cdf->ctf", feed_blocks[d], expand_full, preferred_element_type=f32
        )
        gate, up = gate_up[0], gate_up[1]
        sigma = jax.nn.sigmoid(gate)
        silu = gate * sigma
        hidden.append((silu * up).astype(low))
        slope = (up * sigma * (1.0 + gate * (1.0 - sigma))).astype(low)
        silu = silu.astype(low)
        grad_hidden = dot(grad_blocks[d], shrink_full, NN)
        grad_gate_up.append(
            jnp.stack([grad_hidden * slope.astype(f32), grad_hidden * silu.astype(f32)]).astype(
                low
            )
        )
    for d in planes:
        grad_feed.append(
            jnp.einsum(
                "ctf,cdf->td", grad_gate_up[d], expand_full, preferred_element_type=f32
            ).astype(low)
        )
    for d in planes:
        fed.append(dot(hidden[d], shrink_full, NT).astype(low))

    def chip_sum(block):
        return mv.mates_sum([block[d * rows : (d + 1) * rows] for d in range(S)]).astype(low)

    grad_feed = mv.plane_sum_rows([chip_sum(block) for block in grad_feed])
    resid_back, gain_two = norm_back(grad_feed, normed_two, scale_two, norm_gains[1])
    grad_resid = cotangent.astype(f32) + resid_back
    fed = mv.plane_sum_rows([chip_sum(block) for block in fed])
    layer_output = (resid + fed).astype(low)

    feed_all = jnp.concatenate(feed_blocks, axis=0)
    grad_all = jnp.concatenate(grad_blocks, axis=0)
    hidden_all = jnp.concatenate(hidden, axis=0)
    grad_gate_up_all = jnp.concatenate(grad_gate_up, axis=1)
    shrink_terms = dot(grad_all, hidden_all, TN).astype(low)
    expand_terms = jnp.einsum(
        "td,ctf->cdf", feed_all, grad_gate_up_all, preferred_element_type=f32
    ).astype(low)

    def hidden_part(value, k):
        return lax.slice_in_dim(value, k * hidden_width, (k + 1) * hidden_width, axis=-1)

    shrink_sum = mv.ring_sum([hidden_part(shrink_terms, k) for k in ks]).astype(low)
    expand_sum = mv.ring_sum([hidden_part(expand_terms, k) for k in ks]).astype(low)

    def rows_part(value, d):
        return lax.dynamic_slice_in_dim(value, (mv.f ^ d) * row_block, row_block, -2)

    def columns(value):
        pieces = [rows_part(value, 0)] + [mv.plane(rows_part(value, d), d) for d in planes if d]
        return mv.place(pieces, value.ndim - 1, mv.f).astype(f32)

    shrink_grad = columns(shrink_sum)
    expand_grad = columns(expand_sum)

    grad_attn = mv.place(mv.mates(grad_resid.astype(low)), 0, mv.s)
    grad_acts = 0.0
    attn_terms = []
    for k in ks:
        grad_mixed = dot(grad_attn, attn_full[k][3], NN).astype(low)
        grad_proj = attend_backward(saved[k], grad_mixed, tables)
        inward_terms = jnp.einsum("td,cte->cde", acts, grad_proj, preferred_element_type=f32)
        outward_terms = dot(grad_attn, saved[k][3], TN)
        terms = jnp.concatenate([inward_terms, outward_terms[None]], axis=0).astype(low)
        attn_terms.append(mv.plane_sum([rows_part(terms, d) for d in planes], 1 + k % 2))
        grad_acts = grad_acts + jnp.einsum(
            "cte,cde->td", grad_proj, attn_full[k][:3], preferred_element_type=f32
        )
    attn_grad = mv.ring_sum(attn_terms)
    inward_grad, outward_grad = attn_grad[:3], attn_grad[3]
    grad_acts = grad_acts.astype(low)
    grad_acts = mv.mates_sum([part(grad_acts, d) for d in range(S)])
    input_back, gain_one = norm_back(grad_acts, normed_one, scale_one, norm_gains[0])
    input_grad = (grad_resid + input_back).astype(low)

    owned_squares = (
        jnp.sum(inward_grad * inward_grad)
        + jnp.sum(outward_grad * outward_grad)
        + jnp.sum(expand_grad * expand_grad)
        + jnp.sum(shrink_grad * shrink_grad)
    )
    gains_grad, squares = lax.psum((jnp.stack([gain_one, gain_two]), owned_squares), ("fsdp", "tp"))
    norm = jnp.sqrt(squares + jnp.sum(gains_grad * gains_grad))
    factor = jnp.minimum(1.0, clip_bound / (norm + 1e-06))
    inward_new = adamw(
        inward_weight,
        factor * inward_grad,
        inward_momentum,
        inward_variance,
        decay_rate,
        matrix_rate,
    )
    outward_new = adamw(
        outward_weight,
        factor * outward_grad,
        outward_momentum,
        outward_variance,
        decay_rate,
        outward_rate,
    )
    expand_new = adamw(
        expand_weight,
        factor * expand_grad,
        expand_momentum,
        expand_variance,
        decay_rate,
        matrix_rate,
    )
    shrink_new = adamw(
        shrink_weight,
        factor * shrink_grad,
        shrink_momentum,
        shrink_variance,
        decay_rate,
        matrix_rate,
    )
    gains_new = adamw(
        norm_gains, factor * gains_grad, gains_momentum, gains_variance, 0.0, gains_rate
    )
    return (
        layer_output,
        input_grad,
        inward_grad,
        outward_grad,
        expand_grad,
        shrink_grad,
        gains_grad,
        inward_new[0],
        outward_new[0],
        expand_new[0],
        shrink_new[0],
        gains_new[0],
        inward_new[1],
        inward_new[2],
        outward_new[1],
        outward_new[2],
        expand_new[1],
        expand_new[2],
        shrink_new[1],
        shrink_new[2],
        gains_new[1],
        gains_new[2],
    )


def solution(mesh):
    row_spec = P(("fsdp", "tp"), None)
    three = P(None, "fsdp", "tp")
    two = P("fsdp", "tp")
    moments = (three, three, two, two, three, three, two, two, P(), P())
    return jax.shard_map(
        body,
        mesh=mesh,
        in_specs=(row_spec, three, two, three, two, P(), row_spec) + moments,
        out_specs=(row_spec, row_spec)
        + (three, two, three, two, P())
        + (three, two, three, two, P())
        + moments,
        check_vma=False,
    )
```

time: 2430 us -> 1460 us (0.60)
  waiting for transfers between devices: 1340 us -> 552 us
  matrix products: 504 us -> 349 us
  local copies, waits for them, and re-layouts: 350 us -> 216 us
  Pallas kernels: 0 us -> 72.3 us
  starting transfers between devices: 0.66 us -> 70.8 us
    all_gather x8 -> x0, waiting for transfers between devices: 673 us -> none  [the longest x1 153 us: body(): lax.all_gather((normed_one * norm_gains[0]).astype(jnp.bfloat16), 'tp', a...]
    reduce_scatter x8 -> x0, waiting for transfers between devices: 669 us -> none  [the longest x1 320 us: body(): lax.psum_scatter(lax.dot_general(part_rows, outward_full, contract_last,...]
    ppermute x0 -> x87, waiting for transfers between devices: none -> 552 us  [the longest x49 346 us: plane(): return lax.ppermute(value, 'fsdp', [(i, i ^ mask) for i in range(self.F)])]
    dot_general x68 -> x39, matrix products: 504 us -> 349 us  [the longest x18 120 us: dot(): return lax.dot_general(a, b, (dims, ((), ())), preferred_element_type=f32)]
    dynamic_update_slice x16 -> x23, local copies, waits for them, and re-layouts: 177 us -> 25.3 us  [place(): lax.dynamic_update_slice_in_dim(whole, pieces[d], (index ^ d) * width, axis)]
    pallas_call x0 -> x8, Pallas kernels: none -> 72.3 us  [the longest x4 46.9 us: attend_backward(): pl.pallas_call(functools.partial(backward_kernel, block), out_shape=jax.S...]
    ppermute x0 -> x87, starting transfers between devices: none -> 70.8 us  [the longest x49 53.1 us: plane(): return lax.ppermute(value, 'fsdp', [(i, i ^ mask) for i in range(self.F)])]
    unnamed x108 -> x363, local copies, waits for them, and re-layouts: 78.6 us -> 141 us
  transfers between devices with their start and end apart: 16 -> 87, of which waited for: 11 -> 33; matrix products, arithmetic and copies ran while one was open for 37% -> 42% of each run, Pallas kernels for 0% -> 5%
where the time goes in v1:
time: 1460 us; the launch traced here: 1450 us
  waiting for transfers between devices  552 us (38%)
  matrix products  349 us (24%)
  local copies, waits for them, and re-layouts  216 us (15%)
  other arithmetic  144 us (10%)
  Pallas kernels  72.3 us (5%)
  starting transfers between devices  70.8 us (5%)
  blocking collectives  37.8 us (3%)
    ppermute x49, waiting for transfers between devices, plane(): return lax.ppermute(value, 'fsdp', [(i, i ^ mask) for i in range(self.F)])  346 us
    ppermute x18, waiting for transfers between devices, ring(): return lax.ppermute(value, 'tp', step)  206 us
    unnamed x363, local copies, waits for them, and re-layouts  141 us
    dot_general x18, matrix products, dot(): return lax.dot_general(a, b, (dims, ((), ())), preferred_element_type=f32)  120 us
    dot_general x4, matrix products, body(): jnp.einsum('td,cdf->ctf', feed_blocks[d], expand_full, preferred_element_...  55.6 us
    dot_general x4, matrix products, body(): jnp.einsum('ctf,cdf->td', grad_gate_up[d], expand_full, preferred_element...  54.1 us
    ppermute x49, starting transfers between devices, plane(): return lax.ppermute(value, 'fsdp', [(i, i ^ mask) for i in range(self.F)])  53.1 us
    pallas_call x4, Pallas kernels, attend_backward(): pl.pallas_call(functools.partial(backward_kernel, block), out_shape=jax.S...  46.9 us
  transfers between devices with their start and end apart: 87, of which 33 were waited for; matrix products, arithmetic and copies ran while one was open for 42% of the time, Pallas kernels for 5%

profile of v1, /device:TPU:0, one launch (start us, length us, event | category | flops | bytes accessed | tf_op | source)
XLA Modules:
  0.0 1449.6 jit_solution(10574853317546004648)
XLA Ops:
  40.4 15.7 %collective-permute-done.18 = bf16[3,512,256]{2,1,0:T(8,128)(2,1)S(1)} collective-permute-done((bf16[3,512,256]{2,1,0:T(8,128)(2,1)S(1)}, bf16[3,512,256]{2,1,0:T(8,128)(2,1)S(1)}, u32[]{:S(2)}, u32[]{:S(2)}) %collective-permute-start.18) | collective-permute-done | bytes 786464 | tf_op jit(solution)/shard_map/ppermute | solution.py:50
  98.9 50.9 %collective-permute-done.2 = bf16[4,512,256]{1,2,0:T(8,128)(2,1)S(1)} collective-permute-done((bf16[4,512,256]{1,2,0:T(8,128)(2,1)}, bf16[4,512,256]{1,2,0:T(8,128)(2,1)S(1)}, u32[]{:S(2)}, u32[]{:S(2)}) %collective-permute-start.2) | collective-permute-done | bytes 1048608 | tf_op jit(solution)/shard_map/ppermute | solution.py:50
  156.0 14.6 %collective-permute-done.6 = bf16[4,512,256]{1,2,0:T(8,128)(2,1)S(1)} collective-permute-done((bf16[4,512,256]{1,2,0:T(8,128)(2,1)}, bf16[4,512,256]{1,2,0:T(8,128)(2,1)S(1)}, u32[]{:S(2)}, u32[]{:S(2)}) %collective-permute-start.6) | collective-permute-done | bytes 1048608 | tf_op jit(solution)/shard_map/ppermute | solution.py:50
  178.3 16.0 %collective-permute-done.7 = bf16[4,512,256]{1,2,0:T(8,128)(2,1)S(1)} collective-permute-done((bf16[4,512,256]{1,2,0:T(8,128)(2,1)S(1)}, bf16[4,512,256]{1,2,0:T(8,128)(2,1)S(1)}, u32[]{:S(2)}, u32[]{:S(2)}) %collective-permute-start.7) | collective-permute-done | bytes 1048608 | tf_op jit(solution)/shard_map/ppermute | solution.py:50
  223.7 19.2 %collective-permute-done.11 = bf16[4,512,256]{1,2,0:T(8,128)(2,1)} collective-permute-done((bf16[4,512,256]{1,2,0:T(8,128)(2,1)}, bf16[4,512,256]{1,2,0:T(8,128)(2,1)}, u32[]{:S(2)}, u32[]{:S(2)}) %collective-permute-start.11) | collective-permute-done | bytes 1048608 | tf_op jit(solution)/shard_map/ppermute | solution.py:50
  309.9 19.8 %collective-permute-done.49 = bf16[256,2048]{1,0:T(8,128)(2,1)} collective-permute-done((bf16[256,2048]{1,0:T(8,128)(2,1)S(1)}, bf16[256,2048]{1,0:T(8,128)(2,1)}, u32[]{:S(2)}, u32[]{:S(2)}) %collective-permute-start.49) | collective-permute-done | bytes 1048608 | tf_op jit(solution)/shard_map/ppermute | solution.py:50
  380.6 19.5 %collective-permute-done.25 = bf16[2048,256]{1,0:T(8,128)(2,1)S(1)} collective-permute-done((bf16[2048,256]{1,0:T(8,128)(2,1)}, bf16[2048,256]{1,0:T(8,128)(2,1)S(1)}, u32[]{:S(2)}, u32[]{:S(2)}) %collective-permute-start.25) | collective-permute-done | bytes 1048608 | tf_op jit(solution)/shard_map/ppermute | solution.py:61
  424.9 22.0 %collective-permute-done.32 = bf16[512,2048]{1,0:T(8,128)(2,1)S(1)} collective-permute-done((bf16[512,2048]{1,0:T(8,128)(2,1)S(1)}, bf16[512,2048]{1,0:T(8,128)(2,1)S(1)}, u32[]{:S(2)}, u32[]{:S(2)}) %collective-permute-start.32) | collective-permute-done | bytes 2097184 | tf_op jit(solution)/shard_map/ppermute | solution.py:50
  451.9 14.2 fusion.137
  479.7 14.2 bitcast_convert_fusion.3
  538.9 14.3 bitcast_convert_fusion
  654.6 25.4 %fusion.116 = bf16[2048,1024]{0,1:T(8,128)(2,1)} fusion(bf16[4096,2048]{1,0:T(8,128)(2,1)} %constant_dynamic-update-slice_fusion.9, bf16[1024,1024]{1,0:T(8,128)(2,1)} %get-tuple-element.142, bf16[1024,1024]{1,0:T(8,128)(2,1)S(1)} %copy-done.156, bf16[1024,1024]{1,0:T(8,128)(2,1)} %get-tuple-element.141, bf16[1024,1024]{1,0:T(8,128)(2,1)S(1)} %copy-done.154), kind=kOutput, calls=%fused_computation.218 | convolution fusion | flops 17215520768 | bytes 29360128 | tf_op jit(solution)/shard_map/dot_general | solution.py:31
  683.1 44.8 %convert_bitcast_fusion = bf16[2,2048,1024]{1,2,0:T(8,128)(2,1)} fusion(bf16[4096,2048]{1,0:T(8,128)(2,1)} %constant_dynamic-update-slice_fusion, bf16[1,1024,1024]{2,1,0:T(8,128)(2,1)} %get-tuple-element.137, bf16[1,1024,1024]{2,1,0:T(8,128)(2,1)} %get-tuple-element.136, bf16[1,1024,1024]{2,1,0:T(8,128)(2,1)} %get-tuple-element.139, ...), kind=kOutput, calls=%fused_computation.34 | convolution fusion | flops 34498150400 | bytes 41943040 | tf_op jit(solution)/shard_map/td,ctf->cdf/dot_general | solution.py:399
  767.6 20.8 %collective-permute-done.81 = bf16[2048,256]{0,1:T(8,128)(2,1)S(1)} collective-permute-done((bf16[2048,256]{0,1:T(8,128)(2,1)S(1)}, bf16[2048,256]{0,1:T(8,128)(2,1)S(1)}, u32[]{:S(2)}, u32[]{:S(2)}) %collective-permute-start.81) | collective-permute-done | bytes 1048608 | tf_op jit(solution)/shard_map/ppermute | solution.py:61
  793.1 46.0 %collective-permute-done.75 = bf16[2,2048,256]{1,2,0:T(8,128)(2,1)} collective-permute-done((bf16[2,2048,256]{1,2,0:T(8,128)(2,1)}, bf16[2,2048,256]{1,2,0:T(8,128)(2,1)}, u32[]{:S(2)}, u32[]{:S(2)}) %collective-permute-start.75) | collective-permute-done | bytes 2097184 | tf_op jit(solution)/shard_map/ppermute | solution.py:61
  844.4 15.9 %collective-permute-done.82 = bf16[2048,256]{0,1:T(8,128)(2,1)} collective-permute-done((bf16[2048,256]{0,1:T(8,128)(2,1)S(1)}, bf16[2048,256]{0,1:T(8,128)(2,1)}, u32[]{:S(2)}, u32[]{:S(2)}) %collective-permute-start.82) | collective-permute-done | bytes 1048608 | tf_op jit(solution)/shard_map/ppermute | solution.py:61
  867.4 66.1 %collective-permute-done.83 = bf16[2048,256]{0,1:T(8,128)(2,1)S(1)} collective-permute-done((bf16[2048,256]{0,1:T(8,128)(2,1)S(1)}, bf16[2048,256]{0,1:T(8,128)(2,1)S(1)}, u32[]{:S(2)}, u32[]{:S(2)}) %collective-permute-start.83) | collective-permute-done | bytes 1048608 | tf_op jit(solution)/shard_map/ppermute | solution.py:61
  949.8 32.4 %collective-permute-done.53 = bf16[512,2048]{1,0:T(8,128)(2,1)} collective-permute-done((bf16[512,2048]{1,0:T(8,128)(2,1)S(1)}, bf16[512,2048]{1,0:T(8,128)(2,1)}, u32[]{:S(2)}, u32[]{:S(2)}) %collective-permute-start.53) | collective-permute-done | bytes 2097184 | tf_op jit(solution)/shard_map/ppermute | solution.py:50
  1002.8 22.4 %collective-permute-done.77 = bf16[2,2048,256]{1,2,0:T(8,128)(2,1)} collective-permute-done((bf16[2,2048,256]{1,2,0:T(8,128)(2,1)}, bf16[2,2048,256]{1,2,0:T(8,128)(2,1)}, u32[]{:S(2)}, u32[]{:S(2)}) %collective-permute-start.77) | collective-permute-done | bytes 2097184 | tf_op jit(solution)/shard_map/ppermute | solution.py:61
  1132.7 15.5 %fusion.25 = bf16[1024,2048]{1,0:T(8,128)(2,1)} fusion(f32[1024,2048,1]{1,0,2:T(8,128)} %fusion.139, f32[1024,2048,1]{1,0,2:T(8,128)} %fusion.141, f32[1024,2048,1]{1,0,2:T(8,128)} %fusion.143, bf16[3,1024,256]{2,1,0:T(8,128)(2,1)} %attend_backward.7, bf16[4,2048,256]{1,2,0:T(8,128)(2,1)} %copy-done.54), kind=kOutput, calls=%fused_computation.27 | convolution fusion | flops 3229614080 | bytes 34078720 | tf_op jit(solution)/shard_map/cte,cde->td/dot_general | solution.py:429
  1193.7 27.0 %collective-permute-done.80 = bf16[2,512,256]{1,2,0:T(8,128)(2,1)S(1)} collective-permute-done((bf16[2,512,256]{1,2,0:T(8,128)(2,1)S(1)}, bf16[2,512,256]{1,2,0:T(8,128)(2,1)S(1)}, u32[]{:S(2)}, u32[]{:S(2)}) %collective-permute-start.80) | collective-permute-done | bytes 524320 | tf_op jit(solution)/shard_map/ppermute | solution.py:50
  1253.0 16.6 %collective-permute-done.70 = bf16[4,512,256]{1,2,0:T(8,128)(2,1)} collective-permute-done((bf16[4,512,256]{1,2,0:T(8,128)(2,1)}, bf16[4,512,256]{1,2,0:T(8,128)(2,1)}, u32[]{:S(2)}, u32[]{:S(2)}) %collective-permute-start.70) | collective-permute-done | bytes 1048608 | tf_op jit(solution)/shard_map/ppermute | solution.py:50
  1274.1 41.6 %collective-permute-done.69 = bf16[4,512,256]{1,2,0:T(8,128)(2,1)S(1)} collective-permute-done((bf16[4,512,256]{1,2,0:T(8,128)(2,1)S(1)}, bf16[4,512,256]{1,2,0:T(8,128)(2,1)S(1)}, u32[]{:S(2)}, u32[]{:S(2)}) %collective-permute-start.69) | collective-permute-done | bytes 1048608 | tf_op jit(solution)/shard_map/ppermute | solution.py:50
  1344.6 37.8 %all-reduce = (f32[2,2048]{1,0:T(2,128)S(1)}, f32[]{:T(128)}) all-reduce(f32[2,2048]{1,0:T(2,128)S(1)} %pad_maximum_fusion.20, f32[]{:T(128)S(6)} %add.419), channel_id=1, replica_groups=mesh['fsdp'=4,'tp'=8] {'fsdp','tp'}, use_global_device_ids=true, to_apply=%region_6.0 | all-reduce | flops 4097 | bytes 32776 | tf_op jit(solution)/shard_map/psum | solution.py:445
  (703 shorter events, 809.7 us)
Async XLA Ops:
  13.8 82.3 %collective-permute-start.3 = (bf16[512,2048]{1,0:T(8,128)(2,1)}, bf16[512,2048]{1,0:T(8,128)(2,1)}, u32[]{:S(2)}, u32[]{:S(2)}) collective-permute-start(bf16[512,2048]{1,0:T(8,128)(2,1)} %fusion.34), channel_id=1, source_target_pairs={{0,1},{1,0},{2,3},{3,2},{4,5},{5,4},{6,7},{7,6},{8,9},{9,8},{10,11... | collective-permute-start | bytes 6291464 | tf_op jit(solution)/shard_map/ppermute | solution.py:53
  62.9 239.8 %collective-permute-start.48 = (bf16[512,2048]{1,0:T(8,128)(2,1)}, bf16[512,2048]{1,0:T(8,128)(2,1)}, u32[]{:S(2)}, u32[]{:S(2)}) collective-permute-start(bf16[512,2048]{1,0:T(8,128)(2,1)} %param.23), channel_id=1, source_target_pairs={{0,16},{8,24},{16,0},{24,8},{1,17},{9,25},{17,1},{25,9},{2,18},{10... | collective-permute-start | bytes 6291464 | tf_op jit(solution)/shard_map/ppermute | solution.py:50
  77.5 227.9 %collective-permute-start.44 = (bf16[512,2048]{1,0:T(8,128)(2,1)}, bf16[512,2048]{1,0:T(8,128)(2,1)}, u32[]{:S(2)}, u32[]{:S(2)}) collective-permute-start(bf16[512,2048]{1,0:T(8,128)(2,1)} %param.23), channel_id=1, source_target_pairs={{0,8},{8,0},{16,24},{24,16},{1,9},{9,1},{17,25},{25,17},{2,10},{10... | collective-permute-start | bytes 6291464 | tf_op jit(solution)/shard_map/ppermute | solution.py:50
  96.1 74.5 %collective-permute-start.6 = (bf16[4,512,256]{1,2,0:T(8,128)(2,1)}, bf16[4,512,256]{1,2,0:T(8,128)(2,1)S(1)}, u32[]{:S(2)}, u32[]{:S(2)}) collective-permute-start(bf16[4,512,256]{1,2,0:T(8,128)(2,1)} %collective-permute-done.4), channel_id=1, source_target_pairs={{0,16},{8,24},{16,0},{24,8},{1,17},{9,25},{17,1},{25,9},{2,18},{10... | collective-permute-start | bytes 3145736 | tf_op jit(solution)/shard_map/ppermute | solution.py:50
  329.7 71.9 %collective-permute-start.54 = (bf16[512,2048]{1,0:T(8,128)(2,1)}, bf16[512,2048]{1,0:T(8,128)(2,1)}, u32[]{:S(2)}, u32[]{:S(2)}) collective-permute-start(bf16[512,2048]{1,0:T(8,128)(2,1)} %collective-permute-done.48), channel_id=1, source_target_pairs={{0,1},{1,0},{2,3},{3,2},{4,5},{5,4},{6,7},{7,6},{8,9},{9,8},{10,11... | collective-permute-start | bytes 6291464 | tf_op jit(solution)/shard_map/ppermute | solution.py:53
  331.6 71.2 %collective-permute-start.45 = (bf16[512,2048]{1,0:T(8,128)(2,1)}, bf16[512,2048]{1,0:T(8,128)(2,1)}, u32[]{:S(2)}, u32[]{:S(2)}) collective-permute-start(bf16[512,2048]{1,0:T(8,128)(2,1)} %collective-permute-done.44), channel_id=1, source_target_pairs={{0,1},{1,0},{2,3},{3,2},{4,5},{5,4},{6,7},{7,6},{8,9},{9,8},{10,11... | collective-permute-start | bytes 6291464 | tf_op jit(solution)/shard_map/ppermute | solution.py:53
  378.9 72.9 %collective-permute-start.22 = (bf16[2,2048,256]{2,1,0:T(8,128)(2,1)}, bf16[2,2048,256]{2,1,0:T(8,128)(2,1)}, u32[]{:S(2)}, u32[]{:S(2)}) collective-permute-start(bf16[2,2048,256]{2,1,0:T(8,128)(2,1)} %collective-permute-done.21), channel_id=1, source_target_pairs={{0,2},{1,3},{2,4},{3,5},{4,6},{5,7},{6,0},{7,1},{8,10},{9,11},{10,... | collective-permute-start | bytes 6291464 | tf_op jit(solution)/shard_map/ppermute | solution.py:61
  497.2 450.3 %collective-permute-start.43 = (bf16[512,2048]{1,0:T(8,128)(2,1)}, bf16[512,2048]{1,0:T(8,128)(2,1)}, u32[]{:S(2)}, u32[]{:S(2)}) collective-permute-start(bf16[512,2048]{1,0:T(8,128)(2,1)} %slice.289), channel_id=1, source_target_pairs={{0,1},{1,0},{2,3},{3,2},{4,5},{5,4},{6,7},{7,6},{8,9},{9,8},{10,11... | collective-permute-start | bytes 6291464 | tf_op jit(solution)/shard_map/ppermute | solution.py:53
  512.7 115.7 %collective-permute-start.34 = (bf16[512,2048]{1,0:T(8,128)(2,1)}, bf16[512,2048]{1,0:T(8,128)(2,1)}, u32[]{:S(2)}, u32[]{:S(2)}) collective-permute-start(bf16[512,2048]{1,0:T(8,128)(2,1)} %pad_maximum_fusion.7), channel_id=1, source_target_pairs={{0,1},{1,0},{2,3},{3,2},{4,5},{5,4},{6,7},{7,6},{8,9},{9,8},{10,11... | collective-permute-start | bytes 6291464 | tf_op jit(solution)/shard_map/ppermute | solution.py:53
  556.5 200.6 %collective-permute-start.55 = (bf16[512,2048]{1,0:T(8,128)(2,1)}, bf16[512,2048]{1,0:T(8,128)(2,1)}, u32[]{:S(2)}, u32[]{:S(2)}) collective-permute-start(bf16[512,2048]{1,0:T(8,128)(2,1)} %slice.300), channel_id=1, source_target_pairs={{0,1},{1,0},{2,3},{3,2},{4,5},{5,4},{6,7},{7,6},{8,9},{9,8},{10,11... | collective-permute-start | bytes 6291464 | tf_op jit(solution)/shard_map/ppermute | solution.py:53
  597.6 163.3 %collective-permute-start.46 = (bf16[512,2048]{1,0:T(8,128)(2,1)}, bf16[512,2048]{1,0:T(8,128)(2,1)}, u32[]{:S(2)}, u32[]{:S(2)}) collective-permute-start(bf16[512,2048]{1,0:T(8,128)(2,1)} %slice.291), channel_id=1, source_target_pairs={{0,1},{1,0},{2,3},{3,2},{4,5},{5,4},{6,7},{7,6},{8,9},{9,8},{10,11... | collective-permute-start | bytes 6291464 | tf_op jit(solution)/shard_map/ppermute | solution.py:53
  608.2 155.4 %collective-permute-start.39 = (bf16[512,2048]{1,0:T(8,128)(2,1)}, bf16[512,2048]{1,0:T(8,128)(2,1)}, u32[]{:S(2)}, u32[]{:S(2)}) collective-permute-start(bf16[512,2048]{1,0:T(8,128)(2,1)} %slice.284), channel_id=1, source_target_pairs={{0,1},{1,0},{2,3},{3,2},{4,5},{5,4},{6,7},{7,6},{8,9},{9,8},{10,11... | collective-permute-start | bytes 6291464 | tf_op jit(solution)/shard_map/ppermute | solution.py:53
  628.3 237.5 %collective-permute-start.30 = (bf16[512,2048]{1,0:T(8,128)(2,1)}, bf16[512,2048]{1,0:T(8,128)(2,1)}, u32[]{:S(2)}, u32[]{:S(2)}) collective-permute-start(bf16[512,2048]{1,0:T(8,128)(2,1)} %slice.271), channel_id=1, source_target_pairs={{0,1},{1,0},{2,3},{3,2},{4,5},{5,4},{6,7},{7,6},{8,9},{9,8},{10,11... | collective-permute-start | bytes 6291464 | tf_op jit(solution)/shard_map/ppermute | solution.py:53
  788.8 71.5 %collective-permute-start.82 = (bf16[2048,256]{0,1:T(8,128)(2,1)S(1)}, bf16[2048,256]{0,1:T(8,128)(2,1)}, u32[]{:S(2)}, u32[]{:S(2)}) collective-permute-start(bf16[2048,256]{0,1:T(8,128)(2,1)S(1)} %add_convert_fusion.14), channel_id=1, source_target_pairs={{0,2},{1,3},{2,4},{3,5},{4,6},{5,7},{6,0},{7,1},{8,10},{9,11},{10,... | collective-permute-start | bytes 3145736 | tf_op jit(solution)/shard_map/ppermute | solution.py:61
  790.9 72.1 %collective-permute-start.56 = (bf16[256,2048]{1,0:T(8,128)(2,1)S(1)}, bf16[256,2048]{1,0:T(8,128)(2,1)S(1)}, u32[]{:S(2)}, u32[]{:S(2)}) collective-permute-start(bf16[256,2048]{1,0:T(8,128)(2,1)S(1)} %get-tuple-element.164), channel_id=1, source_target_pairs={{0,8},{8,0},{16,24},{24,16},{1,9},{9,1},{17,25},{25,17},{2,10},{10... | collective-permute-start | bytes 3145736 | tf_op jit(solution)/shard_map/ppermute | solution.py:50
  860.3 77.9 %collective-permute-start.40 = (bf16[256,2048]{1,0:T(8,128)(2,1)}, bf16[256,2048]{1,0:T(8,128)(2,1)S(1)}, u32[]{:S(2)}, u32[]{:S(2)}) collective-permute-start(bf16[256,2048]{1,0:T(8,128)(2,1)} %get-tuple-element.166), channel_id=1, source_target_pairs={{0,8},{8,0},{16,24},{24,16},{1,9},{9,1},{17,25},{25,17},{2,10},{10... | collective-permute-start | bytes 3145736 | tf_op jit(solution)/shard_map/ppermute | solution.py:50
  863.1 81.0 %collective-permute-start.76 = (bf16[2,2048,256]{1,2,0:T(8,128)(2,1)S(1)}, bf16[2,2048,256]{1,2,0:T(8,128)(2,1)S(1)}, u32[]{:S(2)}, u32[]{:S(2)}) collective-permute-start(bf16[2,2048,256]{1,2,0:T(8,128)(2,1)S(1)} %add_convert_fusion.2), channel_id=1, source_target_pairs={{0,2},{1,3},{2,4},{3,5},{4,6},{5,7},{6,0},{7,1},{8,10},{9,11},{10,... | collective-permute-start | bytes 6291464 | tf_op jit(solution)/shard_map/ppermute | solution.py:61
  865.8 81.7 %collective-permute-start.57 = (bf16[512,2048]{1,0:T(8,128)(2,1)}, bf16[512,2048]{1,0:T(8,128)(2,1)}, u32[]{:S(2)}, u32[]{:S(2)}) collective-permute-start(bf16[512,2048]{1,0:T(8,128)(2,1)} %pad_maximum_fusion.12), channel_id=1, source_target_pairs={{0,16},{8,24},{16,0},{24,8},{1,17},{9,25},{17,1},{25,9},{2,18},{10... | collective-permute-start | bytes 6291464 | tf_op jit(solution)/shard_map/ppermute | solution.py:50
  947.5 216.4 %collective-permute-start.86 = (bf16[512,256]{0,1:T(8,128)(2,1)S(1)}, bf16[512,256]{0,1:T(8,128)(2,1)}, u32[]{:S(2)}, u32[]{:S(2)}) collective-permute-start(bf16[512,256]{0,1:T(8,128)(2,1)S(1)} %get-tuple-element.171), channel_id=1, source_target_pairs={{0,24},{8,16},{16,8},{24,0},{1,25},{9,17},{17,9},{25,1},{2,26},{10... | collective-permute-start | bytes 786440 | tf_op jit(solution)/shard_map/ppermute | solution.py:50
  1029.2 142.5 %collective-permute-start.78 = (bf16[2,512,256]{1,2,0:T(8,128)(2,1)}, bf16[2,512,256]{1,2,0:T(8,128)(2,1)}, u32[]{:S(2)}, u32[]{:S(2)}) collective-permute-start(bf16[2,512,256]{1,2,0:T(8,128)(2,1)} %get-tuple-element.161), channel_id=1, source_target_pairs={{0,8},{8,0},{16,24},{24,16},{1,9},{9,1},{17,25},{25,17},{2,10},{10... | collective-permute-start | bytes 1572872 | tf_op jit(solution)/shard_map/ppermute | solution.py:50
  1174.1 96.2 %collective-permute-start.59 = (bf16[512,2048]{1,0:T(8,128)(2,1)}, bf16[512,2048]{1,0:T(8,128)(2,1)}, u32[]{:S(2)}, u32[]{:S(2)}) collective-permute-start(bf16[512,2048]{1,0:T(8,128)(2,1)} %constant_dynamic-slice_fusion.8), channel_id=1, source_target_pairs={{0,1},{1,0},{2,3},{3,2},{4,5},{5,4},{6,7},{7,6},{8,9},{9,8},{10,11... | collective-permute-start | bytes 6291464 | tf_op jit(solution)/shard_map/ppermute | solution.py:53
  1237.6 83.4 %collective-permute-start.27 = (bf16[512,2048]{1,0:T(8,128)(2,1)}, bf16[512,2048]{1,0:T(8,128)(2,1)}, u32[]{:S(2)}, u32[]{:S(2)}) collective-permute-start(bf16[512,2048]{1,0:T(8,128)(2,1)} %slice.267), channel_id=1, source_target_pairs={{0,1},{1,0},{2,3},{3,2},{4,5},{5,4},{6,7},{7,6},{8,9},{9,8},{10,11... | collective-permute-start | bytes 6291464 | tf_op jit(solution)/shard_map/ppermute | solution.py:53
  1247.0 74.0 %collective-permute-start.41 = (bf16[512,2048]{1,0:T(8,128)(2,1)}, bf16[512,2048]{1,0:T(8,128)(2,1)}, u32[]{:S(2)}, u32[]{:S(2)}) collective-permute-start(bf16[512,2048]{1,0:T(8,128)(2,1)} %pad_maximum_fusion.9), channel_id=1, source_target_pairs={{0,16},{8,24},{16,0},{24,8},{1,17},{9,25},{17,1},{25,9},{2,18},{10... | collective-permute-start | bytes 6291464 | tf_op jit(solution)/shard_map/ppermute | solution.py:50
  1247.5 73.5 %collective-permute-start.37 = (bf16[512,2048]{1,0:T(8,128)(2,1)}, bf16[512,2048]{1,0:T(8,128)(2,1)}, u32[]{:S(2)}, u32[]{:S(2)}) collective-permute-start(bf16[512,2048]{1,0:T(8,128)(2,1)} %pad_maximum_fusion.8), channel_id=1, source_target_pairs={{0,8},{8,0},{16,24},{24,16},{1,9},{9,1},{17,25},{25,17},{2,10},{10... | collective-permute-start | bytes 6291464 | tf_op jit(solution)/shard_map/ppermute | solution.py:50
  (226 other events, 5650.1 us)

commit v2 on v1

--- a/solution.py
+++ b/solution.py
@@ -45,9 +45,22 @@
         self.f = lax.axis_index("fsdp")
         self.t = lax.axis_index("tp")
         self.s = lax.rem(self.t, self.S)
+        if self.F == 4:
+            self.masks = [0, 1 + lax.rem(self.s, 2), 2 - lax.rem(self.s, 2), 3]
+        else:
+            self.masks = list(range(self.F))
+        self.partners = jnp.stack([self.f ^ mask for mask in self.masks]).astype(jnp.int32)
 
     def plane(self, value, mask):
         return lax.ppermute(value, "fsdp", [(i, i ^ mask) for i in range(self.F)])
+
+    def hop(self, value, number):
+        pairs = []
+        for f in range(self.F):
+            for t in range(self.T):
+                mask = number if t % self.S % 2 == 0 else 3 - number
+                pairs.append((f * self.T + t, (f ^ mask) * self.T + t))
+        return lax.ppermute(value, ("fsdp", "tp"), pairs)
 
     def mate(self, value, mask):
         return lax.ppermute(value, "tp", [(i, i ^ mask) for i in range(self.T)])
@@ -76,49 +89,21 @@
             total = total + self.mate(blocks[d], d).astype(f32)
         return total
 
-    def plane_gather(self, value, first):
+    def plane_gather(self, value):
         if self.F != 4:
             whole = lax.all_gather(value, "fsdp", axis=0)
             return [lax.dynamic_index_in_dim(whole, self.f ^ d, 0, False) for d in range(self.F)]
-        one = self.plane(value, 1)
-        two = self.plane(value, 2)
-        three = self.plane(one, 2) if first == 1 else self.plane(two, 1)
-        return [value, one, two, three]
-
-    def plane_gather_rows(self, value):
-        if self.F != 4:
-            return self.plane_gather(value, 1)
-        half = value.shape[0] // 2
-        one = self.plane(value, 1)
-        two = self.plane(value, 2)
-        three = jnp.concatenate([self.plane(one[:half], 2), self.plane(two[half:], 1)], axis=0)
-        return [value, one, two, three]
-
-    def plane_sum(self, blocks, first):
+        one = self.hop(value, 1)
+        two = self.hop(value, 2)
+        return [value, one, two, self.hop(one, 2)]
+
+    def plane_sum(self, blocks):
         if self.F != 4:
             whole = self.place([b[None] for b in blocks], 0, self.f)
             return lax.psum_scatter(whole, "fsdp", scatter_dimension=0).astype(f32)
         here, one, two, three = blocks
-        if first == 1:
-            two = (two.astype(f32) + self.plane(three, 1).astype(f32)).astype(low)
-        else:
-            one = (one.astype(f32) + self.plane(three, 2).astype(f32)).astype(low)
-        return here.astype(f32) + self.plane(one, 1).astype(f32) + self.plane(two, 2).astype(f32)
-
-    def plane_sum_rows(self, blocks):
-        if self.F != 4:
-            return self.plane_sum(blocks, 1)
-        here, one, two, three = blocks
-        half = here.shape[0] // 2
-        to_two = self.plane(three[:half], 1)
-        to_one = self.plane(three[half:], 2)
-        two = jnp.concatenate(
-            [(two[:half].astype(f32) + to_two.astype(f32)).astype(low), two[half:]], axis=0
-        )
-        one = jnp.concatenate(
-            [one[:half], (one[half:].astype(f32) + to_one.astype(f32)).astype(low)], axis=0
-        )
-        return here.astype(f32) + self.plane(one, 1).astype(f32) + self.plane(two, 2).astype(f32)
+        two = (two.astype(f32) + self.hop(three, 1).astype(f32)).astype(low)
+        return here.astype(f32) + self.hop(one, 1).astype(f32) + self.hop(two, 2).astype(f32)
 
     def ring_gather(self, value):
         pieces = [value]
@@ -138,6 +123,10 @@
         for d in range(self.T.bit_length() - 1):
             value = value + self.mate(value, 1 << d)
         return value
+
+
+def after(value, *others):
+    return lax.optimization_barrier((value,) + others)[0]
 
 
 def rope_tables(length, width):
@@ -175,12 +164,27 @@
     return jnp.concatenate([scores[:, : columns - block], last], axis=1)
 
 
-def forward_kernel(block, proj, cosine, sine, query, keys, values, mixed, logsum):
+def columns_of(ref, partners, i, width):
+    return ref[:, pl.ds(pl.multiple_of(partners[i] * width, width), width)]
+
+
+def forward_kernel(block, count, partners, acts, cosine, sine, *refs):
+    weights = refs[:count]
+    query, keys, values, mixed, logsum = refs[count:]
     length, width = query.shape
     heads = width // HD
-    query[...] = turn(proj[0], cosine[...], sine[...]).astype(low)
-    keys[...] = turn(proj[1], cosine[...], sine[...]).astype(low)
-    values[...] = proj[2].astype(low)
+    depth = weights[0].shape[1]
+    pieces = [columns_of(acts, partners, i, depth) for i in range(count)]
+
+    def proj(c):
+        total = dot(pieces[0], weights[0][c], NN)
+        for i in range(1, count):
+            total = total + dot(pieces[i], weights[i][c], NN)
+        return total
+
+    query[...] = turn(proj(0), cosine[...], sine[...]).astype(low)
+    keys[...] = turn(proj(1), cosine[...], sine[...]).astype(low)
+    values[...] = proj(2).astype(low)
     for begin in range(0, length, block):
         end = begin + block
         total = jnp.zeros((block, width), f32)
@@ -199,30 +203,57 @@
         logsum[begin:end, :] = sums
 
 
-def attend_forward(proj, tables):
-    length, width = proj.shape[1:]
+VMEM = pl.BlockSpec(memory_space=pltpu.VMEM)
+SMEM = pl.BlockSpec(memory_space=pltpu.SMEM)
+
+
+def params(mebibytes=56):
+    return pltpu.CompilerParams(vmem_limit_bytes=mebibytes * 1024 * 1024)
+
+
+def cost(flops, operands, transcendentals=0):
+    return pl.CostEstimate(
+        flops=flops,
+        bytes_accessed=sum(v.size * v.dtype.itemsize for v in operands),
+        transcendentals=transcendentals,
+    )
+
+
+def attend_forward(partners, acts, weights, tables):
+    length = acts.shape[0]
+    width = weights[0].shape[2]
     block = min(length, 256)
     flat = jax.ShapeDtypeStruct((length, width), low)
     heads = width // HD
     return pl.pallas_call(
-        functools.partial(forward_kernel, block),
+        functools.partial(forward_kernel, block, len(weights)),
         out_shape=[flat, flat, flat, flat, jax.ShapeDtypeStruct((length, 128), f32)],
-        compiler_params=pltpu.CompilerParams(vmem_limit_bytes=40 * 1024 * 1024),
-        cost_estimate=pl.CostEstimate(
-            flops=4 * length * length * 256 * heads,
-            bytes_accessed=length * width * 30,
-            transcendentals=heads * length * length // 2,
+        in_specs=[SMEM] + [VMEM] * (3 + len(weights)),
+        out_specs=[VMEM] * 5,
+        compiler_params=params(),
+        cost_estimate=cost(
+            6 * length * acts.shape[1] * width + 4 * length * length * 256 * heads,
+            [acts, *weights, *tables],
+            heads * length * length // 2,
         ),
         name="attend_forward",
-    )(proj, *tables)
-
-
-def backward_kernel(
-    block, query, keys, values, mixed, logsum, grad, cosine, sine, out, grad_keys, grad_values
-):
+    )(partners, acts, *tables, *weights)
+
+
+def backward_kernel(block, count, partners, query, keys, values, mixed, logsum, acts, grads, *refs):
+    cosine, sine = refs[:2]
+    weights = refs[2 : 2 + count]
+    out = refs[2 + count]
+    terms = refs[3 + count : 3 + 2 * count]
+    grad, grad_keys, grad_values = refs[3 + 2 * count :]
     length, width = query.shape
     heads = width // HD
     scale = HD**-0.5
+    depth = weights[0].shape[1]
+    total = dot(columns_of(grads, partners, 0, depth), weights[0][3], NN)
+    for i in range(1, count):
+        total = total + dot(columns_of(grads, partners, i, depth), weights[i][3], NN)
+    grad[...] = total.astype(low)
     grad_keys[...] = jnp.zeros_like(grad_keys)
     grad_values[...] = jnp.zeros_like(grad_values)
     for begin in range(0, length, block):
@@ -240,29 +271,212 @@
             total = total + of_head(dot(grad_scores, keys[:end, :], NN), head)
             grad_keys[:end, :] += dot(grad_scores, one, TN)
             grad_values[:end, :] += dot(prob.astype(low), grad_one, TN)
-        out[0, begin:end, :] = turn(
+        out[begin:end, :width] = turn(
             total * scale, cosine[begin:end, :], -sine[begin:end, :]
         ).astype(low)
-    out[1] = turn(grad_keys[...], cosine[...], -sine[...]).astype(low)
-    out[2] = grad_values[...].astype(low)
-
-
-def attend_backward(saved, grad, tables):
-    length, width = grad.shape
+    out[:, width : 2 * width] = turn(grad_keys[...], cosine[...], -sine[...]).astype(low)
+    out[:, 2 * width :] = grad_values[...].astype(low)
+    for i in range(count):
+        inward = dot(columns_of(acts, partners, i, depth), out[...], TN).astype(low)
+        for c in range(3):
+            terms[i][c] = inward[:, c * width : (c + 1) * width]
+        terms[i][3] = dot(columns_of(grads, partners, i, depth), mixed[...], TN).astype(low)
+
+
+def attend_backward(partners, saved, acts, grads, weights, tables):
+    length, width = saved[0].shape
     block = min(length, 256)
     heads = width // HD
-    return pl.pallas_call(
-        functools.partial(backward_kernel, block),
-        out_shape=jax.ShapeDtypeStruct((3, length, width), low),
-        scratch_shapes=[pltpu.VMEM((length, width), f32)] * 2,
-        compiler_params=pltpu.CompilerParams(vmem_limit_bytes=48 * 1024 * 1024),
-        cost_estimate=pl.CostEstimate(
-            flops=10 * length * length * 256 * heads,
-            bytes_accessed=length * width * 30,
-            transcendentals=heads * length * length // 2,
+    count = len(weights)
+    operands = [*saved, acts, grads, *tables, *weights]
+    found = pl.pallas_call(
+        functools.partial(backward_kernel, block, count),
+        out_shape=[jax.ShapeDtypeStruct((length, 3 * width), low)]
+        + [jax.ShapeDtypeStruct(weights[0].shape, low)] * count,
+        in_specs=[SMEM] + [VMEM] * len(operands),
+        out_specs=[VMEM] * (1 + count),
+        scratch_shapes=[pltpu.VMEM((length, width), low)]
+        + [pltpu.VMEM((length, width), f32)] * 2,
+        compiler_params=params(),
+        cost_estimate=cost(
+            10 * length * acts.shape[1] * width + 10 * length * length * 256 * heads,
+            operands,
+            heads * length * length // 2,
         ),
         name="attend_backward",
-    )(*saved, grad, *tables)
+    )(partners, *operands)
+    return found[0], found[1:]
+
+
+def spread_kernel(parts, count, slices, partners, *refs):
+    values = refs[:parts]
+    weights = refs[parts:-1]
+    out = refs[-1]
+    depth = weights[0].shape[1]
+    width = weights[0].shape[2]
+    for i in range(count):
+        total = None
+        for k in range(parts):
+            for c in range(slices):
+                one = dot(
+                    values[k][:, c * width : (c + 1) * width], weights[k * count + i][c], NT
+                )
+                total = one if total is None else total + one
+        out[:, pl.ds(pl.multiple_of(partners[i] * depth, depth), depth)] = total.astype(low)
+
+
+def spread(partners, values, weights, first, slices):
+    count = len(weights[0])
+    flat = [w for group in weights for w in group]
+    depth, width = flat[0].shape[1:]
+    rows = values[0].shape[0]
+    return pl.pallas_call(
+        functools.partial(spread_kernel, len(values), count, slices),
+        grid=(1,),
+        out_shape=jax.ShapeDtypeStruct((rows, count * depth), low),
+        in_specs=[SMEM]
+        + [pl.BlockSpec(v.shape, lambda i: (0, 0)) for v in values]
+        + [pl.BlockSpec((slices, depth, width), lambda i: (first, 0, 0)) for w in flat],
+        out_specs=pl.BlockSpec((rows, count * depth), lambda i: (0, 0)),
+        compiler_params=params(60),
+        cost_estimate=cost(
+            2 * rows * count * depth * width * slices * len(values), [*values, *flat]
+        ),
+        name="spread",
+    )(partners, *values, *flat)
+
+
+def resident(value):
+    return pl.BlockSpec(value.shape, lambda i: (0,) * value.ndim)
+
+
+def feed_kernel(parts, *refs):
+    feeds = refs[:parts]
+    expand, hidden, slope, passed = refs[parts:]
+    rows = feeds[0].shape[0]
+    for p in range(parts):
+        gate = dot(feeds[p][...], expand[0, 0], NN)
+        up = dot(feeds[p][...], expand[0, 1], NN)
+        sigma = jax.nn.sigmoid(gate)
+        silu = gate * sigma
+        here = slice(p * rows, (p + 1) * rows)
+        hidden[here, :] = (silu * up).astype(low)
+        slope[here, :] = (up * (sigma + silu * (1.0 - sigma))).astype(low)
+        passed[here, :] = silu.astype(low)
+
+
+def feed_forward(feeds, expand):
+    pieces, _, depth, width = expand.shape
+    rows = sum(v.shape[0] for v in feeds)
+    tile = pl.BlockSpec((rows, width), lambda i: (0, i))
+    return pl.pallas_call(
+        functools.partial(feed_kernel, len(feeds)),
+        grid=(pieces,),
+        out_shape=[jax.ShapeDtypeStruct((rows, pieces * width), low)] * 3,
+        in_specs=[resident(v) for v in feeds]
+        + [pl.BlockSpec((1, 2, depth, width), lambda i: (i, 0, 0, 0))],
+        out_specs=[tile] * 3,
+        compiler_params=params(),
+        cost_estimate=cost(4 * rows * depth * pieces * width, [*feeds, expand]),
+        name="feed_forward",
+    )(*feeds, expand)
+
+
+def hidden_kernel(parts, *refs):
+    grads = refs[:parts]
+    shrink, slope, passed, out = refs[parts:]
+    rows = grads[0].shape[0]
+    for p in range(parts):
+        here = slice(p * rows, (p + 1) * rows)
+        grad = dot(grads[p][...], shrink[0], NN)
+        out[0, here, :] = (grad * slope[here, :].astype(f32)).astype(low)
+        out[1, here, :] = (grad * passed[here, :].astype(f32)).astype(low)
+
+
+def hidden_backward(grads, shrink, slope, passed):
+    pieces, depth, width = shrink.shape
+    rows = sum(v.shape[0] for v in grads)
+    tile = pl.BlockSpec((rows, width), lambda i: (0, i))
+    return pl.pallas_call(
+        functools.partial(hidden_kernel, len(grads)),
+        grid=(pieces,),
+        out_shape=jax.ShapeDtypeStruct((2, rows, pieces * width), low),
+        in_specs=[resident(v) for v in grads]
+        + [pl.BlockSpec((1, depth, width), lambda i: (i, 0, 0)), tile, tile],
+        out_specs=pl.BlockSpec((2, rows, width), lambda i: (0, 0, i)),
+        compiler_params=params(),
+        cost_estimate=cost(2 * rows * depth * pieces * width, [*grads, shrink, slope]),
+        name="hidden_backward",
+    )(*grads, shrink, slope, passed)
+
+
+def back_kernel(value, weight, *outs):
+    several, pieces = weight.shape[1], weight.shape[0]
+    width = weight.shape[3]
+    rows = outs[0].shape[0]
+    for p, out in enumerate(outs):
+        total = None
+        for c in range(several):
+            for k in range(pieces):
+                one = dot(
+                    value[c, p * rows : (p + 1) * rows, k * width : (k + 1) * width],
+                    weight[k, c],
+                    NT,
+                )
+                total = one if total is None else total + one
+        out[...] = total.astype(low)
+
+
+def times_back(value, weight, parts):
+    pieces, several, depth, width = weight.shape
+    rows = value.shape[1] // parts
+    tile = min(depth, 512)
+    return pl.pallas_call(
+        back_kernel,
+        grid=(depth // tile,),
+        out_shape=[jax.ShapeDtypeStruct((rows, depth), low)] * parts,
+        in_specs=[
+            resident(value),
+            pl.BlockSpec((pieces, several, tile, width), lambda i: (0, 0, i, 0)),
+        ],
+        out_specs=[pl.BlockSpec((rows, tile), lambda i: (0, i))] * parts,
+        compiler_params=params(),
+        cost_estimate=cost(2 * value.size * depth, [value, weight]),
+        name="times_back",
+    )(value, weight)
+
+
+def weight_kernel(lefts, rights, *refs):
+    out = refs[-1]
+    per = lefts // rights
+    rows = refs[0].shape[0]
+    for c in range(out.shape[0]):
+        total = None
+        for i in range(lefts):
+            begin = i % per * rows
+            one = dot(refs[i][...], refs[lefts + i // per][c, begin : begin + rows, :], TN)
+            total = one if total is None else total + one
+        out[c] = total.astype(low)
+
+
+def weight_terms(lefts, rights, k, width):
+    depth = lefts[0].shape[1]
+    several = rights[0].shape[0]
+    tile = min(depth, 512)
+    rows = lefts[0].shape[0]
+    return pl.pallas_call(
+        functools.partial(weight_kernel, len(lefts), len(rights)),
+        grid=(depth // tile,),
+        out_shape=jax.ShapeDtypeStruct((several, depth, width), low),
+        in_specs=[pl.BlockSpec((rows, tile), lambda i: (0, i)) for _ in lefts]
+        + [pl.BlockSpec((several, v.shape[1], width), lambda i: (0, 0, k)) for v in rights],
+        out_specs=pl.BlockSpec((several, tile, width), lambda i: (0, i, 0)),
+        compiler_params=params(),
+        cost_estimate=cost(
+            2 * rows * len(lefts) * depth * width * several, [*lefts, rights[0]]
+        ),
+        name="weight_terms",
+    )(*lefts, *rights)
 
 
 def norm_scale(value):
@@ -314,10 +528,7 @@
 
     attn_own = jnp.concatenate([inward_weight, outward_weight[None]], axis=0).astype(low)
     attn_blocks = mv.ring_gather(attn_own)
-    attn_full = []
-    for k in ks:
-        pieces = mv.plane_gather(attn_blocks[k], 1 + k % 2)
-        attn_full.append(mv.place(pieces, 1, mv.f))
+    attn_full = [mv.plane_gather(attn_blocks[k]) for k in ks]
 
     def quarter(d):
         begin = (mv.f ^ d) * hidden_width
@@ -326,21 +537,26 @@
         return jnp.concatenate([both, last[None]], axis=0).astype(low)
 
     ff_own = mv.place([quarter(0)] + [mv.plane(quarter(d), d) for d in planes if d], 1, mv.f)
-    expand_full = jnp.concatenate(mv.ring_gather(ff_own[:2]), axis=2)
-    shrink_full = jnp.concatenate(mv.ring_gather(ff_own[2]), axis=1)
+    expand_blocks = mv.ring_gather(after(ff_own[:2], attn_blocks[-1]))
+    shrink_blocks = mv.ring_gather(after(ff_own[2], expand_blocks[-1]))
+    group = max(1, 128 // hidden_width)
+
+    def grouped(blocks):
+        if group == 1:
+            return jnp.stack(blocks)
+        joined = range(0, Z, group)
+        return jnp.stack([jnp.concatenate(blocks[k : k + group], axis=-1) for k in joined])
+
+    expand_full = grouped(expand_blocks)
+    shrink_full = grouped(shrink_blocks)
 
     source = layer_input.astype(f32)
     scale_one = norm_scale(source)
     normed_one = source * scale_one
     acts = mv.place(mv.mates((normed_one * norm_gains[0]).astype(low)), 0, mv.s)
     tables = rope_tables(LEN, own_width)
-    saved = []
-    for k in ks:
-        proj = jnp.einsum("td,cde->cte", acts, attn_full[k][:3], preferred_element_type=f32)
-        saved.append(attend_forward(proj, tables))
-    mixed = jnp.concatenate([s[3] for s in saved], axis=1)
-    outward_full = jnp.concatenate([w[3] for w in attn_full], axis=1)
-    attended = dot(mixed, outward_full, NT).astype(low)
+    saved = [attend_forward(mv.partners, acts, attn_full[k], tables) for k in ks]
+    attended = spread(mv.partners, [s[3] for s in saved], attn_full, 3, 1)
 
     def part(value, d):
         return lax.dynamic_slice_in_dim(value, (mv.s ^ d) * rows, rows, 0)
@@ -350,61 +566,50 @@
     normed_two = resid * scale_two
     feed_local = (normed_two * norm_gains[1]).astype(low)
 
-    feed_blocks = [
-        jnp.concatenate(mv.mates(block), axis=0) for block in mv.plane_gather_rows(feed_local)
-    ]
-    grad_blocks = [
-        jnp.concatenate(mv.mates(block), axis=0) for block in mv.plane_gather_rows(cotangent)
-    ]
-    hidden, grad_gate_up, grad_feed, fed = [], [], [], []
+    feed_gathered = mv.plane_gather(feed_local)
+    feed_blocks = [mv.mates(block) for block in feed_gathered]
+    grad_gathered = mv.plane_gather(after(cotangent, *feed_gathered[1:3]))
+    grad_blocks = [mv.mates(block) for block in grad_gathered]
+    kept = [feed_forward(feed_blocks[d], expand_full) for d in planes]
+    hidden = [h[0] for h in kept]
+    grad_gate_up = [None] * F
+    grad_feed = [None] * F
+    late_first = list(planes)[::-1]
     for d in planes:
-        gate_up = jnp.einsum(
-            "td,cdf->ctf", feed_blocks[d], expand_full, preferred_element_type=f32
-        )
-        gate, up = gate_up[0], gate_up[1]
-        sigma = jax.nn.sigmoid(gate)
-        silu = gate * sigma
-        hidden.append((silu * up).astype(low))
-        slope = (up * sigma * (1.0 + gate * (1.0 - sigma))).astype(low)
-        silu = silu.astype(low)
-        grad_hidden = dot(grad_blocks[d], shrink_full, NN)
-        grad_gate_up.append(
-            jnp.stack([grad_hidden * slope.astype(f32), grad_hidden * silu.astype(f32)]).astype(
-                low
-            )
-        )
-    for d in planes:
-        grad_feed.append(
-            jnp.einsum(
-                "ctf,cdf->td", grad_gate_up[d], expand_full, preferred_element_type=f32
-            ).astype(low)
-        )
-    for d in planes:
-        fed.append(dot(hidden[d], shrink_full, NT).astype(low))
+        grad_gate_up[d] = hidden_backward(grad_blocks[d], shrink_full, kept[d][1], kept[d][2])
 
     def chip_sum(block):
-        return mv.mates_sum([block[d * rows : (d + 1) * rows] for d in range(S)]).astype(low)
-
-    grad_feed = mv.plane_sum_rows([chip_sum(block) for block in grad_feed])
+        return mv.mates_sum(block).astype(low)
+
+    for d in late_first:
+        grad_feed[d] = chip_sum(times_back(grad_gate_up[d], expand_full, S))
+    fed = [chip_sum(times_back(hidden[d][None], shrink_full[:, None], S)) for d in planes]
+    grad_feed = mv.plane_sum(grad_feed)
     resid_back, gain_two = norm_back(grad_feed, normed_two, scale_two, norm_gains[1])
     grad_resid = cotangent.astype(f32) + resid_back
-    fed = mv.plane_sum_rows([chip_sum(block) for block in fed])
-    layer_output = (resid + fed).astype(low)
-
-    feed_all = jnp.concatenate(feed_blocks, axis=0)
-    grad_all = jnp.concatenate(grad_blocks, axis=0)
-    hidden_all = jnp.concatenate(hidden, axis=0)
-    grad_gate_up_all = jnp.concatenate(grad_gate_up, axis=1)
-    shrink_terms = dot(grad_all, hidden_all, TN).astype(low)
-    expand_terms = jnp.einsum(
-        "td,ctf->cdf", feed_all, grad_gate_up_all, preferred_element_type=f32
-    ).astype(low)
-
-    def hidden_part(value, k):
-        return lax.slice_in_dim(value, k * hidden_width, (k + 1) * hidden_width, axis=-1)
-
-    shrink_sum = mv.ring_sum([hidden_part(shrink_terms, k) for k in ks]).astype(low)
-    expand_sum = mv.ring_sum([hidden_part(expand_terms, k) for k in ks]).astype(low)
+    layer_output = (resid + mv.plane_sum(fed)).astype(low)
+
+    def all_of(blocks):
+        return [v for block in blocks for v in block]
+
+    def terms_of(lefts, rights):
+        if group == 1:
+            return [weight_terms(lefts, rights, k, hidden_width) for k in ks]
+        joined = [weight_terms(lefts, rights, g, group * hidden_width) for g in range(Z // group)]
+        return [
+            lax.slice_in_dim(
+                joined[k // group],
+                k % group * hidden_width,
+                (k % group + 1) * hidden_width,
+                axis=-1,
+            )
+            for k in ks
+        ]
+
+    shrink_sum = mv.ring_sum(
+        terms_of(all_of(grad_blocks), [h[None] for h in hidden])
+    ).astype(low)[0]
+    expand_sum = mv.ring_sum(terms_of(all_of(feed_blocks), grad_gate_up)).astype(low)
 
     def rows_part(value, d):
         return lax.dynamic_slice_in_dim(value, (mv.f ^ d) * row_block, row_block, -2)
@@ -417,21 +622,16 @@
     expand_grad = columns(expand_sum)
 
     grad_attn = mv.place(mv.mates(grad_resid.astype(low)), 0, mv.s)
-    grad_acts = 0.0
-    attn_terms = []
-    for k in ks:
-        grad_mixed = dot(grad_attn, attn_full[k][3], NN).astype(low)
-        grad_proj = attend_backward(saved[k], grad_mixed, tables)
-        inward_terms = jnp.einsum("td,cte->cde", acts, grad_proj, preferred_element_type=f32)
-        outward_terms = dot(grad_attn, saved[k][3], TN)
-        terms = jnp.concatenate([inward_terms, outward_terms[None]], axis=0).astype(low)
-        attn_terms.append(mv.plane_sum([rows_part(terms, d) for d in planes], 1 + k % 2))
-        grad_acts = grad_acts + jnp.einsum(
-            "cte,cde->td", grad_proj, attn_full[k][:3], preferred_element_type=f32
+    attn_terms = [None] * Z
+    grad_proj = [None] * Z
+    for k in list(range(1, Z)) + [0]:
+        grad_proj[k], terms = attend_backward(
+            mv.partners, saved[k], acts, grad_attn, attn_full[k], tables
         )
+        attn_terms[k] = mv.plane_sum(terms)
     attn_grad = mv.ring_sum(attn_terms)
     inward_grad, outward_grad = attn_grad[:3], attn_grad[3]
-    grad_acts = grad_acts.astype(low)
+    grad_acts = spread(mv.partners, grad_proj, attn_full, 0, 3)
     grad_acts = mv.mates_sum([part(grad_acts, d) for d in range(S)])
     input_back, gain_one = norm_back(grad_acts, normed_one, scale_one, norm_gains[0])
     input_grad = (grad_resid + input_back).astype(low)
@@ -442,7 +642,11 @@
         + jnp.sum(expand_grad * expand_grad)
         + jnp.sum(shrink_grad * shrink_grad)
     )
-    gains_grad, squares = lax.psum((jnp.stack([gain_one, gain_two]), owned_squares), ("fsdp", "tp"))
+    sums = jnp.concatenate(
+        [jnp.stack([gain_one, gain_two]), jnp.full((1, gain_one.shape[0]), owned_squares)], axis=0
+    )
+    sums = mv.total(sums)
+    gains_grad, squares = sums[:2], sums[2, 0]
     norm = jnp.sqrt(squares + jnp.sum(gains_grad * gains_grad))
     factor = jnp.minimum(1.0, clip_bound / (norm + 1e-06))
     inward_new = adamw(

time: 1460 us -> 1100 us (0.75)
  Pallas kernels: 72.3 us -> 471 us
  matrix products: 349 us -> 0 us
  waiting for transfers between devices: 552 us -> 362 us
  local copies, waits for them, and re-layouts: 216 us -> 38.5 us
  blocking collectives: 37.8 us -> 0 us
  other arithmetic: 144 us -> 129 us
    pallas_call x8 -> x34, Pallas kernels: 72.3 us -> 471 us  [the longest x8 101 us: weight_terms(): pl.pallas_call(functools.partial(weight_kernel, len(lefts), len(rights)),...]
    dot_general x39 -> x0, matrix products: 349 us -> none  [the longest x18 120 us: dot(): return lax.dot_general(a, b, (dims, ((), ())), preferred_element_type=f32)]
    ppermute x49 -> x11, waiting for transfers between devices: 346 us -> 49.1 us  [plane(): return lax.ppermute(value, 'fsdp', [(i, i ^ mask) for i in range(self.F)])]
    ppermute x0 -> x36, waiting for transfers between devices: none -> 140 us  [hop(): return lax.ppermute(value, ('fsdp', 'tp'), pairs)]
    unnamed x363 -> x150, local copies, waits for them, and re-layouts: 141 us -> 11.3 us
    ppermute x0 -> x36, starting transfers between devices: none -> 42.8 us  [hop(): return lax.ppermute(value, ('fsdp', 'tp'), pairs)]
    ppermute x18, waiting for transfers between devices: 206 us -> 167 us  [ring(): return lax.ppermute(value, 'tp', step)]
    ppermute x49 -> x11, starting transfers between devices: 53.1 us -> 14.8 us  [plane(): return lax.ppermute(value, 'fsdp', [(i, i ^ mask) for i in range(self.F)])]
  transfers between devices with their start and end apart: 87 -> 88, of which waited for: 33 -> 28; matrix products, arithmetic and copies ran while one was open for 42% -> 12% of each run, Pallas kernels for 5% -> 43%
where the time goes in v2:
time: 1100 us; the launch traced here: 1090 us
  Pallas kernels  471 us (43%)
  waiting for transfers between devices  362 us (33%)
  other arithmetic  129 us (12%)
  starting transfers between devices  85 us (8%)
  local copies, waits for them, and re-layouts  38.5 us (4%)
    ppermute x18, waiting for transfers between devices, ring(): return lax.ppermute(value, 'tp', step)  167 us
    ppermute x36, waiting for transfers between devices, hop(): return lax.ppermute(value, ('fsdp', 'tp'), pairs)  140 us
    pallas_call x8, Pallas kernels, weight_terms(): pl.pallas_call(functools.partial(weight_kernel, len(lefts), len(rights)),...  101 us
    pallas_call x4, Pallas kernels, attend_backward(): pl.pallas_call(functools.partial(backward_kernel, block, count), out_shap...  96.3 us
    pallas_call x8, Pallas kernels, times_back(): pl.pallas_call(back_kernel, grid=(depth // tile,), out_shape=[jax.ShapeDt...  85.3 us
    pallas_call x4, Pallas kernels, attend_forward(): pl.pallas_call(functools.partial(forward_kernel, block, len(weights)), ou...  62.5 us
    pallas_call x4, Pallas kernels, feed_forward(): pl.pallas_call(functools.partial(feed_kernel, len(feeds)), grid=(pieces,)...  55.3 us
    ppermute x11, waiting for transfers between devices, plane(): return lax.ppermute(value, 'fsdp', [(i, i ^ mask) for i in range(self.F)])  49.1 us
  transfers between devices with their start and end apart: 88, of which 28 were waited for; matrix products, arithmetic and copies ran while one was open for 12% of the time, Pallas kernels for 43%

profile of v2, /device:TPU:0, one launch (start us, length us, event | category | flops | bytes accessed | tf_op | source)
XLA Modules:
  0.0 1091.3 jit_solution(15082513042895116926)
XLA Ops:
  36.6 18.3 %collective-permute-done.19 = bf16[3,512,256]{2,1,0:T(8,128)(2,1)} collective-permute-done((bf16[3,512,256]{2,1,0:T(8,128)(2,1)}, bf16[3,512,256]{2,1,0:T(8,128)(2,1)}, u32[]{:S(2)}, u32[]{:S(2)}) %collective-permute-start.19) | collective-permute-done | bytes 786464 | tf_op jit(solution)/shard_map/ppermute | solution.py:55
  102.4 23.6 %collective-permute-done.3.refs_3_.refs_7_.refs_5_ = bf16[4,512,256]{2,1,0:T(8,128)(2,1)} collective-permute-done((bf16[4,512,256]{2,1,0:T(8,128)(2,1)}, bf16[4,512,256]{2,1,0:T(8,128)(2,1)}, u32[]{:S(2)}, u32[]{:S(2)}) %collective-permute-start.3) | collective-permute-done | bytes 1048608 | tf_op jit(solution)/shard_map/ppermute | solution.py:63
  130.0 15.5 %attend_forward.4 = (bf16[1024,256]{1,0:T(8,128)(2,1)}, bf16[1024,256]{1,0:T(8,128)(2,1)}, bf16[1024,256]{1,0:T(8,128)(2,1)}, bf16[1024,256]{1,0:T(8,128)(2,1)}, f32[1024,128]{1,0:T(8,128)}) custom-call(s32[4]{0:T(128)} %pad_add_fusion.partners, bf16[1024,2048]{1,0:T(8,128)(2,1)} %copy-done.25, f32[1024,256]{1,0:T(8,128)} %copy.43.cosine.refs_0_, ...), custom_call_target="tpu_custom_call" | custom-call | flops 7516192768 | bytes 10485760 | tf_op jit(solution)/shard_map/attend_forward/pallas_call | solution.py:228
  147.7 15.6 %attend_forward.5 = (bf16[1024,256]{1,0:T(8,128)(2,1)}, bf16[1024,256]{1,0:T(8,128)(2,1)}, bf16[1024,256]{1,0:T(8,128)(2,1)}, bf16[1024,256]{1,0:T(8,128)(2,1)}, f32[1024,128]{1,0:T(8,128)}) custom-call(s32[4]{0:T(128)} %pad_add_fusion.partners, bf16[1024,2048]{1,0:T(8,128)(2,1)} %copy-done.25, f32[1024,256]{1,0:T(8,128)} %copy.43.cosine.refs_0_, ...), custom_call_target="tpu_custom_call" | custom-call | flops 7516192768 | bytes 10485760 | tf_op jit(solution)/shard_map/attend_forward/pallas_call | solution.py:228
  166.4 15.9 %attend_forward.6 = (bf16[1024,256]{1,0:T(8,128)(2,1)}, bf16[1024,256]{1,0:T(8,128)(2,1)}, bf16[1024,256]{1,0:T(8,128)(2,1)}, bf16[1024,256]{1,0:T(8,128)(2,1)}, f32[1024,128]{1,0:T(8,128)}) custom-call(s32[4]{0:T(128)} %pad_add_fusion.partners, bf16[1024,2048]{1,0:T(8,128)(2,1)} %copy-done.25, f32[1024,256]{1,0:T(8,128)} %copy.43.cosine.refs_0_, ...), custom_call_target="tpu_custom_call" | custom-call | flops 7516192768 | bytes 10485760 | tf_op jit(solution)/shard_map/attend_forward/pallas_call | solution.py:228
  188.9 15.5 %attend_forward.7 = (bf16[1024,256]{1,0:T(8,128)(2,1)}, bf16[1024,256]{1,0:T(8,128)(2,1)}, bf16[1024,256]{1,0:T(8,128)(2,1)}, bf16[1024,256]{1,0:T(8,128)(2,1)}, f32[1024,128]{1,0:T(8,128)}) custom-call(s32[4]{0:T(128)} %pad_add_fusion.partners, bf16[1024,2048]{1,0:T(8,128)(2,1)} %copy-done.25, f32[1024,256]{1,0:T(8,128)} %copy.43.cosine.refs_0_, ...), custom_call_target="tpu_custom_call" | custom-call | flops 7516192768 | bytes 10485760 | tf_op jit(solution)/shard_map/attend_forward/pallas_call | solution.py:228
  216.9 13.8 %collective-permute-done.22 = bf16[2,2048,256]{2,1,0:T(8,128)(2,1)} collective-permute-done((bf16[2,2048,256]{2,1,0:T(8,128)(2,1)}, bf16[2,2048,256]{2,1,0:T(8,128)(2,1)}, u32[]{:S(2)}, u32[]{:S(2)}) %collective-permute-start.22) | collective-permute-done | bytes 2097184 | tf_op jit(solution)/shard_map/ppermute | solution.py:74
  240.5 37.6 %collective-permute-done.23 = bf16[2,2048,256]{2,1,0:T(8,128)(2,1)S(1)} collective-permute-done((bf16[2,2048,256]{2,1,0:T(8,128)(2,1)}, bf16[2,2048,256]{2,1,0:T(8,128)(2,1)S(1)}, u32[]{:S(2)}, u32[]{:S(2)}) %collective-permute-start.23) | collective-permute-done | bytes 2097184 | tf_op jit(solution)/shard_map/ppermute | solution.py:74
  284.5 17.3 %collective-permute-done.24 = bf16[2048,256]{1,0:T(8,128)(2,1)} collective-permute-done((bf16[2048,256]{1,0:T(8,128)(2,1)S(1)}, bf16[2048,256]{1,0:T(8,128)(2,1)}, u32[]{:S(2)}, u32[]{:S(2)}) %collective-permute-start.24) | collective-permute-done | bytes 1048608 | tf_op jit(solution)/shard_map/ppermute | solution.py:74
  324.9 13.7 %feed_forward.4 = (bf16[1024,1024]{1,0:T(8,128)(2,1)}, bf16[1024,1024]{1,0:T(8,128)(2,1)}, bf16[1024,1024]{1,0:T(8,128)(2,1)}) custom-call(bf16[512,2048]{1,0:T(8,128)(2,1)} %multiply_convert_fusion.refs_0_, bf16[512,2048]{1,0:T(8,128)(2,1)} %collective-permute-done.17.refs_1_, bf16[4,2,2048,256]{3,2,1,0:T(8,128)(2,1)} %pad_maximum_fusion.refs_2_.weight), custom_call_target="tpu_custom_call" | custom-call | flops 8589934592 | bytes 12582912 | tf_op jit(solution)/shard_map/feed_forward/pallas_call | solution.py:372
  452.3 14.1 %feed_forward.7 = (bf16[1024,1024]{1,0:T(8,128)(2,1)}, bf16[1024,1024]{1,0:T(8,128)(2,1)}, bf16[1024,1024]{1,0:T(8,128)(2,1)}) custom-call(bf16[512,2048]{1,0:T(8,128)(2,1)} %collective-permute-done.35.refs_0_.refs_6_, bf16[512,2048]{1,0:T(8,128)(2,1)} %collective-permute-done.36.refs_1_.refs_7_, bf16[4,2,2048,256]{3,2,1,0:T(8,128)(2,1)} %pad_maximum_fusion.refs_2_.weight), custom_call_target="tpu_custom_call" | custom-call | flops 8589934592 | bytes 12582912 | tf_op jit(solution)/shard_map/feed_forward/pallas_call | solution.py:372
  537.2 14.7 %weight_terms.10 = bf16[2,2048,256]{2,1,0:T(8,128)(2,1)} custom-call(bf16[512,2048]{1,0:T(8,128)(2,1)} %multiply_convert_fusion.refs_0_, bf16[512,2048]{1,0:T(8,128)(2,1)} %collective-permute-done.17.refs_1_, bf16[512,2048]{1,0:T(8,128)(2,1)} %collective-permute-done.28.refs_0_.refs_2_, bf16[512,2048]{1,0:T(8,128)(2,1)} %collective-permute-done.29.refs_1_.refs_3_, ...), custom_call_target="tpu_custom_call" | custom-call | flops 8589934592 | bytes 20971520 | tf_op jit(solution)/shard_map/weight_terms/pallas_call | solution.py:467
  551.9 14.5 %weight_terms.9 = bf16[2,2048,256]{2,1,0:T(8,128)(2,1)} custom-call(bf16[512,2048]{1,0:T(8,128)(2,1)} %multiply_convert_fusion.refs_0_, bf16[512,2048]{1,0:T(8,128)(2,1)} %collective-permute-done.17.refs_1_, bf16[512,2048]{1,0:T(8,128)(2,1)} %collective-permute-done.28.refs_0_.refs_2_, bf16[512,2048]{1,0:T(8,128)(2,1)} %collective-permute-done.29.refs_1_.refs_3_, ...), custom_call_target="tpu_custom_call" | custom-call | flops 8589934592 | bytes 20971520 | tf_op jit(solution)/shard_map/weight_terms/pallas_call | solution.py:467
  566.5 14.6 %weight_terms.8 = bf16[2,2048,256]{2,1,0:T(8,128)(2,1)} custom-call(bf16[512,2048]{1,0:T(8,128)(2,1)} %multiply_convert_fusion.refs_0_, bf16[512,2048]{1,0:T(8,128)(2,1)} %collective-permute-done.17.refs_1_, bf16[512,2048]{1,0:T(8,128)(2,1)} %collective-permute-done.28.refs_0_.refs_2_, bf16[512,2048]{1,0:T(8,128)(2,1)} %collective-permute-done.29.refs_1_.refs_3_, ...), custom_call_target="tpu_custom_call" | custom-call | flops 8589934592 | bytes 20971520 | tf_op jit(solution)/shard_map/weight_terms/pallas_call | solution.py:467
  611.2 20.5 %collective-permute-done.71 = bf16[2,2048,256]{2,1,0:T(8,128)(2,1)S(1)} collective-permute-done((bf16[2,2048,256]{2,1,0:T(8,128)(2,1)}, bf16[2,2048,256]{2,1,0:T(8,128)(2,1)S(1)}, u32[]{:S(2)}, u32[]{:S(2)}) %collective-permute-start.71) | collective-permute-done | bytes 2097184 | tf_op jit(solution)/shard_map/ppermute | solution.py:74
  679.4 45.8 %collective-permute-done.79 = bf16[1,2048,256]{2,1,0:T(8,128)(2,1)} collective-permute-done((bf16[1,2048,256]{2,1,0:T(8,128)(2,1)S(1)}, bf16[1,2048,256]{2,1,0:T(8,128)(2,1)}, u32[]{:S(2)}, u32[]{:S(2)}) %collective-permute-start.79) | collective-permute-done | bytes 1048608 | tf_op jit(solution)/shard_map/ppermute | solution.py:74
  735.8 37.9 %collective-permute-done.31 = bf16[512,2048]{1,0:T(8,128)(2,1)S(1)} collective-permute-done((bf16[512,2048]{1,0:T(8,128)(2,1)S(1)}, bf16[512,2048]{1,0:T(8,128)(2,1)S(1)}, u32[]{:S(2)}, u32[]{:S(2)}) %collective-permute-start.31) | collective-permute-done | bytes 2097184 | tf_op jit(solution)/shard_map/ppermute | solution.py:63
  785.1 14.7 %weight_terms.11 = bf16[2,2048,256]{2,1,0:T(8,128)(2,1)} custom-call(bf16[512,2048]{1,0:T(8,128)(2,1)} %multiply_convert_fusion.refs_0_, bf16[512,2048]{1,0:T(8,128)(2,1)} %collective-permute-done.17.refs_1_, bf16[512,2048]{1,0:T(8,128)(2,1)} %collective-permute-done.28.refs_0_.refs_2_, bf16[512,2048]{1,0:T(8,128)(2,1)} %collective-permute-done.29.refs_1_.refs_3_, ...), custom_call_target="tpu_custom_call" | custom-call | flops 8589934592 | bytes 20971520 | tf_op jit(solution)/shard_map/weight_terms/pallas_call | solution.py:467
  809.5 24.0 %attend_backward.7 = (bf16[1024,768]{1,0:T(8,128)(2,1)}, bf16[4,512,256]{2,1,0:T(8,128)(2,1)}, bf16[4,512,256]{2,1,0:T(8,128)(2,1)}, bf16[4,512,256]{2,1,0:T(8,128)(2,1)}, bf16[4,512,256]{2,1,0:T(8,128)(2,1)}) custom-call(s32[4]{0:T(128)} %pad_add_fusion.partners, bf16[1024,256]{1,0:T(8,128)(2,1)} %get-tuple-element.143.query, ...), custom_call_target="tpu_custom_call" | custom-call | flops 16106127360 | bytes 17301504 | tf_op jit(solution)/shard_map/attend_backward/pallas_call | solution.py:292
  835.6 24.2 %attend_backward.5 = (bf16[1024,768]{1,0:T(8,128)(2,1)}, bf16[4,512,256]{2,1,0:T(8,128)(2,1)}, bf16[4,512,256]{2,1,0:T(8,128)(2,1)}, bf16[4,512,256]{2,1,0:T(8,128)(2,1)}, bf16[4,512,256]{2,1,0:T(8,128)(2,1)}) custom-call(s32[4]{0:T(128)} %pad_add_fusion.partners, bf16[1024,256]{1,0:T(8,128)(2,1)} %get-tuple-element.133.query, ...), custom_call_target="tpu_custom_call" | custom-call | flops 16106127360 | bytes 17301504 | tf_op jit(solution)/shard_map/attend_backward/pallas_call | solution.py:292
  859.8 24.0 %attend_backward.6 = (bf16[1024,768]{1,0:T(8,128)(2,1)}, bf16[4,512,256]{2,1,0:T(8,128)(2,1)}, bf16[4,512,256]{2,1,0:T(8,128)(2,1)}, bf16[4,512,256]{2,1,0:T(8,128)(2,1)}, bf16[4,512,256]{2,1,0:T(8,128)(2,1)}) custom-call(s32[4]{0:T(128)} %pad_add_fusion.partners, bf16[1024,256]{1,0:T(8,128)(2,1)} %get-tuple-element.138.query, ...), custom_call_target="tpu_custom_call" | custom-call | flops 16106127360 | bytes 17301504 | tf_op jit(solution)/shard_map/attend_backward/pallas_call | solution.py:292
  888.3 24.0 %attend_backward.4 = (bf16[1024,768]{1,0:T(8,128)(2,1)}, bf16[4,512,256]{2,1,0:T(8,128)(2,1)}, bf16[4,512,256]{2,1,0:T(8,128)(2,1)}, bf16[4,512,256]{2,1,0:T(8,128)(2,1)}, bf16[4,512,256]{2,1,0:T(8,128)(2,1)}) custom-call(s32[4]{0:T(128)} %pad_add_fusion.partners, bf16[1024,256]{1,0:T(8,128)(2,1)} %get-tuple-element.128.query, ...), custom_call_target="tpu_custom_call" | custom-call | flops 16106127360 | bytes 17301504 | tf_op jit(solution)/shard_map/attend_backward/pallas_call | solution.py:292
  926.3 21.6 %spread.3 = bf16[1024,2048]{1,0:T(8,128)(2,1)} custom-call(s32[4]{0:T(128)} %pad_add_fusion.partners, bf16[1024,768]{1,0:T(8,128)(2,1)} %get-tuple-element.132.refs_0_, bf16[1024,768]{1,0:T(8,128)(2,1)} %get-tuple-element.137.refs_1_, bf16[1024,768]{1,0:T(8,128)(2,1)} %get-tuple-element.142.refs_2_, bf16[1024,768]{1,0:T(8,128)(2,1)} %get-tuple-element.147.refs_3_, ...), custom_call_target="tpu_custom_call" | custom-call | flops 12884901888 | bytes 23068672 | tf_op jit(solution)/shard_map/spread/pallas_call | solution.py:333
  992.2 17.5 %collective-permute-done.64 = bf16[4,512,256]{2,1,0:T(8,128)(2,1)S(1)} collective-permute-done((bf16[4,512,256]{2,1,0:T(8,128)(2,1)S(1)}, bf16[4,512,256]{2,1,0:T(8,128)(2,1)S(1)}, u32[]{:S(2)}, u32[]{:S(2)}) %collective-permute-start.64) | collective-permute-done | bytes 1048608 | tf_op jit(solution)/shard_map/ppermute | solution.py:63
  (427 shorter events, 586.4 us)
Async XLA Ops:
  9.0 74.4 %collective-permute-start = (bf16[512,2048]{1,0:T(8,128)(2,1)}, bf16[512,2048]{1,0:T(8,128)(2,1)}, u32[]{:S(2)}, u32[]{:S(2)}) collective-permute-start(bf16[512,2048]{1,0:T(8,128)(2,1)} %fusion.4), channel_id=1, source_target_pairs={{0,1},{1,0},{2,3},{3,2},{4,5},{5,4},{6,7},{7,6},{8,9},{9,8},{10,11... | collective-permute-start | bytes 6291464 | tf_op jit(solution)/shard_map/ppermute | solution.py:66
  237.6 64.3 %collective-permute-start.28 = (bf16[512,2048]{1,0:T(8,128)(2,1)}, bf16[512,2048]{1,0:T(8,128)(2,1)}, u32[]{:S(2)}, u32[]{:S(2)}) collective-permute-start(bf16[512,2048]{1,0:T(8,128)(2,1)} %multiply_convert_fusion.refs_0_), channel_id=1, source_target_pairs={{0,8},{1,17},{2,10},{3,19},{4,12},{5,21},{6,14},{7,23},{8,0},{9,25... | collective-permute-start | bytes 6291464 | tf_op jit(solution)/shard_map/ppermute | solution.py:63
  240.4 72.2 %collective-permute-start.17 = (bf16[512,2048]{1,0:T(8,128)(2,1)}, bf16[512,2048]{1,0:T(8,128)(2,1)}, u32[]{:S(2)}, u32[]{:S(2)}) collective-permute-start(bf16[512,2048]{1,0:T(8,128)(2,1)} %multiply_convert_fusion.refs_0_), channel_id=1, source_target_pairs={{0,1},{1,0},{2,3},{3,2},{4,5},{5,4},{6,7},{7,6},{8,9},{9,8},{10,11... | collective-permute-start | bytes 6291464 | tf_op jit(solution)/shard_map/ppermute | solution.py:66
  312.6 61.9 %collective-permute-start.46 = (bf16[512,2048]{1,0:T(8,128)(2,1)S(1)}, bf16[512,2048]{1,0:T(8,128)(2,1)S(1)}, u32[]{:S(2)}, u32[]{:S(2)}) collective-permute-start(bf16[512,2048]{1,0:T(8,128)(2,1)S(1)} %copy-done), channel_id=1, source_target_pairs={{0,16},{1,9},{2,18},{3,11},{4,20},{5,13},{6,22},{7,15},{8,24},{9,1... | collective-permute-start | bytes 6291464 | tf_op jit(solution)/shard_map/ppermute | solution.py:63
  352.6 99.2 %collective-permute-start.49 = (bf16[512,2048]{1,0:T(8,128)(2,1)S(1)}, bf16[512,2048]{1,0:T(8,128)(2,1)}, u32[]{:S(2)}, u32[]{:S(2)}) collective-permute-start(bf16[512,2048]{1,0:T(8,128)(2,1)S(1)} %collective-permute-done.42.refs_0_.refs_2_), channel_id=1, source_target_pairs={{0,16},{1,9},{2,18},{3,11},{4,20},{5,13},{6,22},{7,15},{8,24},{9,1... | collective-permute-start | bytes 6291464 | tf_op jit(solution)/shard_map/ppermute | solution.py:63
  368.3 59.6 %collective-permute-start.43 = (bf16[512,2048]{1,0:T(8,128)(2,1)S(1)}, bf16[512,2048]{1,0:T(8,128)(2,1)}, u32[]{:S(2)}, u32[]{:S(2)}) collective-permute-start(bf16[512,2048]{1,0:T(8,128)(2,1)S(1)} %collective-permute-done.42.refs_0_.refs_2_), channel_id=1, source_target_pairs={{0,1},{1,0},{2,3},{3,2},{4,5},{5,4},{6,7},{7,6},{8,9},{9,8},{10,11... | collective-permute-start | bytes 6291464 | tf_op jit(solution)/shard_map/ppermute | solution.py:66
  374.6 77.2 %collective-permute-start.36 = (bf16[512,2048]{1,0:T(8,128)(2,1)}, bf16[512,2048]{1,0:T(8,128)(2,1)}, u32[]{:S(2)}, u32[]{:S(2)}) collective-permute-start(bf16[512,2048]{1,0:T(8,128)(2,1)} %collective-permute-done.35.refs_0_.refs_6_), channel_id=1, source_target_pairs={{0,1},{1,0},{2,3},{3,2},{4,5},{5,4},{6,7},{7,6},{8,9},{9,8},{10,11... | collective-permute-start | bytes 6291464 | tf_op jit(solution)/shard_map/ppermute | solution.py:66
  374.7 99.8 %collective-permute-start.47 = (bf16[512,2048]{1,0:T(8,128)(2,1)S(1)}, bf16[512,2048]{1,0:T(8,128)(2,1)}, u32[]{:S(2)}, u32[]{:S(2)}) collective-permute-start(bf16[512,2048]{1,0:T(8,128)(2,1)S(1)} %collective-permute-done.46.refs_0_.refs_4_), channel_id=1, source_target_pairs={{0,1},{1,0},{2,3},{3,2},{4,5},{5,4},{6,7},{7,6},{8,9},{9,8},{10,11... | collective-permute-start | bytes 6291464 | tf_op jit(solution)/shard_map/ppermute | solution.py:66
  404.7 257.3 %collective-permute-start.34 = (bf16[512,2048]{1,0:T(8,128)(2,1)}, bf16[512,2048]{1,0:T(8,128)(2,1)}, u32[]{:S(2)}, u32[]{:S(2)}) collective-permute-start(bf16[512,2048]{1,0:T(8,128)(2,1)} %get-tuple-element.107), channel_id=1, source_target_pairs={{0,1},{1,0},{2,3},{3,2},{4,5},{5,4},{6,7},{7,6},{8,9},{9,8},{10,11... | collective-permute-start | bytes 6291464 | tf_op jit(solution)/shard_map/ppermute | solution.py:66
  427.9 70.1 %collective-permute-start.30 = (bf16[512,2048]{1,0:T(8,128)(2,1)}, bf16[512,2048]{1,0:T(8,128)(2,1)}, u32[]{:S(2)}, u32[]{:S(2)}) collective-permute-start(bf16[512,2048]{1,0:T(8,128)(2,1)} %get-tuple-element.104), channel_id=1, source_target_pairs={{0,1},{1,0},{2,3},{3,2},{4,5},{5,4},{6,7},{7,6},{8,9},{9,8},{10,11... | collective-permute-start | bytes 6291464 | tf_op jit(solution)/shard_map/ppermute | solution.py:66
  451.8 129.3 %collective-permute-start.44 = (bf16[512,2048]{1,0:T(8,128)(2,1)}, bf16[512,2048]{1,0:T(8,128)(2,1)}, u32[]{:S(2)}, u32[]{:S(2)}) collective-permute-start(bf16[512,2048]{1,0:T(8,128)(2,1)} %get-tuple-element.119), channel_id=1, source_target_pairs={{0,1},{1,0},{2,3},{3,2},{4,5},{5,4},{6,7},{7,6},{8,9},{9,8},{10,11... | collective-permute-start | bytes 6291464 | tf_op jit(solution)/shard_map/ppermute | solution.py:66
  474.5 132.6 %collective-permute-start.37 = (bf16[512,2048]{1,0:T(8,128)(2,1)}, bf16[512,2048]{1,0:T(8,128)(2,1)S(1)}, u32[]{:S(2)}, u32[]{:S(2)}) collective-permute-start(bf16[512,2048]{1,0:T(8,128)(2,1)} %get-tuple-element.110), channel_id=1, source_target_pairs={{0,1},{1,0},{2,3},{3,2},{4,5},{5,4},{6,7},{7,6},{8,9},{9,8},{10,11... | collective-permute-start | bytes 6291464 | tf_op jit(solution)/shard_map/ppermute | solution.py:66
  526.3 72.6 %collective-permute-start.51 = (bf16[512,2048]{1,0:T(8,128)(2,1)}, bf16[512,2048]{1,0:T(8,128)(2,1)}, u32[]{:S(2)}, u32[]{:S(2)}) collective-permute-start(bf16[512,2048]{1,0:T(8,128)(2,1)} %get-tuple-element.127), channel_id=1, source_target_pairs={{0,1},{1,0},{2,3},{3,2},{4,5},{5,4},{6,7},{7,6},{8,9},{9,8},{10,11... | collective-permute-start | bytes 6291464 | tf_op jit(solution)/shard_map/ppermute | solution.py:66
  537.2 58.9 %collective-permute-start.77 = (bf16[1,2048,256]{2,1,0:T(8,128)(2,1)}, bf16[1,2048,256]{2,1,0:T(8,128)(2,1)S(1)}, u32[]{:S(2)}, u32[]{:S(2)}) collective-permute-start(bf16[1,2048,256]{2,1,0:T(8,128)(2,1)} %weight_terms.12), channel_id=1, source_target_pairs={{0,2},{1,3},{2,4},{3,5},{4,6},{5,7},{6,0},{7,1},{8,10},{9,11},{10,... | collective-permute-start | bytes 3145736 | tf_op jit(solution)/shard_map/ppermute | solution.py:74
  653.6 73.6 %collective-permute-start.72 = (bf16[2,2048,256]{2,1,0:T(8,128)(2,1)}, bf16[2,2048,256]{2,1,0:T(8,128)(2,1)}, u32[]{:S(2)}, u32[]{:S(2)}) collective-permute-start(bf16[2,2048,256]{2,1,0:T(8,128)(2,1)} %add_convert_fusion.2), channel_id=1, source_target_pairs={{0,2},{1,3},{2,4},{3,5},{4,6},{5,7},{6,0},{7,1},{8,10},{9,11},{10,... | collective-permute-start | bytes 6291464 | tf_op jit(solution)/shard_map/ppermute | solution.py:74
  655.1 78.0 %collective-permute-start.45 = (bf16[512,2048]{1,0:T(8,128)(2,1)}, bf16[512,2048]{1,0:T(8,128)(2,1)S(1)}, u32[]{:S(2)}, u32[]{:S(2)}) collective-permute-start(bf16[512,2048]{1,0:T(8,128)(2,1)} %add_convert_fusion.6), channel_id=1, source_target_pairs={{0,8},{1,17},{2,10},{3,19},{4,12},{5,21},{6,14},{7,23},{8,0},{9,25... | collective-permute-start | bytes 6291464 | tf_op jit(solution)/shard_map/ppermute | solution.py:63
  662.0 63.2 %collective-permute-start.79 = (bf16[1,2048,256]{2,1,0:T(8,128)(2,1)S(1)}, bf16[1,2048,256]{2,1,0:T(8,128)(2,1)}, u32[]{:S(2)}, u32[]{:S(2)}) collective-permute-start(bf16[1,2048,256]{2,1,0:T(8,128)(2,1)S(1)} %add_convert_fusion.15), channel_id=1, source_target_pairs={{0,2},{1,3},{2,4},{3,5},{4,6},{5,7},{6,0},{7,1},{8,10},{9,11},{10,... | collective-permute-start | bytes 3145736 | tf_op jit(solution)/shard_map/ppermute | solution.py:74
  664.5 68.7 %collective-permute-start.53 = (bf16[512,2048]{1,0:T(8,128)(2,1)}, bf16[512,2048]{1,0:T(8,128)(2,1)S(1)}, u32[]{:S(2)}, u32[]{:S(2)}) collective-permute-start(bf16[512,2048]{1,0:T(8,128)(2,1)} %add_convert_fusion.3), channel_id=1, source_target_pairs={{0,16},{1,9},{2,18},{3,11},{4,20},{5,13},{6,22},{7,15},{8,24},{9,1... | collective-permute-start | bytes 6291464 | tf_op jit(solution)/shard_map/ppermute | solution.py:63
  679.3 56.5 %collective-permute-start.27 = (bf16[512,2048]{1,0:T(8,128)(2,1)S(1)}, bf16[512,2048]{1,0:T(8,128)(2,1)S(1)}, u32[]{:S(2)}, u32[]{:S(2)}) collective-permute-start(bf16[512,2048]{1,0:T(8,128)(2,1)S(1)} %copy-done.71), channel_id=1, source_target_pairs={{0,1},{1,0},{2,3},{3,2},{4,5},{5,4},{6,7},{7,6},{8,9},{9,8},{10,11... | collective-permute-start | bytes 6291464 | tf_op jit(solution)/shard_map/ppermute | solution.py:66
  733.1 66.9 %collective-permute-start.80 = (bf16[512,256]{1,0:T(8,128)(2,1)S(1)}, bf16[512,256]{1,0:T(8,128)(2,1)}, u32[]{:S(2)}, u32[]{:S(2)}) collective-permute-start(bf16[512,256]{1,0:T(8,128)(2,1)S(1)} %get-tuple-element.214), channel_id=1, source_target_pairs={{0,8},{8,0},{16,24},{24,16},{1,9},{9,1},{17,25},{25,17},{2,10},{10... | collective-permute-start | bytes 786440 | tf_op jit(solution)/shard_map/ppermute | solution.py:55
  733.2 67.8 %collective-permute-start.73 = (bf16[2,2048,256]{2,1,0:T(8,128)(2,1)}, bf16[2,2048,256]{2,1,0:T(8,128)(2,1)}, u32[]{:S(2)}, u32[]{:S(2)}) collective-permute-start(bf16[2,2048,256]{2,1,0:T(8,128)(2,1)} %add_convert_fusion.1), channel_id=1, source_target_pairs={{0,2},{1,3},{2,4},{3,5},{4,6},{5,7},{6,0},{7,1},{8,10},{9,11},{10,... | collective-permute-start | bytes 6291464 | tf_op jit(solution)/shard_map/ppermute | solution.py:74
  799.8 157.1 %collective-permute-start.81 = (bf16[512,256]{1,0:T(8,128)(2,1)}, bf16[512,256]{1,0:T(8,128)(2,1)}, u32[]{:S(2)}, u32[]{:S(2)}) collective-permute-start(bf16[512,256]{1,0:T(8,128)(2,1)} %get-tuple-element.213), channel_id=1, source_target_pairs={{0,16},{8,24},{16,0},{24,8},{1,17},{9,25},{17,1},{25,9},{2,18},{10... | collective-permute-start | bytes 786440 | tf_op jit(solution)/shard_map/ppermute | solution.py:55
  833.5 116.3 %collective-permute-start.65 = (bf16[4,512,256]{2,1,0:T(8,128)(2,1)}, bf16[4,512,256]{2,1,0:T(8,128)(2,1)S(1)}, u32[]{:S(2)}, u32[]{:S(2)}) collective-permute-start(bf16[4,512,256]{2,1,0:T(8,128)(2,1)} %get-tuple-element.159), channel_id=1, source_target_pairs={{0,8},{1,17},{2,10},{3,19},{4,12},{5,21},{6,14},{7,23},{8,0},{9,25... | collective-permute-start | bytes 3145736 | tf_op jit(solution)/shard_map/ppermute | solution.py:63
  956.9 72.4 %collective-permute-start.55 = (bf16[512,2048]{1,0:T(8,128)(2,1)S(1)}, bf16[512,2048]{1,0:T(8,128)(2,1)S(1)}, u32[]{:S(2)}, u32[]{:S(2)}) collective-permute-start(bf16[512,2048]{1,0:T(8,128)(2,1)S(1)} %constant_dynamic-slice_fusion.4), channel_id=1, source_target_pairs={{0,1},{1,0},{2,3},{3,2},{4,5},{5,4},{6,7},{7,6},{8,9},{9,8},{10,11... | collective-permute-start | bytes 6291464 | tf_op jit(solution)/shard_map/ppermute | solution.py:66
  (139 other events, 3579.2 us)

commit v3 on v2

--- a/solution.py
+++ b/solution.py
@@ -24,6 +24,7 @@
 clip_bound = 1.0
 masked_score = -1e30
 low = jnp.bfloat16
+cost_scale = 0.2
 f32 = jnp.float32
 
 
@@ -75,8 +76,10 @@
 
     def place(self, pieces, axis, index):
         width = pieces[0].shape[axis]
-        whole = jnp.concatenate([pieces[0]] * len(pieces), axis=axis)
-        for d in range(1, len(pieces)):
+        shape = list(pieces[0].shape)
+        shape[axis] = width * len(pieces)
+        whole = jnp.zeros(shape, pieces[0].dtype)
+        for d in range(len(pieces)):
             whole = lax.dynamic_update_slice_in_dim(whole, pieces[d], (index ^ d) * width, axis)
         return whole
 
@@ -126,7 +129,83 @@
 
 
 def after(value, *others):
-    return lax.optimization_barrier((value,) + others)[0]
+    return lax.optimization_barrier((value, *others))[0]
+
+
+class Gather:
+    def __init__(self, mv, value):
+        self.mv = mv
+        self.blocks = [value]
+
+    def __call__(self, count, *deps):
+        mv, blocks = self.mv, self.blocks
+        found = []
+        for _ in range(count):
+            if mv.F != 4:
+                if len(blocks) == 1:
+                    blocks[:] = mv.plane_gather(blocks[0])
+                    found += blocks[1:2]
+                continue
+            number = len(blocks)
+            value = blocks[1] if number == 3 else blocks[0]
+            found.append(mv.hop(after(value, *deps), 1 if number == 1 else 2))
+            blocks.append(found[-1])
+        return found
+
+
+class Sum:
+    def __init__(self, mv):
+        self.mv = mv
+        self.blocks = [None] * mv.F
+        self.got = []
+
+    def __call__(self, count, *deps):
+        mv, blocks, got = self.mv, self.blocks, self.got
+        if mv.F != 4:
+            return []
+        for _ in range(count):
+            source = blocks[(3, 1, 2)[len(got)]]
+            if len(got) == 2:
+                source = (source.astype(f32) + got[0].astype(f32)).astype(low)
+            got.append(mv.hop(after(source, *deps), 2 if len(got) == 2 else 1))
+        return got[-count:]
+
+    def total(self):
+        if self.mv.F != 4:
+            return self.mv.plane_sum(self.blocks)
+        return self.blocks[0].astype(f32) + self.got[1].astype(f32) + self.got[2].astype(f32)
+
+
+class RingGather:
+    def __init__(self, mv, value):
+        self.mv = mv
+        self.blocks = [value]
+
+    def __call__(self, *deps):
+        if len(self.blocks) == self.mv.Z:
+            return []
+        self.blocks.append(self.mv.ring(after(self.blocks[-1], *deps)))
+        return self.blocks[-1:]
+
+
+class RingSum:
+    def __init__(self, mv):
+        self.mv = mv
+        self.terms = {}
+        self.got = []
+
+    def __call__(self, *deps):
+        number = len(self.got)
+        if number < self.mv.Z - 1:
+            value = self.terms[number + 1]
+            if number:
+                value = (value.astype(f32) + self.got[-1].astype(f32)).astype(low)
+            self.got.append(self.mv.ring(after(value.astype(low), *deps)))
+            return self.got[-1:]
+        return []
+
+    def total(self):
+        return self.terms[0].astype(f32) + self.got[-1].astype(f32)
 
 
 def rope_tables(length, width):
@@ -213,9 +292,9 @@
 
 def cost(flops, operands, transcendentals=0):
     return pl.CostEstimate(
-        flops=flops,
-        bytes_accessed=sum(v.size * v.dtype.itemsize for v in operands),
-        transcendentals=transcendentals,
+        flops=int(flops * cost_scale),
+        bytes_accessed=int(sum(v.size * v.dtype.itemsize for v in operands) * cost_scale),
+        transcendentals=int(transcendentals * cost_scale),
     )
 
 
@@ -346,135 +425,219 @@
     )(partners, *values, *flat)
 
 
-def resident(value):
-    return pl.BlockSpec(value.shape, lambda i: (0,) * value.ndim)
-
-
-def feed_kernel(parts, *refs):
-    feeds = refs[:parts]
-    expand, hidden, slope, passed = refs[parts:]
-    rows = feeds[0].shape[0]
-    for p in range(parts):
-        gate = dot(feeds[p][...], expand[0, 0], NN)
-        up = dot(feeds[p][...], expand[0, 1], NN)
-        sigma = jax.nn.sigmoid(gate)
-        silu = gate * sigma
-        here = slice(p * rows, (p + 1) * rows)
-        hidden[here, :] = (silu * up).astype(low)
-        slope[here, :] = (up * (sigma + silu * (1.0 - sigma))).astype(low)
-        passed[here, :] = silu.astype(low)
-
-
-def feed_forward(feeds, expand):
-    pieces, _, depth, width = expand.shape
-    rows = sum(v.shape[0] for v in feeds)
-    tile = pl.BlockSpec((rows, width), lambda i: (0, i))
+ANY = pl.BlockSpec(memory_space=pl.ANY)
+
+
+def held(value):
+    return pl.BlockSpec(
+        value.shape, lambda i: (0,) * value.ndim, pipeline_mode=pl.Buffered(1)
+    )
+
+
+def take_item(items, slots, sems):
+    step = pl.program_id(0)
+
+    def copy(i):
+        return pltpu.make_async_copy(items[i], slots.at[i % 2], sems.at[i % 2])
+
+    for i in range(len(items)):
+
+        @pl.when(step == i)
+        def _(i=i):
+            if i == 0:
+                copy(0).start()
+            if i + 1 < len(items):
+                copy(i + 1).start()
+            copy(i).wait()
+
+    return slots[lax.rem(step, 2)]
+
+
+def give_item(value, items, slots, sems):
+    step = pl.program_id(0)
+    last = len(items) - 1
+
+    def copy(i):
+        return pltpu.make_async_copy(slots.at[i % 2], items[i], sems.at[i % 2])
+
+    for i in range(2, len(items)):
+
+        @pl.when(step == i)
+        def _(i=i):
+            copy(i - 2).wait()
+
+    value(slots.at[lax.rem(step, 2)])
+    for i in range(len(items)):
+
+        @pl.when(step == i)
+        def _(i=i):
+            copy(i).start()
+            if i == last:
+                if i:
+                    copy(i - 1).wait()
+                copy(i).wait()
+
+
+def feed_kernel(count, width, *refs):
+    items = refs[:count]
+    expand, hidden, slope, passed, slots, sems = refs[count:]
+    value = take_item(items, slots, sems)
+    several = 2 if hidden.shape[1] % (2 * width) == 0 else 1
+    step = 2 * width * several
+    for n in range(hidden.shape[1] // (width * several)):
+        both = dot(value, expand[:, n * step : (n + 1) * step], NN)
+        for m in range(several):
+            gate = both[:, 2 * m * width : (2 * m + 1) * width]
+            up = both[:, (2 * m + 1) * width : (2 * m + 2) * width]
+            sigma = jax.nn.sigmoid(gate)
+            silu = gate * sigma
+            here = slice((n * several + m) * width, (n * several + m + 1) * width)
+            hidden[:, here] = (silu * up).astype(low)
+            slope[:, here] = (up * (sigma + silu * (1.0 - sigma))).astype(low)
+            passed[:, here] = silu.astype(low)
+
+
+def feed_forward(items, expand, width):
+    rows, depth = items[0].shape
+    count = len(items)
+    hidden = expand.shape[1] // 2
+    tile = pl.BlockSpec((rows, hidden), lambda i: (i, 0))
     return pl.pallas_call(
-        functools.partial(feed_kernel, len(feeds)),
-        grid=(pieces,),
-        out_shape=[jax.ShapeDtypeStruct((rows, pieces * width), low)] * 3,
-        in_specs=[resident(v) for v in feeds]
-        + [pl.BlockSpec((1, 2, depth, width), lambda i: (i, 0, 0, 0))],
+        functools.partial(feed_kernel, count, width),
+        grid=(count,),
+        out_shape=[jax.ShapeDtypeStruct((count * rows, hidden), low)] * 3,
+        in_specs=[ANY] * count + [held(expand)],
         out_specs=[tile] * 3,
-        compiler_params=params(),
-        cost_estimate=cost(4 * rows * depth * pieces * width, [*feeds, expand]),
+        scratch_shapes=[pltpu.VMEM((2, rows, depth), low), pltpu.SemaphoreType.DMA((2,))],
+        compiler_params=params(40),
+        cost_estimate=cost(2 * count * rows * expand.size, [*items, expand]),
         name="feed_forward",
-    )(*feeds, expand)
-
-
-def hidden_kernel(parts, *refs):
-    grads = refs[:parts]
-    shrink, slope, passed, out = refs[parts:]
-    rows = grads[0].shape[0]
-    for p in range(parts):
-        here = slice(p * rows, (p + 1) * rows)
-        grad = dot(grads[p][...], shrink[0], NN)
-        out[0, here, :] = (grad * slope[here, :].astype(f32)).astype(low)
-        out[1, here, :] = (grad * passed[here, :].astype(f32)).astype(low)
-
-
-def hidden_backward(grads, shrink, slope, passed):
-    pieces, depth, width = shrink.shape
-    rows = sum(v.shape[0] for v in grads)
-    tile = pl.BlockSpec((rows, width), lambda i: (0, i))
-    return pl.pallas_call(
-        functools.partial(hidden_kernel, len(grads)),
-        grid=(pieces,),
-        out_shape=jax.ShapeDtypeStruct((2, rows, pieces * width), low),
-        in_specs=[resident(v) for v in grads]
-        + [pl.BlockSpec((1, depth, width), lambda i: (i, 0, 0)), tile, tile],
-        out_specs=pl.BlockSpec((2, rows, width), lambda i: (0, 0, i)),
-        compiler_params=params(),
-        cost_estimate=cost(2 * rows * depth * pieces * width, [*grads, shrink, slope]),
-        name="hidden_backward",
-    )(*grads, shrink, slope, passed)
-
-
-def back_kernel(value, weight, *outs):
-    several, pieces = weight.shape[1], weight.shape[0]
-    width = weight.shape[3]
-    rows = outs[0].shape[0]
-    for p, out in enumerate(outs):
-        total = None
-        for c in range(several):
-            for k in range(pieces):
-                one = dot(
-                    value[c, p * rows : (p + 1) * rows, k * width : (k + 1) * width],
-                    weight[k, c],
-                    NT,
-                )
-                total = one if total is None else total + one
-        out[...] = total.astype(low)
-
-
-def times_back(value, weight, parts):
-    pieces, several, depth, width = weight.shape
-    rows = value.shape[1] // parts
-    tile = min(depth, 512)
+    )(*items, expand)
+
+
+def feed_back_kernel(count, width, *refs):
+    items = refs[:count]
+    shrink, expand, slope, passed, grads = refs[count : count + 5]
+    outs = refs[count + 5 : 2 * count + 5]
+    slots, sems, out_slots, out_sems = refs[2 * count + 5 :]
+    value = take_item(items, slots, sems)
+    hidden = slope.shape[1]
+    grad = dot(value, shrink[...], NN)
+    for n in range(hidden // width):
+        here = slice(n * width, (n + 1) * width)
+        grads[:, 2 * n * width : (2 * n + 1) * width] = (
+            grad[:, here] * slope[:, here].astype(f32)
+        ).astype(low)
+        grads[:, (2 * n + 1) * width : (2 * n + 2) * width] = (
+            grad[:, here] * passed[:, here].astype(f32)
+        ).astype(low)
+
+    def result(slot):
+        depth = expand.shape[0]
+        tile = min(depth, 1024)
+        for n in range(depth // tile):
+            here = slice(n * tile, (n + 1) * tile)
+            slot[:, here] = dot(grads[...], expand[here, :], NT).astype(low)
+
+    give_item(result, outs, out_slots, out_sems)
+
+
+def feed_backward(items, shrink, expand, slope, passed, places, width):
+    rows, depth = items[0].shape
+    count = len(items)
+    hidden = shrink.shape[1]
+    first, stride = places[0], (places[-1] - places[0]) // max(count - 1, 1)
+    assert list(places) == [first + stride * i for i in range(count)]
+    tile = pl.BlockSpec((rows, hidden), lambda i: (first + stride * i, 0))
+    found = pl.pallas_call(
+        functools.partial(feed_back_kernel, count, width),
+        grid=(count,),
+        out_shape=[jax.ShapeDtypeStruct((count * rows, 2 * hidden), low)]
+        + [jax.ShapeDtypeStruct((rows, depth), low)] * count,
+        in_specs=[ANY] * count + [held(shrink), held(expand), tile, tile],
+        out_specs=[pl.BlockSpec((rows, 2 * hidden), lambda i: (i, 0))] + [ANY] * count,
+        scratch_shapes=[
+            pltpu.VMEM((2, rows, depth), low),
+            pltpu.SemaphoreType.DMA((2,)),
+            pltpu.VMEM((2, rows, depth), low),
+            pltpu.SemaphoreType.DMA((2,)),
+        ],
+        compiler_params=params(48),
+        cost_estimate=cost(
+            2 * count * rows * (expand.size + shrink.size), [*items, shrink, expand, slope]
+        ),
+        name="feed_backward",
+    )(*items, shrink, expand, slope, passed)
+    return found[0], list(found[1:])
+
+
+def back_kernel(value, weight, *refs):
+    count = len(refs) - 2
+    outs = refs[:count]
+    slots, sems = refs[count:]
+
+    def result(slot):
+        depth = weight.shape[0]
+        tile = min(depth, 1024)
+        for n in range(depth // tile):
+            here = slice(n * tile, (n + 1) * tile)
+            slot[:, here] = dot(value[...], weight[here, :], NT).astype(low)
+
+    give_item(result, outs, slots, sems)
+
+
+def times_back(value, weight, count):
+    rows = value.shape[0] // count
+    depth, width = weight.shape
     return pl.pallas_call(
         back_kernel,
-        grid=(depth // tile,),
-        out_shape=[jax.ShapeDtypeStruct((rows, depth), low)] * parts,
-        in_specs=[
-            resident(value),
-            pl.BlockSpec((pieces, several, tile, width), lambda i: (0, 0, i, 0)),
-        ],
-        out_specs=[pl.BlockSpec((rows, tile), lambda i: (0, i))] * parts,
-        compiler_params=params(),
+        grid=(count,),
+        out_shape=[jax.ShapeDtypeStruct((rows, depth), low)] * count,
+        in_specs=[pl.BlockSpec((rows, width), lambda i: (i, 0)), held(weight)],
+        out_specs=[ANY] * count,
+        scratch_shapes=[pltpu.VMEM((2, rows, depth), low), pltpu.SemaphoreType.DMA((2,))],
+        compiler_params=params(32),
         cost_estimate=cost(2 * value.size * depth, [value, weight]),
         name="times_back",
     )(value, weight)
 
 
-def weight_kernel(lefts, rights, *refs):
-    out = refs[-1]
-    per = lefts // rights
-    rows = refs[0].shape[0]
-    for c in range(out.shape[0]):
-        total = None
-        for i in range(lefts):
-            begin = i % per * rows
-            one = dot(refs[i][...], refs[lefts + i // per][c, begin : begin + rows, :], TN)
-            total = one if total is None else total + one
-        out[c] = total.astype(low)
-
-
-def weight_terms(lefts, rights, k, width):
-    depth = lefts[0].shape[1]
-    several = rights[0].shape[0]
+def weight_kernel(count, rights, *refs):
+    lefts = refs[:count]
+    rows = lefts[0].shape[0]
+    begins = [
+        (ref, begin)
+        for ref in refs[count : count + rights]
+        for begin in range(0, ref.shape[0], rows)
+    ]
+    outs = refs[count + rights :]
+    total = None
+    for left, (right, begin) in zip(lefts, begins):
+        one = dot(left[...], right[begin : begin + rows, :], TN)
+        total = one if total is None else total + one
+    width = outs[0].shape[1]
+    for i, out in enumerate(outs):
+        out[...] = total[:, i * width : (i + 1) * width].astype(low)
+
+
+def weight_terms(lefts, rights, part, pieces, width):
+    rows, depth = lefts[0].shape
     tile = min(depth, 512)
-    rows = lefts[0].shape[0]
+    across = pieces * width
     return pl.pallas_call(
         functools.partial(weight_kernel, len(lefts), len(rights)),
         grid=(depth // tile,),
-        out_shape=jax.ShapeDtypeStruct((several, depth, width), low),
+        out_shape=[jax.ShapeDtypeStruct((depth, width), low)] * pieces,
         in_specs=[pl.BlockSpec((rows, tile), lambda i: (0, i)) for _ in lefts]
-        + [pl.BlockSpec((several, v.shape[1], width), lambda i: (0, 0, k)) for v in rights],
-        out_specs=pl.BlockSpec((several, tile, width), lambda i: (0, i, 0)),
-        compiler_params=params(),
-        cost_estimate=cost(
-            2 * rows * len(lefts) * depth * width * several, [*lefts, rights[0]]
-        ),
+        + [
+            pl.BlockSpec(
+                (v.shape[0], across), lambda i: (0, part), pipeline_mode=pl.Buffered(1)
+            )
+            for v in rights
+        ],
+        out_specs=[pl.BlockSpec((tile, width), lambda i: (i, 0))] * pieces,
+        compiler_params=params(40),
+        cost_estimate=cost(2 * rows * len(lefts) * depth * across, [*lefts, *rights]),
         name="weight_terms",
     )(*lefts, *rights)
 
@@ -526,37 +689,53 @@
     planes = range(F)
     ks = range(Z)
 
+    ring_order = list(range(1, Z)) + [0]
+
     attn_own = jnp.concatenate([inward_weight, outward_weight[None]], axis=0).astype(low)
-    attn_blocks = mv.ring_gather(attn_own)
-    attn_full = [mv.plane_gather(attn_blocks[k]) for k in ks]
-
-    def quarter(d):
+
+    def quarter(weight, d):
         begin = (mv.f ^ d) * hidden_width
-        both = lax.dynamic_slice_in_dim(expand_weight, begin, hidden_width, 2)
-        last = lax.dynamic_slice_in_dim(shrink_weight, begin, hidden_width, 1)
-        return jnp.concatenate([both, last[None]], axis=0).astype(low)
-
-    ff_own = mv.place([quarter(0)] + [mv.plane(quarter(d), d) for d in planes if d], 1, mv.f)
-    expand_blocks = mv.ring_gather(after(ff_own[:2], attn_blocks[-1]))
-    shrink_blocks = mv.ring_gather(after(ff_own[2], expand_blocks[-1]))
-    group = max(1, 128 // hidden_width)
-
-    def grouped(blocks):
-        if group == 1:
-            return jnp.stack(blocks)
-        joined = range(0, Z, group)
-        return jnp.stack([jnp.concatenate(blocks[k : k + group], axis=-1) for k in joined])
-
-    expand_full = grouped(expand_blocks)
-    shrink_full = grouped(shrink_blocks)
-
+        return lax.dynamic_slice_in_dim(weight, begin, hidden_width, weight.ndim - 1).astype(low)
+
+    expand_own = [quarter(expand_weight, d) for d in planes]
+    shrink_own = [quarter(shrink_weight, d) for d in planes]
+    attn_ring = RingGather(mv, attn_own)
+    attn = [Gather(mv, attn_own)]
     source = layer_input.astype(f32)
     scale_one = norm_scale(source)
     normed_one = source * scale_one
+    expand_own[1:] = [mv.plane(expand_own[d], d) for d in planes if d]
+    deps = attn[0](2) + attn_ring() + expand_own[1:]
     acts = mv.place(mv.mates((normed_one * norm_gains[0]).astype(low)), 0, mv.s)
     tables = rope_tables(LEN, own_width)
-    saved = [attend_forward(mv.partners, acts, attn_full[k], tables) for k in ks]
+    deps += [acts, *tables]
+    attn.append(Gather(mv, attn_ring.blocks[-1]))
+    deps = attn[0](1, *deps) + attn[1](2, *deps) + attn_ring(*deps)
+    placed = mv.place(expand_own, 1, mv.f)
+    gate_ring, up_ring = RingGather(mv, placed[0]), RingGather(mv, placed[1])
+    deps += [gate_ring.blocks[0], up_ring.blocks[0]]
+    attn.append(Gather(mv, attn_ring.blocks[-1]))
+    saved = []
+
+    def attend(k):
+        saved.append(
+            attend_forward(after(mv.partners, *deps), acts, attn[k].blocks, tables)
+        )
+        return [saved[-1][3]]
+
+    deps = attn[1](1, *deps) + attn[2](2, *deps) + attn_ring(*deps) + attend(0)
+    attn.append(Gather(mv, attn_ring.blocks[-1]))
+    deps = attn[2](1, *deps) + attn[3](2, *deps) + gate_ring(*deps) + attend(1)
+    deps = attn[3](1, *deps) + gate_ring(*deps) + attend(2)
+    attn_full = [g.blocks for g in attn]
+    cot = Gather(mv, cotangent)
+    moved = cot(1, *deps) + gate_ring(*deps)
+    attend(3)
     attended = spread(mv.partners, [s[3] for s in saved], attn_full, 3, 1)
+    deps = moved + [attended]
+    attended = after(attended, *moved)
+    shrink_own[1:] = [mv.plane(after(shrink_own[d], *deps), d) for d in planes if d]
+    moved = up_ring(*deps) + shrink_own[1:] + cot(1, *deps)
 
     def part(value, d):
         return lax.dynamic_slice_in_dim(value, (mv.s ^ d) * rows, rows, 0)
@@ -565,76 +744,186 @@
     scale_two = norm_scale(resid)
     normed_two = resid * scale_two
     feed_local = (normed_two * norm_gains[1]).astype(low)
-
-    feed_gathered = mv.plane_gather(feed_local)
-    feed_blocks = [mv.mates(block) for block in feed_gathered]
-    grad_gathered = mv.plane_gather(after(cotangent, *feed_gathered[1:3]))
-    grad_blocks = [mv.mates(block) for block in grad_gathered]
-    kept = [feed_forward(feed_blocks[d], expand_full) for d in planes]
-    hidden = [h[0] for h in kept]
-    grad_gate_up = [None] * F
-    grad_feed = [None] * F
-    late_first = list(planes)[::-1]
-    for d in planes:
-        grad_gate_up[d] = hidden_backward(grad_blocks[d], shrink_full, kept[d][1], kept[d][2])
+    deps = moved + [feed_local]
+    shrink_ring = RingGather(mv, mv.place(shrink_own, 0, mv.f))
+    feed = Gather(mv, feed_local)
+    own_mates = mv.mates(after(feed_local, *deps))
+    moved = feed(1, *deps) + up_ring(*deps)
+    deps = moved + own_mates[1:]
+    first_mates = mv.mates(after(feed.blocks[1], *deps)) if F == 4 else []
+    moved = feed(1, *deps) + up_ring(*deps)
+    deps = moved + first_mates[1:]
+    if F == 4:
+        feed_blocks = [own_mates, first_mates, mv.mates(after(feed.blocks[2], *deps))]
+    else:
+        feed_blocks = [own_mates] + [mv.mates(block) for block in feed.blocks[1:]]
+
+    def items_of(blocks, batches):
+        return [value for i in batches for value in blocks[i]]
 
     def chip_sum(block):
-        return mv.mates_sum(block).astype(low)
-
-    for d in late_first:
-        grad_feed[d] = chip_sum(times_back(grad_gate_up[d], expand_full, S))
-    fed = [chip_sum(times_back(hidden[d][None], shrink_full[:, None], S)) for d in planes]
-    grad_feed = mv.plane_sum(grad_feed)
-    resid_back, gain_two = norm_back(grad_feed, normed_two, scale_two, norm_gains[1])
+        return sum(value.astype(f32) for value in block).astype(low)
+
+    def trade(block):
+        return [block[0]] + [mv.mate(block[d], d) for d in range(1, S)]
+
+    def columns(value, *deps):
+        cut = [
+            lax.dynamic_slice_in_dim(value, (mv.f ^ d) * row_block, row_block, 0) for d in planes
+        ]
+        moved = [mv.plane(after(cut[d], *deps), d) for d in planes if d]
+        return moved, mv.place(cut[:1] + moved, 1, mv.f).astype(f32)
+
+    expand_full = jnp.concatenate(
+        [g.blocks[k] for k in ring_order for g in (gate_ring, up_ring)], axis=1
+    )
+    early, late = list(planes)[:-1], [F - 1]
+    deps = [v for block in feed_blocks for v in block[1:]]
+    moved = feed(1, *deps) + shrink_ring(*deps)
+    kept_early = feed_forward(
+        items_of(feed_blocks, early), after(expand_full, *deps), hidden_width
+    )
+    deps = moved + [kept_early[0]]
+    moved = cot(1, *deps) + shrink_ring(*deps)
+    if F == 4:
+        feed_blocks.append(mv.mates(after(feed.blocks[-1], *deps)))
+    grad_blocks = [mv.mates(after(block, *deps)) for block in cot.blocks[:3]]
+    kept_late = feed_forward(items_of(feed_blocks, late), after(expand_full, *deps), hidden_width)
+    deps = moved + [kept_late[0]] + [v for block in grad_blocks for v in block[1:]]
+    hidden = (kept_early[0], kept_late[0])
+    moved = shrink_ring(*deps)
+    grad_blocks += [mv.mates(after(block, *deps)) for block in cot.blocks[3:]]
+    pieces = max(Z // 2, 1)
+    parts = Z // pieces
+    grad_items = items_of(grad_blocks, early + late)
+    shrink_terms = []
+    for i in range(parts):
+        shrink_terms += weight_terms(grad_items, after(hidden, *deps), i, pieces, hidden_width)
+    deps = moved + shrink_terms
+    shrink_back = RingSum(mv)
+    shrink_back.terms.update(zip(ring_order, shrink_terms))
+    moved = shrink_back(*deps)
+    shrink_full = jnp.concatenate([shrink_ring.blocks[k] for k in ring_order], axis=1)
+    terms_late, back_late = feed_backward(
+        items_of(grad_blocks, late),
+        after(shrink_full, *deps),
+        expand_full,
+        *kept_late[1:],
+        range(S),
+        hidden_width,
+    )
+    deps = moved + [terms_late]
+    fed_sums, feed_sums = Sum(mv), Sum(mv)
+    moved = shrink_back(*deps)
+    back_late = trade([after(v, *deps) for v in back_late])
+    gated = after(shrink_full, *deps)
+    fed = list(times_back(hidden[0], gated, len(early) * S))
+    fed += list(times_back(hidden[1], gated, S))
+    feed_sums.blocks[-1] = chip_sum(back_late)
+    deps = moved + fed + feed_sums.blocks[-1:]
+    moved = feed_sums(1, *deps) + shrink_back(*deps)
+    fed = [after(v, *deps) for v in fed]
+    fed = [trade(fed[i * S : (i + 1) * S]) for i in planes]
+    middle, own = early[1:], early[:1]
+    terms_middle, back_middle = feed_backward(
+        items_of(grad_blocks, middle),
+        after(shrink_full, *deps),
+        expand_full,
+        *kept_early[1:],
+        [i * S + p for i in middle for p in range(S)],
+        hidden_width,
+    )
+    fed_sums.blocks[-1] = chip_sum(fed[-1])
+    deps = moved + [terms_middle] + fed_sums.blocks[-1:]
+    moved = fed_sums(1, *deps)
+    back_middle = [after(v, *deps) for v in back_middle]
+    back_middle = [trade(back_middle[i * S : (i + 1) * S]) for i in range(len(middle))]
+    terms_own, back_own = feed_backward(
+        items_of(grad_blocks, own),
+        after(shrink_full, *deps),
+        expand_full,
+        *kept_early[1:],
+        range(S),
+        hidden_width,
+    )
+    for i, block in zip(middle, back_middle):
+        feed_sums.blocks[i] = chip_sum(block)
+    deps = moved + [terms_own] + [feed_sums.blocks[i] for i in middle]
+    moved = feed_sums(1, *deps)
+    back_own = trade([after(v, *deps) for v in back_own])
+    gate_up = (terms_own, terms_middle, terms_late)
+    feed_items = items_of(feed_blocks, own + middle + late)
+    expand_terms = list(
+        weight_terms(feed_items, after(gate_up, *deps), 0, 2 * pieces, hidden_width)
+    )
+    feed_sums.blocks[0] = chip_sum(back_own)
+    for i in planes[:-1]:
+        fed_sums.blocks[i] = chip_sum([after(v, *deps) for v in fed[i]])
+    deps = moved + expand_terms[-1:] + feed_sums.blocks[:1]
+    gate_back, up_back = RingSum(mv), RingSum(mv)
+
+    def known():
+        gate_back.terms.update(zip(ring_order, expand_terms[0::2]))
+        up_back.terms.update(zip(ring_order, expand_terms[1::2]))
+
+    known()
+    moved = feed_sums(1, *deps) + gate_back(*deps)
+    for i in range(1, parts):
+        expand_terms += weight_terms(
+            feed_items, after(gate_up, *deps), i, 2 * pieces, hidden_width
+        )
+    known()
+    deps = moved + expand_terms[-1:]
+    moved = fed_sums(1, *deps) + up_back(*deps)
+    resid_back, gain_two = norm_back(
+        after(feed_sums.total(), *deps), normed_two, scale_two, norm_gains[1]
+    )
     grad_resid = cotangent.astype(f32) + resid_back
-    layer_output = (resid + mv.plane_sum(fed)).astype(low)
-
-    def all_of(blocks):
-        return [v for block in blocks for v in block]
-
-    def terms_of(lefts, rights):
-        if group == 1:
-            return [weight_terms(lefts, rights, k, hidden_width) for k in ks]
-        joined = [weight_terms(lefts, rights, g, group * hidden_width) for g in range(Z // group)]
-        return [
-            lax.slice_in_dim(
-                joined[k // group],
-                k % group * hidden_width,
-                (k % group + 1) * hidden_width,
-                axis=-1,
-            )
-            for k in ks
-        ]
-
-    shrink_sum = mv.ring_sum(
-        terms_of(all_of(grad_blocks), [h[None] for h in hidden])
-    ).astype(low)[0]
-    expand_sum = mv.ring_sum(terms_of(all_of(feed_blocks), grad_gate_up)).astype(low)
-
-    def rows_part(value, d):
-        return lax.dynamic_slice_in_dim(value, (mv.f ^ d) * row_block, row_block, -2)
-
-    def columns(value):
-        pieces = [rows_part(value, 0)] + [mv.plane(rows_part(value, d), d) for d in planes if d]
-        return mv.place(pieces, value.ndim - 1, mv.f).astype(f32)
-
-    shrink_grad = columns(shrink_sum)
-    expand_grad = columns(expand_sum)
-
     grad_attn = mv.place(mv.mates(grad_resid.astype(low)), 0, mv.s)
-    attn_terms = [None] * Z
+    deps = moved + [grad_attn]
+    order = (ring_order * 4)[:4] if Z < 4 else ring_order
+    attn_sums = {}
     grad_proj = [None] * Z
-    for k in list(range(1, Z)) + [0]:
+
+    def attend_back(k):
         grad_proj[k], terms = attend_backward(
-            mv.partners, saved[k], acts, grad_attn, attn_full[k], tables
+            after(mv.partners, *deps), saved[k], acts, grad_attn, attn_full[k], tables
         )
-        attn_terms[k] = mv.plane_sum(terms)
-    attn_grad = mv.ring_sum(attn_terms)
-    inward_grad, outward_grad = attn_grad[:3], attn_grad[3]
-    grad_acts = spread(mv.partners, grad_proj, attn_full, 0, 3)
+        attn_sums[k] = Sum(mv)
+        attn_sums[k].blocks[:] = terms
+        return [grad_proj[k]]
+
+    moved = fed_sums(1, *deps) + gate_back(*deps)
+    deps = moved + attend_back(order[0])
+    moved = attn_sums[order[0]](2, *deps) + up_back(*deps)
+    deps = moved + attend_back(order[1])
+    layer_output = (resid + fed_sums.total()).astype(low)
+    moved = attn_sums[order[0]](1, *deps) + attn_sums[order[1]](1, *deps) + gate_back(*deps)
+    deps = moved + attend_back(order[2])
+    moved = attn_sums[order[1]](2, *deps) + up_back(*deps)
+    deps = moved + attend_back(order[3])
+    shrink_moved, shrink_grad = columns(shrink_back.total().astype(low), *deps)
+    moved = attn_sums[order[2]](2, *deps) + shrink_moved
+    grad_acts = spread(after(mv.partners, *deps), grad_proj, attn_full, 0, 3)
+    deps = moved + [grad_acts]
+    attn_back = RingSum(mv)
+    for k in order[:2]:
+        attn_back.terms[k] = attn_sums[k].total()
+    moved = attn_sums[order[2]](1, *deps) + attn_sums[order[3]](1, *deps) + attn_back(*deps)
     grad_acts = mv.mates_sum([part(grad_acts, d) for d in range(S)])
     input_back, gain_one = norm_back(grad_acts, normed_one, scale_one, norm_gains[0])
     input_grad = (grad_resid + input_back).astype(low)
+    deps = moved + [input_grad]
+    attn_back.terms[order[2]] = attn_sums[order[2]].total()
+    moved = attn_sums[order[3]](2, *deps) + attn_back(*deps)
+    deps = moved
+    attn_back.terms[order[3]] = attn_sums[order[3]].total()
+    gate_grad = columns(gate_back.total().astype(low), *deps)[1]
+    up_grad = columns(up_back.total().astype(low), *deps)[1]
+    attn_back(*deps)
+    attn_grad = attn_back.total()
+    expand_grad = jnp.stack([gate_grad, up_grad])
+    inward_grad, outward_grad = attn_grad[:3], attn_grad[3]
 
     owned_squares = (
         jnp.sum(inward_grad * inward_grad)

time: 1100 us -> 981 us (0.89)
  waiting for transfers between devices: 362 us -> 299 us
  Pallas kernels: 471 us -> 416 us
  local copies, waits for them, and re-layouts: 38.5 us -> 55.6 us
  other arithmetic: 129 us -> 112 us
    ppermute x36, waiting for transfers between devices: 140 us -> 51.8 us  [hop(): return lax.ppermute(value, ('fsdp', 'tp'), pairs)]
    ppermute x11 -> x17, waiting for transfers between devices: 49.1 us -> 97 us  [plane(): return lax.ppermute(value, 'fsdp', [(i, i ^ mask) for i in range(self.F)])]
    ppermute x18 -> x24, waiting for transfers between devices: 167 us -> 134 us  [ring(): return lax.ppermute(value, 'tp', step)]
    pallas_call x8 -> x4, Pallas kernels: 101 us -> 72.8 us  [weight_terms(): pl.pallas_call(functools.partial(weight_kernel, len(lefts), len(rights)),...]
    pallas_call x16 -> x7, Pallas kernels: 181 us -> 154 us  [the longest x3 83.6 us: feed_backward(): pl.pallas_call(functools.partial(feed_back_kernel, count, width), grid=(c...]
    another operation x3 -> x1, other arithmetic: 14.1 us -> 0.08 us  [the longest x2 12.5 us: grouped(): return jnp.stack(blocks)]
    unnamed x150 -> x233, local copies, waits for them, and re-layouts: 11.3 us -> 22.2 us
    convert_element_type x21 -> x22, other arithmetic: 54.4 us -> 50.5 us  [the longest x6 16.8 us: __call__(): source = (source.astype(f32) + got[0].astype(f32)).astype(low)]
  transfers between devices with their start and end apart: 88 -> 100, of which waited for: 28 -> 37; matrix products, arithmetic and copies ran while one was open for 12% -> 12% of each run, Pallas kernels for 43% -> 43%
where the time goes in v3:
time: 981 us; the launch traced here: 976 us
  Pallas kernels  416 us (42%)
  waiting for transfers between devices  299 us (30%)
  other arithmetic  112 us (11%)
  starting transfers between devices  87.4 us (9%)
  local copies, waits for them, and re-layouts  55.6 us (6%)
    ppermute x24, waiting for transfers between devices, ring(): return lax.ppermute(value, 'tp', step)  134 us
    ppermute x17, waiting for transfers between devices, plane(): return lax.ppermute(value, 'fsdp', [(i, i ^ mask) for i in range(self.F)])  97 us
    pallas_call x4, Pallas kernels, attend_backward(): pl.pallas_call(functools.partial(backward_kernel, block, count), out_shap...  96.5 us
    pallas_call x3, Pallas kernels, feed_backward(): pl.pallas_call(functools.partial(feed_back_kernel, count, width), grid=(c...  83.6 us
    pallas_call x4, Pallas kernels, weight_terms(): pl.pallas_call(functools.partial(weight_kernel, len(lefts), len(rights)),...  72.8 us
    pallas_call x4, Pallas kernels, attend_forward(): pl.pallas_call(functools.partial(forward_kernel, block, len(weights)), ou...  62.2 us
    ppermute x36, waiting for transfers between devices, hop(): return lax.ppermute(value, ('fsdp', 'tp'), pairs)  51.8 us
    pallas_call x2, Pallas kernels, feed_forward(): pl.pallas_call(functools.partial(feed_kernel, count, width), grid=(count,...  47.4 us
  transfers between devices with their start and end apart: 100, of which 37 were waited for; matrix products, arithmetic and copies ran while one was open for 12% of the time, Pallas kernels for 43%

profile of v3, /device:TPU:0, one launch (start us, length us, event | category | flops | bytes accessed | tf_op | source)
XLA Modules:
  0.0 976.1 jit_solution(11173862519677232618)
XLA Ops:
  35.5 27.9 %collective-permute-done.4 = bf16[2,512,256]{2,1,0:T(8,128)(2,1)S(1)} collective-permute-done((bf16[2,512,256]{2,1,0:T(8,128)(2,1)}, bf16[2,512,256]{2,1,0:T(8,128)(2,1)S(1)}, u32[]{:S(2)}, u32[]{:S(2)}) %collective-permute-start.4) | collective-permute-done | bytes 524320 | tf_op jit(solution)/shard_map/ppermute | solution.py:56
  77.4 14.8 %collective-permute-done.10.refs_0_.refs_12_.refs_2_ = bf16[4,512,256]{2,1,0:T(8,128)(2,1)S(1)} collective-permute-done((bf16[4,512,256]{2,1,0:T(8,128)(2,1)}, bf16[4,512,256]{2,1,0:T(8,128)(2,1)S(1)}, u32[]{:S(2)}, u32[]{:S(2)}) %collective-permute-start.10) | collective-permute-done | bytes 1048608 | tf_op jit(solution)/shard_map/ppermute | solution.py:75
  114.2 15.6 %attend_forward.4 = (bf16[1024,256]{1,0:T(8,128)(2,1)}, bf16[1024,256]{1,0:T(8,128)(2,1)}, bf16[1024,256]{1,0:T(8,128)(2,1)}, bf16[1024,256]{1,0:T(8,128)(2,1)}, f32[1024,128]{1,0:T(8,128)}) custom-call(s32[4]{0:T(128)} %pad_add_fusion.partners, bf16[1024,2048]{1,0:T(8,128)(2,1)} %constant_dynamic-update-slice_fusion.19.acts, ...), custom_call_target="tpu_custom_call" | custom-call | flops 1503238528 | bytes 2097152 | tf_op jit(solution)/shard_map/attend_forward/pallas_call | solution.py:307
  145.7 15.5 %attend_forward.5 = (bf16[1024,256]{1,0:T(8,128)(2,1)}, bf16[1024,256]{1,0:T(8,128)(2,1)}, bf16[1024,256]{1,0:T(8,128)(2,1)}, bf16[1024,256]{1,0:T(8,128)(2,1)}, f32[1024,128]{1,0:T(8,128)}) custom-call(s32[4]{0:T(128)} %pad_add_fusion.partners, bf16[1024,2048]{1,0:T(8,128)(2,1)} %constant_dynamic-update-slice_fusion.19.acts, ...), custom_call_target="tpu_custom_call" | custom-call | flops 1503238528 | bytes 2097152 | tf_op jit(solution)/shard_map/attend_forward/pallas_call | solution.py:307
  179.3 15.6 %attend_forward.6 = (bf16[1024,256]{1,0:T(8,128)(2,1)}, bf16[1024,256]{1,0:T(8,128)(2,1)}, bf16[1024,256]{1,0:T(8,128)(2,1)}, bf16[1024,256]{1,0:T(8,128)(2,1)}, f32[1024,128]{1,0:T(8,128)}) custom-call(s32[4]{0:T(128)} %pad_add_fusion.partners, bf16[1024,2048]{1,0:T(8,128)(2,1)} %constant_dynamic-update-slice_fusion.19.acts, ...), custom_call_target="tpu_custom_call" | custom-call | flops 1503238528 | bytes 2097152 | tf_op jit(solution)/shard_map/attend_forward/pallas_call | solution.py:307
  206.3 15.5 %attend_forward.7 = (bf16[1024,256]{1,0:T(8,128)(2,1)}, bf16[1024,256]{1,0:T(8,128)(2,1)}, bf16[1024,256]{1,0:T(8,128)(2,1)}, bf16[1024,256]{1,0:T(8,128)(2,1)}, f32[1024,128]{1,0:T(8,128)}) custom-call(s32[4]{0:T(128)} %pad_add_fusion.partners, bf16[1024,2048]{1,0:T(8,128)(2,1)} %constant_dynamic-update-slice_fusion.19.acts, ...), custom_call_target="tpu_custom_call" | custom-call | flops 1503238528 | bytes 2097152 | tf_op jit(solution)/shard_map/attend_forward/pallas_call | solution.py:307
  248.2 23.8 %collective-permute-done.26 = bf16[512,256]{1,0:T(8,128)(2,1)S(1)} collective-permute-done((bf16[512,256]{1,0:T(8,128)(2,1)S(1)}, bf16[512,256]{1,0:T(8,128)(2,1)S(1)}, u32[]{:S(2)}, u32[]{:S(2)}) %collective-permute-start.26) | collective-permute-done | bytes 262176 | tf_op jit(solution)/shard_map/ppermute | solution.py:56
  273.5 26.4 %collective-permute-done.31 = bf16[2048,256]{1,0:T(8,128)(2,1)S(1)} collective-permute-done((bf16[2048,256]{1,0:T(8,128)(2,1)S(1)}, bf16[2048,256]{1,0:T(8,128)(2,1)S(1)}, u32[]{:S(2)}, u32[]{:S(2)}) %collective-permute-start.31) | collective-permute-done | bytes 1048608 | tf_op jit(solution)/shard_map/ppermute | solution.py:75
  301.3 27.3 %collective-permute-done.34 = bf16[2048,256]{1,0:T(8,128)(2,1)S(1)} collective-permute-done((bf16[2048,256]{1,0:T(8,128)(2,1)S(1)}, bf16[2048,256]{1,0:T(8,128)(2,1)S(1)}, u32[]{:S(2)}, u32[]{:S(2)}) %collective-permute-start.34) | collective-permute-done | bytes 1048608 | tf_op jit(solution)/shard_map/ppermute | solution.py:75
  340.2 33.8 %feed_forward.2 = (bf16[3072,1024]{1,0:T(8,128)(2,1)}, bf16[3072,1024]{1,0:T(8,128)(2,1)}, bf16[3072,1024]{1,0:T(8,128)(2,1)}) custom-call(bf16[512,2048]{1,0:T(8,128)(2,1)S(1)} %multiply_convert_fusion.refs_0_, bf16[512,2048]{1,0:T(8,128)(2,1)S(1)} %collective-permute-done.29.refs_1_, bf16[512,2048]{1,0:T(8,128)(2,1)S(1)} %collective-permute-done.30.refs_2_, ...), custom_call_target="tpu_custom_call" | custom-call | flops 5153960960 | bytes 4194304 | tf_op jit(solution)/shard_map/feed_forward/pallas_call | solution.py:505
  425.0 13.9 %weight_terms.4 = (bf16[2048,256]{1,0:T(8,128)(2,1)}, bf16[2048,256]{1,0:T(8,128)(2,1)S(1)}) custom-call(bf16[512,2048]{1,0:T(8,128)(2,1)S(1)} %copy-done.1, bf16[512,2048]{1,0:T(8,128)(2,1)S(1)} %collective-permute-done.41.refs_1_, bf16[512,2048]{1,0:T(8,128)(2,1)} %collective-permute-done.21.refs_2_.refs_0_, ...), custom_call_target="tpu_custom_call" | custom-call | flops 1717986944 | bytes 5033164 | tf_op jit(solution)/shard_map/weight_terms/pallas_call | solution.py:627
  442.8 23.1 %feed_backward.3 = (bf16[1024,2048]{1,0:T(8,128)(2,1)}, bf16[512,2048]{1,0:T(8,128)(2,1)S(1)}, bf16[512,2048]{1,0:T(8,128)(2,1)S(1)}) custom-call(bf16[512,2048]{1,0:T(8,128)(2,1)} %collective-permute-done.39.refs_6_.refs_0_, bf16[512,2048]{1,0:T(8,128)(2,1)} %copy-done.54, bf16[2048,1024]{1,0:T(8,128)(2,1)} %pad_maximum_fusion.refs_2_.weight.refs_4_, ...), custom_call_target="tpu_custom_call" | custom-call | flops 2576980480 | bytes 3774873 | tf_op jit(solution)/shard_map/feed_backward/pallas_call | solution.py:552
  473.8 16.3 %times_back.2 = (bf16[512,2048]{1,0:T(8,128)(2,1)S(1)}, bf16[512,2048]{1,0:T(8,128)(2,1)}, bf16[512,2048]{1,0:T(8,128)(2,1)S(1)}, bf16[512,2048]{1,0:T(8,128)(2,...) custom-call(bf16[3072,1024]{1,0:T(8,128)(2,1)} %get-tuple-element.260.refs_8_.value, ...), custom_call_target="tpu_custom_call" | custom-call | flops 2576980480 | bytes 2097152 | tf_op jit(solution)/shard_map/times_back/pallas_call | solution.py:592
  498.5 37.9 %feed_backward.4 = (bf16[2048,2048]{1,0:T(8,128)(2,1)}, bf16[512,2048]{1,0:T(8,128)(2,1)S(1)}, bf16[512,2048]{1,0:T(8,128)(2,1)S(1)}, bf16[512,2048]{1,0:T(8,128)(2,1)}, bf16[512,2048]{1,0:T(8,128)(2,1)}) custom-call(bf16[512,2048]{1,0:T(8,128)(2,1)} %collective-permute-done.21.refs_2_.refs_0_, bf16[512,2048]{1,0:T(8,128)(2,1)} %copy-done.13, ...), custom_call_target="tpu_custom_call" | custom-call | flops 5153960960 | bytes 5452595 | tf_op jit(solution)/shard_map/feed_backward/pallas_call | solution.py:552
  540.2 22.5 %feed_backward.5 = (bf16[1024,2048]{1,0:T(8,128)(2,1)}, bf16[512,2048]{1,0:T(8,128)(2,1)S(1)}, bf16[512,2048]{1,0:T(8,128)(2,1)S(1)}) custom-call(bf16[512,2048]{1,0:T(8,128)(2,1)} %refs_0_.2, bf16[512,2048]{1,0:T(8,128)(2,1)} %copy-done.3, bf16[2048,1024]{1,0:T(8,128)(2,1)} %pad_maximum_fusion.refs_2_.weight.refs_4_, ...), custom_call_target="tpu_custom_call" | custom-call | flops 2576980480 | bytes 4613734 | tf_op jit(solution)/shard_map/feed_backward/pallas_call | solution.py:552
  573.3 23.2 %weight_terms.6 = (bf16[2048,256]{1,0:T(8,128)(2,1)}, bf16[2048,256]{1,0:T(8,128)(2,1)S(1)}, bf16[2048,256]{1,0:T(8,128)(2,1)S(1)}, bf16[2048,256]{1,0:T(8,128)(2,1)S(1)}) custom-call(bf16[512,2048]{1,0:T(8,128)(2,1)S(1)} %multiply_convert_fusion.refs_0_, bf16[512,2048]{1,0:T(8,128)(2,1)S(1)} %copy-done.5, bf16[512,2048]{1,0:T(8,128)(2,1)S(1)} %copy-done.7, ...), custom_call_target="tpu_custom_call" | custom-call | flops 3435973888 | bytes 6710886 | tf_op jit(solution)/shard_map/weight_terms/pallas_call | solution.py:627
  603.7 22.9 %weight_terms.7 = (bf16[2048,256]{1,0:T(8,128)(2,1)S(1)}, bf16[2048,256]{1,0:T(8,128)(2,1)S(1)}, bf16[2048,256]{1,0:T(8,128)(2,1)S(1)}, bf16[2048,256]{1,0:T(8,128)(2,1)S(1)}) custom-call(bf16[512,2048]{1,0:T(8,128)(2,1)S(1)} %multiply_convert_fusion.refs_0_, bf16[512,2048]{1,0:T(8,128)(2,1)S(1)} %copy-done.5, bf16[512,2048]{1,0:T(8,128)(2,1)S(1)} %copy-done.7, ...), custom_call_target="tpu_custom_call" | custom-call | flops 3435973888 | bytes 6710886 | tf_op jit(solution)/shard_map/weight_terms/pallas_call | solution.py:627
  650.1 21.6 %collective-permute-done.63 = bf16[2048,256]{1,0:T(8,128)(2,1)S(1)} collective-permute-done((bf16[2048,256]{1,0:T(8,128)(2,1)S(1)}, bf16[2048,256]{1,0:T(8,128)(2,1)S(1)}, u32[]{:S(2)}, u32[]{:S(2)}) %collective-permute-start.63) | collective-permute-done | bytes 1048608 | tf_op jit(solution)/shard_map/ppermute | solution.py:75
  675.7 24.2 %attend_backward.4 = (bf16[1024,768]{1,0:T(8,128)(2,1)}, bf16[4,512,256]{2,1,0:T(8,128)(2,1)}, bf16[4,512,256]{2,1,0:T(8,128)(2,1)}, bf16[4,512,256]{2,1,0:T(8,128)(2,1)}, bf16[4,512,256]{2,1,0:T(8,128)(2,1)}) custom-call(s32[4]{0:T(128)} %pad_add_fusion.partners, bf16[1024,256]{1,0:T(8,128)(2,1)} %get-tuple-element.340.query, ...), custom_call_target="tpu_custom_call" | custom-call | flops 3221225472 | bytes 3460300 | tf_op jit(solution)/shard_map/attend_backward/pallas_call | solution.py:371
  704.9 24.3 %attend_backward.5 = (bf16[1024,768]{1,0:T(8,128)(2,1)}, bf16[4,512,256]{2,1,0:T(8,128)(2,1)}, bf16[4,512,256]{2,1,0:T(8,128)(2,1)}, bf16[4,512,256]{2,1,0:T(8,128)(2,1)}, bf16[4,512,256]{2,1,0:T(8,128)(2,1)}) custom-call(s32[4]{0:T(128)} %pad_add_fusion.partners, bf16[1024,256]{1,0:T(8,128)(2,1)} %get-tuple-element.346.query, ...), custom_call_target="tpu_custom_call" | custom-call | flops 3221225472 | bytes 3460300 | tf_op jit(solution)/shard_map/attend_backward/pallas_call | solution.py:371
  734.1 24.1 %attend_backward.6 = (bf16[1024,768]{1,0:T(8,128)(2,1)}, bf16[4,512,256]{2,1,0:T(8,128)(2,1)}, bf16[4,512,256]{2,1,0:T(8,128)(2,1)}, bf16[4,512,256]{2,1,0:T(8,128)(2,1)}, bf16[4,512,256]{2,1,0:T(8,128)(2,1)}) custom-call(s32[4]{0:T(128)} %pad_add_fusion.partners, bf16[1024,256]{1,0:T(8,128)(2,1)} %get-tuple-element.364.query, ...), custom_call_target="tpu_custom_call" | custom-call | flops 3221225472 | bytes 3460300 | tf_op jit(solution)/shard_map/attend_backward/pallas_call | solution.py:371
  766.2 24.0 %attend_backward.7 = (bf16[1024,768]{1,0:T(8,128)(2,1)}, bf16[4,512,256]{2,1,0:T(8,128)(2,1)}, bf16[4,512,256]{2,1,0:T(8,128)(2,1)}, bf16[4,512,256]{2,1,0:T(8,128)(2,1)}, bf16[4,512,256]{2,1,0:T(8,128)(2,1)}) custom-call(s32[4]{0:T(128)} %pad_add_fusion.partners, bf16[1024,256]{1,0:T(8,128)(2,1)} %get-tuple-element.375.query, ...), custom_call_target="tpu_custom_call" | custom-call | flops 3221225472 | bytes 3460300 | tf_op jit(solution)/shard_map/attend_backward/pallas_call | solution.py:371
  793.2 21.6 %spread.3 = bf16[1024,2048]{1,0:T(8,128)(2,1)} custom-call(s32[4]{0:T(128)} %pad_add_fusion.partners, bf16[1024,768]{1,0:T(8,128)(2,1)} %get-tuple-element.379.refs_0_, bf16[1024,768]{1,0:T(8,128)(2,1)} %get-tuple-element.344.refs_1_, bf16[1024,768]{1,0:T(8,128)(2,1)} %get-tuple-element.357.refs_2_, bf16[1024,768]{1,0:T(8,128)(2,1)} %get-tuple-element.368.refs_3_, ...), custom_call_target="tpu_custom_call" | custom-call | flops 2576980480 | bytes 4613734 | tf_op jit(solution)/shard_map/spread/pallas_call | solution.py:412
  876.2 16.8 %collective-permute-done.86 = bf16[4,512,256]{2,1,0:T(8,128)(2,1)S(1)} collective-permute-done((bf16[4,512,256]{2,1,0:T(8,128)(2,1)}, bf16[4,512,256]{2,1,0:T(8,128)(2,1)S(1)}, u32[]{:S(2)}, u32[]{:S(2)}) %collective-permute-start.86) | collective-permute-done | bytes 1048608 | tf_op jit(solution)/shard_map/ppermute | solution.py:64
  (532 shorter events, 437.0 us)
Async XLA Ops:
  15.6 47.8 %collective-permute-start = (bf16[4,512,256]{2,1,0:T(8,128)(2,1)S(1)}, bf16[4,512,256]{2,1,0:T(8,128)(2,1)S(1)}, u32[]{:S(2)}, u32[]{:S(2)}) collective-permute-start(bf16[4,512,256]{2,1,0:T(8,128)(2,1)S(1)} %pad_maximum_fusion.1.refs_0_.refs_4_.refs_2_), channel_id=1, source_target_pairs={{0,8},{1,17},{2,10},{3,19},{4,12},{5,21},{6,14},{7,23},{8,0},{9,25... | collective-permute-start | bytes 3145736 | tf_op jit(solution)/shard_map/ppermute | solution.py:64
  16.9 46.5 %collective-permute-start.1 = (bf16[4,512,256]{2,1,0:T(8,128)(2,1)S(1)}, bf16[4,512,256]{2,1,0:T(8,128)(2,1)}, u32[]{:S(2)}, u32[]{:S(2)}) collective-permute-start(bf16[4,512,256]{2,1,0:T(8,128)(2,1)S(1)} %pad_maximum_fusion.1.refs_0_.refs_4_.refs_2_), channel_id=1, source_target_pairs={{0,16},{1,9},{2,18},{3,11},{4,20},{5,13},{6,22},{7,15},{8,24},{9,1... | collective-permute-start | bytes 3145736 | tf_op jit(solution)/shard_map/ppermute | solution.py:64
  18.4 45.0 %collective-permute-start.2 = (bf16[4,512,256]{2,1,0:T(8,128)(2,1)S(1)}, bf16[4,512,256]{2,1,0:T(8,128)(2,1)}, u32[]{:S(2)}, u32[]{:S(2)}) collective-permute-start(bf16[4,512,256]{2,1,0:T(8,128)(2,1)S(1)} %pad_maximum_fusion.1.refs_0_.refs_4_.refs_2_), channel_id=1, source_target_pairs={{0,2},{1,3},{2,4},{3,5},{4,6},{5,7},{6,0},{7,1},{8,10},{9,11},{10,... | collective-permute-start | bytes 3145736 | tf_op jit(solution)/shard_map/ppermute | solution.py:75
  28.3 35.1 %collective-permute-start.4 = (bf16[2,512,256]{2,1,0:T(8,128)(2,1)}, bf16[2,512,256]{2,1,0:T(8,128)(2,1)S(1)}, u32[]{:S(2)}, u32[]{:S(2)}) collective-permute-start(bf16[2,512,256]{2,1,0:T(8,128)(2,1)} %get-tuple-element.451), channel_id=1, source_target_pairs={{0,16},{8,24},{16,0},{24,8},{1,17},{9,25},{17,1},{25,9},{2,18},{10... | collective-permute-start | bytes 1572872 | tf_op jit(solution)/shard_map/ppermute | solution.py:56
  30.3 33.1 %collective-permute-start.5 = (bf16[2,512,256]{2,1,0:T(8,128)(2,1)}, bf16[2,512,256]{2,1,0:T(8,128)(2,1)S(1)}, u32[]{:S(2)}, u32[]{:S(2)}) collective-permute-start(bf16[2,512,256]{2,1,0:T(8,128)(2,1)} %get-tuple-element.450), channel_id=1, source_target_pairs={{0,24},{8,16},{16,8},{24,0},{1,25},{9,17},{17,9},{25,1},{2,26},{10... | collective-permute-start | bytes 1572872 | tf_op jit(solution)/shard_map/ppermute | solution.py:56
  70.4 32.6 %collective-permute-start.7 = (bf16[4,512,256]{2,1,0:T(8,128)(2,1)S(1)}, bf16[4,512,256]{2,1,0:T(8,128)(2,1)}, u32[]{:S(2)}, u32[]{:S(2)}) collective-permute-start(bf16[4,512,256]{2,1,0:T(8,128)(2,1)S(1)} %collective-permute-done.refs_1_.refs_5_.refs_3_), channel_id=1, source_target_pairs={{0,16},{1,9},{2,18},{3,11},{4,20},{5,13},{6,22},{7,15},{8,24},{9,1... | collective-permute-start | bytes 3145736 | tf_op jit(solution)/shard_map/ppermute | solution.py:64
  107.5 32.4 %collective-permute-start.11 = (bf16[4,512,256]{2,1,0:T(8,128)(2,1)}, bf16[4,512,256]{2,1,0:T(8,128)(2,1)}, u32[]{:S(2)}, u32[]{:S(2)}) collective-permute-start(bf16[4,512,256]{2,1,0:T(8,128)(2,1)} %collective-permute-done.8.refs_1_.refs_9_.refs_3_), channel_id=1, source_target_pairs={{0,16},{1,9},{2,18},{3,11},{4,20},{5,13},{6,22},{7,15},{8,24},{9,1... | collective-permute-start | bytes 3145736 | tf_op jit(solution)/shard_map/ppermute | solution.py:64
  144.6 32.2 %collective-permute-start.15 = (bf16[4,512,256]{2,1,0:T(8,128)(2,1)S(1)}, bf16[4,512,256]{2,1,0:T(8,128)(2,1)S(1)}, u32[]{:S(2)}, u32[]{:S(2)}) collective-permute-start(bf16[4,512,256]{2,1,0:T(8,128)(2,1)S(1)} %collective-permute-done.12.refs_1_.refs_13_.refs_3_), channel_id=1, source_target_pairs={{0,16},{1,9},{2,18},{3,11},{4,20},{5,13},{6,22},{7,15},{8,24},{9,1... | collective-permute-start | bytes 3145736 | tf_op jit(solution)/shard_map/ppermute | solution.py:64
  234.7 37.3 %collective-permute-start.28 = (bf16[512,2048]{1,0:T(8,128)(2,1)S(1)}, bf16[512,2048]{1,0:T(8,128)(2,1)S(1)}, u32[]{:S(2)}, u32[]{:S(2)}) collective-permute-start(bf16[512,2048]{1,0:T(8,128)(2,1)S(1)} %copy-done.1), channel_id=1, source_target_pairs={{0,16},{1,9},{2,18},{3,11},{4,20},{5,13},{6,22},{7,15},{8,24},{9,1... | collective-permute-start | bytes 6291464 | tf_op jit(solution)/shard_map/ppermute | solution.py:64
  237.2 34.8 %collective-permute-start.24 = (bf16[2048,256]{1,0:T(8,128)(2,1)S(1)}, bf16[2048,256]{1,0:T(8,128)(2,1)S(1)}, u32[]{:S(2)}, u32[]{:S(2)}) collective-permute-start(bf16[2048,256]{1,0:T(8,128)(2,1)S(1)} %copy-done.92), channel_id=1, source_target_pairs={{0,2},{1,3},{2,4},{3,5},{4,6},{5,7},{6,0},{7,1},{8,10},{9,11},{10,... | collective-permute-start | bytes 3145736 | tf_op jit(solution)/shard_map/ppermute | solution.py:75
  239.8 32.2 %collective-permute-start.26 = (bf16[512,256]{1,0:T(8,128)(2,1)S(1)}, bf16[512,256]{1,0:T(8,128)(2,1)S(1)}, u32[]{:S(2)}, u32[]{:S(2)}) collective-permute-start(bf16[512,256]{1,0:T(8,128)(2,1)S(1)} %get-tuple-element.238), channel_id=1, source_target_pairs={{0,16},{8,24},{16,0},{24,8},{1,17},{9,25},{17,1},{25,9},{2,18},{10... | collective-permute-start | bytes 786440 | tf_op jit(solution)/shard_map/ppermute | solution.py:56
  241.0 31.0 %collective-permute-start.25 = (bf16[512,256]{1,0:T(8,128)(2,1)S(1)}, bf16[512,256]{1,0:T(8,128)(2,1)S(1)}, u32[]{:S(2)}, u32[]{:S(2)}) collective-permute-start(bf16[512,256]{1,0:T(8,128)(2,1)S(1)} %get-tuple-element.237), channel_id=1, source_target_pairs={{0,8},{8,0},{16,24},{24,16},{1,9},{9,1},{17,25},{25,17},{2,10},{10... | collective-permute-start | bytes 786440 | tf_op jit(solution)/shard_map/ppermute | solution.py:56
  333.9 40.2 %collective-permute-start.37 = (bf16[512,2048]{1,0:T(8,128)(2,1)S(1)}, bf16[512,2048]{1,0:T(8,128)(2,1)S(1)}, u32[]{:S(2)}, u32[]{:S(2)}) collective-permute-start(bf16[512,2048]{1,0:T(8,128)(2,1)S(1)} %collective-permute-done.30.refs_2_), channel_id=1, source_target_pairs={{0,16},{1,9},{2,18},{3,11},{4,20},{5,13},{6,22},{7,15},{8,24},{9,1... | collective-permute-start | bytes 6291464 | tf_op jit(solution)/shard_map/ppermute | solution.py:64
  337.9 36.1 %collective-permute-start.36 = (bf16[2048,256]{1,0:T(8,128)(2,1)S(1)}, bf16[2048,256]{1,0:T(8,128)(2,1)S(1)}, u32[]{:S(2)}, u32[]{:S(2)}) collective-permute-start(bf16[2048,256]{1,0:T(8,128)(2,1)S(1)} %constant_dynamic-update-slice_fusion.13), channel_id=1, source_target_pairs={{0,2},{1,3},{2,4},{3,5},{4,6},{5,7},{6,0},{7,1},{8,10},{9,11},{10,... | collective-permute-start | bytes 3145736 | tf_op jit(solution)/shard_map/ppermute | solution.py:75
  375.0 31.3 %collective-permute-start.43 = (bf16[512,2048]{1,0:T(8,128)(2,1)S(1)}, bf16[512,2048]{1,0:T(8,128)(2,1)S(1)}, u32[]{:S(2)}, u32[]{:S(2)}) collective-permute-start(bf16[512,2048]{1,0:T(8,128)(2,1)S(1)} %collective-permute-done.28.refs_4_.refs_2_), channel_id=1, source_target_pairs={{0,1},{1,0},{2,3},{3,2},{4,5},{5,4},{6,7},{7,6},{8,9},{9,8},{10,11... | collective-permute-start | bytes 6291464 | tf_op jit(solution)/shard_map/ppermute | solution.py:67
  406.5 32.4 %collective-permute-start.44 = (bf16[2048,256]{1,0:T(8,128)(2,1)}, bf16[2048,256]{1,0:T(8,128)(2,1)}, u32[]{:S(2)}, u32[]{:S(2)}) collective-permute-start(bf16[2048,256]{1,0:T(8,128)(2,1)} %collective-permute-done.38), channel_id=1, source_target_pairs={{0,2},{1,3},{2,4},{3,5},{4,6},{5,7},{6,0},{7,1},{8,10},{9,11},{10,... | collective-permute-start | bytes 3145736 | tf_op jit(solution)/shard_map/ppermute | solution.py:75
  494.1 42.3 %collective-permute-start.49 = (bf16[512,2048]{1,0:T(8,128)(2,1)}, bf16[512,2048]{1,0:T(8,128)(2,1)}, u32[]{:S(2)}, u32[]{:S(2)}) collective-permute-start(bf16[512,2048]{1,0:T(8,128)(2,1)} %get-tuple-element.287), channel_id=1, source_target_pairs={{0,1},{1,0},{2,3},{3,2},{4,5},{5,4},{6,7},{7,6},{8,9},{9,8},{10,11... | collective-permute-start | bytes 6291464 | tf_op jit(solution)/shard_map/ppermute | solution.py:67
  494.2 44.7 %collective-permute-start.50 = (bf16[512,2048]{1,0:T(8,128)(2,1)S(1)}, bf16[512,2048]{1,0:T(8,128)(2,1)}, u32[]{:S(2)}, u32[]{:S(2)}) collective-permute-start(bf16[512,2048]{1,0:T(8,128)(2,1)S(1)} %add_convert_fusion.10), channel_id=1, source_target_pairs={{0,8},{1,17},{2,10},{3,19},{4,12},{5,21},{6,14},{7,23},{8,0},{9,25... | collective-permute-start | bytes 6291464 | tf_op jit(solution)/shard_map/ppermute | solution.py:64
  496.8 42.1 %collective-permute-start.51 = (bf16[2048,256]{1,0:T(8,128)(2,1)}, bf16[2048,256]{1,0:T(8,128)(2,1)}, u32[]{:S(2)}, u32[]{:S(2)}) collective-permute-start(bf16[2048,256]{1,0:T(8,128)(2,1)} %add_convert_fusion.25), channel_id=1, source_target_pairs={{0,2},{1,3},{2,4},{3,5},{4,6},{5,7},{6,0},{7,1},{8,10},{9,11},{10,... | collective-permute-start | bytes 3145736 | tf_op jit(solution)/shard_map/ppermute | solution.py:75
  539.5 32.4 %collective-permute-start.52 = (bf16[512,2048]{1,0:T(8,128)(2,1)S(1)}, bf16[512,2048]{1,0:T(8,128)(2,1)}, u32[]{:S(2)}, u32[]{:S(2)}) collective-permute-start(bf16[512,2048]{1,0:T(8,128)(2,1)S(1)} %add_convert_fusion.9), channel_id=1, source_target_pairs={{0,8},{1,17},{2,10},{3,19},{4,12},{5,21},{6,14},{7,23},{8,0},{9,25... | collective-permute-start | bytes 6291464 | tf_op jit(solution)/shard_map/ppermute | solution.py:64
  603.7 42.6 %collective-permute-start.62 = (bf16[512,2048]{1,0:T(8,128)(2,1)S(1)}, bf16[512,2048]{1,0:T(8,128)(2,1)}, u32[]{:S(2)}, u32[]{:S(2)}) collective-permute-start(bf16[512,2048]{1,0:T(8,128)(2,1)S(1)} %copy-done.37), channel_id=1, source_target_pairs={{0,1},{1,0},{2,3},{3,2},{4,5},{5,4},{6,7},{7,6},{8,9},{9,8},{10,11... | collective-permute-start | bytes 6291464 | tf_op jit(solution)/shard_map/ppermute | solution.py:67
  766.2 54.0 %collective-permute-start.55 = (bf16[512,2048]{1,0:T(8,128)(2,1)}, bf16[512,2048]{1,0:T(8,128)(2,1)}, u32[]{:S(2)}, u32[]{:S(2)}) collective-permute-start(bf16[512,2048]{1,0:T(8,128)(2,1)} %get-tuple-element.306), channel_id=1, source_target_pairs={{0,1},{1,0},{2,3},{3,2},{4,5},{5,4},{6,7},{7,6},{8,9},{9,8},{10,11... | collective-permute-start | bytes 6291464 | tf_op jit(solution)/shard_map/ppermute | solution.py:67
  791.2 44.9 %collective-permute-start.78 = (bf16[4,512,256]{2,1,0:T(8,128)(2,1)}, bf16[4,512,256]{2,1,0:T(8,128)(2,1)}, u32[]{:S(2)}, u32[]{:S(2)}) collective-permute-start(bf16[4,512,256]{2,1,0:T(8,128)(2,1)} %get-tuple-element.387), channel_id=1, source_target_pairs={{0,8},{1,17},{2,10},{3,19},{4,12},{5,21},{6,14},{7,23},{8,0},{9,25... | collective-permute-start | bytes 3145736 | tf_op jit(solution)/shard_map/ppermute | solution.py:64
  792.6 43.4 %collective-permute-start.77 = (bf16[4,512,256]{2,1,0:T(8,128)(2,1)}, bf16[4,512,256]{2,1,0:T(8,128)(2,1)}, u32[]{:S(2)}, u32[]{:S(2)}) collective-permute-start(bf16[4,512,256]{2,1,0:T(8,128)(2,1)} %get-tuple-element.385), channel_id=1, source_target_pairs={{0,8},{1,17},{2,10},{3,19},{4,12},{5,21},{6,14},{7,23},{8,0},{9,25... | collective-permute-start | bytes 3145736 | tf_op jit(solution)/shard_map/ppermute | solution.py:64
  (189 other events, 3304.5 us)

commit v4 on v3

--- a/solution.py
+++ b/solution.py
@@ -121,10 +121,11 @@
         return total
 
     def total(self, value):
-        for d in range(self.F.bit_length() - 1):
-            value = value + self.plane(value, 1 << d)
-        for d in range(self.T.bit_length() - 1):
-            value = value + self.mate(value, 1 << d)
+        moves = [[functools.partial(self.plane, mask=d) for d in range(1, self.F)]]
+        moves.append([functools.partial(self.mate, mask=d * self.S) for d in range(1, self.Z)])
+        moves.append([functools.partial(self.mate, mask=d) for d in range(1, self.S)])
+        for group in moves:
+            value = value + sum(move(value) for move in group)
         return value
 
 
@@ -158,6 +159,7 @@
         self.mv = mv
         self.blocks = [None] * mv.F
         self.got = []
+        self.merged = None
 
     def __call__(self, count, *deps):
         mv, blocks, got = self.mv, self.blocks, self.got
@@ -166,9 +168,15 @@
         for _ in range(count):
             source = blocks[(3, 1, 2)[len(got)]]
             if len(got) == 2:
-                source = (source.astype(f32) + got[0].astype(f32)).astype(low)
+                source = self.merge()
             got.append(mv.hop(after(source, *deps), 2 if len(got) == 2 else 1))
         return got[-count:]
+
+    def merge(self):
+        if self.merged is None and self.mv.F == 4:
+            both = self.blocks[2].astype(f32) + self.got[0].astype(f32)
+            self.merged = both.astype(low)
+        return self.merged
 
     def total(self):
         if self.mv.F != 4:
@@ -319,19 +327,32 @@
     )(partners, acts, *tables, *weights)
 
 
-def backward_kernel(block, count, partners, query, keys, values, mixed, logsum, acts, grads, *refs):
+def backward_kernel(
+    block, count, halves, partners, places, query, keys, values, mixed, logsum, acts_from, *refs
+):
+    parts, refs = refs[:halves], refs[halves:]
     cosine, sine = refs[:2]
     weights = refs[2 : 2 + count]
     out = refs[2 + count]
     terms = refs[3 + count : 3 + 2 * count]
-    grad, grad_keys, grad_values = refs[3 + 2 * count :]
+    grad, grad_keys, grad_values, acts, grads, acts_sem, sems = refs[3 + 2 * count :]
+    rows = parts[0].shape[0]
+    acts_copy = pltpu.make_async_copy(acts_from, acts, acts_sem.at[0])
+    copies = []
+    for i, part in enumerate(parts):
+        here = pl.ds(pl.multiple_of(places[i] * rows, rows), rows)
+        copies.append(pltpu.make_async_copy(part, grads.at[here, :], sems.at[i]))
+        copies[-1].start()
+    acts_copy.start()
+    for copy in copies:
+        copy.wait()
     length, width = query.shape
     heads = width // HD
     scale = HD**-0.5
     depth = weights[0].shape[1]
-    total = dot(columns_of(grads, partners, 0, depth), weights[0][3], NN)
+    total = dot(columns_of(grads, partners, 0, depth), weights[0][0], NN)
     for i in range(1, count):
-        total = total + dot(columns_of(grads, partners, i, depth), weights[i][3], NN)
+        total = total + dot(columns_of(grads, partners, i, depth), weights[i][0], NN)
     grad[...] = total.astype(low)
     grad_keys[...] = jnp.zeros_like(grad_keys)
     grad_values[...] = jnp.zeros_like(grad_values)
@@ -355,6 +376,7 @@
         ).astype(low)
     out[:, width : 2 * width] = turn(grad_keys[...], cosine[...], -sine[...]).astype(low)
     out[:, 2 * width :] = grad_values[...].astype(low)
+    acts_copy.wait()
     for i in range(count):
         inward = dot(columns_of(acts, partners, i, depth), out[...], TN).astype(low)
         for c in range(3):
@@ -362,28 +384,41 @@
         terms[i][3] = dot(columns_of(grads, partners, i, depth), mixed[...], TN).astype(low)
 
 
-def attend_backward(partners, saved, acts, grads, weights, tables):
+def attend_backward(partners, places, saved, acts, grads, weights, tables):
     length, width = saved[0].shape
     block = min(length, 256)
     heads = width // HD
     count = len(weights)
-    operands = [*saved, acts, grads, *tables, *weights]
+    depth = weights[0].shape[1]
+    near = [*saved, *tables]
+
+    def whole(value):
+        return pl.BlockSpec(value.shape, lambda i: (0, 0))
+
     found = pl.pallas_call(
-        functools.partial(backward_kernel, block, count),
+        functools.partial(backward_kernel, block, count, len(grads)),
+        grid=(1,),
         out_shape=[jax.ShapeDtypeStruct((length, 3 * width), low)]
         + [jax.ShapeDtypeStruct(weights[0].shape, low)] * count,
-        in_specs=[SMEM] + [VMEM] * len(operands),
-        out_specs=[VMEM] * (1 + count),
+        in_specs=[SMEM, SMEM]
+        + [whole(v) for v in saved]
+        + [ANY] * (1 + len(grads))
+        + [whole(v) for v in tables]
+        + [pl.BlockSpec((1, depth, width), lambda i: (3, 0, 0))] * count,
+        out_specs=[pl.BlockSpec((length, 3 * width), lambda i: (0, 0))]
+        + [pl.BlockSpec(weights[0].shape, lambda i: (0, 0, 0))] * count,
         scratch_shapes=[pltpu.VMEM((length, width), low)]
-        + [pltpu.VMEM((length, width), f32)] * 2,
+        + [pltpu.VMEM((length, width), f32)] * 2
+        + [pltpu.VMEM(acts.shape, low)] * 2
+        + [pltpu.SemaphoreType.DMA((1,)), pltpu.SemaphoreType.DMA((len(grads),))],
         compiler_params=params(),
         cost_estimate=cost(
             10 * length * acts.shape[1] * width + 10 * length * length * 256 * heads,
-            operands,
+            [*near, acts],
             heads * length * length // 2,
         ),
         name="attend_backward",
-    )(partners, *operands)
+    )(partners, places, *saved, acts, *grads, *tables, *weights)
     return found[0], found[1:]
 
 
@@ -428,29 +463,26 @@
 ANY = pl.BlockSpec(memory_space=pl.ANY)
 
 
-def held(value):
-    return pl.BlockSpec(
-        value.shape, lambda i: (0,) * value.ndim, pipeline_mode=pl.Buffered(1)
-    )
-
-
-def take_item(items, slots, sems):
+def take_item(items, slots, sems, then):
     step = pl.program_id(0)
 
     def copy(i):
         return pltpu.make_async_copy(items[i], slots.at[i % 2], sems.at[i % 2])
 
+    @pl.when(step == 0)
+    def _():
+        copy(0).start()
+
+    found = then()
     for i in range(len(items)):
 
         @pl.when(step == i)
         def _(i=i):
-            if i == 0:
-                copy(0).start()
             if i + 1 < len(items):
                 copy(i + 1).start()
             copy(i).wait()
 
-    return slots[lax.rem(step, 2)]
+    return slots[lax.rem(step, 2)], found
 
 
 def give_item(value, items, slots, sems):
@@ -478,13 +510,41 @@
                 copy(i).wait()
 
 
-def feed_kernel(count, width, *refs):
+def join(pieces, whole, sems):
+    width = pieces[0].shape[1]
+
+    def copy(i):
+        return pltpu.make_async_copy(
+            pieces[i], whole.at[:, i * width : (i + 1) * width], sems.at[i]
+        )
+
+    def when_first(what, first, last):
+        @pl.when(pl.program_id(0) == 0)
+        def _():
+            for i in range(first, last):
+                what(copy(i))
+
+    when_first(lambda c: c.start(), 0, len(pieces))
+    return lambda first, last: when_first(lambda c: c.wait(), -(-first // width), -(-last // width))
+
+
+def joined(pieces):
+    depth, width = pieces[0].shape
+    return [
+        pltpu.VMEM((depth, width * len(pieces)), low),
+        pltpu.SemaphoreType.DMA((len(pieces),)),
+    ]
+
+
+def feed_kernel(count, pieces, width, *refs):
     items = refs[:count]
-    expand, hidden, slope, passed, slots, sems = refs[count:]
-    value = take_item(items, slots, sems)
+    parts = refs[count : count + pieces]
+    hidden, slope, passed, slots, sems, expand, expand_sems = refs[count + pieces :]
+    value, ready = take_item(items, slots, sems, lambda: join(parts, expand, expand_sems))
     several = 2 if hidden.shape[1] % (2 * width) == 0 else 1
     step = 2 * width * several
     for n in range(hidden.shape[1] // (width * several)):
+        ready(n * step, (n + 1) * step)
         both = dot(value, expand[:, n * step : (n + 1) * step], NN)
         for m in range(several):
             gate = both[:, 2 * m * width : (2 * m + 1) * width]
@@ -500,27 +560,39 @@
 def feed_forward(items, expand, width):
     rows, depth = items[0].shape
     count = len(items)
-    hidden = expand.shape[1] // 2
+    hidden = expand[0].shape[1] * len(expand) // 2
     tile = pl.BlockSpec((rows, hidden), lambda i: (i, 0))
     return pl.pallas_call(
-        functools.partial(feed_kernel, count, width),
+        functools.partial(feed_kernel, count, len(expand), width),
         grid=(count,),
         out_shape=[jax.ShapeDtypeStruct((count * rows, hidden), low)] * 3,
-        in_specs=[ANY] * count + [held(expand)],
+        in_specs=[ANY] * (count + len(expand)),
         out_specs=[tile] * 3,
-        scratch_shapes=[pltpu.VMEM((2, rows, depth), low), pltpu.SemaphoreType.DMA((2,))],
+        scratch_shapes=[pltpu.VMEM((2, rows, depth), low), pltpu.SemaphoreType.DMA((2,))]
+        + joined(expand),
         compiler_params=params(40),
-        cost_estimate=cost(2 * count * rows * expand.size, [*items, expand]),
+        cost_estimate=cost(4 * count * rows * depth * hidden, [*items, *expand]),
         name="feed_forward",
-    )(*items, expand)
-
-
-def feed_back_kernel(count, width, *refs):
+    )(*items, *expand)
+
+
+def feed_back_kernel(count, shrinks, expands, width, *refs):
     items = refs[:count]
-    shrink, expand, slope, passed, grads = refs[count : count + 5]
-    outs = refs[count + 5 : 2 * count + 5]
-    slots, sems, out_slots, out_sems = refs[2 * count + 5 :]
-    value = take_item(items, slots, sems)
+    shrink_parts, refs = refs[count : count + shrinks], refs[count + shrinks :]
+    expand_parts, refs = refs[:expands], refs[expands:]
+    slope, passed, grads = refs[:3]
+    outs, refs = refs[3 : 3 + count], refs[3 + count :]
+    slots, sems, out_slots, out_sems, shrink, shrink_sems, expand, expand_sems = refs
+    value, (shrink_ready, expand_ready) = take_item(
+        items,
+        slots,
+        sems,
+        lambda: (
+            join(shrink_parts, shrink, shrink_sems),
+            join(expand_parts, expand, expand_sems),
+        ),
+    )
+    shrink_ready(0, shrink.shape[1])
     hidden = slope.shape[1]
     grad = dot(value, shrink[...], NN)
     for n in range(hidden // width):
@@ -532,6 +604,8 @@
             grad[:, here] * passed[:, here].astype(f32)
         ).astype(low)
 
+    expand_ready(0, expand.shape[1])
+
     def result(slot):
         depth = expand.shape[0]
         tile = min(depth, 1024)
@@ -545,36 +619,40 @@
 def feed_backward(items, shrink, expand, slope, passed, places, width):
     rows, depth = items[0].shape
     count = len(items)
-    hidden = shrink.shape[1]
+    hidden = shrink[0].shape[1] * len(shrink)
     first, stride = places[0], (places[-1] - places[0]) // max(count - 1, 1)
     assert list(places) == [first + stride * i for i in range(count)]
     tile = pl.BlockSpec((rows, hidden), lambda i: (first + stride * i, 0))
     found = pl.pallas_call(
-        functools.partial(feed_back_kernel, count, width),
+        functools.partial(feed_back_kernel, count, len(shrink), len(expand), width),
         grid=(count,),
         out_shape=[jax.ShapeDtypeStruct((count * rows, 2 * hidden), low)]
         + [jax.ShapeDtypeStruct((rows, depth), low)] * count,
-        in_specs=[ANY] * count + [held(shrink), held(expand), tile, tile],
+        in_specs=[ANY] * (count + len(shrink) + len(expand)) + [tile, tile],
         out_specs=[pl.BlockSpec((rows, 2 * hidden), lambda i: (i, 0))] + [ANY] * count,
         scratch_shapes=[
             pltpu.VMEM((2, rows, depth), low),
             pltpu.SemaphoreType.DMA((2,)),
             pltpu.VMEM((2, rows, depth), low),
             pltpu.SemaphoreType.DMA((2,)),
+            *joined(shrink),
+            *joined(expand),
         ],
         compiler_params=params(48),
         cost_estimate=cost(
-            2 * count * rows * (expand.size + shrink.size), [*items, shrink, expand, slope]
+            6 * count * rows * depth * hidden, [*items, *shrink, *expand, slope]
         ),
         name="feed_backward",
-    )(*items, shrink, expand, slope, passed)
+    )(*items, *shrink, *expand, slope, passed)
     return found[0], list(found[1:])
 
 
-def back_kernel(value, weight, *refs):
-    count = len(refs) - 2
+def back_kernel(pieces, value, *refs):
+    parts, refs = refs[:pieces], refs[pieces:]
+    count = len(refs) - 4
     outs = refs[:count]
-    slots, sems = refs[count:]
+    slots, sems, weight, weight_sems = refs[count:]
+    join(parts, weight, weight_sems)(0, weight.shape[1])
 
     def result(slot):
         depth = weight.shape[0]
@@ -588,18 +666,20 @@
 
 def times_back(value, weight, count):
     rows = value.shape[0] // count
-    depth, width = weight.shape
+    depth = weight[0].shape[0]
+    width = value.shape[1]
     return pl.pallas_call(
-        back_kernel,
+        functools.partial(back_kernel, len(weight)),
         grid=(count,),
         out_shape=[jax.ShapeDtypeStruct((rows, depth), low)] * count,
-        in_specs=[pl.BlockSpec((rows, width), lambda i: (i, 0)), held(weight)],
+        in_specs=[pl.BlockSpec((rows, width), lambda i: (i, 0))] + [ANY] * len(weight),
         out_specs=[ANY] * count,
-        scratch_shapes=[pltpu.VMEM((2, rows, depth), low), pltpu.SemaphoreType.DMA((2,))],
+        scratch_shapes=[pltpu.VMEM((2, rows, depth), low), pltpu.SemaphoreType.DMA((2,))]
+        + joined(weight),
         compiler_params=params(32),
-        cost_estimate=cost(2 * value.size * depth, [value, weight]),
+        cost_estimate=cost(2 * value.size * depth, [value, *weight]),
         name="times_back",
-    )(value, weight)
+    )(value, *weight)
 
 
 def weight_kernel(count, rights, *refs):
@@ -704,6 +784,7 @@
     source = layer_input.astype(f32)
     scale_one = norm_scale(source)
     normed_one = source * scale_one
+    expand_own = after(expand_own, attn_own)
     expand_own[1:] = [mv.plane(expand_own[d], d) for d in planes if d]
     deps = attn[0](2) + attn_ring() + expand_own[1:]
     acts = mv.place(mv.mates((normed_one * norm_gains[0]).astype(low)), 0, mv.s)
@@ -726,7 +807,8 @@
     deps = attn[1](1, *deps) + attn[2](2, *deps) + attn_ring(*deps) + attend(0)
     attn.append(Gather(mv, attn_ring.blocks[-1]))
     deps = attn[2](1, *deps) + attn[3](2, *deps) + gate_ring(*deps) + attend(1)
-    deps = attn[3](1, *deps) + gate_ring(*deps) + attend(2)
+    shrink_own[1:] = [mv.plane(after(shrink_own[d], *deps), d) for d in planes if d]
+    deps = attn[3](1, *deps) + gate_ring(*deps) + attend(2) + shrink_own[1:]
     attn_full = [g.blocks for g in attn]
     cot = Gather(mv, cotangent)
     moved = cot(1, *deps) + gate_ring(*deps)
@@ -734,8 +816,7 @@
     attended = spread(mv.partners, [s[3] for s in saved], attn_full, 3, 1)
     deps = moved + [attended]
     attended = after(attended, *moved)
-    shrink_own[1:] = [mv.plane(after(shrink_own[d], *deps), d) for d in planes if d]
-    moved = up_ring(*deps) + shrink_own[1:] + cot(1, *deps)
+    moved = up_ring(*deps) + cot(1, *deps)
 
     def part(value, d):
         return lax.dynamic_slice_in_dim(value, (mv.s ^ d) * rows, rows, 0)
@@ -772,12 +853,23 @@
             lax.dynamic_slice_in_dim(value, (mv.f ^ d) * row_block, row_block, 0) for d in planes
         ]
         moved = [mv.plane(after(cut[d], *deps), d) for d in planes if d]
-        return moved, mv.place(cut[:1] + moved, 1, mv.f).astype(f32)
-
-    expand_full = jnp.concatenate(
-        [g.blocks[k] for k in ring_order for g in (gate_ring, up_ring)], axis=1
-    )
-    early, late = list(planes)[:-1], [F - 1]
+        halves = range(0, value.shape[1], hidden_width)
+        return moved, [
+            mv.place([v[:, n : n + hidden_width] for v in cut[:1] + moved], 1, mv.f).astype(f32)
+            for n in halves
+        ]
+
+
+    def grouped(blocks):
+        group = max(1, 128 // hidden_width)
+        if group == 1:
+            return blocks
+        return [
+            jnp.concatenate(blocks[i : i + group], axis=1) for i in range(0, len(blocks), group)
+        ]
+
+    expand_full = grouped([g.blocks[k] for k in ring_order for g in (gate_ring, up_ring)])
+    early, others, late = list(planes)[: F // 2], list(planes)[F // 2 :], [F - 1]
     deps = [v for block in feed_blocks for v in block[1:]]
     moved = feed(1, *deps) + shrink_ring(*deps)
     kept_early = feed_forward(
@@ -788,14 +880,16 @@
     if F == 4:
         feed_blocks.append(mv.mates(after(feed.blocks[-1], *deps)))
     grad_blocks = [mv.mates(after(block, *deps)) for block in cot.blocks[:3]]
-    kept_late = feed_forward(items_of(feed_blocks, late), after(expand_full, *deps), hidden_width)
+    kept_late = feed_forward(
+        items_of(feed_blocks, others), after(expand_full, *deps), hidden_width
+    )
     deps = moved + [kept_late[0]] + [v for block in grad_blocks for v in block[1:]]
     hidden = (kept_early[0], kept_late[0])
     moved = shrink_ring(*deps)
     grad_blocks += [mv.mates(after(block, *deps)) for block in cot.blocks[3:]]
     pieces = max(Z // 2, 1)
     parts = Z // pieces
-    grad_items = items_of(grad_blocks, early + late)
+    grad_items = items_of(grad_blocks, planes)
     shrink_terms = []
     for i in range(parts):
         shrink_terms += weight_terms(grad_items, after(hidden, *deps), i, pieces, hidden_width)
@@ -803,13 +897,13 @@
     shrink_back = RingSum(mv)
     shrink_back.terms.update(zip(ring_order, shrink_terms))
     moved = shrink_back(*deps)
-    shrink_full = jnp.concatenate([shrink_ring.blocks[k] for k in ring_order], axis=1)
+    shrink_full = grouped([shrink_ring.blocks[k] for k in ring_order])
     terms_late, back_late = feed_backward(
         items_of(grad_blocks, late),
         after(shrink_full, *deps),
         expand_full,
         *kept_late[1:],
-        range(S),
+        range((len(others) - 1) * S, len(others) * S),
         hidden_width,
     )
     deps = moved + [terms_late]
@@ -818,48 +912,56 @@
     back_late = trade([after(v, *deps) for v in back_late])
     gated = after(shrink_full, *deps)
     fed = list(times_back(hidden[0], gated, len(early) * S))
-    fed += list(times_back(hidden[1], gated, S))
+    fed += list(times_back(hidden[1], gated, len(others) * S))
     feed_sums.blocks[-1] = chip_sum(back_late)
     deps = moved + fed + feed_sums.blocks[-1:]
     moved = feed_sums(1, *deps) + shrink_back(*deps)
     fed = [after(v, *deps) for v in fed]
     fed = [trade(fed[i * S : (i + 1) * S]) for i in planes]
-    middle, own = early[1:], early[:1]
+    middle = others[:-1]
+    terms_early, back_early = feed_backward(
+        items_of(grad_blocks, early),
+        after(shrink_full, *deps),
+        expand_full,
+        *kept_early[1:],
+        range(len(early) * S),
+        hidden_width,
+    )
+    fed_sums.blocks[-1] = chip_sum(fed[-1])
+    deps = moved + [terms_early] + fed_sums.blocks[-1:]
+    shrink_moved, (shrink_grad,) = columns(shrink_back.total().astype(low), *deps)
+    moved = fed_sums(1, *deps) + shrink_moved
+    back_early = [after(v, *deps) for v in back_early]
+    back_early = [trade(back_early[i * S : (i + 1) * S]) for i in early]
     terms_middle, back_middle = feed_backward(
         items_of(grad_blocks, middle),
         after(shrink_full, *deps),
         expand_full,
-        *kept_early[1:],
-        [i * S + p for i in middle for p in range(S)],
+        *kept_late[1:],
+        range(len(middle) * S),
         hidden_width,
     )
-    fed_sums.blocks[-1] = chip_sum(fed[-1])
-    deps = moved + [terms_middle] + fed_sums.blocks[-1:]
-    moved = fed_sums(1, *deps)
+    for i in early[1:]:
+        feed_sums.blocks[i] = chip_sum(back_early[i])
+    deps = moved + [terms_middle] + [feed_sums.blocks[i] for i in early[1:]]
+    moved = feed_sums(1, *deps)
     back_middle = [after(v, *deps) for v in back_middle]
     back_middle = [trade(back_middle[i * S : (i + 1) * S]) for i in range(len(middle))]
-    terms_own, back_own = feed_backward(
-        items_of(grad_blocks, own),
-        after(shrink_full, *deps),
-        expand_full,
-        *kept_early[1:],
-        range(S),
-        hidden_width,
-    )
-    for i, block in zip(middle, back_middle):
-        feed_sums.blocks[i] = chip_sum(block)
-    deps = moved + [terms_own] + [feed_sums.blocks[i] for i in middle]
-    moved = feed_sums(1, *deps)
-    back_own = trade([after(v, *deps) for v in back_own])
-    gate_up = (terms_own, terms_middle, terms_late)
-    feed_items = items_of(feed_blocks, own + middle + late)
+    gate_up = (terms_early, terms_middle, terms_late)
+    feed_items = items_of(feed_blocks, planes)
     expand_terms = list(
         weight_terms(feed_items, after(gate_up, *deps), 0, 2 * pieces, hidden_width)
     )
-    feed_sums.blocks[0] = chip_sum(back_own)
+    for i, block in zip(middle, back_middle):
+        feed_sums.blocks[i] = sum(value.astype(f32) for value in block)
+        if F != 4:
+            feed_sums.blocks[i] = feed_sums.blocks[i].astype(low)
+    feed_sums.blocks[0] = chip_sum([after(v, *deps) for v in back_early[0]])
     for i in planes[:-1]:
         fed_sums.blocks[i] = chip_sum([after(v, *deps) for v in fed[i]])
     deps = moved + expand_terms[-1:] + feed_sums.blocks[:1]
+    if F == 4:
+        deps += [feed_sums.merge(), fed_sums.merge()]
     gate_back, up_back = RingSum(mv), RingSum(mv)
 
     def known():
@@ -879,15 +981,18 @@
         after(feed_sums.total(), *deps), normed_two, scale_two, norm_gains[1]
     )
     grad_resid = cotangent.astype(f32) + resid_back
-    grad_attn = mv.place(mv.mates(grad_resid.astype(low)), 0, mv.s)
-    deps = moved + [grad_attn]
+    grad_low = grad_resid.astype(low)
+    deps = moved + [grad_low]
+    grad_attn = mv.mates(after(grad_low, *deps))
+    places = jnp.stack([mv.s ^ d for d in range(S)]).astype(jnp.int32)
+    deps = grad_attn[1:]
     order = (ring_order * 4)[:4] if Z < 4 else ring_order
     attn_sums = {}
     grad_proj = [None] * Z
 
     def attend_back(k):
         grad_proj[k], terms = attend_backward(
-            after(mv.partners, *deps), saved[k], acts, grad_attn, attn_full[k], tables
+            after(mv.partners, *deps), places, saved[k], acts, grad_attn, attn_full[k], tables
         )
         attn_sums[k] = Sum(mv)
         attn_sums[k].blocks[:] = terms
@@ -902,27 +1007,25 @@
     deps = moved + attend_back(order[2])
     moved = attn_sums[order[1]](2, *deps) + up_back(*deps)
     deps = moved + attend_back(order[3])
-    shrink_moved, shrink_grad = columns(shrink_back.total().astype(low), *deps)
-    moved = attn_sums[order[2]](2, *deps) + shrink_moved
+    attn_back = RingSum(mv)
+    attn_back.terms[order[0]] = attn_sums[order[0]].total()
+    moved = attn_sums[order[2]](2, *deps) + attn_back(*deps)
     grad_acts = spread(after(mv.partners, *deps), grad_proj, attn_full, 0, 3)
-    deps = moved + [grad_acts]
-    attn_back = RingSum(mv)
-    for k in order[:2]:
-        attn_back.terms[k] = attn_sums[k].total()
+    expand_sum = jnp.concatenate([gate_back.total(), up_back.total()], axis=1).astype(low)
+    deps = moved + [grad_acts, expand_sum]
+    attn_back.terms[order[1]] = attn_sums[order[1]].total()
     moved = attn_sums[order[2]](1, *deps) + attn_sums[order[3]](1, *deps) + attn_back(*deps)
     grad_acts = mv.mates_sum([part(grad_acts, d) for d in range(S)])
     input_back, gain_one = norm_back(grad_acts, normed_one, scale_one, norm_gains[0])
     input_grad = (grad_resid + input_back).astype(low)
-    deps = moved + [input_grad]
+    deps = moved
     attn_back.terms[order[2]] = attn_sums[order[2]].total()
     moved = attn_sums[order[3]](2, *deps) + attn_back(*deps)
-    deps = moved
+    deps = moved + [input_grad]
     attn_back.terms[order[3]] = attn_sums[order[3]].total()
-    gate_grad = columns(gate_back.total().astype(low), *deps)[1]
-    up_grad = columns(up_back.total().astype(low), *deps)[1]
-    attn_back(*deps)
+    expand_both = columns(expand_sum, *deps)[1]
     attn_grad = attn_back.total()
-    expand_grad = jnp.stack([gate_grad, up_grad])
+    expand_grad = jnp.stack(expand_both)
     inward_grad, outward_grad = attn_grad[:3], attn_grad[3]
 
     owned_squares = (

time: 981 us -> 957 us (0.976)
  waiting for transfers between devices: 299 us -> 276 us
    ppermute x17 -> x15, waiting for transfers between devices: 97 us -> 64.4 us  [plane(): return lax.ppermute(value, 'fsdp', [(i, i ^ mask) for i in range(self.F)])]
    unnamed x233 -> x230, local copies, waits for them, and re-layouts: 22.2 us -> 29.2 us
    ppermute x17 -> x15, starting transfers between devices: 22 us -> 20.4 us  [plane(): return lax.ppermute(value, 'fsdp', [(i, i ^ mask) for i in range(self.F)])]
  transfers between devices with their start and end apart: 100 -> 99, of which waited for: 37 -> 41; matrix products, arithmetic and copies ran while one was open for 12% -> 11% of each run, Pallas kernels for 43% -> 43%
where the time goes in v4:
time: 957 us; the launch traced here: 952 us
  Pallas kernels  408 us (43%)
  waiting for transfers between devices  276 us (29%)
  other arithmetic  112 us (12%)
  starting transfers between devices  90.2 us (9%)
  local copies, waits for them, and re-layouts  59.7 us (6%)
    ppermute x24, waiting for transfers between devices, ring(): return lax.ppermute(value, 'tp', step)  142 us
    pallas_call x4, Pallas kernels, attend_backward(): pl.pallas_call(functools.partial(backward_kernel, block, count, len(grads...  97.8 us
    pallas_call x3, Pallas kernels, feed_backward(): pl.pallas_call(functools.partial(feed_back_kernel, count, len(shrink), le...  75.8 us
    pallas_call x4, Pallas kernels, weight_terms(): pl.pallas_call(functools.partial(weight_kernel, len(lefts), len(rights)),...  72.1 us
    ppermute x15, waiting for transfers between devices, plane(): return lax.ppermute(value, 'fsdp', [(i, i ^ mask) for i in range(self.F)])  64.4 us
    pallas_call x4, Pallas kernels, attend_forward(): pl.pallas_call(functools.partial(forward_kernel, block, len(weights)), ou...  62.2 us
    ppermute x36, waiting for transfers between devices, hop(): return lax.ppermute(value, ('fsdp', 'tp'), pairs)  50.1 us
    pallas_call x2, Pallas kernels, feed_forward(): pl.pallas_call(functools.partial(feed_kernel, count, len(expand), width),...  46.4 us
  transfers between devices with their start and end apart: 99, of which 41 were waited for; matrix products, arithmetic and copies ran while one was open for 11% of the time, Pallas kernels for 43%

profile of v4, /device:TPU:0, one launch (start us, length us, event | category | flops | bytes accessed | tf_op | source)
XLA Modules:
  0.0 952.5 jit_solution(12621131363856780247)
XLA Ops:
  37.1 25.9 %collective-permute-done.4 = bf16[2,512,256]{2,1,0:T(8,128)(2,1)S(1)} collective-permute-done((bf16[2,512,256]{2,1,0:T(8,128)(2,1)}, bf16[2,512,256]{2,1,0:T(8,128)(2,1)S(1)}, u32[]{:S(2)}, u32[]{:S(2)}) %collective-permute-start.4) | collective-permute-done | bytes 524320 | tf_op jit(solution)/shard_map/ppermute | solution.py:56
  74.0 18.4 %collective-permute-done.10.refs_0_.refs_12_.refs_4_ = bf16[4,512,256]{2,1,0:T(8,128)(2,1)} collective-permute-done((bf16[4,512,256]{2,1,0:T(8,128)(2,1)}, bf16[4,512,256]{2,1,0:T(8,128)(2,1)}, u32[]{:S(2)}, u32[]{:S(2)}) %collective-permute-start.10) | collective-permute-done | bytes 1048608 | tf_op jit(solution)/shard_map/ppermute | solution.py:75
  114.0 15.5 %attend_forward.4 = (bf16[1024,256]{1,0:T(8,128)(2,1)}, bf16[1024,256]{1,0:T(8,128)(2,1)}, bf16[1024,256]{1,0:T(8,128)(2,1)}, bf16[1024,256]{1,0:T(8,128)(2,1)}, f32[1024,128]{1,0:T(8,128)}) custom-call(s32[4]{0:T(128)} %pad_add_fusion.partners, bf16[1024,2048]{1,0:T(8,128)(2,1)} %constant_dynamic-update-slice_fusion.10.acts.acts_from, ...), custom_call_target="tpu_custom_call" | custom-call | flops 1503238528 | bytes 2097152 | tf_op jit(solution)/shard_map/attend_forward/pallas_call | solution.py:315
  145.1 15.5 %attend_forward.5 = (bf16[1024,256]{1,0:T(8,128)(2,1)}, bf16[1024,256]{1,0:T(8,128)(2,1)}, bf16[1024,256]{1,0:T(8,128)(2,1)}, bf16[1024,256]{1,0:T(8,128)(2,1)}, f32[1024,128]{1,0:T(8,128)}) custom-call(s32[4]{0:T(128)} %pad_add_fusion.partners, bf16[1024,2048]{1,0:T(8,128)(2,1)} %constant_dynamic-update-slice_fusion.10.acts.acts_from, ...), custom_call_target="tpu_custom_call" | custom-call | flops 1503238528 | bytes 2097152 | tf_op jit(solution)/shard_map/attend_forward/pallas_call | solution.py:315
  185.8 15.6 %attend_forward.6 = (bf16[1024,256]{1,0:T(8,128)(2,1)}, bf16[1024,256]{1,0:T(8,128)(2,1)}, bf16[1024,256]{1,0:T(8,128)(2,1)}, bf16[1024,256]{1,0:T(8,128)(2,1)}, f32[1024,128]{1,0:T(8,128)}) custom-call(s32[4]{0:T(128)} %pad_add_fusion.partners, bf16[1024,2048]{1,0:T(8,128)(2,1)} %constant_dynamic-update-slice_fusion.10.acts.acts_from, ...), custom_call_target="tpu_custom_call" | custom-call | flops 1503238528 | bytes 2097152 | tf_op jit(solution)/shard_map/attend_forward/pallas_call | solution.py:315
  208.3 15.6 %attend_forward.7 = (bf16[1024,256]{1,0:T(8,128)(2,1)}, bf16[1024,256]{1,0:T(8,128)(2,1)}, bf16[1024,256]{1,0:T(8,128)(2,1)}, bf16[1024,256]{1,0:T(8,128)(2,1)}, f32[1024,128]{1,0:T(8,128)}) custom-call(s32[4]{0:T(128)} %pad_add_fusion.partners, bf16[1024,2048]{1,0:T(8,128)(2,1)} %constant_dynamic-update-slice_fusion.10.acts.acts_from, ...), custom_call_target="tpu_custom_call" | custom-call | flops 1503238528 | bytes 2097152 | tf_op jit(solution)/shard_map/attend_forward/pallas_call | solution.py:315
  244.1 19.3 %collective-permute-done.27.refs_5_.refs_7_.refs_9_ = bf16[2048,256]{1,0:T(8,128)(2,1)S(1)} collective-permute-done((bf16[2048,256]{1,0:T(8,128)(2,1)S(1)}, bf16[2048,256]{1,0:T(8,128)(2,1)S(1)}, u32[]{:S(2)}, u32[]{:S(2)}) %collective-permute-start.27) | collective-permute-done | bytes 1048608 | tf_op jit(solution)/shard_map/ppermute | solution.py:75
  264.6 26.5 %collective-permute-done.31.refs_7_.refs_9_.refs_11_ = bf16[2048,256]{1,0:T(8,128)(2,1)S(1)} collective-permute-done((bf16[2048,256]{1,0:T(8,128)(2,1)S(1)}, bf16[2048,256]{1,0:T(8,128)(2,1)S(1)}, u32[]{:S(2)}, u32[]{:S(2)}) %collective-permute-start.31) | collective-permute-done | bytes 1048608 | tf_op jit(solution)/shard_map/ppermute | solution.py:75
  292.8 26.9 %collective-permute-done.33.refs_9_.refs_11_.refs_13_ = bf16[2048,256]{1,0:T(8,128)(2,1)S(1)} collective-permute-done((bf16[2048,256]{1,0:T(8,128)(2,1)S(1)}, bf16[2048,256]{1,0:T(8,128)(2,1)S(1)}, u32[]{:S(2)}, u32[]{:S(2)}) %collective-permute-start.33) | collective-permute-done | bytes 1048608 | tf_op jit(solution)/shard_map/ppermute | solution.py:75
  326.6 23.2 %feed_forward.2 = (bf16[2048,1024]{1,0:T(8,128)(2,1)}, bf16[2048,1024]{1,0:T(8,128)(2,1)}, bf16[2048,1024]{1,0:T(8,128)(2,1)}) custom-call(bf16[512,2048]{1,0:T(8,128)(2,1)S(1)} %multiply_convert_fusion.refs_0_, bf16[512,2048]{1,0:T(8,128)(2,1)S(1)} %collective-permute-done.29.refs_1_, bf16[512,2048]{1,0:T(8,128)(2,1)} %copy-done.25, ...), custom_call_target="tpu_custom_call" | custom-call | flops 3435973888 | bytes 3355443 | tf_op jit(solution)/shard_map/feed_forward/pallas_call | solution.py:565
  361.7 23.1 %feed_forward.3 = (bf16[2048,1024]{1,0:T(8,128)(2,1)}, bf16[2048,1024]{1,0:T(8,128)(2,1)}, bf16[2048,1024]{1,0:T(8,128)(2,1)}) custom-call(bf16[512,2048]{1,0:T(8,128)(2,1)S(1)} %copy-done.30, bf16[512,2048]{1,0:T(8,128)(2,1)S(1)} %copy-done.32, bf16[512,2048]{1,0:T(8,128)(2,1)} %collective-permute-done.37.refs_2_.refs_6_, bf16[512,2048]{1,0:T(8,128)(2,1)} %copy-done.59, ...), custom_call_target="tpu_custom_call" | custom-call | flops 3435973888 | bytes 3355443 | tf_op jit(solution)/shard_map/feed_forward/pallas_call | solution.py:565
  409.6 13.0 %weight_terms.4 = (bf16[2048,256]{1,0:T(8,128)(2,1)S(1)}, bf16[2048,256]{1,0:T(8,128)(2,1)S(1)}) custom-call(bf16[512,2048]{1,0:T(8,128)(2,1)S(1)} %copy-done, bf16[512,2048]{1,0:T(8,128)(2,1)S(1)} %copy-done.22, bf16[512,2048]{1,0:T(8,128)(2,1)} %collective-permute-done.24.refs_2_, bf16[512,2048]{1,0:T(8,128)(2,1)} %collective-permute-done.42.refs_3_, ...), custom_call_target="tpu_custom_call" | custom-call | flops 1717986944 | bytes 5033164 | tf_op jit(solution)/shard_map/weight_terms/pallas_call | solution.py:707
  423.9 20.4 %feed_backward.3 = (bf16[1024,2048]{1,0:T(8,128)(2,1)}, bf16[512,2048]{1,0:T(8,128)(2,1)}, bf16[512,2048]{1,0:T(8,128)(2,1)}) custom-call(bf16[512,2048]{1,0:T(8,128)(2,1)} %copy-done.57, bf16[512,2048]{1,0:T(8,128)(2,1)} %copy-done.58, bf16[2048,256]{1,0:T(8,128)(2,1)S(1)} %copy-done.17, bf16[2048,256]{1,0:T(8,128)(2,1)S(1)} %copy-done.19, ...), custom_call_target="tpu_custom_call" | custom-call | flops 2576980480 | bytes 4194304 | tf_op jit(solution)/shard_map/feed_backward/pallas_call | solution.py:626
  480.3 34.6 %feed_backward.4 = (bf16[2048,2048]{1,0:T(8,128)(2,1)}, bf16[512,2048]{1,0:T(8,128)(2,1)}, bf16[512,2048]{1,0:T(8,128)(2,1)}, bf16[512,2048]{1,0:T(8,128)(2,1)}, bf16[512,2048]{1,0:T(8,128)(2,1)}) custom-call(bf16[512,2048]{1,0:T(8,128)(2,1)} %refs_0_.2, bf16[512,2048]{1,0:T(8,128)(2,1)} %copy-done.21, bf16[512,2048]{1,0:T(8,128)(2,1)} %collective-permute-done.24.refs_2_, ...), custom_call_target="tpu_custom_call" | custom-call | flops 5153960960 | bytes 5033164 | tf_op jit(solution)/shard_map/feed_backward/pallas_call | solution.py:626
  524.9 20.7 %feed_backward.5 = (bf16[1024,2048]{1,0:T(8,128)(2,1)}, bf16[512,2048]{1,0:T(8,128)(2,1)}, bf16[512,2048]{1,0:T(8,128)(2,1)}) custom-call(bf16[512,2048]{1,0:T(8,128)(2,1)} %collective-permute-done.28.refs_4_.refs_0_, bf16[512,2048]{1,0:T(8,128)(2,1)} %copy-done.56, bf16[2048,256]{1,0:T(8,128)(2,1)S(1)} %copy-done.17, bf16[2048,256]{1,0:T(8,128)(2,1)S(1)} %copy-done.20, ...), custom_call_target="tpu_custom_call" | custom-call | flops 2576980480 | bytes 4194304 | tf_op jit(solution)/shard_map/feed_backward/pallas_call | solution.py:626
  568.9 23.2 %weight_terms.6 = (bf16[2048,256]{1,0:T(8,128)(2,1)S(1)}, bf16[2048,256]{1,0:T(8,128)(2,1)S(1)}, bf16[2048,256]{1,0:T(8,128)(2,1)S(1)}, bf16[2048,256]{1,0:T(8,128)(2,1)S(1)}) custom-call(bf16[512,2048]{1,0:T(8,128)(2,1)S(1)} %copy-done.10, bf16[512,2048]{1,0:T(8,128)(2,1)S(1)} %copy-done.24, bf16[512,2048]{1,0:T(8,128)(2,1)S(1)} %copy-done.26, ...), custom_call_target="tpu_custom_call" | custom-call | flops 3435973888 | bytes 6710886 | tf_op jit(solution)/shard_map/weight_terms/pallas_call | solution.py:707
  602.7 22.8 %weight_terms.7 = (bf16[2048,256]{1,0:T(8,128)(2,1)S(1)}, bf16[2048,256]{1,0:T(8,128)(2,1)S(1)}, bf16[2048,256]{1,0:T(8,128)(2,1)S(1)}, bf16[2048,256]{1,0:T(8,128)(2,1)S(1)}) custom-call(bf16[512,2048]{1,0:T(8,128)(2,1)S(1)} %copy-done.10, bf16[512,2048]{1,0:T(8,128)(2,1)S(1)} %copy-done.24, bf16[512,2048]{1,0:T(8,128)(2,1)S(1)} %copy-done.26, ...), custom_call_target="tpu_custom_call" | custom-call | flops 3435973888 | bytes 6710886 | tf_op jit(solution)/shard_map/weight_terms/pallas_call | solution.py:707
  638.1 15.0 %collective-permute-done.66 = bf16[2048,256]{1,0:T(8,128)(2,1)S(1)} collective-permute-done((bf16[2048,256]{1,0:T(8,128)(2,1)S(1)}, bf16[2048,256]{1,0:T(8,128)(2,1)S(1)}, u32[]{:S(2)}, u32[]{:S(2)}) %collective-permute-start.66) | collective-permute-done | bytes 1048608 | tf_op jit(solution)/shard_map/ppermute | solution.py:75
  665.3 24.6 %attend_backward.4 = (bf16[1024,768]{1,0:T(8,128)(2,1)}, bf16[4,512,256]{2,1,0:T(8,128)(2,1)}, bf16[4,512,256]{2,1,0:T(8,128)(2,1)}, bf16[4,512,256]{2,1,0:T(8,128)(2,1)}, bf16[4,512,256]{2,1,0:T(8,128)(2,1)}) custom-call(s32[4]{0:T(128)} %pad_add_fusion.partners, s32[2]{0:T(128)} %pad_add_fusion.1.places, bf16[1024,256]{1,0:T(8,128)(2,1)} %get-tuple-element.406.query, ...), custom_call_target="tpu_custom_call" | custom-call | flops 3221225472 | bytes 1782579 | tf_op jit(solution)/shard_map/attend_backward/pallas_call | solution.py:398
  695.5 24.3 %attend_backward.5 = (bf16[1024,768]{1,0:T(8,128)(2,1)}, bf16[4,512,256]{2,1,0:T(8,128)(2,1)}, bf16[4,512,256]{2,1,0:T(8,128)(2,1)}, bf16[4,512,256]{2,1,0:T(8,128)(2,1)}, bf16[4,512,256]{2,1,0:T(8,128)(2,1)}) custom-call(s32[4]{0:T(128)} %pad_add_fusion.partners, s32[2]{0:T(128)} %pad_add_fusion.1.places, bf16[1024,256]{1,0:T(8,128)(2,1)} %get-tuple-element.412.query, ...), custom_call_target="tpu_custom_call" | custom-call | flops 3221225472 | bytes 1782579 | tf_op jit(solution)/shard_map/attend_backward/pallas_call | solution.py:398
  726.9 24.6 %attend_backward.6 = (bf16[1024,768]{1,0:T(8,128)(2,1)}, bf16[4,512,256]{2,1,0:T(8,128)(2,1)}, bf16[4,512,256]{2,1,0:T(8,128)(2,1)}, bf16[4,512,256]{2,1,0:T(8,128)(2,1)}, bf16[4,512,256]{2,1,0:T(8,128)(2,1)}) custom-call(s32[4]{0:T(128)} %pad_add_fusion.partners, s32[2]{0:T(128)} %pad_add_fusion.1.places, bf16[1024,256]{1,0:T(8,128)(2,1)} %get-tuple-element.430.query, ...), custom_call_target="tpu_custom_call" | custom-call | flops 3221225472 | bytes 1782579 | tf_op jit(solution)/shard_map/attend_backward/pallas_call | solution.py:398
  759.1 24.4 %attend_backward.7 = (bf16[1024,768]{1,0:T(8,128)(2,1)}, bf16[4,512,256]{2,1,0:T(8,128)(2,1)}, bf16[4,512,256]{2,1,0:T(8,128)(2,1)}, bf16[4,512,256]{2,1,0:T(8,128)(2,1)}, bf16[4,512,256]{2,1,0:T(8,128)(2,1)}) custom-call(s32[4]{0:T(128)} %pad_add_fusion.partners, s32[2]{0:T(128)} %pad_add_fusion.1.places, bf16[1024,256]{1,0:T(8,128)(2,1)} %get-tuple-element.441.query, ...), custom_call_target="tpu_custom_call" | custom-call | flops 3221225472 | bytes 1782579 | tf_op jit(solution)/shard_map/attend_backward/pallas_call | solution.py:398
  791.2 21.6 %spread.3 = bf16[1024,2048]{1,0:T(8,128)(2,1)} custom-call(s32[4]{0:T(128)} %pad_add_fusion.partners, bf16[1024,768]{1,0:T(8,128)(2,1)} %get-tuple-element.445.refs_0_, bf16[1024,768]{1,0:T(8,128)(2,1)} %get-tuple-element.410.refs_1_, bf16[1024,768]{1,0:T(8,128)(2,1)} %get-tuple-element.423.refs_2_, bf16[1024,768]{1,0:T(8,128)(2,1)} %get-tuple-element.434.refs_3_, ...), custom_call_target="tpu_custom_call" | custom-call | flops 2576980480 | bytes 4613734 | tf_op jit(solution)/shard_map/spread/pallas_call | solution.py:447
  826.9 13.9 %collective-permute-done.84 = bf16[4,512,256]{2,1,0:T(8,128)(2,1)S(1)} collective-permute-done((bf16[4,512,256]{2,1,0:T(8,128)(2,1)S(1)}, bf16[4,512,256]{2,1,0:T(8,128)(2,1)S(1)}, u32[]{:S(2)}, u32[]{:S(2)}) %collective-permute-start.84) | collective-permute-done | bytes 1048608 | tf_op jit(solution)/shard_map/ppermute | solution.py:64
  (519 shorter events, 437.2 us)
Async XLA Ops:
  16.8 47.1 %collective-permute-start = (bf16[4,512,256]{2,1,0:T(8,128)(2,1)S(1)}, bf16[4,512,256]{2,1,0:T(8,128)(2,1)S(1)}, u32[]{:S(2)}, u32[]{:S(2)}) collective-permute-start(bf16[4,512,256]{2,1,0:T(8,128)(2,1)S(1)} %pad_maximum_fusion.1.refs_0_.refs_4_), channel_id=1, source_target_pairs={{0,8},{1,17},{2,10},{3,19},{4,12},{5,21},{6,14},{7,23},{8,0},{9,25... | collective-permute-start | bytes 3145736 | tf_op jit(solution)/shard_map/ppermute | solution.py:64
  16.8 47.1 %collective-permute-start.1 = (bf16[4,512,256]{2,1,0:T(8,128)(2,1)S(1)}, bf16[4,512,256]{2,1,0:T(8,128)(2,1)S(1)}, u32[]{:S(2)}, u32[]{:S(2)}) collective-permute-start(bf16[4,512,256]{2,1,0:T(8,128)(2,1)S(1)} %pad_maximum_fusion.1.refs_0_.refs_4_), channel_id=1, source_target_pairs={{0,16},{1,9},{2,18},{3,11},{4,20},{5,13},{6,22},{7,15},{8,24},{9,1... | collective-permute-start | bytes 3145736 | tf_op jit(solution)/shard_map/ppermute | solution.py:64
  18.8 45.1 %collective-permute-start.2 = (bf16[4,512,256]{2,1,0:T(8,128)(2,1)S(1)}, bf16[4,512,256]{2,1,0:T(8,128)(2,1)}, u32[]{:S(2)}, u32[]{:S(2)}) collective-permute-start(bf16[4,512,256]{2,1,0:T(8,128)(2,1)S(1)} %pad_maximum_fusion.1.refs_0_.refs_4_), channel_id=1, source_target_pairs={{0,2},{1,3},{2,4},{3,5},{4,6},{5,7},{6,0},{7,1},{8,10},{9,11},{10,... | collective-permute-start | bytes 3145736 | tf_op jit(solution)/shard_map/ppermute | solution.py:75
  29.9 33.2 %collective-permute-start.4 = (bf16[2,512,256]{2,1,0:T(8,128)(2,1)}, bf16[2,512,256]{2,1,0:T(8,128)(2,1)S(1)}, u32[]{:S(2)}, u32[]{:S(2)}) collective-permute-start(bf16[2,512,256]{2,1,0:T(8,128)(2,1)} %get-tuple-element.247), channel_id=1, source_target_pairs={{0,16},{8,24},{16,0},{24,8},{1,17},{9,25},{17,1},{25,9},{2,18},{10... | collective-permute-start | bytes 1572872 | tf_op jit(solution)/shard_map/ppermute | solution.py:56
  69.8 33.2 %collective-permute-start.7 = (bf16[4,512,256]{2,1,0:T(8,128)(2,1)S(1)}, bf16[4,512,256]{2,1,0:T(8,128)(2,1)}, u32[]{:S(2)}, u32[]{:S(2)}) collective-permute-start(bf16[4,512,256]{2,1,0:T(8,128)(2,1)S(1)} %collective-permute-done.refs_1_.refs_5_), channel_id=1, source_target_pairs={{0,16},{1,9},{2,18},{3,11},{4,20},{5,13},{6,22},{7,15},{8,24},{9,1... | collective-permute-start | bytes 3145736 | tf_op jit(solution)/shard_map/ppermute | solution.py:64
  106.8 33.0 %collective-permute-start.11 = (bf16[4,512,256]{2,1,0:T(8,128)(2,1)}, bf16[4,512,256]{2,1,0:T(8,128)(2,1)}, u32[]{:S(2)}, u32[]{:S(2)}) collective-permute-start(bf16[4,512,256]{2,1,0:T(8,128)(2,1)} %collective-permute-done.8.refs_1_.refs_9_.refs_5_), channel_id=1, source_target_pairs={{0,16},{1,9},{2,18},{3,11},{4,20},{5,13},{6,22},{7,15},{8,24},{9,1... | collective-permute-start | bytes 3145736 | tf_op jit(solution)/shard_map/ppermute | solution.py:64
  144.5 32.5 %collective-permute-start.15 = (bf16[4,512,256]{2,1,0:T(8,128)(2,1)S(1)}, bf16[4,512,256]{2,1,0:T(8,128)(2,1)S(1)}, u32[]{:S(2)}, u32[]{:S(2)}) collective-permute-start(bf16[4,512,256]{2,1,0:T(8,128)(2,1)S(1)} %collective-permute-done.12.refs_1_.refs_13_.refs_5_), channel_id=1, source_target_pairs={{0,16},{1,9},{2,18},{3,11},{4,20},{5,13},{6,22},{7,15},{8,24},{9,1... | collective-permute-start | bytes 3145736 | tf_op jit(solution)/shard_map/ppermute | solution.py:64
  352.8 32.7 %collective-permute-start.43 = (bf16[512,2048]{1,0:T(8,128)(2,1)}, bf16[512,2048]{1,0:T(8,128)(2,1)S(1)}, u32[]{:S(2)}, u32[]{:S(2)}) collective-permute-start(bf16[512,2048]{1,0:T(8,128)(2,1)} %collective-permute-done.28.refs_4_.refs_0_), channel_id=1, source_target_pairs={{0,1},{1,0},{2,3},{3,2},{4,5},{5,4},{6,7},{7,6},{8,9},{9,8},{10,11... | collective-permute-start | bytes 6291464 | tf_op jit(solution)/shard_map/ppermute | solution.py:67
  353.3 32.2 %collective-permute-start.41 = (bf16[512,2048]{1,0:T(8,128)(2,1)S(1)}, bf16[512,2048]{1,0:T(8,128)(2,1)S(1)}, u32[]{:S(2)}, u32[]{:S(2)}) collective-permute-start(bf16[512,2048]{1,0:T(8,128)(2,1)S(1)} %copy-done), channel_id=1, source_target_pairs={{0,1},{1,0},{2,3},{3,2},{4,5},{5,4},{6,7},{7,6},{8,9},{9,8},{10,11... | collective-permute-start | bytes 6291464 | tf_op jit(solution)/shard_map/ppermute | solution.py:67
  353.4 33.5 %collective-permute-start.39 = (bf16[512,2048]{1,0:T(8,128)(2,1)}, bf16[512,2048]{1,0:T(8,128)(2,1)S(1)}, u32[]{:S(2)}, u32[]{:S(2)}) collective-permute-start(bf16[512,2048]{1,0:T(8,128)(2,1)} %collective-permute-done.24.refs_2_), channel_id=1, source_target_pairs={{0,16},{1,9},{2,18},{3,11},{4,20},{5,13},{6,22},{7,15},{8,24},{9,1... | collective-permute-start | bytes 6291464 | tf_op jit(solution)/shard_map/ppermute | solution.py:64
  387.5 35.1 %collective-permute-start.44 = (bf16[2048,256]{1,0:T(8,128)(2,1)S(1)}, bf16[2048,256]{1,0:T(8,128)(2,1)S(1)}, u32[]{:S(2)}, u32[]{:S(2)}) collective-permute-start(bf16[2048,256]{1,0:T(8,128)(2,1)S(1)} %collective-permute-done.38.refs_3_.refs_1_.refs_5_), channel_id=1, source_target_pairs={{0,2},{1,3},{2,4},{3,5},{4,6},{5,7},{6,0},{7,1},{8,10},{9,11},{10,... | collective-permute-start | bytes 3145736 | tf_op jit(solution)/shard_map/ppermute | solution.py:75
  477.5 37.4 %collective-permute-start.49 = (bf16[512,2048]{1,0:T(8,128)(2,1)S(1)}, bf16[512,2048]{1,0:T(8,128)(2,1)}, u32[]{:S(2)}, u32[]{:S(2)}) collective-permute-start(bf16[512,2048]{1,0:T(8,128)(2,1)S(1)} %get-tuple-element.341), channel_id=1, source_target_pairs={{0,1},{1,0},{2,3},{3,2},{4,5},{5,4},{6,7},{7,6},{8,9},{9,8},{10,11... | collective-permute-start | bytes 6291464 | tf_op jit(solution)/shard_map/ppermute | solution.py:67
  477.5 41.4 %collective-permute-start.50 = (bf16[512,2048]{1,0:T(8,128)(2,1)S(1)}, bf16[512,2048]{1,0:T(8,128)(2,1)}, u32[]{:S(2)}, u32[]{:S(2)}) collective-permute-start(bf16[512,2048]{1,0:T(8,128)(2,1)S(1)} %add_convert_fusion.9), channel_id=1, source_target_pairs={{0,8},{1,17},{2,10},{3,19},{4,12},{5,21},{6,14},{7,23},{8,0},{9,25... | collective-permute-start | bytes 6291464 | tf_op jit(solution)/shard_map/ppermute | solution.py:64
  480.1 38.8 %collective-permute-start.51 = (bf16[2048,256]{1,0:T(8,128)(2,1)}, bf16[2048,256]{1,0:T(8,128)(2,1)}, u32[]{:S(2)}, u32[]{:S(2)}) collective-permute-start(bf16[2048,256]{1,0:T(8,128)(2,1)} %add_convert_fusion.24), channel_id=1, source_target_pairs={{0,2},{1,3},{2,4},{3,5},{4,6},{5,7},{6,0},{7,1},{8,10},{9,11},{10,... | collective-permute-start | bytes 3145736 | tf_op jit(solution)/shard_map/ppermute | solution.py:75
  518.9 35.9 %collective-permute-start.56 = (bf16[512,2048]{1,0:T(8,128)(2,1)}, bf16[512,2048]{1,0:T(8,128)(2,1)}, u32[]{:S(2)}, u32[]{:S(2)}) collective-permute-start(bf16[512,2048]{1,0:T(8,128)(2,1)} %get-tuple-element.363), channel_id=1, source_target_pairs={{0,1},{1,0},{2,3},{3,2},{4,5},{5,4},{6,7},{7,6},{8,9},{9,8},{10,11... | collective-permute-start | bytes 6291464 | tf_op jit(solution)/shard_map/ppermute | solution.py:67
  519.3 41.9 %collective-permute-start.52 = (bf16[512,2048]{1,0:T(8,128)(2,1)}, bf16[512,2048]{1,0:T(8,128)(2,1)S(1)}, u32[]{:S(2)}, u32[]{:S(2)}) collective-permute-start(bf16[512,2048]{1,0:T(8,128)(2,1)} %add_convert_fusion.8), channel_id=1, source_target_pairs={{0,8},{1,17},{2,10},{3,19},{4,12},{5,21},{6,14},{7,23},{8,0},{9,25... | collective-permute-start | bytes 6291464 | tf_op jit(solution)/shard_map/ppermute | solution.py:64
  520.3 42.0 %collective-permute-start.62 = (bf16[512,2048]{1,0:T(8,128)(2,1)S(1)}, bf16[512,2048]{1,0:T(8,128)(2,1)}, u32[]{:S(2)}, u32[]{:S(2)}) collective-permute-start(bf16[512,2048]{1,0:T(8,128)(2,1)S(1)} %get-tuple-element.388), channel_id=1, source_target_pairs={{0,1},{1,0},{2,3},{3,2},{4,5},{5,4},{6,7},{7,6},{8,9},{9,8},{10,11... | collective-permute-start | bytes 6291464 | tf_op jit(solution)/shard_map/ppermute | solution.py:67
  520.3 42.0 %collective-permute-start.61 = (bf16[512,2048]{1,0:T(8,128)(2,1)}, bf16[512,2048]{1,0:T(8,128)(2,1)}, u32[]{:S(2)}, u32[]{:S(2)}) collective-permute-start(bf16[512,2048]{1,0:T(8,128)(2,1)} %get-tuple-element.384), channel_id=1, source_target_pairs={{0,1},{1,0},{2,3},{3,2},{4,5},{5,4},{6,7},{7,6},{8,9},{9,8},{10,11... | collective-permute-start | bytes 6291464 | tf_op jit(solution)/shard_map/ppermute | solution.py:67
  561.1 36.0 %collective-permute-start.60 = (bf16[512,2048]{1,0:T(8,128)(2,1)}, bf16[512,2048]{1,0:T(8,128)(2,1)}, u32[]{:S(2)}, u32[]{:S(2)}) collective-permute-start(bf16[512,2048]{1,0:T(8,128)(2,1)} %add_convert_fusion.7), channel_id=1, source_target_pairs={{0,8},{1,17},{2,10},{3,19},{4,12},{5,21},{6,14},{7,23},{8,0},{9,25... | collective-permute-start | bytes 6291464 | tf_op jit(solution)/shard_map/ppermute | solution.py:64
  562.2 36.7 %collective-permute-start.58 = (bf16[512,2048]{1,0:T(8,128)(2,1)}, bf16[512,2048]{1,0:T(8,128)(2,1)}, u32[]{:S(2)}, u32[]{:S(2)}) collective-permute-start(bf16[512,2048]{1,0:T(8,128)(2,1)} %get-tuple-element.369), channel_id=1, source_target_pairs={{0,1},{1,0},{2,3},{3,2},{4,5},{5,4},{6,7},{7,6},{8,9},{9,8},{10,11... | collective-permute-start | bytes 6291464 | tf_op jit(solution)/shard_map/ppermute | solution.py:67
  693.0 132.3 %collective-permute-start.57 = (bf16[512,2048]{1,0:T(8,128)(2,1)}, bf16[512,2048]{1,0:T(8,128)(2,1)}, u32[]{:S(2)}, u32[]{:S(2)}) collective-permute-start(bf16[512,2048]{1,0:T(8,128)(2,1)} %copy-done.43), channel_id=1, source_target_pairs={{0,1},{1,0},{2,3},{3,2},{4,5},{5,4},{6,7},{7,6},{8,9},{9,8},{10,11... | collective-permute-start | bytes 6291464 | tf_op jit(solution)/shard_map/ppermute | solution.py:67
  719.8 33.0 %collective-permute-start.75 = (bf16[2048,256]{1,0:T(8,128)(2,1)}, bf16[2048,256]{1,0:T(8,128)(2,1)S(1)}, u32[]{:S(2)}, u32[]{:S(2)}) collective-permute-start(bf16[2048,256]{1,0:T(8,128)(2,1)} %add_convert_fusion.19), channel_id=1, source_target_pairs={{0,2},{1,3},{2,4},{3,5},{4,6},{5,7},{6,0},{7,1},{8,10},{9,11},{10,... | collective-permute-start | bytes 3145736 | tf_op jit(solution)/shard_map/ppermute | solution.py:75
  752.8 34.8 %collective-permute-start.78 = (bf16[2048,256]{1,0:T(8,128)(2,1)}, bf16[2048,256]{1,0:T(8,128)(2,1)}, u32[]{:S(2)}, u32[]{:S(2)}) collective-permute-start(bf16[2048,256]{1,0:T(8,128)(2,1)} %add_convert_fusion.17), channel_id=1, source_target_pairs={{0,2},{1,3},{2,4},{3,5},{4,6},{5,7},{6,0},{7,1},{8,10},{9,11},{10,... | collective-permute-start | bytes 3145736 | tf_op jit(solution)/shard_map/ppermute | solution.py:75
  814.5 41.1 %collective-permute-start.79 = (bf16[512,2048]{1,0:T(8,128)(2,1)S(1)}, bf16[512,2048]{1,0:T(8,128)(2,1)S(1)}, u32[]{:S(2)}, u32[]{:S(2)}) collective-permute-start(bf16[512,2048]{1,0:T(8,128)(2,1)S(1)} %constant_dynamic-slice_fusion), channel_id=1, source_target_pairs={{0,1},{1,0},{2,3},{3,2},{4,5},{5,4},{6,7},{7,6},{8,9},{9,8},{10,11... | collective-permute-start | bytes 6291464 | tf_op jit(solution)/shard_map/ppermute | solution.py:67
  (190 other events, 3796.1 us)

commit v5 on v4

--- a/solution.py
+++ b/solution.py
@@ -181,7 +181,8 @@
     def total(self):
         if self.mv.F != 4:
             return self.mv.plane_sum(self.blocks)
-        return self.blocks[0].astype(f32) + self.got[1].astype(f32) + self.got[2].astype(f32)
+        own = self.blocks[0] if isinstance(self.blocks[0], list) else self.blocks[:1]
+        return sum(value.astype(f32) for value in own + self.got[1:])
 
 
 class RingGather:
@@ -292,6 +293,7 @@
 
 VMEM = pl.BlockSpec(memory_space=pltpu.VMEM)
 SMEM = pl.BlockSpec(memory_space=pltpu.SMEM)
+ANY = pl.BlockSpec(memory_space=pl.ANY)
 
 
 def params(mebibytes=56):
@@ -327,26 +329,37 @@
     )(partners, acts, *tables, *weights)
 
 
-def backward_kernel(
-    block, count, halves, partners, places, query, keys, values, mixed, logsum, acts_from, *refs
-):
+def backward_kernel(block, count, halves, partners, places, *refs):
+    saved_from, refs = refs[:5], refs[5:]
+    acts_from, refs = refs[0], refs[1:]
     parts, refs = refs[:halves], refs[halves:]
-    cosine, sine = refs[:2]
-    weights = refs[2 : 2 + count]
-    out = refs[2 + count]
-    terms = refs[3 + count : 3 + 2 * count]
-    grad, grad_keys, grad_values, acts, grads, acts_sem, sems = refs[3 + 2 * count :]
+    tables_from, refs = refs[:2], refs[2:]
+    weights, refs = refs[:count], refs[count:]
+    out_to, terms_to, refs = refs[0], refs[1 : 1 + count], refs[1 + count :]
+    grad, grad_keys, grad_values, acts, grads, acts_sem, sems = refs[:7]
+    query, keys, values, mixed, logsum, cosine, sine, near_sems, out, terms, out_sems = refs[7:]
+    length, width = query.shape
     rows = parts[0].shape[0]
+    near = [
+        pltpu.make_async_copy(source, target, near_sems.at[i])
+        for i, (source, target) in enumerate(
+            zip(
+                [*saved_from, *tables_from],
+                [query, keys, values, mixed, logsum, cosine, sine],
+            )
+        )
+    ]
     acts_copy = pltpu.make_async_copy(acts_from, acts, acts_sem.at[0])
     copies = []
     for i, part in enumerate(parts):
         here = pl.ds(pl.multiple_of(places[i] * rows, rows), rows)
         copies.append(pltpu.make_async_copy(part, grads.at[here, :], sems.at[i]))
         copies[-1].start()
+    for copy in near:
+        copy.start()
     acts_copy.start()
     for copy in copies:
         copy.wait()
-    length, width = query.shape
     heads = width // HD
     scale = HD**-0.5
     depth = weights[0].shape[1]
@@ -354,6 +367,8 @@
     for i in range(1, count):
         total = total + dot(columns_of(grads, partners, i, depth), weights[i][0], NN)
     grad[...] = total.astype(low)
+    for copy in near:
+        copy.wait()
     grad_keys[...] = jnp.zeros_like(grad_keys)
     grad_values[...] = jnp.zeros_like(grad_values)
     for begin in range(0, length, block):
@@ -376,12 +391,19 @@
         ).astype(low)
     out[:, width : 2 * width] = turn(grad_keys[...], cosine[...], -sine[...]).astype(low)
     out[:, 2 * width :] = grad_values[...].astype(low)
+    out_copy = pltpu.make_async_copy(out, out_to, out_sems.at[count])
+    out_copy.start()
     acts_copy.wait()
+    sent = []
     for i in range(count):
         inward = dot(columns_of(acts, partners, i, depth), out[...], TN).astype(low)
         for c in range(3):
-            terms[i][c] = inward[:, c * width : (c + 1) * width]
-        terms[i][3] = dot(columns_of(grads, partners, i, depth), mixed[...], TN).astype(low)
+            terms[i, c] = inward[:, c * width : (c + 1) * width]
+        terms[i, 3] = dot(columns_of(grads, partners, i, depth), mixed[...], TN).astype(low)
+        sent.append(pltpu.make_async_copy(terms.at[i], terms_to[i], out_sems.at[i]))
+        sent[-1].start()
+    for copy in [out_copy] + sent:
+        copy.wait()
 
 
 def attend_backward(partners, places, saved, acts, grads, weights, tables):
@@ -392,25 +414,23 @@
     depth = weights[0].shape[1]
     near = [*saved, *tables]
 
-    def whole(value):
-        return pl.BlockSpec(value.shape, lambda i: (0, 0))
-
     found = pl.pallas_call(
         functools.partial(backward_kernel, block, count, len(grads)),
         grid=(1,),
         out_shape=[jax.ShapeDtypeStruct((length, 3 * width), low)]
         + [jax.ShapeDtypeStruct(weights[0].shape, low)] * count,
         in_specs=[SMEM, SMEM]
-        + [whole(v) for v in saved]
-        + [ANY] * (1 + len(grads))
-        + [whole(v) for v in tables]
+        + [ANY] * (len(saved) + 1 + len(grads) + len(tables))
         + [pl.BlockSpec((1, depth, width), lambda i: (3, 0, 0))] * count,
-        out_specs=[pl.BlockSpec((length, 3 * width), lambda i: (0, 0))]
-        + [pl.BlockSpec(weights[0].shape, lambda i: (0, 0, 0))] * count,
+        out_specs=[ANY] * (1 + count),
         scratch_shapes=[pltpu.VMEM((length, width), low)]
         + [pltpu.VMEM((length, width), f32)] * 2
         + [pltpu.VMEM(acts.shape, low)] * 2
-        + [pltpu.SemaphoreType.DMA((1,)), pltpu.SemaphoreType.DMA((len(grads),))],
+        + [pltpu.SemaphoreType.DMA((1,)), pltpu.SemaphoreType.DMA((len(grads),))]
+        + [pltpu.VMEM(v.shape, v.dtype) for v in near]
+        + [pltpu.SemaphoreType.DMA((len(near),))]
+        + [pltpu.VMEM((length, 3 * width), low), pltpu.VMEM((count, *weights[0].shape), low)]
+        + [pltpu.SemaphoreType.DMA((count + 1,))],
         compiler_params=params(),
         cost_estimate=cost(
             10 * length * acts.shape[1] * width + 10 * length * length * 256 * heads,
@@ -458,9 +478,6 @@
         ),
         name="spread",
     )(partners, *values, *flat)
-
-
-ANY = pl.BlockSpec(memory_space=pl.ANY)
 
 
 def take_item(items, slots, sems, then):
@@ -785,12 +802,16 @@
     scale_one = norm_scale(source)
     normed_one = source * scale_one
     expand_own = after(expand_own, attn_own)
-    expand_own[1:] = [mv.plane(expand_own[d], d) for d in planes if d]
-    deps = attn[0](2) + attn_ring() + expand_own[1:]
+    near = [d for d in planes if d and d != 3]
+    for d in near:
+        expand_own[d] = mv.plane(expand_own[d], d)
+    deps = attn[0](2) + attn_ring() + [expand_own[d] for d in near]
     acts = mv.place(mv.mates((normed_one * norm_gains[0]).astype(low)), 0, mv.s)
     tables = rope_tables(LEN, own_width)
     deps += [acts, *tables]
     attn.append(Gather(mv, attn_ring.blocks[-1]))
+    if F > 3:
+        expand_own[3] = mv.plane(after(expand_own[3], *deps), 3)
     deps = attn[0](1, *deps) + attn[1](2, *deps) + attn_ring(*deps)
     placed = mv.place(expand_own, 1, mv.f)
     gate_ring, up_ring = RingGather(mv, placed[0]), RingGather(mv, placed[1])
@@ -828,16 +849,25 @@
     deps = moved + [feed_local]
     shrink_ring = RingGather(mv, mv.place(shrink_own, 0, mv.f))
     feed = Gather(mv, feed_local)
-    own_mates = mv.mates(after(feed_local, *deps))
+
+    def mates_of(gather, i, *deps):
+        if F == 4:
+            return [mv.mates(after(gather.blocks[i], *deps))]
+        return [] if i < 3 else [mv.mates(after(block, *deps)) for block in gather.blocks]
+
+    def arrived(blocks):
+        return [v for block in blocks for v in block[1:]]
+
     moved = feed(1, *deps) + up_ring(*deps)
-    deps = moved + own_mates[1:]
-    first_mates = mv.mates(after(feed.blocks[1], *deps)) if F == 4 else []
+    feed_blocks = mates_of(feed, 0, *deps)
+    grad_blocks = mates_of(cot, 0, *deps) + mates_of(cot, 1, *deps)
+    deps = moved + arrived(feed_blocks + grad_blocks)
     moved = feed(1, *deps) + up_ring(*deps)
-    deps = moved + first_mates[1:]
-    if F == 4:
-        feed_blocks = [own_mates, first_mates, mv.mates(after(feed.blocks[2], *deps))]
-    else:
-        feed_blocks = [own_mates] + [mv.mates(block) for block in feed.blocks[1:]]
+    feed_blocks += mates_of(feed, 1, *deps)
+    grad_blocks += mates_of(cot, 2, *deps)
+    deps = moved + arrived(feed_blocks[1:] + grad_blocks[2:])
+    if F != 4:
+        feed_blocks = mates_of(feed, 3, *deps)
 
     def items_of(blocks, batches):
         return [value for i in batches for value in blocks[i]]
@@ -870,23 +900,23 @@
 
     expand_full = grouped([g.blocks[k] for k in ring_order for g in (gate_ring, up_ring)])
     early, others, late = list(planes)[: F // 2], list(planes)[F // 2 :], [F - 1]
-    deps = [v for block in feed_blocks for v in block[1:]]
     moved = feed(1, *deps) + shrink_ring(*deps)
+    if F == 4:
+        feed_blocks += mates_of(feed, 2, *deps)
     kept_early = feed_forward(
         items_of(feed_blocks, early), after(expand_full, *deps), hidden_width
     )
-    deps = moved + [kept_early[0]]
+    deps = moved + [kept_early[0]] + arrived(feed_blocks[2:])
     moved = cot(1, *deps) + shrink_ring(*deps)
     if F == 4:
-        feed_blocks.append(mv.mates(after(feed.blocks[-1], *deps)))
-    grad_blocks = [mv.mates(after(block, *deps)) for block in cot.blocks[:3]]
+        feed_blocks += mates_of(feed, 3, *deps)
     kept_late = feed_forward(
         items_of(feed_blocks, others), after(expand_full, *deps), hidden_width
     )
-    deps = moved + [kept_late[0]] + [v for block in grad_blocks for v in block[1:]]
+    deps = moved + [kept_late[0]]
     hidden = (kept_early[0], kept_late[0])
     moved = shrink_ring(*deps)
-    grad_blocks += [mv.mates(after(block, *deps)) for block in cot.blocks[3:]]
+    grad_blocks += mates_of(cot, 3, *deps)
     pieces = max(Z // 2, 1)
     parts = Z // pieces
     grad_items = items_of(grad_blocks, planes)
@@ -928,11 +958,16 @@
         hidden_width,
     )
     fed_sums.blocks[-1] = chip_sum(fed[-1])
-    deps = moved + [terms_early] + fed_sums.blocks[-1:]
-    shrink_moved, (shrink_grad,) = columns(shrink_back.total().astype(low), *deps)
-    moved = fed_sums(1, *deps) + shrink_moved
+    deps = moved + [terms_early] + fed_sums.blocks[-1:] + arrived(fed[:-1])
+    shrink_sum = shrink_back.total().astype(low)
+    moved = fed_sums(1, *deps)
     back_early = [after(v, *deps) for v in back_early]
-    back_early = [trade(back_early[i * S : (i + 1) * S]) for i in early]
+    back_early = [back_early[i * S : (i + 1) * S] for i in early]
+    back_early = back_early[:1] + [trade(block) for block in back_early[1:]]
+    for i in early:
+        fed_sums.blocks[i] = [after(v, *deps) for v in fed[i]]
+        if i or F != 4:
+            fed_sums.blocks[i] = chip_sum(fed_sums.blocks[i])
     terms_middle, back_middle = feed_backward(
         items_of(grad_blocks, middle),
         after(shrink_full, *deps),
@@ -944,7 +979,9 @@
     for i in early[1:]:
         feed_sums.blocks[i] = chip_sum(back_early[i])
     deps = moved + [terms_middle] + [feed_sums.blocks[i] for i in early[1:]]
-    moved = feed_sums(1, *deps)
+    deps += [fed_sums.blocks[i] for i in early if i] + [shrink_sum]
+    shrink_moved, (shrink_grad,) = columns(shrink_sum, *deps)
+    moved = feed_sums(1, *deps) + shrink_moved
     back_middle = [after(v, *deps) for v in back_middle]
     back_middle = [trade(back_middle[i * S : (i + 1) * S]) for i in range(len(middle))]
     gate_up = (terms_early, terms_middle, terms_late)
@@ -956,10 +993,15 @@
         feed_sums.blocks[i] = sum(value.astype(f32) for value in block)
         if F != 4:
             feed_sums.blocks[i] = feed_sums.blocks[i].astype(low)
-    feed_sums.blocks[0] = chip_sum([after(v, *deps) for v in back_early[0]])
-    for i in planes[:-1]:
-        fed_sums.blocks[i] = chip_sum([after(v, *deps) for v in fed[i]])
-    deps = moved + expand_terms[-1:] + feed_sums.blocks[:1]
+    feed_sums.blocks[0] = trade([after(v, *deps) for v in back_early[0]])
+    own_traded = feed_sums.blocks[0][1:]
+    if F != 4:
+        feed_sums.blocks[0] = chip_sum(feed_sums.blocks[0])
+    for i in middle:
+        fed_sums.blocks[i] = sum(v.astype(f32) for v in fed[i])
+        if F != 4:
+            fed_sums.blocks[i] = fed_sums.blocks[i].astype(low)
+    deps = moved + expand_terms[-1:] + own_traded
     if F == 4:
         deps += [feed_sums.merge(), fed_sums.merge()]
     gate_back, up_back = RingSum(mv), RingSum(mv)
@@ -985,7 +1027,6 @@
     deps = moved + [grad_low]
     grad_attn = mv.mates(after(grad_low, *deps))
     places = jnp.stack([mv.s ^ d for d in range(S)]).astype(jnp.int32)
-    deps = grad_attn[1:]
     order = (ring_order * 4)[:4] if Z < 4 else ring_order
     attn_sums = {}
     grad_proj = [None] * Z
@@ -1014,31 +1055,30 @@
     expand_sum = jnp.concatenate([gate_back.total(), up_back.total()], axis=1).astype(low)
     deps = moved + [grad_acts, expand_sum]
     attn_back.terms[order[1]] = attn_sums[order[1]].total()
-    moved = attn_sums[order[2]](1, *deps) + attn_sums[order[3]](1, *deps) + attn_back(*deps)
+    moved = attn_sums[order[2]](1, *deps) + attn_sums[order[3]](1, *deps)
+    attn_back(*deps)
     grad_acts = mv.mates_sum([part(grad_acts, d) for d in range(S)])
     input_back, gain_one = norm_back(grad_acts, normed_one, scale_one, norm_gains[0])
     input_grad = (grad_resid + input_back).astype(low)
     deps = moved
     attn_back.terms[order[2]] = attn_sums[order[2]].total()
-    moved = attn_sums[order[3]](2, *deps) + attn_back(*deps)
-    deps = moved + [input_grad]
-    attn_back.terms[order[3]] = attn_sums[order[3]].total()
-    expand_both = columns(expand_sum, *deps)[1]
+    moved = attn_sums[order[3]](2, *deps)
+    attn_back()
+    deps = moved
+    attn_back.terms[order[3]] = after(attn_sums[order[3]].total(), input_grad)
     attn_grad = attn_back.total()
+    inward_grad, outward_grad = attn_grad[:3], attn_grad[3]
+    owned = [attn_grad, expand_sum, shrink_sum]
+    owned_squares = sum(jnp.sum(jnp.square(v.astype(f32))) for v in owned)
+    moved, expand_both = columns(expand_sum, *deps)
     expand_grad = jnp.stack(expand_both)
-    inward_grad, outward_grad = attn_grad[:3], attn_grad[3]
-
-    owned_squares = (
-        jnp.sum(inward_grad * inward_grad)
-        + jnp.sum(outward_grad * outward_grad)
-        + jnp.sum(expand_grad * expand_grad)
-        + jnp.sum(shrink_grad * shrink_grad)
-    )
+
     sums = jnp.concatenate(
         [jnp.stack([gain_one, gain_two]), jnp.full((1, gain_one.shape[0]), owned_squares)], axis=0
     )
     sums = mv.total(sums)
     gains_grad, squares = sums[:2], sums[2, 0]
+    squares = after(squares, *moved)
     norm = jnp.sqrt(squares + jnp.sum(gains_grad * gains_grad))
     factor = jnp.minimum(1.0, clip_bound / (norm + 1e-06))
     inward_new = adamw(

time: 957 us -> 927 us (0.969)
  starting transfers between devices: 90.2 us -> 78.2 us
    ppermute x36, waiting for transfers between devices: 50.1 us -> 83.2 us  [hop(): return lax.ppermute(value, ('fsdp', 'tp'), pairs)]
    ppermute x24, waiting for transfers between devices: 142 us -> 120 us  [ring(): return lax.ppermute(value, 'tp', step)]
  transfers between devices with their start and end apart: 99 -> 99, of which waited for: 41 -> 34; matrix products, arithmetic and copies ran while one was open for 11% -> 10% of each run, Pallas kernels for 43% -> 44%
where the time goes in v5:
time: 927 us; the launch traced here: 922 us
  Pallas kernels  405 us (44%)
  waiting for transfers between devices  269 us (29%)
  other arithmetic  103 us (11%)
  starting transfers between devices  78.2 us (8%)
  local copies, waits for them, and re-layouts  60.7 us (7%)
    ppermute x24, waiting for transfers between devices, ring(): return lax.ppermute(value, 'tp', step)  120 us
    pallas_call x4, Pallas kernels, attend_backward(): pl.pallas_call(functools.partial(backward_kernel, block, count, len(grads...  95.3 us
    ppermute x36, waiting for transfers between devices, hop(): return lax.ppermute(value, ('fsdp', 'tp'), pairs)  83.2 us
    pallas_call x3, Pallas kernels, feed_backward(): pl.pallas_call(functools.partial(feed_back_kernel, count, len(shrink), le...  75.7 us
    pallas_call x4, Pallas kernels, weight_terms(): pl.pallas_call(functools.partial(weight_kernel, len(lefts), len(rights)),...  71.9 us
    pallas_call x4, Pallas kernels, attend_forward(): pl.pallas_call(functools.partial(forward_kernel, block, len(weights)), ou...  62.1 us
    ppermute x15, waiting for transfers between devices, plane(): return lax.ppermute(value, 'fsdp', [(i, i ^ mask) for i in range(self.F)])  55.8 us
    pallas_call x2, Pallas kernels, feed_forward(): pl.pallas_call(functools.partial(feed_kernel, count, len(expand), width),...  46.6 us
  transfers between devices with their start and end apart: 99, of which 34 were waited for; matrix products, arithmetic and copies ran while one was open for 10% of the time, Pallas kernels for 44%

profile of v5, /device:TPU:0, one launch (start us, length us, event | category | flops | bytes accessed | tf_op | source)
XLA Modules:
  0.0 922.0 jit_solution(11113754550996952737)
XLA Ops:
  22.8 24.5 %collective-permute-done.3 = bf16[2,512,256]{2,1,0:T(8,128)(2,1)} collective-permute-done((bf16[2,512,256]{2,1,0:T(8,128)(2,1)}, bf16[2,512,256]{2,1,0:T(8,128)(2,1)}, u32[]{:S(2)}, u32[]{:S(2)}) %collective-permute-start.3) | collective-permute-done | bytes 524320 | tf_op jit(solution)/shard_map/ppermute | solution.py:56
  66.9 21.2 %collective-permute-done.6.refs_3_.refs_7_.refs_13_ = bf16[4,512,256]{2,1,0:T(8,128)(2,1)} collective-permute-done((bf16[4,512,256]{2,1,0:T(8,128)(2,1)}, bf16[4,512,256]{2,1,0:T(8,128)(2,1)}, u32[]{:S(2)}, u32[]{:S(2)}) %collective-permute-start.6) | collective-permute-done | bytes 1048608 | tf_op jit(solution)/shard_map/ppermute | solution.py:64
  109.2 15.5 %attend_forward.4 = (bf16[1024,256]{1,0:T(8,128)(2,1)}, bf16[1024,256]{1,0:T(8,128)(2,1)}, bf16[1024,256]{1,0:T(8,128)(2,1)}, bf16[1024,256]{1,0:T(8,128)(2,1)}, f32[1024,128]{1,0:T(8,128)}) custom-call(s32[4]{0:T(128)} %pad_add_fusion.partners, bf16[1024,2048]{1,0:T(8,128)(2,1)} %constant_dynamic-update-slice_fusion.10.acts.refs_5_, ...), custom_call_target="tpu_custom_call" | custom-call | flops 1503238528 | bytes 2097152 | tf_op jit(solution)/shard_map/attend_forward/pallas_call | solution.py:317
  141.2 15.5 %attend_forward.5 = (bf16[1024,256]{1,0:T(8,128)(2,1)}, bf16[1024,256]{1,0:T(8,128)(2,1)}, bf16[1024,256]{1,0:T(8,128)(2,1)}, bf16[1024,256]{1,0:T(8,128)(2,1)}, f32[1024,128]{1,0:T(8,128)}) custom-call(s32[4]{0:T(128)} %pad_add_fusion.partners, bf16[1024,2048]{1,0:T(8,128)(2,1)} %constant_dynamic-update-slice_fusion.10.acts.refs_5_, ...), custom_call_target="tpu_custom_call" | custom-call | flops 1503238528 | bytes 2097152 | tf_op jit(solution)/shard_map/attend_forward/pallas_call | solution.py:317
  156.7 16.1 %collective-permute-done.15.refs_3_.refs_15_.refs_13_ = bf16[4,512,256]{2,1,0:T(8,128)(2,1)S(1)} collective-permute-done((bf16[4,512,256]{2,1,0:T(8,128)(2,1)}, bf16[4,512,256]{2,1,0:T(8,128)(2,1)S(1)}, u32[]{:S(2)}, u32[]{:S(2)}) %collective-permute-start.15) | collective-permute-done | bytes 1048608 | tf_op jit(solution)/shard_map/ppermute | solution.py:64
  182.7 15.5 %attend_forward.6 = (bf16[1024,256]{1,0:T(8,128)(2,1)}, bf16[1024,256]{1,0:T(8,128)(2,1)}, bf16[1024,256]{1,0:T(8,128)(2,1)}, bf16[1024,256]{1,0:T(8,128)(2,1)}, f32[1024,128]{1,0:T(8,128)}) custom-call(s32[4]{0:T(128)} %pad_add_fusion.partners, bf16[1024,2048]{1,0:T(8,128)(2,1)} %constant_dynamic-update-slice_fusion.10.acts.refs_5_, ...), custom_call_target="tpu_custom_call" | custom-call | flops 1503238528 | bytes 2097152 | tf_op jit(solution)/shard_map/attend_forward/pallas_call | solution.py:317
  202.5 15.5 %attend_forward.7 = (bf16[1024,256]{1,0:T(8,128)(2,1)}, bf16[1024,256]{1,0:T(8,128)(2,1)}, bf16[1024,256]{1,0:T(8,128)(2,1)}, bf16[1024,256]{1,0:T(8,128)(2,1)}, f32[1024,128]{1,0:T(8,128)}) custom-call(s32[4]{0:T(128)} %pad_add_fusion.partners, bf16[1024,2048]{1,0:T(8,128)(2,1)} %constant_dynamic-update-slice_fusion.10.acts.refs_5_, ...), custom_call_target="tpu_custom_call" | custom-call | flops 1503238528 | bytes 2097152 | tf_op jit(solution)/shard_map/attend_forward/pallas_call | solution.py:317
  238.8 19.1 %collective-permute-done.27.refs_5_.refs_7_.refs_9_ = bf16[2048,256]{1,0:T(8,128)(2,1)S(1)} collective-permute-done((bf16[2048,256]{1,0:T(8,128)(2,1)S(1)}, bf16[2048,256]{1,0:T(8,128)(2,1)S(1)}, u32[]{:S(2)}, u32[]{:S(2)}) %collective-permute-start.27) | collective-permute-done | bytes 1048608 | tf_op jit(solution)/shard_map/ppermute | solution.py:75
  259.7 27.4 %collective-permute-done.31.refs_7_.refs_9_.refs_11_ = bf16[2048,256]{1,0:T(8,128)(2,1)S(1)} collective-permute-done((bf16[2048,256]{1,0:T(8,128)(2,1)S(1)}, bf16[2048,256]{1,0:T(8,128)(2,1)S(1)}, u32[]{:S(2)}, u32[]{:S(2)}) %collective-permute-start.31) | collective-permute-done | bytes 1048608 | tf_op jit(solution)/shard_map/ppermute | solution.py:75
  292.8 27.4 %collective-permute-done.35.refs_9_.refs_11_.refs_13_ = bf16[2048,256]{1,0:T(8,128)(2,1)S(1)} collective-permute-done((bf16[2048,256]{1,0:T(8,128)(2,1)S(1)}, bf16[2048,256]{1,0:T(8,128)(2,1)S(1)}, u32[]{:S(2)}, u32[]{:S(2)}) %collective-permute-start.35) | collective-permute-done | bytes 1048608 | tf_op jit(solution)/shard_map/ppermute | solution.py:75
  323.8 23.2 %feed_forward.2 = (bf16[2048,1024]{1,0:T(8,128)(2,1)}, bf16[2048,1024]{1,0:T(8,128)(2,1)}, bf16[2048,1024]{1,0:T(8,128)(2,1)}) custom-call(bf16[512,2048]{1,0:T(8,128)(2,1)S(1)} %multiply_convert_fusion.refs_0_, bf16[512,2048]{1,0:T(8,128)(2,1)S(1)} %copy-done.30, bf16[512,2048]{1,0:T(8,128)(2,1)} %copy-done.27, bf16[512,2048]{1,0:T(8,128)(2,1)} %copy-done.32, ...), custom_call_target="tpu_custom_call" | custom-call | flops 3435973888 | bytes 3355443 | tf_op jit(solution)/shard_map/feed_forward/pallas_call | solution.py:582
  354.6 23.4 %feed_forward.3 = (bf16[2048,1024]{1,0:T(8,128)(2,1)}, bf16[2048,1024]{1,0:T(8,128)(2,1)}, bf16[2048,1024]{1,0:T(8,128)(2,1)}) custom-call(bf16[512,2048]{1,0:T(8,128)(2,1)} %collective-permute-done.36.refs_0_.refs_4_, bf16[512,2048]{1,0:T(8,128)(2,1)} %collective-permute-done.40.refs_1_.refs_5_, bf16[512,2048]{1,0:T(8,128)(2,1)} %collective-permute-done.39.refs_2_.refs_6_, ...), custom_call_target="tpu_custom_call" | custom-call | flops 3435973888 | bytes 3355443 | tf_op jit(solution)/shard_map/feed_forward/pallas_call | solution.py:582
  417.5 20.4 %feed_backward.3 = (bf16[1024,2048]{1,0:T(8,128)(2,1)}, bf16[512,2048]{1,0:T(8,128)(2,1)}, bf16[512,2048]{1,0:T(8,128)(2,1)}) custom-call(bf16[512,2048]{1,0:T(8,128)(2,1)} %copy-done.58, bf16[512,2048]{1,0:T(8,128)(2,1)} %copy-done.59, bf16[2048,256]{1,0:T(8,128)(2,1)S(1)} %copy-done.17, bf16[2048,256]{1,0:T(8,128)(2,1)S(1)} %copy-done.19, ...), custom_call_target="tpu_custom_call" | custom-call | flops 2576980480 | bytes 4194304 | tf_op jit(solution)/shard_map/feed_backward/pallas_call | solution.py:643
  476.8 34.8 %feed_backward.4 = (bf16[2048,2048]{1,0:T(8,128)(2,1)}, bf16[512,2048]{1,0:T(8,128)(2,1)}, bf16[512,2048]{1,0:T(8,128)(2,1)}, bf16[512,2048]{1,0:T(8,128)(2,1)}, bf16[512,2048]{1,0:T(8,128)(2,1)}) custom-call(bf16[512,2048]{1,0:T(8,128)(2,1)} %refs_0_.2, bf16[512,2048]{1,0:T(8,128)(2,1)} %copy-done.21, bf16[512,2048]{1,0:T(8,128)(2,1)} %collective-permute-done.24.refs_2_, ...), custom_call_target="tpu_custom_call" | custom-call | flops 5153960960 | bytes 5033164 | tf_op jit(solution)/shard_map/feed_backward/pallas_call | solution.py:643
  517.6 20.5 %feed_backward.5 = (bf16[1024,2048]{1,0:T(8,128)(2,1)}, bf16[512,2048]{1,0:T(8,128)(2,1)}, bf16[512,2048]{1,0:T(8,128)(2,1)}) custom-call(bf16[512,2048]{1,0:T(8,128)(2,1)} %copy-done.25, bf16[512,2048]{1,0:T(8,128)(2,1)} %copy-done.57, bf16[2048,256]{1,0:T(8,128)(2,1)S(1)} %copy-done.17, bf16[2048,256]{1,0:T(8,128)(2,1)S(1)} %copy-done.20, ...), custom_call_target="tpu_custom_call" | custom-call | flops 2576980480 | bytes 4194304 | tf_op jit(solution)/shard_map/feed_backward/pallas_call | solution.py:643
  546.7 23.3 %weight_terms.6 = (bf16[2048,256]{1,0:T(8,128)(2,1)S(1)}, bf16[2048,256]{1,0:T(8,128)(2,1)S(1)}, bf16[2048,256]{1,0:T(8,128)(2,1)S(1)}, bf16[2048,256]{1,0:T(8,128)(2,1)S(1)}) custom-call(bf16[512,2048]{1,0:T(8,128)(2,1)S(1)} %copy-done.10, bf16[512,2048]{1,0:T(8,128)(2,1)S(1)} %copy-done.31, bf16[512,2048]{1,0:T(8,128)(2,1)S(1)} %copy-done.28, ...), custom_call_target="tpu_custom_call" | custom-call | flops 3435973888 | bytes 6710886 | tf_op jit(solution)/shard_map/weight_terms/pallas_call | solution.py:724
  586.1 22.9 %weight_terms.7 = (bf16[2048,256]{1,0:T(8,128)(2,1)S(1)}, bf16[2048,256]{1,0:T(8,128)(2,1)S(1)}, bf16[2048,256]{1,0:T(8,128)(2,1)S(1)}, bf16[2048,256]{1,0:T(8,128)(2,1)S(1)}) custom-call(bf16[512,2048]{1,0:T(8,128)(2,1)S(1)} %copy-done.10, bf16[512,2048]{1,0:T(8,128)(2,1)S(1)} %copy-done.31, bf16[512,2048]{1,0:T(8,128)(2,1)S(1)} %copy-done.28, ...), custom_call_target="tpu_custom_call" | custom-call | flops 3435973888 | bytes 6710886 | tf_op jit(solution)/shard_map/weight_terms/pallas_call | solution.py:724
  620.7 20.9 %collective-permute-done.66 = bf16[2048,256]{1,0:T(8,128)(2,1)S(1)} collective-permute-done((bf16[2048,256]{1,0:T(8,128)(2,1)S(1)}, bf16[2048,256]{1,0:T(8,128)(2,1)S(1)}, u32[]{:S(2)}, u32[]{:S(2)}) %collective-permute-start.66) | collective-permute-done | bytes 1048608 | tf_op jit(solution)/shard_map/ppermute | solution.py:75
  648.2 23.9 %attend_backward.4 = (bf16[1024,768]{1,0:T(8,128)(2,1)}, bf16[4,512,256]{2,1,0:T(8,128)(2,1)}, bf16[4,512,256]{2,1,0:T(8,128)(2,1)}, bf16[4,512,256]{2,1,0:T(8,128)(2,1)}, bf16[4,512,256]{2,1,0:T(8,128)(2,1)}) custom-call(s32[4]{0:T(128)} %pad_add_fusion.partners, s32[2]{0:T(128)} %pad_add_fusion.1.places, bf16[1024,256]{1,0:T(8,128)(2,1)} %get-tuple-element.406.refs_0_, ...), custom_call_target="tpu_custom_call" | custom-call | flops 3221225472 | bytes 1782579 | tf_op jit(solution)/shard_map/attend_backward/pallas_call | solution.py:417
  677.1 23.8 %attend_backward.5 = (bf16[1024,768]{1,0:T(8,128)(2,1)}, bf16[4,512,256]{2,1,0:T(8,128)(2,1)}, bf16[4,512,256]{2,1,0:T(8,128)(2,1)}, bf16[4,512,256]{2,1,0:T(8,128)(2,1)}, bf16[4,512,256]{2,1,0:T(8,128)(2,1)}) custom-call(s32[4]{0:T(128)} %pad_add_fusion.partners, s32[2]{0:T(128)} %pad_add_fusion.1.places, bf16[1024,256]{1,0:T(8,128)(2,1)} %get-tuple-element.413.refs_0_, ...), custom_call_target="tpu_custom_call" | custom-call | flops 3221225472 | bytes 1782579 | tf_op jit(solution)/shard_map/attend_backward/pallas_call | solution.py:417
  707.3 23.9 %attend_backward.6 = (bf16[1024,768]{1,0:T(8,128)(2,1)}, bf16[4,512,256]{2,1,0:T(8,128)(2,1)}, bf16[4,512,256]{2,1,0:T(8,128)(2,1)}, bf16[4,512,256]{2,1,0:T(8,128)(2,1)}, bf16[4,512,256]{2,1,0:T(8,128)(2,1)}) custom-call(s32[4]{0:T(128)} %pad_add_fusion.partners, s32[2]{0:T(128)} %pad_add_fusion.1.places, bf16[1024,256]{1,0:T(8,128)(2,1)} %get-tuple-element.431.refs_0_, ...), custom_call_target="tpu_custom_call" | custom-call | flops 3221225472 | bytes 1782579 | tf_op jit(solution)/shard_map/attend_backward/pallas_call | solution.py:417
  738.7 23.7 %attend_backward.7 = (bf16[1024,768]{1,0:T(8,128)(2,1)}, bf16[4,512,256]{2,1,0:T(8,128)(2,1)}, bf16[4,512,256]{2,1,0:T(8,128)(2,1)}, bf16[4,512,256]{2,1,0:T(8,128)(2,1)}, bf16[4,512,256]{2,1,0:T(8,128)(2,1)}) custom-call(s32[4]{0:T(128)} %pad_add_fusion.partners, s32[2]{0:T(128)} %pad_add_fusion.1.places, bf16[1024,256]{1,0:T(8,128)(2,1)} %get-tuple-element.442.refs_0_, ...), custom_call_target="tpu_custom_call" | custom-call | flops 3221225472 | bytes 1782579 | tf_op jit(solution)/shard_map/attend_backward/pallas_call | solution.py:417
  768.8 21.6 %spread.3 = bf16[1024,2048]{1,0:T(8,128)(2,1)} custom-call(s32[4]{0:T(128)} %pad_add_fusion.partners, bf16[1024,768]{1,0:T(8,128)(2,1)} %get-tuple-element.446.refs_0_, bf16[1024,768]{1,0:T(8,128)(2,1)} %get-tuple-element.411.refs_1_, bf16[1024,768]{1,0:T(8,128)(2,1)} %get-tuple-element.424.refs_2_, bf16[1024,768]{1,0:T(8,128)(2,1)} %get-tuple-element.435.refs_3_, ...), custom_call_target="tpu_custom_call" | custom-call | flops 2576980480 | bytes 4613734 | tf_op jit(solution)/shard_map/spread/pallas_call | solution.py:467
  803.4 17.9 %collective-permute-done.84 = bf16[4,512,256]{2,1,0:T(8,128)(2,1)S(1)} collective-permute-done((bf16[4,512,256]{2,1,0:T(8,128)(2,1)S(1)}, bf16[4,512,256]{2,1,0:T(8,128)(2,1)S(1)}, u32[]{:S(2)}, u32[]{:S(2)}) %collective-permute-start.84) | collective-permute-done | bytes 1048608 | tf_op jit(solution)/shard_map/ppermute | solution.py:64
  (517 shorter events, 394.2 us)
Async XLA Ops:
  8.3 40.1 %collective-permute-start.2 = (bf16[4,512,256]{2,1,0:T(8,128)(2,1)S(1)}, bf16[4,512,256]{2,1,0:T(8,128)(2,1)S(1)}, u32[]{:S(2)}, u32[]{:S(2)}) collective-permute-start(bf16[4,512,256]{2,1,0:T(8,128)(2,1)S(1)} %pad_maximum_fusion.1.refs_0_.refs_4_.refs_10_), channel_id=1, source_target_pairs={{0,2},{1,3},{2,4},{3,5},{4,6},{5,7},{6,0},{7,1},{8,10},{9,11},{10,... | collective-permute-start | bytes 3145736 | tf_op jit(solution)/shard_map/ppermute | solution.py:75
  11.3 37.1 %collective-permute-start.1 = (bf16[4,512,256]{2,1,0:T(8,128)(2,1)S(1)}, bf16[4,512,256]{2,1,0:T(8,128)(2,1)S(1)}, u32[]{:S(2)}, u32[]{:S(2)}) collective-permute-start(bf16[4,512,256]{2,1,0:T(8,128)(2,1)S(1)} %pad_maximum_fusion.1.refs_0_.refs_4_.refs_10_), channel_id=1, source_target_pairs={{0,16},{1,9},{2,18},{3,11},{4,20},{5,13},{6,22},{7,15},{8,24},{9,1... | collective-permute-start | bytes 3145736 | tf_op jit(solution)/shard_map/ppermute | solution.py:64
  12.8 35.6 %collective-permute-start = (bf16[4,512,256]{2,1,0:T(8,128)(2,1)S(1)}, bf16[4,512,256]{2,1,0:T(8,128)(2,1)}, u32[]{:S(2)}, u32[]{:S(2)}) collective-permute-start(bf16[4,512,256]{2,1,0:T(8,128)(2,1)S(1)} %pad_maximum_fusion.1.refs_0_.refs_4_.refs_10_), channel_id=1, source_target_pairs={{0,8},{1,17},{2,10},{3,19},{4,12},{5,21},{6,14},{7,23},{8,0},{9,25... | collective-permute-start | bytes 3145736 | tf_op jit(solution)/shard_map/ppermute | solution.py:64
  52.2 35.8 %collective-permute-start.6 = (bf16[4,512,256]{2,1,0:T(8,128)(2,1)}, bf16[4,512,256]{2,1,0:T(8,128)(2,1)}, u32[]{:S(2)}, u32[]{:S(2)}) collective-permute-start(bf16[4,512,256]{2,1,0:T(8,128)(2,1)} %collective-permute-done.refs_1_.refs_5_.refs_11_), channel_id=1, source_target_pairs={{0,16},{1,9},{2,18},{3,11},{4,20},{5,13},{6,22},{7,15},{8,24},{9,1... | collective-permute-start | bytes 3145736 | tf_op jit(solution)/shard_map/ppermute | solution.py:64
  52.7 35.3 %collective-permute-start.9 = (bf16[4,512,256]{2,1,0:T(8,128)(2,1)S(1)}, bf16[4,512,256]{2,1,0:T(8,128)(2,1)}, u32[]{:S(2)}, u32[]{:S(2)}) collective-permute-start(bf16[4,512,256]{2,1,0:T(8,128)(2,1)S(1)} %collective-permute-done.2.refs_0_.refs_8_.refs_10_), channel_id=1, source_target_pairs={{0,2},{1,3},{2,4},{3,5},{4,6},{5,7},{6,0},{7,1},{8,10},{9,11},{10,... | collective-permute-start | bytes 3145736 | tf_op jit(solution)/shard_map/ppermute | solution.py:75
  54.3 45.1 %collective-permute-start.8 = (bf16[4,512,256]{2,1,0:T(8,128)(2,1)S(1)}, bf16[4,512,256]{2,1,0:T(8,128)(2,1)}, u32[]{:S(2)}, u32[]{:S(2)}) collective-permute-start(bf16[4,512,256]{2,1,0:T(8,128)(2,1)S(1)} %collective-permute-done.2.refs_0_.refs_8_.refs_10_), channel_id=1, source_target_pairs={{0,16},{1,9},{2,18},{3,11},{4,20},{5,13},{6,22},{7,15},{8,24},{9,1... | collective-permute-start | bytes 3145736 | tf_op jit(solution)/shard_map/ppermute | solution.py:64
  55.8 43.6 %collective-permute-start.7 = (bf16[4,512,256]{2,1,0:T(8,128)(2,1)S(1)}, bf16[4,512,256]{2,1,0:T(8,128)(2,1)}, u32[]{:S(2)}, u32[]{:S(2)}) collective-permute-start(bf16[4,512,256]{2,1,0:T(8,128)(2,1)S(1)} %collective-permute-done.2.refs_0_.refs_8_.refs_10_), channel_id=1, source_target_pairs={{0,8},{1,17},{2,10},{3,19},{4,12},{5,21},{6,14},{7,23},{8,0},{9,25... | collective-permute-start | bytes 3145736 | tf_op jit(solution)/shard_map/ppermute | solution.py:64
  102.7 34.3 %collective-permute-start.13 = (bf16[4,512,256]{2,1,0:T(8,128)(2,1)}, bf16[4,512,256]{2,1,0:T(8,128)(2,1)}, u32[]{:S(2)}, u32[]{:S(2)}) collective-permute-start(bf16[4,512,256]{2,1,0:T(8,128)(2,1)} %collective-permute-done.9.refs_0_.refs_12_.refs_10_), channel_id=1, source_target_pairs={{0,16},{1,9},{2,18},{3,11},{4,20},{5,13},{6,22},{7,15},{8,24},{9,1... | collective-permute-start | bytes 3145736 | tf_op jit(solution)/shard_map/ppermute | solution.py:64
  103.2 33.8 %collective-permute-start.12 = (bf16[4,512,256]{2,1,0:T(8,128)(2,1)}, bf16[4,512,256]{2,1,0:T(8,128)(2,1)}, u32[]{:S(2)}, u32[]{:S(2)}) collective-permute-start(bf16[4,512,256]{2,1,0:T(8,128)(2,1)} %collective-permute-done.9.refs_0_.refs_12_.refs_10_), channel_id=1, source_target_pairs={{0,8},{1,17},{2,10},{3,19},{4,12},{5,21},{6,14},{7,23},{8,0},{9,25... | collective-permute-start | bytes 3145736 | tf_op jit(solution)/shard_map/ppermute | solution.py:64
  137.0 35.8 %collective-permute-start.17 = (bf16[4,512,256]{2,1,0:T(8,128)(2,1)}, bf16[4,512,256]{2,1,0:T(8,128)(2,1)S(1)}, u32[]{:S(2)}, u32[]{:S(2)}) collective-permute-start(bf16[4,512,256]{2,1,0:T(8,128)(2,1)} %collective-permute-done.14.refs_0_.refs_16_.refs_10_), channel_id=1, source_target_pairs={{0,16},{1,9},{2,18},{3,11},{4,20},{5,13},{6,22},{7,15},{8,24},{9,1... | collective-permute-start | bytes 3145736 | tf_op jit(solution)/shard_map/ppermute | solution.py:64
  138.5 34.3 %collective-permute-start.16 = (bf16[4,512,256]{2,1,0:T(8,128)(2,1)}, bf16[4,512,256]{2,1,0:T(8,128)(2,1)S(1)}, u32[]{:S(2)}, u32[]{:S(2)}) collective-permute-start(bf16[4,512,256]{2,1,0:T(8,128)(2,1)} %collective-permute-done.14.refs_0_.refs_16_.refs_10_), channel_id=1, source_target_pairs={{0,8},{1,17},{2,10},{3,19},{4,12},{5,21},{6,14},{7,23},{8,0},{9,25... | collective-permute-start | bytes 3145736 | tf_op jit(solution)/shard_map/ppermute | solution.py:64
  138.5 34.3 %collective-permute-start.15 = (bf16[4,512,256]{2,1,0:T(8,128)(2,1)}, bf16[4,512,256]{2,1,0:T(8,128)(2,1)S(1)}, u32[]{:S(2)}, u32[]{:S(2)}) collective-permute-start(bf16[4,512,256]{2,1,0:T(8,128)(2,1)} %collective-permute-done.12.refs_1_.refs_13_.refs_11_), channel_id=1, source_target_pairs={{0,16},{1,9},{2,18},{3,11},{4,20},{5,13},{6,22},{7,15},{8,24},{9,1... | collective-permute-start | bytes 3145736 | tf_op jit(solution)/shard_map/ppermute | solution.py:64
  139.4 33.4 %collective-permute-start.18 = (bf16[2048,256]{1,0:T(8,128)(2,1)S(1)}, bf16[2048,256]{1,0:T(8,128)(2,1)S(1)}, u32[]{:S(2)}, u32[]{:S(2)}) collective-permute-start(bf16[2048,256]{1,0:T(8,128)(2,1)S(1)} %get-tuple-element.306.refs_10_.refs_12_.refs_14_), channel_id=1, source_target_pairs={{0,2},{1,3},{2,4},{3,5},{4,6},{5,7},{6,0},{7,1},{8,10},{9,11},{10,... | collective-permute-start | bytes 3145736 | tf_op jit(solution)/shard_map/ppermute | solution.py:75
  378.3 38.0 %collective-permute-start.44 = (bf16[2048,256]{1,0:T(8,128)(2,1)S(1)}, bf16[2048,256]{1,0:T(8,128)(2,1)S(1)}, u32[]{:S(2)}, u32[]{:S(2)}) collective-permute-start(bf16[2048,256]{1,0:T(8,128)(2,1)S(1)} %collective-permute-done.41.refs_3_.refs_1_.refs_5_), channel_id=1, source_target_pairs={{0,2},{1,3},{2,4},{3,5},{4,6},{5,7},{6,0},{7,1},{8,10},{9,11},{10,... | collective-permute-start | bytes 3145736 | tf_op jit(solution)/shard_map/ppermute | solution.py:75
  472.4 41.5 %collective-permute-start.49 = (bf16[512,2048]{1,0:T(8,128)(2,1)S(1)}, bf16[512,2048]{1,0:T(8,128)(2,1)}, u32[]{:S(2)}, u32[]{:S(2)}) collective-permute-start(bf16[512,2048]{1,0:T(8,128)(2,1)S(1)} %add_convert_fusion.6), channel_id=1, source_target_pairs={{0,8},{1,17},{2,10},{3,19},{4,12},{5,21},{6,14},{7,23},{8,0},{9,25... | collective-permute-start | bytes 6291464 | tf_op jit(solution)/shard_map/ppermute | solution.py:64
  473.2 40.7 %collective-permute-start.52 = (bf16[512,2048]{1,0:T(8,128)(2,1)}, bf16[512,2048]{1,0:T(8,128)(2,1)}, u32[]{:S(2)}, u32[]{:S(2)}) collective-permute-start(bf16[512,2048]{1,0:T(8,128)(2,1)} %get-tuple-element.354), channel_id=1, source_target_pairs={{0,1},{1,0},{2,3},{3,2},{4,5},{5,4},{6,7},{7,6},{8,9},{9,8},{10,11... | collective-permute-start | bytes 6291464 | tf_op jit(solution)/shard_map/ppermute | solution.py:67
  473.6 40.2 %collective-permute-start.53 = (bf16[512,2048]{1,0:T(8,128)(2,1)}, bf16[512,2048]{1,0:T(8,128)(2,1)S(1)}, u32[]{:S(2)}, u32[]{:S(2)}) collective-permute-start(bf16[512,2048]{1,0:T(8,128)(2,1)} %get-tuple-element.355), channel_id=1, source_target_pairs={{0,1},{1,0},{2,3},{3,2},{4,5},{5,4},{6,7},{7,6},{8,9},{9,8},{10,11... | collective-permute-start | bytes 6291464 | tf_op jit(solution)/shard_map/ppermute | solution.py:67
  473.7 40.2 %collective-permute-start.54 = (bf16[512,2048]{1,0:T(8,128)(2,1)}, bf16[512,2048]{1,0:T(8,128)(2,1)}, u32[]{:S(2)}, u32[]{:S(2)}) collective-permute-start(bf16[512,2048]{1,0:T(8,128)(2,1)} %get-tuple-element.356), channel_id=1, source_target_pairs={{0,1},{1,0},{2,3},{3,2},{4,5},{5,4},{6,7},{7,6},{8,9},{9,8},{10,11... | collective-permute-start | bytes 6291464 | tf_op jit(solution)/shard_map/ppermute | solution.py:67
  476.6 37.3 %collective-permute-start.50 = (bf16[2048,256]{1,0:T(8,128)(2,1)}, bf16[2048,256]{1,0:T(8,128)(2,1)}, u32[]{:S(2)}, u32[]{:S(2)}) collective-permute-start(bf16[2048,256]{1,0:T(8,128)(2,1)} %add_convert_fusion.21), channel_id=1, source_target_pairs={{0,2},{1,3},{2,4},{3,5},{4,6},{5,7},{6,0},{7,1},{8,10},{9,11},{10,... | collective-permute-start | bytes 3145736 | tf_op jit(solution)/shard_map/ppermute | solution.py:75
  543.2 40.9 %collective-permute-start.58 = (bf16[512,2048]{1,0:T(8,128)(2,1)S(1)}, bf16[512,2048]{1,0:T(8,128)(2,1)S(1)}, u32[]{:S(2)}, u32[]{:S(2)}) collective-permute-start(bf16[512,2048]{1,0:T(8,128)(2,1)S(1)} %add_convert_fusion.3), channel_id=1, source_target_pairs={{0,8},{1,17},{2,10},{3,19},{4,12},{5,21},{6,14},{7,23},{8,0},{9,25... | collective-permute-start | bytes 6291464 | tf_op jit(solution)/shard_map/ppermute | solution.py:64
  544.1 40.1 %collective-permute-start.62 = (bf16[512,2048]{1,0:T(8,128)(2,1)}, bf16[512,2048]{1,0:T(8,128)(2,1)S(1)}, u32[]{:S(2)}, u32[]{:S(2)}) collective-permute-start(bf16[512,2048]{1,0:T(8,128)(2,1)} %get-tuple-element.386), channel_id=1, source_target_pairs={{0,1},{1,0},{2,3},{3,2},{4,5},{5,4},{6,7},{7,6},{8,9},{9,8},{10,11... | collective-permute-start | bytes 6291464 | tf_op jit(solution)/shard_map/ppermute | solution.py:67
  544.7 35.4 %collective-permute-start.59 = (bf16[512,256]{1,0:T(8,128)(2,1)S(1)}, bf16[512,256]{1,0:T(8,128)(2,1)S(1)}, u32[]{:S(2)}, u32[]{:S(2)}) collective-permute-start(bf16[512,256]{1,0:T(8,128)(2,1)S(1)} %get-tuple-element.377), channel_id=1, source_target_pairs={{0,8},{8,0},{16,24},{24,16},{1,9},{9,1},{17,25},{25,17},{2,10},{10... | collective-permute-start | bytes 786440 | tf_op jit(solution)/shard_map/ppermute | solution.py:56
  545.6 34.5 %collective-permute-start.60 = (bf16[512,256]{1,0:T(8,128)(2,1)S(1)}, bf16[512,256]{1,0:T(8,128)(2,1)S(1)}, u32[]{:S(2)}, u32[]{:S(2)}) collective-permute-start(bf16[512,256]{1,0:T(8,128)(2,1)S(1)} %get-tuple-element.378), channel_id=1, source_target_pairs={{0,16},{8,24},{16,0},{24,8},{1,17},{9,25},{17,1},{25,9},{2,18},{10... | collective-permute-start | bytes 786440 | tf_op jit(solution)/shard_map/ppermute | solution.py:56
  792.1 38.1 %collective-permute-start.79 = (bf16[512,2048]{1,0:T(8,128)(2,1)S(1)}, bf16[512,2048]{1,0:T(8,128)(2,1)S(1)}, u32[]{:S(2)}, u32[]{:S(2)}) collective-permute-start(bf16[512,2048]{1,0:T(8,128)(2,1)S(1)} %constant_dynamic-slice_fusion), channel_id=1, source_target_pairs={{0,1},{1,0},{2,3},{3,2},{4,5},{5,4},{6,7},{7,6},{8,9},{9,8},{10,11... | collective-permute-start | bytes 6291464 | tf_op jit(solution)/shard_map/ppermute | solution.py:67
  (190 other events, 3637.8 us)

commit v6 on v5

--- a/solution.py
+++ b/solution.py
@@ -120,17 +120,70 @@
             total = self.ring(total.astype(low)).astype(f32) + blocks[k].astype(f32)
         return total
 
-    def total(self, value):
-        moves = [[functools.partial(self.plane, mask=d) for d in range(1, self.F)]]
-        moves.append([functools.partial(self.mate, mask=d * self.S) for d in range(1, self.Z)])
-        moves.append([functools.partial(self.mate, mask=d) for d in range(1, self.S)])
-        for group in moves:
-            value = value + sum(move(value) for move in group)
-        return value
-
 
 def after(value, *others):
     return lax.optimization_barrier((value, *others))[0]
+
+
+def total_kernel(F, Z, S, value, out, held, slots, send_sems, recv_sems):
+    f, t = lax.axis_index("fsdp"), lax.axis_index("tp")
+    z, s = t // S, t % S
+    rounds = [
+        [((f + d) % F, t) for d in range(1, F)],
+        [(f, (z + d) % Z * S + s) for d in range(1, Z)],
+        [(f, z * S + (s + d) % S) for d in range(1, S)],
+    ]
+    peers = [peer for group in rounds for peer in group]
+    barrier = pltpu.get_barrier_semaphore()
+    for peer in peers:
+        pl.semaphore_signal(barrier, inc=1, device_id=peer, device_id_type=pl.DeviceIdType.MESH)
+    pl.semaphore_wait(barrier, len(peers))
+    held[0] = value[...]
+    place = 0
+    for i, group in enumerate(rounds):
+        copies = []
+        for peer in group:
+            copies.append(
+                pltpu.make_async_remote_copy(
+                    src_ref=held.at[i],
+                    dst_ref=slots.at[place],
+                    send_sem=send_sems.at[place],
+                    recv_sem=recv_sems.at[place],
+                    device_id=peer,
+                    device_id_type=pl.DeviceIdType.MESH,
+                )
+            )
+            copies[-1].start()
+            place += 1
+        total = held[i]
+        for j, copy in enumerate(copies):
+            copy.wait()
+            total = total + slots[place - len(group) + j]
+        held[i + 1] = total
+    out[...] = held[len(rounds)]
+
+
+def total_of(mv, value):
+    peers = mv.F + mv.Z + mv.S - 3
+    return pl.pallas_call(
+        functools.partial(total_kernel, mv.F, mv.Z, mv.S),
+        out_shape=jax.ShapeDtypeStruct(value.shape, f32),
+        in_specs=[pl.BlockSpec(memory_space=pltpu.VMEM)],
+        out_specs=pl.BlockSpec(memory_space=pltpu.VMEM),
+        scratch_shapes=[
+            pltpu.VMEM((4, *value.shape), f32),
+            pltpu.VMEM((peers, *value.shape), f32),
+            pltpu.SemaphoreType.DMA((peers,)),
+            pltpu.SemaphoreType.DMA((peers,)),
+        ],
+        compiler_params=pltpu.CompilerParams(
+            collective_id=0, has_side_effects=True, vmem_limit_bytes=8 * 1024 * 1024
+        ),
+        cost_estimate=pl.CostEstimate(
+            flops=value.size * peers, bytes_accessed=value.size * 8, transcendentals=0
+        ),
+        name="total",
+    )(value)
 
 
 class Gather:
@@ -808,7 +861,7 @@
     deps = attn[0](2) + attn_ring() + [expand_own[d] for d in near]
     acts = mv.place(mv.mates((normed_one * norm_gains[0]).astype(low)), 0, mv.s)
     tables = rope_tables(LEN, own_width)
-    deps += [acts, *tables]
+    deps += [acts]
     attn.append(Gather(mv, attn_ring.blocks[-1]))
     if F > 3:
         expand_own[3] = mv.plane(after(expand_own[3], *deps), 3)
@@ -993,17 +1046,13 @@
         feed_sums.blocks[i] = sum(value.astype(f32) for value in block)
         if F != 4:
             feed_sums.blocks[i] = feed_sums.blocks[i].astype(low)
-    feed_sums.blocks[0] = trade([after(v, *deps) for v in back_early[0]])
-    own_traded = feed_sums.blocks[0][1:]
-    if F != 4:
-        feed_sums.blocks[0] = chip_sum(feed_sums.blocks[0])
     for i in middle:
         fed_sums.blocks[i] = sum(v.astype(f32) for v in fed[i])
         if F != 4:
             fed_sums.blocks[i] = fed_sums.blocks[i].astype(low)
-    deps = moved + expand_terms[-1:] + own_traded
+    deps = moved + expand_terms[-1:]
     if F == 4:
-        deps += [feed_sums.merge(), fed_sums.merge()]
+        deps += [feed_sums.merge()]
     gate_back, up_back = RingSum(mv), RingSum(mv)
 
     def known():
@@ -1012,6 +1061,10 @@
 
     known()
     moved = feed_sums(1, *deps) + gate_back(*deps)
+    feed_sums.blocks[0] = trade([after(v, *deps) for v in back_early[0]])
+    moved += feed_sums.blocks[0][1:]
+    if F != 4:
+        feed_sums.blocks[0] = chip_sum(feed_sums.blocks[0])
     for i in range(1, parts):
         expand_terms += weight_terms(
             feed_items, after(gate_up, *deps), i, 2 * pieces, hidden_width
@@ -1025,6 +1078,8 @@
     grad_resid = cotangent.astype(f32) + resid_back
     grad_low = grad_resid.astype(low)
     deps = moved + [grad_low]
+    if F == 4:
+        deps += [fed_sums.merge()]
     grad_attn = mv.mates(after(grad_low, *deps))
     places = jnp.stack([mv.s ^ d for d in range(S)]).astype(jnp.int32)
     order = (ring_order * 4)[:4] if Z < 4 else ring_order
@@ -1073,12 +1128,11 @@
     moved, expand_both = columns(expand_sum, *deps)
     expand_grad = jnp.stack(expand_both)
 
-    sums = jnp.concatenate(
-        [jnp.stack([gain_one, gain_two]), jnp.full((1, gain_one.shape[0]), owned_squares)], axis=0
-    )
-    sums = mv.total(sums)
-    gains_grad, squares = sums[:2], sums[2, 0]
-    squares = after(squares, *moved)
+    gains_shape = norm_gains.shape
+    lines = [gain.reshape(-1, 128) for gain in (gain_one, gain_two)]
+    sums = jnp.concatenate(lines + [jnp.full((8, 128), owned_squares)], axis=0)
+    sums = total_of(mv, after(sums, *moved))
+    gains_grad, squares = sums[:-8].reshape(gains_shape), sums[-1, 0]
     norm = jnp.sqrt(squares + jnp.sum(gains_grad * gains_grad))
     factor = jnp.minimum(1.0, clip_bound / (norm + 1e-06))
     inward_new = adamw(

time: 927 us -> 919 us (level)
  waiting for transfers between devices: 269 us -> 256 us
  Pallas kernels: 405 us -> 416 us
    pallas_call x0 -> x1, Pallas kernels: none -> 10.8 us  [total_of(): pl.pallas_call(functools.partial(total_kernel, mv.F, mv.Z, mv.S), out_sha...]
    unnamed x230 -> x218, local copies, waits for them, and re-layouts: 31.9 us -> 28.3 us
    ppermute x15 -> x12, waiting for transfers between devices: 55.8 us -> 53.5 us  [plane(): return lax.ppermute(value, 'fsdp', [(i, i ^ mask) for i in range(self.F)])]
  transfers between devices with their start and end apart: 99 -> 92, of which waited for: 34 -> 28; matrix products, arithmetic and copies ran while one was open for 10% -> 10% of each run, Pallas kernels for 44% -> 44%
where the time goes in v6:
time: 919 us; the launch traced here: 914 us
  Pallas kernels  416 us (45%)
  waiting for transfers between devices  256 us (28%)
  other arithmetic  102 us (11%)
  starting transfers between devices  75.3 us (8%)
  local copies, waits for them, and re-layouts  58.2 us (6%)
    ppermute x24, waiting for transfers between devices, ring(): return lax.ppermute(value, 'tp', step)  114 us
    pallas_call x4, Pallas kernels, attend_backward(): pl.pallas_call(functools.partial(backward_kernel, block, count, len(grads...  95.7 us
    ppermute x36, waiting for transfers between devices, hop(): return lax.ppermute(value, ('fsdp', 'tp'), pairs)  79.8 us
    pallas_call x3, Pallas kernels, feed_backward(): pl.pallas_call(functools.partial(feed_back_kernel, count, len(shrink), le...  75.7 us
    pallas_call x4, Pallas kernels, weight_terms(): pl.pallas_call(functools.partial(weight_kernel, len(lefts), len(rights)),...  71.8 us
    pallas_call x4, Pallas kernels, attend_forward(): pl.pallas_call(functools.partial(forward_kernel, block, len(weights)), ou...  62.2 us
    ppermute x12, waiting for transfers between devices, plane(): return lax.ppermute(value, 'fsdp', [(i, i ^ mask) for i in range(self.F)])  53.5 us
    pallas_call x2, Pallas kernels, feed_forward(): pl.pallas_call(functools.partial(feed_kernel, count, len(expand), width),...  46.6 us
  transfers between devices with their start and end apart: 92, of which 28 were waited for; matrix products, arithmetic and copies ran while one was open for 10% of the time, Pallas kernels for 44%

profile of v6, /device:TPU:0, one launch (start us, length us, event | category | flops | bytes accessed | tf_op | source)
XLA Modules:
  0.0 914.4 jit_solution(8562761037317914302)
XLA Ops:
  22.1 25.2 %collective-permute-done.3 = bf16[2,512,256]{2,1,0:T(8,128)(2,1)} collective-permute-done((bf16[2,512,256]{2,1,0:T(8,128)(2,1)}, bf16[2,512,256]{2,1,0:T(8,128)(2,1)}, u32[]{:S(2)}, u32[]{:S(2)}) %collective-permute-start.3) | collective-permute-done | bytes 524320 | tf_op jit(solution)/shard_map/ppermute | solution.py:56
  64.8 21.2 %collective-permute-done.6.refs_3_.refs_7_.refs_13_ = bf16[4,512,256]{2,1,0:T(8,128)(2,1)} collective-permute-done((bf16[4,512,256]{2,1,0:T(8,128)(2,1)}, bf16[4,512,256]{2,1,0:T(8,128)(2,1)}, u32[]{:S(2)}, u32[]{:S(2)}) %collective-permute-start.6) | collective-permute-done | bytes 1048608 | tf_op jit(solution)/shard_map/ppermute | solution.py:64
  109.8 15.6 %attend_forward.4 = (bf16[1024,256]{1,0:T(8,128)(2,1)}, bf16[1024,256]{1,0:T(8,128)(2,1)}, bf16[1024,256]{1,0:T(8,128)(2,1)}, bf16[1024,256]{1,0:T(8,128)(2,1)}, f32[1024,128]{1,0:T(8,128)}) custom-call(s32[4]{0:T(128)} %pad_add_fusion.partners, bf16[1024,2048]{1,0:T(8,128)(2,1)} %constant_dynamic-update-slice_fusion.10.acts.refs_5_, ...), custom_call_target="tpu_custom_call" | custom-call | flops 1503238528 | bytes 2097152 | tf_op jit(solution)/shard_map/attend_forward/pallas_call | solution.py:370
  139.0 15.5 %attend_forward.5 = (bf16[1024,256]{1,0:T(8,128)(2,1)}, bf16[1024,256]{1,0:T(8,128)(2,1)}, bf16[1024,256]{1,0:T(8,128)(2,1)}, bf16[1024,256]{1,0:T(8,128)(2,1)}, f32[1024,128]{1,0:T(8,128)}) custom-call(s32[4]{0:T(128)} %pad_add_fusion.partners, bf16[1024,2048]{1,0:T(8,128)(2,1)} %constant_dynamic-update-slice_fusion.10.acts.refs_5_, ...), custom_call_target="tpu_custom_call" | custom-call | flops 1503238528 | bytes 2097152 | tf_op jit(solution)/shard_map/attend_forward/pallas_call | solution.py:370
  154.5 16.1 %collective-permute-done.15.refs_3_.refs_15_.refs_13_ = bf16[4,512,256]{2,1,0:T(8,128)(2,1)S(1)} collective-permute-done((bf16[4,512,256]{2,1,0:T(8,128)(2,1)}, bf16[4,512,256]{2,1,0:T(8,128)(2,1)S(1)}, u32[]{:S(2)}, u32[]{:S(2)}) %collective-permute-start.15) | collective-permute-done | bytes 1048608 | tf_op jit(solution)/shard_map/ppermute | solution.py:64
  180.5 15.5 %attend_forward.6 = (bf16[1024,256]{1,0:T(8,128)(2,1)}, bf16[1024,256]{1,0:T(8,128)(2,1)}, bf16[1024,256]{1,0:T(8,128)(2,1)}, bf16[1024,256]{1,0:T(8,128)(2,1)}, f32[1024,128]{1,0:T(8,128)}) custom-call(s32[4]{0:T(128)} %pad_add_fusion.partners, bf16[1024,2048]{1,0:T(8,128)(2,1)} %constant_dynamic-update-slice_fusion.10.acts.refs_5_, ...), custom_call_target="tpu_custom_call" | custom-call | flops 1503238528 | bytes 2097152 | tf_op jit(solution)/shard_map/attend_forward/pallas_call | solution.py:370
  200.3 15.6 %attend_forward.7 = (bf16[1024,256]{1,0:T(8,128)(2,1)}, bf16[1024,256]{1,0:T(8,128)(2,1)}, bf16[1024,256]{1,0:T(8,128)(2,1)}, bf16[1024,256]{1,0:T(8,128)(2,1)}, f32[1024,128]{1,0:T(8,128)}) custom-call(s32[4]{0:T(128)} %pad_add_fusion.partners, bf16[1024,2048]{1,0:T(8,128)(2,1)} %constant_dynamic-update-slice_fusion.10.acts.refs_5_, ...), custom_call_target="tpu_custom_call" | custom-call | flops 1503238528 | bytes 2097152 | tf_op jit(solution)/shard_map/attend_forward/pallas_call | solution.py:370
  236.7 19.1 %collective-permute-done.27.refs_5_.refs_7_.refs_9_ = bf16[2048,256]{1,0:T(8,128)(2,1)S(1)} collective-permute-done((bf16[2048,256]{1,0:T(8,128)(2,1)S(1)}, bf16[2048,256]{1,0:T(8,128)(2,1)S(1)}, u32[]{:S(2)}, u32[]{:S(2)}) %collective-permute-start.27) | collective-permute-done | bytes 1048608 | tf_op jit(solution)/shard_map/ppermute | solution.py:75
  257.6 27.4 %collective-permute-done.31.refs_7_.refs_9_.refs_11_ = bf16[2048,256]{1,0:T(8,128)(2,1)S(1)} collective-permute-done((bf16[2048,256]{1,0:T(8,128)(2,1)S(1)}, bf16[2048,256]{1,0:T(8,128)(2,1)S(1)}, u32[]{:S(2)}, u32[]{:S(2)}) %collective-permute-start.31) | collective-permute-done | bytes 1048608 | tf_op jit(solution)/shard_map/ppermute | solution.py:75
  290.7 27.4 %collective-permute-done.35.refs_9_.refs_11_.refs_13_ = bf16[2048,256]{1,0:T(8,128)(2,1)S(1)} collective-permute-done((bf16[2048,256]{1,0:T(8,128)(2,1)S(1)}, bf16[2048,256]{1,0:T(8,128)(2,1)S(1)}, u32[]{:S(2)}, u32[]{:S(2)}) %collective-permute-start.35) | collective-permute-done | bytes 1048608 | tf_op jit(solution)/shard_map/ppermute | solution.py:75
  321.7 23.2 %feed_forward.2 = (bf16[2048,1024]{1,0:T(8,128)(2,1)}, bf16[2048,1024]{1,0:T(8,128)(2,1)}, bf16[2048,1024]{1,0:T(8,128)(2,1)}) custom-call(bf16[512,2048]{1,0:T(8,128)(2,1)S(1)} %multiply_convert_fusion.refs_0_, bf16[512,2048]{1,0:T(8,128)(2,1)S(1)} %copy-done.30, bf16[512,2048]{1,0:T(8,128)(2,1)} %copy-done.27, bf16[512,2048]{1,0:T(8,128)(2,1)} %copy-done.32, ...), custom_call_target="tpu_custom_call" | custom-call | flops 3435973888 | bytes 3355443 | tf_op jit(solution)/shard_map/feed_forward/pallas_call | solution.py:635
  352.5 23.4 %feed_forward.3 = (bf16[2048,1024]{1,0:T(8,128)(2,1)}, bf16[2048,1024]{1,0:T(8,128)(2,1)}, bf16[2048,1024]{1,0:T(8,128)(2,1)}) custom-call(bf16[512,2048]{1,0:T(8,128)(2,1)} %collective-permute-done.36.refs_0_.refs_4_, bf16[512,2048]{1,0:T(8,128)(2,1)} %collective-permute-done.40.refs_1_.refs_5_, bf16[512,2048]{1,0:T(8,128)(2,1)} %collective-permute-done.39.refs_2_.refs_6_, ...), custom_call_target="tpu_custom_call" | custom-call | flops 3435973888 | bytes 3355443 | tf_op jit(solution)/shard_map/feed_forward/pallas_call | solution.py:635
  415.5 20.4 %feed_backward.3 = (bf16[1024,2048]{1,0:T(8,128)(2,1)}, bf16[512,2048]{1,0:T(8,128)(2,1)}, bf16[512,2048]{1,0:T(8,128)(2,1)}) custom-call(bf16[512,2048]{1,0:T(8,128)(2,1)} %copy-done.58, bf16[512,2048]{1,0:T(8,128)(2,1)} %copy-done.59, bf16[2048,256]{1,0:T(8,128)(2,1)S(1)} %copy-done.17, bf16[2048,256]{1,0:T(8,128)(2,1)S(1)} %copy-done.19, ...), custom_call_target="tpu_custom_call" | custom-call | flops 2576980480 | bytes 4194304 | tf_op jit(solution)/shard_map/feed_backward/pallas_call | solution.py:696
  474.7 34.7 %feed_backward.4 = (bf16[2048,2048]{1,0:T(8,128)(2,1)}, bf16[512,2048]{1,0:T(8,128)(2,1)}, bf16[512,2048]{1,0:T(8,128)(2,1)}, bf16[512,2048]{1,0:T(8,128)(2,1)}, bf16[512,2048]{1,0:T(8,128)(2,1)}) custom-call(bf16[512,2048]{1,0:T(8,128)(2,1)} %refs_0_.2, bf16[512,2048]{1,0:T(8,128)(2,1)} %copy-done.21, bf16[512,2048]{1,0:T(8,128)(2,1)} %collective-permute-done.24.refs_2_, ...), custom_call_target="tpu_custom_call" | custom-call | flops 5153960960 | bytes 5033164 | tf_op jit(solution)/shard_map/feed_backward/pallas_call | solution.py:696
  515.5 20.5 %feed_backward.5 = (bf16[1024,2048]{1,0:T(8,128)(2,1)}, bf16[512,2048]{1,0:T(8,128)(2,1)}, bf16[512,2048]{1,0:T(8,128)(2,1)}) custom-call(bf16[512,2048]{1,0:T(8,128)(2,1)} %copy-done.25, bf16[512,2048]{1,0:T(8,128)(2,1)} %copy-done.57, bf16[2048,256]{1,0:T(8,128)(2,1)S(1)} %copy-done.17, bf16[2048,256]{1,0:T(8,128)(2,1)S(1)} %copy-done.20, ...), custom_call_target="tpu_custom_call" | custom-call | flops 2576980480 | bytes 4194304 | tf_op jit(solution)/shard_map/feed_backward/pallas_call | solution.py:696
  545.8 23.2 %weight_terms.6 = (bf16[2048,256]{1,0:T(8,128)(2,1)S(1)}, bf16[2048,256]{1,0:T(8,128)(2,1)S(1)}, bf16[2048,256]{1,0:T(8,128)(2,1)S(1)}, bf16[2048,256]{1,0:T(8,128)(2,1)S(1)}) custom-call(bf16[512,2048]{1,0:T(8,128)(2,1)S(1)} %copy-done.10, bf16[512,2048]{1,0:T(8,128)(2,1)S(1)} %copy-done.31, bf16[512,2048]{1,0:T(8,128)(2,1)S(1)} %copy-done.28, ...), custom_call_target="tpu_custom_call" | custom-call | flops 3435973888 | bytes 6710886 | tf_op jit(solution)/shard_map/weight_terms/pallas_call | solution.py:777
  585.2 22.9 %weight_terms.7 = (bf16[2048,256]{1,0:T(8,128)(2,1)S(1)}, bf16[2048,256]{1,0:T(8,128)(2,1)S(1)}, bf16[2048,256]{1,0:T(8,128)(2,1)S(1)}, bf16[2048,256]{1,0:T(8,128)(2,1)S(1)}) custom-call(bf16[512,2048]{1,0:T(8,128)(2,1)S(1)} %copy-done.10, bf16[512,2048]{1,0:T(8,128)(2,1)S(1)} %copy-done.31, bf16[512,2048]{1,0:T(8,128)(2,1)S(1)} %copy-done.28, ...), custom_call_target="tpu_custom_call" | custom-call | flops 3435973888 | bytes 6710886 | tf_op jit(solution)/shard_map/weight_terms/pallas_call | solution.py:777
  619.7 22.5 %collective-permute-done.66 = bf16[2048,256]{1,0:T(8,128)(2,1)S(1)} collective-permute-done((bf16[2048,256]{1,0:T(8,128)(2,1)S(1)}, bf16[2048,256]{1,0:T(8,128)(2,1)S(1)}, u32[]{:S(2)}, u32[]{:S(2)}) %collective-permute-start.66) | collective-permute-done | bytes 1048608 | tf_op jit(solution)/shard_map/ppermute | solution.py:75
  648.1 24.0 %attend_backward.4 = (bf16[1024,768]{1,0:T(8,128)(2,1)}, bf16[4,512,256]{2,1,0:T(8,128)(2,1)}, bf16[4,512,256]{2,1,0:T(8,128)(2,1)}, bf16[4,512,256]{2,1,0:T(8,128)(2,1)}, bf16[4,512,256]{2,1,0:T(8,128)(2,1)}) custom-call(s32[4]{0:T(128)} %pad_add_fusion.partners, s32[2]{0:T(128)} %pad_add_fusion.1.places, bf16[1024,256]{1,0:T(8,128)(2,1)} %get-tuple-element.406.refs_0_, ...), custom_call_target="tpu_custom_call" | custom-call | flops 3221225472 | bytes 1782579 | tf_op jit(solution)/shard_map/attend_backward/pallas_call | solution.py:470
  679.0 23.8 %attend_backward.5 = (bf16[1024,768]{1,0:T(8,128)(2,1)}, bf16[4,512,256]{2,1,0:T(8,128)(2,1)}, bf16[4,512,256]{2,1,0:T(8,128)(2,1)}, bf16[4,512,256]{2,1,0:T(8,128)(2,1)}, bf16[4,512,256]{2,1,0:T(8,128)(2,1)}) custom-call(s32[4]{0:T(128)} %pad_add_fusion.partners, s32[2]{0:T(128)} %pad_add_fusion.1.places, bf16[1024,256]{1,0:T(8,128)(2,1)} %get-tuple-element.413.refs_0_, ...), custom_call_target="tpu_custom_call" | custom-call | flops 3221225472 | bytes 1782579 | tf_op jit(solution)/shard_map/attend_backward/pallas_call | solution.py:470
  707.4 24.3 %attend_backward.6 = (bf16[1024,768]{1,0:T(8,128)(2,1)}, bf16[4,512,256]{2,1,0:T(8,128)(2,1)}, bf16[4,512,256]{2,1,0:T(8,128)(2,1)}, bf16[4,512,256]{2,1,0:T(8,128)(2,1)}, bf16[4,512,256]{2,1,0:T(8,128)(2,1)}) custom-call(s32[4]{0:T(128)} %pad_add_fusion.partners, s32[2]{0:T(128)} %pad_add_fusion.1.places, bf16[1024,256]{1,0:T(8,128)(2,1)} %get-tuple-element.431.refs_0_, ...), custom_call_target="tpu_custom_call" | custom-call | flops 3221225472 | bytes 1782579 | tf_op jit(solution)/shard_map/attend_backward/pallas_call | solution.py:470
  739.3 23.7 %attend_backward.7 = (bf16[1024,768]{1,0:T(8,128)(2,1)}, bf16[4,512,256]{2,1,0:T(8,128)(2,1)}, bf16[4,512,256]{2,1,0:T(8,128)(2,1)}, bf16[4,512,256]{2,1,0:T(8,128)(2,1)}, bf16[4,512,256]{2,1,0:T(8,128)(2,1)}) custom-call(s32[4]{0:T(128)} %pad_add_fusion.partners, s32[2]{0:T(128)} %pad_add_fusion.1.places, bf16[1024,256]{1,0:T(8,128)(2,1)} %get-tuple-element.442.refs_0_, ...), custom_call_target="tpu_custom_call" | custom-call | flops 3221225472 | bytes 1782579 | tf_op jit(solution)/shard_map/attend_backward/pallas_call | solution.py:470
  769.7 21.6 %spread.3 = bf16[1024,2048]{1,0:T(8,128)(2,1)} custom-call(s32[4]{0:T(128)} %pad_add_fusion.partners, bf16[1024,768]{1,0:T(8,128)(2,1)} %get-tuple-element.446.refs_0_, bf16[1024,768]{1,0:T(8,128)(2,1)} %get-tuple-element.411.refs_1_, bf16[1024,768]{1,0:T(8,128)(2,1)} %get-tuple-element.424.refs_2_, bf16[1024,768]{1,0:T(8,128)(2,1)} %get-tuple-element.435.refs_3_, ...), custom_call_target="tpu_custom_call" | custom-call | flops 2576980480 | bytes 4613734 | tf_op jit(solution)/shard_map/spread/pallas_call | solution.py:520
  806.3 15.2 %collective-permute-done.84 = bf16[4,512,256]{2,1,0:T(8,128)(2,1)S(1)} collective-permute-done((bf16[4,512,256]{2,1,0:T(8,128)(2,1)S(1)}, bf16[4,512,256]{2,1,0:T(8,128)(2,1)S(1)}, u32[]{:S(2)}, u32[]{:S(2)}) %collective-permute-start.84) | collective-permute-done | bytes 1048608 | tf_op jit(solution)/shard_map/ppermute | solution.py:64
  (491 shorter events, 386.7 us)
Async XLA Ops:
  8.3 40.2 %collective-permute-start.2 = (bf16[4,512,256]{2,1,0:T(8,128)(2,1)S(1)}, bf16[4,512,256]{2,1,0:T(8,128)(2,1)S(1)}, u32[]{:S(2)}, u32[]{:S(2)}) collective-permute-start(bf16[4,512,256]{2,1,0:T(8,128)(2,1)S(1)} %pad_maximum_fusion.1.refs_0_.refs_4_.refs_10_), channel_id=1, source_target_pairs={{0,2},{1,3},{2,4},{3,5},{4,6},{5,7},{6,0},{7,1},{8,10},{9,11},{10,... | collective-permute-start | bytes 3145736 | tf_op jit(solution)/shard_map/ppermute | solution.py:75
  11.3 37.2 %collective-permute-start.1 = (bf16[4,512,256]{2,1,0:T(8,128)(2,1)S(1)}, bf16[4,512,256]{2,1,0:T(8,128)(2,1)S(1)}, u32[]{:S(2)}, u32[]{:S(2)}) collective-permute-start(bf16[4,512,256]{2,1,0:T(8,128)(2,1)S(1)} %pad_maximum_fusion.1.refs_0_.refs_4_.refs_10_), channel_id=1, source_target_pairs={{0,16},{1,9},{2,18},{3,11},{4,20},{5,13},{6,22},{7,15},{8,24},{9,1... | collective-permute-start | bytes 3145736 | tf_op jit(solution)/shard_map/ppermute | solution.py:64
  12.8 35.7 %collective-permute-start = (bf16[4,512,256]{2,1,0:T(8,128)(2,1)S(1)}, bf16[4,512,256]{2,1,0:T(8,128)(2,1)}, u32[]{:S(2)}, u32[]{:S(2)}) collective-permute-start(bf16[4,512,256]{2,1,0:T(8,128)(2,1)S(1)} %pad_maximum_fusion.1.refs_0_.refs_4_.refs_10_), channel_id=1, source_target_pairs={{0,8},{1,17},{2,10},{3,19},{4,12},{5,21},{6,14},{7,23},{8,0},{9,25... | collective-permute-start | bytes 3145736 | tf_op jit(solution)/shard_map/ppermute | solution.py:64
  50.1 35.8 %collective-permute-start.6 = (bf16[4,512,256]{2,1,0:T(8,128)(2,1)}, bf16[4,512,256]{2,1,0:T(8,128)(2,1)}, u32[]{:S(2)}, u32[]{:S(2)}) collective-permute-start(bf16[4,512,256]{2,1,0:T(8,128)(2,1)} %collective-permute-done.refs_1_.refs_5_.refs_11_), channel_id=1, source_target_pairs={{0,16},{1,9},{2,18},{3,11},{4,20},{5,13},{6,22},{7,15},{8,24},{9,1... | collective-permute-start | bytes 3145736 | tf_op jit(solution)/shard_map/ppermute | solution.py:64
  50.6 35.3 %collective-permute-start.9 = (bf16[4,512,256]{2,1,0:T(8,128)(2,1)S(1)}, bf16[4,512,256]{2,1,0:T(8,128)(2,1)}, u32[]{:S(2)}, u32[]{:S(2)}) collective-permute-start(bf16[4,512,256]{2,1,0:T(8,128)(2,1)S(1)} %collective-permute-done.2.refs_0_.refs_8_.refs_10_), channel_id=1, source_target_pairs={{0,2},{1,3},{2,4},{3,5},{4,6},{5,7},{6,0},{7,1},{8,10},{9,11},{10,... | collective-permute-start | bytes 3145736 | tf_op jit(solution)/shard_map/ppermute | solution.py:75
  52.2 45.1 %collective-permute-start.8 = (bf16[4,512,256]{2,1,0:T(8,128)(2,1)S(1)}, bf16[4,512,256]{2,1,0:T(8,128)(2,1)}, u32[]{:S(2)}, u32[]{:S(2)}) collective-permute-start(bf16[4,512,256]{2,1,0:T(8,128)(2,1)S(1)} %collective-permute-done.2.refs_0_.refs_8_.refs_10_), channel_id=1, source_target_pairs={{0,16},{1,9},{2,18},{3,11},{4,20},{5,13},{6,22},{7,15},{8,24},{9,1... | collective-permute-start | bytes 3145736 | tf_op jit(solution)/shard_map/ppermute | solution.py:64
  53.7 43.6 %collective-permute-start.7 = (bf16[4,512,256]{2,1,0:T(8,128)(2,1)S(1)}, bf16[4,512,256]{2,1,0:T(8,128)(2,1)}, u32[]{:S(2)}, u32[]{:S(2)}) collective-permute-start(bf16[4,512,256]{2,1,0:T(8,128)(2,1)S(1)} %collective-permute-done.2.refs_0_.refs_8_.refs_10_), channel_id=1, source_target_pairs={{0,8},{1,17},{2,10},{3,19},{4,12},{5,21},{6,14},{7,23},{8,0},{9,25... | collective-permute-start | bytes 3145736 | tf_op jit(solution)/shard_map/ppermute | solution.py:64
  100.5 34.3 %collective-permute-start.13 = (bf16[4,512,256]{2,1,0:T(8,128)(2,1)}, bf16[4,512,256]{2,1,0:T(8,128)(2,1)}, u32[]{:S(2)}, u32[]{:S(2)}) collective-permute-start(bf16[4,512,256]{2,1,0:T(8,128)(2,1)} %collective-permute-done.9.refs_0_.refs_12_.refs_10_), channel_id=1, source_target_pairs={{0,16},{1,9},{2,18},{3,11},{4,20},{5,13},{6,22},{7,15},{8,24},{9,1... | collective-permute-start | bytes 3145736 | tf_op jit(solution)/shard_map/ppermute | solution.py:64
  101.0 33.8 %collective-permute-start.12 = (bf16[4,512,256]{2,1,0:T(8,128)(2,1)}, bf16[4,512,256]{2,1,0:T(8,128)(2,1)}, u32[]{:S(2)}, u32[]{:S(2)}) collective-permute-start(bf16[4,512,256]{2,1,0:T(8,128)(2,1)} %collective-permute-done.9.refs_0_.refs_12_.refs_10_), channel_id=1, source_target_pairs={{0,8},{1,17},{2,10},{3,19},{4,12},{5,21},{6,14},{7,23},{8,0},{9,25... | collective-permute-start | bytes 3145736 | tf_op jit(solution)/shard_map/ppermute | solution.py:64
  134.8 35.8 %collective-permute-start.17 = (bf16[4,512,256]{2,1,0:T(8,128)(2,1)}, bf16[4,512,256]{2,1,0:T(8,128)(2,1)S(1)}, u32[]{:S(2)}, u32[]{:S(2)}) collective-permute-start(bf16[4,512,256]{2,1,0:T(8,128)(2,1)} %collective-permute-done.14.refs_0_.refs_16_.refs_10_), channel_id=1, source_target_pairs={{0,16},{1,9},{2,18},{3,11},{4,20},{5,13},{6,22},{7,15},{8,24},{9,1... | collective-permute-start | bytes 3145736 | tf_op jit(solution)/shard_map/ppermute | solution.py:64
  136.4 34.3 %collective-permute-start.16 = (bf16[4,512,256]{2,1,0:T(8,128)(2,1)}, bf16[4,512,256]{2,1,0:T(8,128)(2,1)S(1)}, u32[]{:S(2)}, u32[]{:S(2)}) collective-permute-start(bf16[4,512,256]{2,1,0:T(8,128)(2,1)} %collective-permute-done.14.refs_0_.refs_16_.refs_10_), channel_id=1, source_target_pairs={{0,8},{1,17},{2,10},{3,19},{4,12},{5,21},{6,14},{7,23},{8,0},{9,25... | collective-permute-start | bytes 3145736 | tf_op jit(solution)/shard_map/ppermute | solution.py:64
  136.4 34.3 %collective-permute-start.15 = (bf16[4,512,256]{2,1,0:T(8,128)(2,1)}, bf16[4,512,256]{2,1,0:T(8,128)(2,1)S(1)}, u32[]{:S(2)}, u32[]{:S(2)}) collective-permute-start(bf16[4,512,256]{2,1,0:T(8,128)(2,1)} %collective-permute-done.12.refs_1_.refs_13_.refs_11_), channel_id=1, source_target_pairs={{0,16},{1,9},{2,18},{3,11},{4,20},{5,13},{6,22},{7,15},{8,24},{9,1... | collective-permute-start | bytes 3145736 | tf_op jit(solution)/shard_map/ppermute | solution.py:64
  137.2 33.4 %collective-permute-start.18 = (bf16[2048,256]{1,0:T(8,128)(2,1)S(1)}, bf16[2048,256]{1,0:T(8,128)(2,1)S(1)}, u32[]{:S(2)}, u32[]{:S(2)}) collective-permute-start(bf16[2048,256]{1,0:T(8,128)(2,1)S(1)} %get-tuple-element.306.refs_10_.refs_12_.refs_14_), channel_id=1, source_target_pairs={{0,2},{1,3},{2,4},{3,5},{4,6},{5,7},{6,0},{7,1},{8,10},{9,11},{10,... | collective-permute-start | bytes 3145736 | tf_op jit(solution)/shard_map/ppermute | solution.py:75
  376.2 38.0 %collective-permute-start.44 = (bf16[2048,256]{1,0:T(8,128)(2,1)S(1)}, bf16[2048,256]{1,0:T(8,128)(2,1)S(1)}, u32[]{:S(2)}, u32[]{:S(2)}) collective-permute-start(bf16[2048,256]{1,0:T(8,128)(2,1)S(1)} %collective-permute-done.41.refs_3_.refs_1_.refs_5_), channel_id=1, source_target_pairs={{0,2},{1,3},{2,4},{3,5},{4,6},{5,7},{6,0},{7,1},{8,10},{9,11},{10,... | collective-permute-start | bytes 3145736 | tf_op jit(solution)/shard_map/ppermute | solution.py:75
  470.3 41.5 %collective-permute-start.49 = (bf16[512,2048]{1,0:T(8,128)(2,1)S(1)}, bf16[512,2048]{1,0:T(8,128)(2,1)}, u32[]{:S(2)}, u32[]{:S(2)}) collective-permute-start(bf16[512,2048]{1,0:T(8,128)(2,1)S(1)} %add_convert_fusion.6), channel_id=1, source_target_pairs={{0,8},{1,17},{2,10},{3,19},{4,12},{5,21},{6,14},{7,23},{8,0},{9,25... | collective-permute-start | bytes 6291464 | tf_op jit(solution)/shard_map/ppermute | solution.py:64
  471.1 40.7 %collective-permute-start.52 = (bf16[512,2048]{1,0:T(8,128)(2,1)}, bf16[512,2048]{1,0:T(8,128)(2,1)}, u32[]{:S(2)}, u32[]{:S(2)}) collective-permute-start(bf16[512,2048]{1,0:T(8,128)(2,1)} %get-tuple-element.354), channel_id=1, source_target_pairs={{0,1},{1,0},{2,3},{3,2},{4,5},{5,4},{6,7},{7,6},{8,9},{9,8},{10,11... | collective-permute-start | bytes 6291464 | tf_op jit(solution)/shard_map/ppermute | solution.py:67
  471.5 40.2 %collective-permute-start.53 = (bf16[512,2048]{1,0:T(8,128)(2,1)}, bf16[512,2048]{1,0:T(8,128)(2,1)S(1)}, u32[]{:S(2)}, u32[]{:S(2)}) collective-permute-start(bf16[512,2048]{1,0:T(8,128)(2,1)} %get-tuple-element.355), channel_id=1, source_target_pairs={{0,1},{1,0},{2,3},{3,2},{4,5},{5,4},{6,7},{7,6},{8,9},{9,8},{10,11... | collective-permute-start | bytes 6291464 | tf_op jit(solution)/shard_map/ppermute | solution.py:67
  471.6 40.2 %collective-permute-start.54 = (bf16[512,2048]{1,0:T(8,128)(2,1)}, bf16[512,2048]{1,0:T(8,128)(2,1)}, u32[]{:S(2)}, u32[]{:S(2)}) collective-permute-start(bf16[512,2048]{1,0:T(8,128)(2,1)} %get-tuple-element.356), channel_id=1, source_target_pairs={{0,1},{1,0},{2,3},{3,2},{4,5},{5,4},{6,7},{7,6},{8,9},{9,8},{10,11... | collective-permute-start | bytes 6291464 | tf_op jit(solution)/shard_map/ppermute | solution.py:67
  474.5 37.3 %collective-permute-start.50 = (bf16[2048,256]{1,0:T(8,128)(2,1)}, bf16[2048,256]{1,0:T(8,128)(2,1)}, u32[]{:S(2)}, u32[]{:S(2)}) collective-permute-start(bf16[2048,256]{1,0:T(8,128)(2,1)} %add_convert_fusion.21), channel_id=1, source_target_pairs={{0,2},{1,3},{2,4},{3,5},{4,6},{5,7},{6,0},{7,1},{8,10},{9,11},{10,... | collective-permute-start | bytes 3145736 | tf_op jit(solution)/shard_map/ppermute | solution.py:75
  541.1 38.3 %collective-permute-start.58 = (bf16[512,2048]{1,0:T(8,128)(2,1)S(1)}, bf16[512,2048]{1,0:T(8,128)(2,1)S(1)}, u32[]{:S(2)}, u32[]{:S(2)}) collective-permute-start(bf16[512,2048]{1,0:T(8,128)(2,1)S(1)} %add_convert_fusion.3), channel_id=1, source_target_pairs={{0,8},{1,17},{2,10},{3,19},{4,12},{5,21},{6,14},{7,23},{8,0},{9,25... | collective-permute-start | bytes 6291464 | tf_op jit(solution)/shard_map/ppermute | solution.py:64
  542.2 33.4 %collective-permute-start.59 = (bf16[512,256]{1,0:T(8,128)(2,1)S(1)}, bf16[512,256]{1,0:T(8,128)(2,1)S(1)}, u32[]{:S(2)}, u32[]{:S(2)}) collective-permute-start(bf16[512,256]{1,0:T(8,128)(2,1)S(1)} %get-tuple-element.377), channel_id=1, source_target_pairs={{0,8},{8,0},{16,24},{24,16},{1,9},{9,1},{17,25},{25,17},{2,10},{10... | collective-permute-start | bytes 786440 | tf_op jit(solution)/shard_map/ppermute | solution.py:56
  544.5 34.9 %collective-permute-start.61 = (bf16[512,256]{1,0:T(8,128)(2,1)S(1)}, bf16[512,256]{1,0:T(8,128)(2,1)S(1)}, u32[]{:S(2)}, u32[]{:S(2)}) collective-permute-start(bf16[512,256]{1,0:T(8,128)(2,1)S(1)} %get-tuple-element.379), channel_id=1, source_target_pairs={{0,24},{8,16},{16,8},{24,0},{1,25},{9,17},{17,9},{25,1},{2,26},{10... | collective-permute-start | bytes 786440 | tf_op jit(solution)/shard_map/ppermute | solution.py:56
  609.0 33.2 %collective-permute-start.65 = (bf16[512,2048]{1,0:T(8,128)(2,1)}, bf16[512,2048]{1,0:T(8,128)(2,1)S(1)}, u32[]{:S(2)}, u32[]{:S(2)}) collective-permute-start(bf16[512,2048]{1,0:T(8,128)(2,1)} %add_convert_fusion.4), channel_id=1, source_target_pairs={{0,8},{1,17},{2,10},{3,19},{4,12},{5,21},{6,14},{7,23},{8,0},{9,25... | collective-permute-start | bytes 6291464 | tf_op jit(solution)/shard_map/ppermute | solution.py:64
  793.0 38.1 %collective-permute-start.79 = (bf16[512,2048]{1,0:T(8,128)(2,1)S(1)}, bf16[512,2048]{1,0:T(8,128)(2,1)S(1)}, u32[]{:S(2)}, u32[]{:S(2)}) collective-permute-start(bf16[512,2048]{1,0:T(8,128)(2,1)S(1)} %constant_dynamic-slice_fusion), channel_id=1, source_target_pairs={{0,1},{1,0},{2,3},{3,2},{4,5},{5,4},{6,7},{7,6},{8,9},{9,8},{10,11... | collective-permute-start | bytes 6291464 | tf_op jit(solution)/shard_map/ppermute | solution.py:67
  (177 other events, 3600.1 us)

commit v7 on v6

--- a/solution.py
+++ b/solution.py
@@ -770,7 +770,7 @@
         out[...] = total[:, i * width : (i + 1) * width].astype(low)
 
 
-def weight_terms(lefts, rights, part, pieces, width):
+def weight_terms(lefts, rights, part, pieces, width, mebibytes=40):
     rows, depth = lefts[0].shape
     tile = min(depth, 512)
     across = pieces * width
@@ -786,7 +786,7 @@
             for v in rights
         ],
         out_specs=[pl.BlockSpec((tile, width), lambda i: (i, 0))] * pieces,
-        compiler_params=params(40),
+        compiler_params=params(mebibytes),
         cost_estimate=cost(2 * rows * len(lefts) * depth * across, [*lefts, *rights]),
         name="weight_terms",
     )(*lefts, *rights)
@@ -975,7 +975,9 @@
     grad_items = items_of(grad_blocks, planes)
     shrink_terms = []
     for i in range(parts):
-        shrink_terms += weight_terms(grad_items, after(hidden, *deps), i, pieces, hidden_width)
+        shrink_terms += weight_terms(
+            grad_items, after(hidden, *deps), i, pieces, hidden_width, 60
+        )
     deps = moved + shrink_terms
     shrink_back = RingSum(mv)
     shrink_back.terms.update(zip(ring_order, shrink_terms))
@@ -1033,8 +1035,7 @@
         feed_sums.blocks[i] = chip_sum(back_early[i])
     deps = moved + [terms_middle] + [feed_sums.blocks[i] for i in early[1:]]
     deps += [fed_sums.blocks[i] for i in early if i] + [shrink_sum]
-    shrink_moved, (shrink_grad,) = columns(shrink_sum, *deps)
-    moved = feed_sums(1, *deps) + shrink_moved
+    moved = feed_sums(1, *deps)
     back_middle = [after(v, *deps) for v in back_middle]
     back_middle = [trade(back_middle[i * S : (i + 1) * S]) for i in range(len(middle))]
     gate_up = (terms_early, terms_middle, terms_late)
@@ -1094,13 +1095,27 @@
         attn_sums[k].blocks[:] = terms
         return [grad_proj[k]]
 
-    moved = fed_sums(1, *deps) + gate_back(*deps)
+    shrink_pieces = [
+        lax.dynamic_slice_in_dim(shrink_sum, (mv.f ^ d) * row_block, row_block, 0) for d in planes
+    ]
+
+    def give_shrink(which, *deps):
+        found = []
+        for d in planes:
+            if d and d % 3 == which:
+                shrink_pieces[d] = mv.plane(after(shrink_pieces[d], *deps), d)
+                found.append(shrink_pieces[d])
+        return found
+
+    moved = fed_sums(1, *deps) + gate_back(*deps) + give_shrink(1, *deps)
     deps = moved + attend_back(order[0])
-    moved = attn_sums[order[0]](2, *deps) + up_back(*deps)
+    moved = attn_sums[order[0]](2, *deps) + up_back(*deps) + give_shrink(2, *deps)
     deps = moved + attend_back(order[1])
     layer_output = (resid + fed_sums.total()).astype(low)
     moved = attn_sums[order[0]](1, *deps) + attn_sums[order[1]](1, *deps) + gate_back(*deps)
+    moved += give_shrink(0, *deps)
     deps = moved + attend_back(order[2])
+    shrink_grad = mv.place(shrink_pieces, 1, mv.f).astype(f32)
     moved = attn_sums[order[1]](2, *deps) + up_back(*deps)
     deps = moved + attend_back(order[3])
     attn_back = RingSum(mv)
@@ -1131,8 +1146,9 @@
     gains_shape = norm_gains.shape
     lines = [gain.reshape(-1, 128) for gain in (gain_one, gain_two)]
     sums = jnp.concatenate(lines + [jnp.full((8, 128), owned_squares)], axis=0)
-    sums = total_of(mv, after(sums, *moved))
+    sums = total_of(mv, after(sums, *moved[:1]))
     gains_grad, squares = sums[:-8].reshape(gains_shape), sums[-1, 0]
+    squares = after(squares, *moved[1:])
     norm = jnp.sqrt(squares + jnp.sum(gains_grad * gains_grad))
     factor = jnp.minimum(1.0, clip_bound / (norm + 1e-06))
     inward_new = adamw(

time: 919 us -> 910 us (level)
  Pallas kernels: 416 us -> 429 us
  waiting for transfers between devices: 256 us -> 243 us
  local copies, waits for them, and re-layouts: 58.2 us -> 48.7 us
    ppermute x12, waiting for transfers between devices: 53.5 us -> 41.2 us  [plane(): return lax.ppermute(value, 'fsdp', [(i, i ^ mask) for i in range(self.F)])]
    unnamed x218 -> x176, local copies, waits for them, and re-layouts: 28.3 us -> 16.8 us
  transfers between devices with their start and end apart: 92 -> 92, of which waited for: 28 -> 28; matrix products, arithmetic and copies ran while one was open for 10% -> 11% of each run, Pallas kernels for 44% -> 47%
where the time goes in v7:
time: 910 us; the launch traced here: 906 us
  Pallas kernels  429 us (47%)
  waiting for transfers between devices  243 us (27%)
  other arithmetic  104 us (11%)
  starting transfers between devices  76.1 us (8%)
  local copies, waits for them, and re-layouts  48.7 us (5%)
    ppermute x24, waiting for transfers between devices, ring(): return lax.ppermute(value, 'tp', step)  113 us
    pallas_call x4, Pallas kernels, attend_backward(): pl.pallas_call(functools.partial(backward_kernel, block, count, len(grads...  95.4 us
    ppermute x36, waiting for transfers between devices, hop(): return lax.ppermute(value, ('fsdp', 'tp'), pairs)  78.6 us
    pallas_call x3, Pallas kernels, feed_backward(): pl.pallas_call(functools.partial(feed_back_kernel, count, len(shrink), le...  77.6 us
    pallas_call x4, Pallas kernels, weight_terms(): pl.pallas_call(functools.partial(weight_kernel, len(lefts), len(rights)),...  74.7 us
    pallas_call x4, Pallas kernels, attend_forward(): pl.pallas_call(functools.partial(forward_kernel, block, len(weights)), ou...  62.1 us
    pallas_call x2, Pallas kernels, feed_forward(): pl.pallas_call(functools.partial(feed_kernel, count, len(expand), width),...  46.4 us
    ppermute x12, waiting for transfers between devices, plane(): return lax.ppermute(value, 'fsdp', [(i, i ^ mask) for i in range(self.F)])  41.2 us
  transfers between devices with their start and end apart: 92, of which 28 were waited for; matrix products, arithmetic and copies ran while one was open for 11% of the time, Pallas kernels for 47%

profile of v7, /device:TPU:0, one launch (start us, length us, event | category | flops | bytes accessed | tf_op | source)
XLA Modules:
  0.0 905.7 jit_solution(7929953505592681783)
XLA Ops:
  21.9 25.2 %collective-permute-done.3 = bf16[2,512,256]{2,1,0:T(8,128)(2,1)S(1)} collective-permute-done((bf16[2,512,256]{2,1,0:T(8,128)(2,1)}, bf16[2,512,256]{2,1,0:T(8,128)(2,1)S(1)}, u32[]{:S(2)}, u32[]{:S(2)}) %collective-permute-start.3) | collective-permute-done | bytes 524320 | tf_op jit(solution)/shard_map/ppermute | solution.py:56
  64.7 21.2 %collective-permute-done.6.refs_3_.refs_7_.refs_13_ = bf16[4,512,256]{2,1,0:T(8,128)(2,1)} collective-permute-done((bf16[4,512,256]{2,1,0:T(8,128)(2,1)}, bf16[4,512,256]{2,1,0:T(8,128)(2,1)}, u32[]{:S(2)}, u32[]{:S(2)}) %collective-permute-start.6) | collective-permute-done | bytes 1048608 | tf_op jit(solution)/shard_map/ppermute | solution.py:64
  109.8 15.5 %attend_forward.4 = (bf16[1024,256]{1,0:T(8,128)(2,1)}, bf16[1024,256]{1,0:T(8,128)(2,1)}, bf16[1024,256]{1,0:T(8,128)(2,1)}, bf16[1024,256]{1,0:T(8,128)(2,1)}, f32[1024,128]{1,0:T(8,128)}) custom-call(s32[4]{0:T(128)} %pad_add_fusion.partners, bf16[1024,2048]{1,0:T(8,128)(2,1)} %constant_dynamic-update-slice_fusion.10.acts.refs_5_, ...), custom_call_target="tpu_custom_call" | custom-call | flops 1503238528 | bytes 2097152 | tf_op jit(solution)/shard_map/attend_forward/pallas_call | solution.py:370
  139.0 15.5 %attend_forward.5 = (bf16[1024,256]{1,0:T(8,128)(2,1)}, bf16[1024,256]{1,0:T(8,128)(2,1)}, bf16[1024,256]{1,0:T(8,128)(2,1)}, bf16[1024,256]{1,0:T(8,128)(2,1)}, f32[1024,128]{1,0:T(8,128)}) custom-call(s32[4]{0:T(128)} %pad_add_fusion.partners, bf16[1024,2048]{1,0:T(8,128)(2,1)} %constant_dynamic-update-slice_fusion.10.acts.refs_5_, ...), custom_call_target="tpu_custom_call" | custom-call | flops 1503238528 | bytes 2097152 | tf_op jit(solution)/shard_map/attend_forward/pallas_call | solution.py:370
  154.5 16.1 %collective-permute-done.15.refs_3_.refs_15_.refs_13_ = bf16[4,512,256]{2,1,0:T(8,128)(2,1)S(1)} collective-permute-done((bf16[4,512,256]{2,1,0:T(8,128)(2,1)}, bf16[4,512,256]{2,1,0:T(8,128)(2,1)S(1)}, u32[]{:S(2)}, u32[]{:S(2)}) %collective-permute-start.15) | collective-permute-done | bytes 1048608 | tf_op jit(solution)/shard_map/ppermute | solution.py:64
  179.4 15.5 %attend_forward.6 = (bf16[1024,256]{1,0:T(8,128)(2,1)}, bf16[1024,256]{1,0:T(8,128)(2,1)}, bf16[1024,256]{1,0:T(8,128)(2,1)}, bf16[1024,256]{1,0:T(8,128)(2,1)}, f32[1024,128]{1,0:T(8,128)}) custom-call(s32[4]{0:T(128)} %pad_add_fusion.partners, bf16[1024,2048]{1,0:T(8,128)(2,1)} %constant_dynamic-update-slice_fusion.10.acts.refs_5_, ...), custom_call_target="tpu_custom_call" | custom-call | flops 1503238528 | bytes 2097152 | tf_op jit(solution)/shard_map/attend_forward/pallas_call | solution.py:370
  200.3 15.6 %attend_forward.7 = (bf16[1024,256]{1,0:T(8,128)(2,1)}, bf16[1024,256]{1,0:T(8,128)(2,1)}, bf16[1024,256]{1,0:T(8,128)(2,1)}, bf16[1024,256]{1,0:T(8,128)(2,1)}, f32[1024,128]{1,0:T(8,128)}) custom-call(s32[4]{0:T(128)} %pad_add_fusion.partners, bf16[1024,2048]{1,0:T(8,128)(2,1)} %constant_dynamic-update-slice_fusion.10.acts.refs_5_, ...), custom_call_target="tpu_custom_call" | custom-call | flops 1503238528 | bytes 2097152 | tf_op jit(solution)/shard_map/attend_forward/pallas_call | solution.py:370
  236.2 19.3 %collective-permute-done.27.refs_5_.refs_7_.refs_9_ = bf16[2048,256]{1,0:T(8,128)(2,1)S(1)} collective-permute-done((bf16[2048,256]{1,0:T(8,128)(2,1)S(1)}, bf16[2048,256]{1,0:T(8,128)(2,1)S(1)}, u32[]{:S(2)}, u32[]{:S(2)}) %collective-permute-start.27) | collective-permute-done | bytes 1048608 | tf_op jit(solution)/shard_map/ppermute | solution.py:75
  257.3 27.4 %collective-permute-done.31.refs_7_.refs_9_.refs_11_ = bf16[2048,256]{1,0:T(8,128)(2,1)S(1)} collective-permute-done((bf16[2048,256]{1,0:T(8,128)(2,1)S(1)}, bf16[2048,256]{1,0:T(8,128)(2,1)S(1)}, u32[]{:S(2)}, u32[]{:S(2)}) %collective-permute-start.31) | collective-permute-done | bytes 1048608 | tf_op jit(solution)/shard_map/ppermute | solution.py:75
  288.3 27.4 %collective-permute-done.35.refs_9_.refs_11_.refs_13_ = bf16[2048,256]{1,0:T(8,128)(2,1)S(1)} collective-permute-done((bf16[2048,256]{1,0:T(8,128)(2,1)S(1)}, bf16[2048,256]{1,0:T(8,128)(2,1)S(1)}, u32[]{:S(2)}, u32[]{:S(2)}) %collective-permute-start.35) | collective-permute-done | bytes 1048608 | tf_op jit(solution)/shard_map/ppermute | solution.py:75
  317.9 23.3 %feed_forward.2 = (bf16[2048,1024]{1,0:T(8,128)(2,1)}, bf16[2048,1024]{1,0:T(8,128)(2,1)}, bf16[2048,1024]{1,0:T(8,128)(2,1)}) custom-call(bf16[512,2048]{1,0:T(8,128)(2,1)S(1)} %multiply_convert_fusion.refs_0_, bf16[512,2048]{1,0:T(8,128)(2,1)S(1)} %collective-permute-done.29.refs_1_, bf16[512,2048]{1,0:T(8,128)(2,1)} %copy-done.14, ...), custom_call_target="tpu_custom_call" | custom-call | flops 3435973888 | bytes 3355443 | tf_op jit(solution)/shard_map/feed_forward/pallas_call | solution.py:635
  350.2 23.1 %feed_forward.3 = (bf16[2048,1024]{1,0:T(8,128)(2,1)}, bf16[2048,1024]{1,0:T(8,128)(2,1)}, bf16[2048,1024]{1,0:T(8,128)(2,1)}) custom-call(bf16[512,2048]{1,0:T(8,128)(2,1)S(1)} %collective-permute-done.36.refs_0_.refs_4_, bf16[512,2048]{1,0:T(8,128)(2,1)S(1)} %collective-permute-done.40.refs_1_.refs_5_, ...), custom_call_target="tpu_custom_call" | custom-call | flops 3435973888 | bytes 3355443 | tf_op jit(solution)/shard_map/feed_forward/pallas_call | solution.py:635
  409.3 21.7 %feed_backward.3 = (bf16[1024,2048]{1,0:T(8,128)(2,1)}, bf16[512,2048]{1,0:T(8,128)(2,1)}, bf16[512,2048]{1,0:T(8,128)(2,1)}) custom-call(bf16[512,2048]{1,0:T(8,128)(2,1)} %copy-done.41, bf16[512,2048]{1,0:T(8,128)(2,1)} %copy-done.42, bf16[2048,256]{1,0:T(8,128)(2,1)S(1)} %copy-done.13, bf16[2048,256]{1,0:T(8,128)(2,1)} %collective-permute-done.41.refs_3_.refs_1_.refs_5_, ...), custom_call_target="tpu_custom_call" | custom-call | flops 2576980480 | bytes 4194304 | tf_op jit(solution)/shard_map/feed_backward/pallas_call | solution.py:696
  469.9 35.0 %feed_backward.4 = (bf16[2048,2048]{1,0:T(8,128)(2,1)}, bf16[512,2048]{1,0:T(8,128)(2,1)}, bf16[512,2048]{1,0:T(8,128)(2,1)}, bf16[512,2048]{1,0:T(8,128)(2,1)}, bf16[512,2048]{1,0:T(8,128)(2,1)}) custom-call(bf16[512,2048]{1,0:T(8,128)(2,1)} %refs_0_.2, bf16[512,2048]{1,0:T(8,128)(2,1)} %copy-done.37, bf16[512,2048]{1,0:T(8,128)(2,1)} %collective-permute-done.24.refs_2_, ...), custom_call_target="tpu_custom_call" | custom-call | flops 5153960960 | bytes 5033164 | tf_op jit(solution)/shard_map/feed_backward/pallas_call | solution.py:696
  513.4 20.9 %feed_backward.5 = (bf16[1024,2048]{1,0:T(8,128)(2,1)}, bf16[512,2048]{1,0:T(8,128)(2,1)}, bf16[512,2048]{1,0:T(8,128)(2,1)}) custom-call(bf16[512,2048]{1,0:T(8,128)(2,1)} %copy-done.39, bf16[512,2048]{1,0:T(8,128)(2,1)} %copy-done.40, bf16[2048,256]{1,0:T(8,128)(2,1)S(1)} %copy-done.13, bf16[2048,256]{1,0:T(8,128)(2,1)} %collective-permute-done.41.refs_3_.refs_1_.refs_5_, ...), custom_call_target="tpu_custom_call" | custom-call | flops 2576980480 | bytes 4194304 | tf_op jit(solution)/shard_map/feed_backward/pallas_call | solution.py:696
  540.3 22.8 %weight_terms.6 = (bf16[2048,256]{1,0:T(8,128)(2,1)S(1)}, bf16[2048,256]{1,0:T(8,128)(2,1)S(1)}, bf16[2048,256]{1,0:T(8,128)(2,1)S(1)}, bf16[2048,256]{1,0:T(8,128)(2,1)S(1)}) custom-call(bf16[512,2048]{1,0:T(8,128)(2,1)S(1)} %copy-done.5, bf16[512,2048]{1,0:T(8,128)(2,1)S(1)} %copy-done.17, bf16[512,2048]{1,0:T(8,128)(2,1)S(1)} %copy-done.15, ...), custom_call_target="tpu_custom_call" | custom-call | flops 3435973888 | bytes 6710886 | tf_op jit(solution)/shard_map/weight_terms/pallas_call | solution.py:777
  575.0 22.9 %weight_terms.7 = (bf16[2048,256]{1,0:T(8,128)(2,1)S(1)}, bf16[2048,256]{1,0:T(8,128)(2,1)S(1)}, bf16[2048,256]{1,0:T(8,128)(2,1)S(1)}, bf16[2048,256]{1,0:T(8,128)(2,1)S(1)}) custom-call(bf16[512,2048]{1,0:T(8,128)(2,1)S(1)} %copy-done.5, bf16[512,2048]{1,0:T(8,128)(2,1)S(1)} %copy-done.17, bf16[512,2048]{1,0:T(8,128)(2,1)S(1)} %copy-done.15, ...), custom_call_target="tpu_custom_call" | custom-call | flops 3435973888 | bytes 6710886 | tf_op jit(solution)/shard_map/weight_terms/pallas_call | solution.py:777
  610.7 20.0 %collective-permute-done.63 = bf16[2048,256]{1,0:T(8,128)(2,1)S(1)} collective-permute-done((bf16[2048,256]{1,0:T(8,128)(2,1)S(1)}, bf16[2048,256]{1,0:T(8,128)(2,1)S(1)}, u32[]{:S(2)}, u32[]{:S(2)}) %collective-permute-start.63) | collective-permute-done | bytes 1048608 | tf_op jit(solution)/shard_map/ppermute | solution.py:75
  639.8 23.9 %attend_backward.4 = (bf16[1024,768]{1,0:T(8,128)(2,1)}, bf16[4,512,256]{2,1,0:T(8,128)(2,1)}, bf16[4,512,256]{2,1,0:T(8,128)(2,1)}, bf16[4,512,256]{2,1,0:T(8,128)(2,1)}, bf16[4,512,256]{2,1,0:T(8,128)(2,1)}) custom-call(s32[4]{0:T(128)} %pad_add_fusion.partners, s32[2]{0:T(128)} %pad_add_fusion.1.places, bf16[1024,256]{1,0:T(8,128)(2,1)} %get-tuple-element.405.refs_0_, ...), custom_call_target="tpu_custom_call" | custom-call | flops 3221225472 | bytes 1782579 | tf_op jit(solution)/shard_map/attend_backward/pallas_call | solution.py:470
  669.7 23.8 %attend_backward.5 = (bf16[1024,768]{1,0:T(8,128)(2,1)}, bf16[4,512,256]{2,1,0:T(8,128)(2,1)}, bf16[4,512,256]{2,1,0:T(8,128)(2,1)}, bf16[4,512,256]{2,1,0:T(8,128)(2,1)}, bf16[4,512,256]{2,1,0:T(8,128)(2,1)}) custom-call(s32[4]{0:T(128)} %pad_add_fusion.partners, s32[2]{0:T(128)} %pad_add_fusion.1.places, bf16[1024,256]{1,0:T(8,128)(2,1)} %get-tuple-element.412.refs_0_, ...), custom_call_target="tpu_custom_call" | custom-call | flops 3221225472 | bytes 1782579 | tf_op jit(solution)/shard_map/attend_backward/pallas_call | solution.py:470
  701.4 24.0 %attend_backward.6 = (bf16[1024,768]{1,0:T(8,128)(2,1)}, bf16[4,512,256]{2,1,0:T(8,128)(2,1)}, bf16[4,512,256]{2,1,0:T(8,128)(2,1)}, bf16[4,512,256]{2,1,0:T(8,128)(2,1)}, bf16[4,512,256]{2,1,0:T(8,128)(2,1)}) custom-call(s32[4]{0:T(128)} %pad_add_fusion.partners, s32[2]{0:T(128)} %pad_add_fusion.1.places, bf16[1024,256]{1,0:T(8,128)(2,1)} %get-tuple-element.432.refs_0_, ...), custom_call_target="tpu_custom_call" | custom-call | flops 3221225472 | bytes 1782579 | tf_op jit(solution)/shard_map/attend_backward/pallas_call | solution.py:470
  731.8 23.7 %attend_backward.7 = (bf16[1024,768]{1,0:T(8,128)(2,1)}, bf16[4,512,256]{2,1,0:T(8,128)(2,1)}, bf16[4,512,256]{2,1,0:T(8,128)(2,1)}, bf16[4,512,256]{2,1,0:T(8,128)(2,1)}, bf16[4,512,256]{2,1,0:T(8,128)(2,1)}) custom-call(s32[4]{0:T(128)} %pad_add_fusion.partners, s32[2]{0:T(128)} %pad_add_fusion.1.places, bf16[1024,256]{1,0:T(8,128)(2,1)} %get-tuple-element.443.refs_0_, ...), custom_call_target="tpu_custom_call" | custom-call | flops 3221225472 | bytes 1782579 | tf_op jit(solution)/shard_map/attend_backward/pallas_call | solution.py:470
  762.9 21.6 %spread.3 = bf16[1024,2048]{1,0:T(8,128)(2,1)} custom-call(s32[4]{0:T(128)} %pad_add_fusion.partners, bf16[1024,768]{1,0:T(8,128)(2,1)} %get-tuple-element.447.refs_0_, bf16[1024,768]{1,0:T(8,128)(2,1)} %get-tuple-element.410.refs_1_, bf16[1024,768]{1,0:T(8,128)(2,1)} %get-tuple-element.424.refs_2_, bf16[1024,768]{1,0:T(8,128)(2,1)} %get-tuple-element.436.refs_3_, ...), custom_call_target="tpu_custom_call" | custom-call | flops 2576980480 | bytes 4613734 | tf_op jit(solution)/shard_map/spread/pallas_call | solution.py:520
  856.9 17.7 %total.1 = f32[40,128]{1,0:T(8,128)S(1)} custom-call(f32[40,128]{1,0:T(8,128)S(1)} %maximum_maximum_fusion.value), custom_call_target="tpu_custom_call" | custom-call | flops 35840 | bytes 40960 | tf_op jit(solution)/shard_map/total/pallas_call | solution.py:168
  (449 shorter events, 376.9 us)
Async XLA Ops:
  8.3 40.2 %collective-permute-start.2 = (bf16[4,512,256]{2,1,0:T(8,128)(2,1)S(1)}, bf16[4,512,256]{2,1,0:T(8,128)(2,1)}, u32[]{:S(2)}, u32[]{:S(2)}) collective-permute-start(bf16[4,512,256]{2,1,0:T(8,128)(2,1)S(1)} %pad_maximum_fusion.1.refs_0_.refs_4_.refs_10_), channel_id=1, source_target_pairs={{0,2},{1,3},{2,4},{3,5},{4,6},{5,7},{6,0},{7,1},{8,10},{9,11},{10,... | collective-permute-start | bytes 3145736 | tf_op jit(solution)/shard_map/ppermute | solution.py:75
  11.3 37.2 %collective-permute-start.1 = (bf16[4,512,256]{2,1,0:T(8,128)(2,1)S(1)}, bf16[4,512,256]{2,1,0:T(8,128)(2,1)S(1)}, u32[]{:S(2)}, u32[]{:S(2)}) collective-permute-start(bf16[4,512,256]{2,1,0:T(8,128)(2,1)S(1)} %pad_maximum_fusion.1.refs_0_.refs_4_.refs_10_), channel_id=1, source_target_pairs={{0,16},{1,9},{2,18},{3,11},{4,20},{5,13},{6,22},{7,15},{8,24},{9,1... | collective-permute-start | bytes 3145736 | tf_op jit(solution)/shard_map/ppermute | solution.py:64
  12.8 35.7 %collective-permute-start = (bf16[4,512,256]{2,1,0:T(8,128)(2,1)S(1)}, bf16[4,512,256]{2,1,0:T(8,128)(2,1)}, u32[]{:S(2)}, u32[]{:S(2)}) collective-permute-start(bf16[4,512,256]{2,1,0:T(8,128)(2,1)S(1)} %pad_maximum_fusion.1.refs_0_.refs_4_.refs_10_), channel_id=1, source_target_pairs={{0,8},{1,17},{2,10},{3,19},{4,12},{5,21},{6,14},{7,23},{8,0},{9,25... | collective-permute-start | bytes 3145736 | tf_op jit(solution)/shard_map/ppermute | solution.py:64
  50.1 35.8 %collective-permute-start.6 = (bf16[4,512,256]{2,1,0:T(8,128)(2,1)}, bf16[4,512,256]{2,1,0:T(8,128)(2,1)}, u32[]{:S(2)}, u32[]{:S(2)}) collective-permute-start(bf16[4,512,256]{2,1,0:T(8,128)(2,1)} %collective-permute-done.refs_1_.refs_5_.refs_11_), channel_id=1, source_target_pairs={{0,16},{1,9},{2,18},{3,11},{4,20},{5,13},{6,22},{7,15},{8,24},{9,1... | collective-permute-start | bytes 3145736 | tf_op jit(solution)/shard_map/ppermute | solution.py:64
  50.6 35.3 %collective-permute-start.9 = (bf16[4,512,256]{2,1,0:T(8,128)(2,1)}, bf16[4,512,256]{2,1,0:T(8,128)(2,1)}, u32[]{:S(2)}, u32[]{:S(2)}) collective-permute-start(bf16[4,512,256]{2,1,0:T(8,128)(2,1)} %collective-permute-done.2.refs_0_.refs_8_.refs_10_), channel_id=1, source_target_pairs={{0,2},{1,3},{2,4},{3,5},{4,6},{5,7},{6,0},{7,1},{8,10},{9,11},{10,... | collective-permute-start | bytes 3145736 | tf_op jit(solution)/shard_map/ppermute | solution.py:75
  52.2 45.1 %collective-permute-start.8 = (bf16[4,512,256]{2,1,0:T(8,128)(2,1)}, bf16[4,512,256]{2,1,0:T(8,128)(2,1)}, u32[]{:S(2)}, u32[]{:S(2)}) collective-permute-start(bf16[4,512,256]{2,1,0:T(8,128)(2,1)} %collective-permute-done.2.refs_0_.refs_8_.refs_10_), channel_id=1, source_target_pairs={{0,16},{1,9},{2,18},{3,11},{4,20},{5,13},{6,22},{7,15},{8,24},{9,1... | collective-permute-start | bytes 3145736 | tf_op jit(solution)/shard_map/ppermute | solution.py:64
  53.7 43.6 %collective-permute-start.7 = (bf16[4,512,256]{2,1,0:T(8,128)(2,1)}, bf16[4,512,256]{2,1,0:T(8,128)(2,1)}, u32[]{:S(2)}, u32[]{:S(2)}) collective-permute-start(bf16[4,512,256]{2,1,0:T(8,128)(2,1)} %collective-permute-done.2.refs_0_.refs_8_.refs_10_), channel_id=1, source_target_pairs={{0,8},{1,17},{2,10},{3,19},{4,12},{5,21},{6,14},{7,23},{8,0},{9,25... | collective-permute-start | bytes 3145736 | tf_op jit(solution)/shard_map/ppermute | solution.py:64
  100.5 34.3 %collective-permute-start.13 = (bf16[4,512,256]{2,1,0:T(8,128)(2,1)}, bf16[4,512,256]{2,1,0:T(8,128)(2,1)}, u32[]{:S(2)}, u32[]{:S(2)}) collective-permute-start(bf16[4,512,256]{2,1,0:T(8,128)(2,1)} %collective-permute-done.9.refs_0_.refs_12_.refs_10_), channel_id=1, source_target_pairs={{0,16},{1,9},{2,18},{3,11},{4,20},{5,13},{6,22},{7,15},{8,24},{9,1... | collective-permute-start | bytes 3145736 | tf_op jit(solution)/shard_map/ppermute | solution.py:64
  101.0 33.8 %collective-permute-start.12 = (bf16[4,512,256]{2,1,0:T(8,128)(2,1)}, bf16[4,512,256]{2,1,0:T(8,128)(2,1)}, u32[]{:S(2)}, u32[]{:S(2)}) collective-permute-start(bf16[4,512,256]{2,1,0:T(8,128)(2,1)} %collective-permute-done.9.refs_0_.refs_12_.refs_10_), channel_id=1, source_target_pairs={{0,8},{1,17},{2,10},{3,19},{4,12},{5,21},{6,14},{7,23},{8,0},{9,25... | collective-permute-start | bytes 3145736 | tf_op jit(solution)/shard_map/ppermute | solution.py:64
  134.8 35.8 %collective-permute-start.17 = (bf16[4,512,256]{2,1,0:T(8,128)(2,1)}, bf16[4,512,256]{2,1,0:T(8,128)(2,1)S(1)}, u32[]{:S(2)}, u32[]{:S(2)}) collective-permute-start(bf16[4,512,256]{2,1,0:T(8,128)(2,1)} %collective-permute-done.14.refs_0_.refs_16_.refs_10_), channel_id=1, source_target_pairs={{0,16},{1,9},{2,18},{3,11},{4,20},{5,13},{6,22},{7,15},{8,24},{9,1... | collective-permute-start | bytes 3145736 | tf_op jit(solution)/shard_map/ppermute | solution.py:64
  136.4 34.3 %collective-permute-start.16 = (bf16[4,512,256]{2,1,0:T(8,128)(2,1)}, bf16[4,512,256]{2,1,0:T(8,128)(2,1)S(1)}, u32[]{:S(2)}, u32[]{:S(2)}) collective-permute-start(bf16[4,512,256]{2,1,0:T(8,128)(2,1)} %collective-permute-done.14.refs_0_.refs_16_.refs_10_), channel_id=1, source_target_pairs={{0,8},{1,17},{2,10},{3,19},{4,12},{5,21},{6,14},{7,23},{8,0},{9,25... | collective-permute-start | bytes 3145736 | tf_op jit(solution)/shard_map/ppermute | solution.py:64
  136.4 34.3 %collective-permute-start.15 = (bf16[4,512,256]{2,1,0:T(8,128)(2,1)}, bf16[4,512,256]{2,1,0:T(8,128)(2,1)S(1)}, u32[]{:S(2)}, u32[]{:S(2)}) collective-permute-start(bf16[4,512,256]{2,1,0:T(8,128)(2,1)} %collective-permute-done.12.refs_1_.refs_13_.refs_11_), channel_id=1, source_target_pairs={{0,16},{1,9},{2,18},{3,11},{4,20},{5,13},{6,22},{7,15},{8,24},{9,1... | collective-permute-start | bytes 3145736 | tf_op jit(solution)/shard_map/ppermute | solution.py:64
  137.2 33.4 %collective-permute-start.18 = (bf16[2048,256]{1,0:T(8,128)(2,1)S(1)}, bf16[2048,256]{1,0:T(8,128)(2,1)S(1)}, u32[]{:S(2)}, u32[]{:S(2)}) collective-permute-start(bf16[2048,256]{1,0:T(8,128)(2,1)S(1)} %get-tuple-element.307.refs_10_.refs_12_.refs_14_), channel_id=1, source_target_pairs={{0,2},{1,3},{2,4},{3,5},{4,6},{5,7},{6,0},{7,1},{8,10},{9,11},{10,... | collective-permute-start | bytes 3145736 | tf_op jit(solution)/shard_map/ppermute | solution.py:75
  374.8 34.4 %collective-permute-start.44 = (bf16[2048,256]{1,0:T(8,128)(2,1)}, bf16[2048,256]{1,0:T(8,128)(2,1)}, u32[]{:S(2)}, u32[]{:S(2)}) collective-permute-start(bf16[2048,256]{1,0:T(8,128)(2,1)} %collective-permute-done.41.refs_3_.refs_1_.refs_5_), channel_id=1, source_target_pairs={{0,2},{1,3},{2,4},{3,5},{4,6},{5,7},{6,0},{7,1},{8,10},{9,11},{10,... | collective-permute-start | bytes 3145736 | tf_op jit(solution)/shard_map/ppermute | solution.py:75
  464.4 44.5 %collective-permute-start.49 = (bf16[512,2048]{1,0:T(8,128)(2,1)}, bf16[512,2048]{1,0:T(8,128)(2,1)}, u32[]{:S(2)}, u32[]{:S(2)}) collective-permute-start(bf16[512,2048]{1,0:T(8,128)(2,1)} %add_convert_fusion.6), channel_id=1, source_target_pairs={{0,8},{1,17},{2,10},{3,19},{4,12},{5,21},{6,14},{7,23},{8,0},{9,25... | collective-permute-start | bytes 6291464 | tf_op jit(solution)/shard_map/ppermute | solution.py:64
  465.5 43.4 %collective-permute-start.52 = (bf16[512,2048]{1,0:T(8,128)(2,1)}, bf16[512,2048]{1,0:T(8,128)(2,1)}, u32[]{:S(2)}, u32[]{:S(2)}) collective-permute-start(bf16[512,2048]{1,0:T(8,128)(2,1)} %get-tuple-element.355), channel_id=1, source_target_pairs={{0,1},{1,0},{2,3},{3,2},{4,5},{5,4},{6,7},{7,6},{8,9},{9,8},{10,11... | collective-permute-start | bytes 6291464 | tf_op jit(solution)/shard_map/ppermute | solution.py:67
  465.6 43.3 %collective-permute-start.53 = (bf16[512,2048]{1,0:T(8,128)(2,1)S(1)}, bf16[512,2048]{1,0:T(8,128)(2,1)S(1)}, u32[]{:S(2)}, u32[]{:S(2)}) collective-permute-start(bf16[512,2048]{1,0:T(8,128)(2,1)S(1)} %get-tuple-element.356), channel_id=1, source_target_pairs={{0,1},{1,0},{2,3},{3,2},{4,5},{5,4},{6,7},{7,6},{8,9},{9,8},{10,11... | collective-permute-start | bytes 6291464 | tf_op jit(solution)/shard_map/ppermute | solution.py:67
  466.0 42.9 %collective-permute-start.54 = (bf16[512,2048]{1,0:T(8,128)(2,1)}, bf16[512,2048]{1,0:T(8,128)(2,1)}, u32[]{:S(2)}, u32[]{:S(2)}) collective-permute-start(bf16[512,2048]{1,0:T(8,128)(2,1)} %get-tuple-element.357), channel_id=1, source_target_pairs={{0,1},{1,0},{2,3},{3,2},{4,5},{5,4},{6,7},{7,6},{8,9},{9,8},{10,11... | collective-permute-start | bytes 6291464 | tf_op jit(solution)/shard_map/ppermute | solution.py:67
  469.9 39.0 %collective-permute-start.50 = (bf16[2048,256]{1,0:T(8,128)(2,1)}, bf16[2048,256]{1,0:T(8,128)(2,1)}, u32[]{:S(2)}, u32[]{:S(2)}) collective-permute-start(bf16[2048,256]{1,0:T(8,128)(2,1)} %add_convert_fusion.21), channel_id=1, source_target_pairs={{0,2},{1,3},{2,4},{3,5},{4,6},{5,7},{6,0},{7,1},{8,10},{9,11},{10,... | collective-permute-start | bytes 3145736 | tf_op jit(solution)/shard_map/ppermute | solution.py:75
  598.0 32.7 %collective-permute-start.62 = (bf16[512,2048]{1,0:T(8,128)(2,1)S(1)}, bf16[512,2048]{1,0:T(8,128)(2,1)}, u32[]{:S(2)}, u32[]{:S(2)}) collective-permute-start(bf16[512,2048]{1,0:T(8,128)(2,1)S(1)} %add_convert_fusion.4), channel_id=1, source_target_pairs={{0,8},{1,17},{2,10},{3,19},{4,12},{5,21},{6,14},{7,23},{8,0},{9,25... | collective-permute-start | bytes 6291464 | tf_op jit(solution)/shard_map/ppermute | solution.py:64
  630.7 33.0 %collective-permute-start.64 = (bf16[512,2048]{1,0:T(8,128)(2,1)}, bf16[512,2048]{1,0:T(8,128)(2,1)}, u32[]{:S(2)}, u32[]{:S(2)}) collective-permute-start(bf16[512,2048]{1,0:T(8,128)(2,1)} %add_convert_fusion.1), channel_id=1, source_target_pairs={{0,16},{1,9},{2,18},{3,11},{4,20},{5,13},{6,22},{7,15},{8,24},{9,1... | collective-permute-start | bytes 6291464 | tf_op jit(solution)/shard_map/ppermute | solution.py:64
  694.9 33.0 %collective-permute-start.72 = (bf16[4,512,256]{2,1,0:T(8,128)(2,1)S(1)}, bf16[4,512,256]{2,1,0:T(8,128)(2,1)}, u32[]{:S(2)}, u32[]{:S(2)}) collective-permute-start(bf16[4,512,256]{2,1,0:T(8,128)(2,1)S(1)} %add_convert_fusion.18), channel_id=1, source_target_pairs={{0,16},{1,9},{2,18},{3,11},{4,20},{5,13},{6,22},{7,15},{8,24},{9,1... | collective-permute-start | bytes 3145736 | tf_op jit(solution)/shard_map/ppermute | solution.py:64
  786.2 37.9 %collective-permute-start.79 = (bf16[512,2048]{1,0:T(8,128)(2,1)S(1)}, bf16[512,2048]{1,0:T(8,128)(2,1)S(1)}, u32[]{:S(2)}, u32[]{:S(2)}) collective-permute-start(bf16[512,2048]{1,0:T(8,128)(2,1)S(1)} %constant_dynamic-slice_fusion), channel_id=1, source_target_pairs={{0,1},{1,0},{2,3},{3,2},{4,5},{5,4},{6,7},{7,6},{8,9},{9,8},{10,11... | collective-permute-start | bytes 6291464 | tf_op jit(solution)/shard_map/ppermute | solution.py:67
  843.0 32.7 %collective-permute-start.90 = (bf16[512,512]{1,0:T(8,128)(2,1)}, bf16[512,512]{1,0:T(8,128)(2,1)}, u32[]{:S(2)}, u32[]{:S(2)}) collective-permute-start(bf16[512,512]{1,0:T(8,128)(2,1)} %get-tuple-element.470), channel_id=1, source_target_pairs={{0,16},{8,24},{16,0},{24,8},{1,17},{9,25},{17,1},{25,9},{2,18},{10... | collective-permute-start | bytes 1572872 | tf_op jit(solution)/shard_map/ppermute | solution.py:56
  (156 other events, 3622.7 us)
